TPU v7x, 32 devices: a whole 2x2x4 slice. The times are simulated.
32 devices in a mesh: groups: 2 (over y), seq: 4 (over z), head: 2 (over x), side: 2 (over core).
Axes of the slice: x: 2, y: 2, z: 4, core: 2. Of those that a mesh axis runs over, the one named last changes fastest.
Arguments:
- hidden: bfloat16 [32, 8192], P('groups', ('seq', 'side')), parts along dimension 0
- gain: float32 [8192], P(('seq', 'side')), may hold values from 0.25 to 1.75
- w_query: bfloat16 [8192, 8192], P(('seq', 'side'), 'head')
- w_key: bfloat16 [8192, 1024], P(('seq', 'side'), 'head')
- w_value: bfloat16 [8192, 1024], P(('seq', 'side'), 'head'), may hold values from -0.0625 to 0.0625
- w_out: bfloat16 [8192, 8192], P('head', ('seq', 'side')), may hold values from -0.0625 to 0.0625
- prefix_keys: bfloat16 [2, 8, 32768, 128], P('groups', 'head', ('seq', 'side')), parts along dimension 0, may hold values from -6 to 6
- prefix_values: bfloat16 [2, 8, 32768, 128], P('groups', 'head', ('seq', 'side')), parts along dimension 0
- suffix_keys: bfloat16 [256, 8, 128, 128], P(('groups', 'seq', 'side'), 'head'), parts along dimension 0, may hold values from -15 to 15
- suffix_values: bfloat16 [256, 8, 128, 128], P(('groups', 'seq', 'side'), 'head'), parts along dimension 0, may hold values from -6 to 6
- suffix_lengths: int32 [32], P('groups'), parts along dimension 0, may hold values from 1 to 1024, 8192 in all
- page_table: int32 [32, 8], P('groups'), parts along dimension 0, may hold values from 0 to 15, as said below
Outputs:
- hidden_out: bfloat16 [32, 8192], P('groups', ('seq', 'side')), parts along dimension 0
- update: float32 [32, 8192], P('groups', ('seq', 'side')), parts along dimension 0
There are 2 independent parts, one for each index of `groups`. A program takes and returns all parts, laid end to end along the dimension named above; an argument that names none is the same for every part. Nothing has to cross between parts.
Inputs may be any that keep to these rules, and one draw needn't show every extreme that they name: `suffix_lengths`: the lengths sum to 8192 and the longest is exactly 1024. `page_table`: entries are slots within the holding block (s // 2) xor 1; the 2 samples of one block of sample rows use every slot of their holding block exactly once.
All inputs are finite; a program needn't handle non-finite values.
Results may differ from a plain program's by a relative error of at most 0.0081.
Values may be sent and summed in bfloat16 or wider, within the bound.
No kernel may reach another device: no remote copies, remote signals or barrier semaphores. Data moves between devices by JAX's collectives and lax.ppermute only.
A program may use at most 128 MiB of HBM per device.

v0:
```python
import math

import jax
import jax.numpy as jnp
from jax import lax
from jax.sharding import PartitionSpec as P

D = 8192
HD = 128
GROUP = 8
SAMP_DEV = 2
PREFIX = 32768
STEPS = 3


def combined_all(array, axis, combine):
    everything = jax.tree.map(lambda part: lax.all_gather(part, axis), array)
    first = jax.tree.map(lambda part: part[0], everything)

    def lap(k, so_far):
        return combine(so_far, jax.tree.map(lambda part: part[k], everything))

    return lax.fori_loop(1, lax.axis_size(axis), lap, first)


def rotate(vectors, position):
    half = vectors.shape[-1] // 2
    freq = 500000.0 ** (-(jnp.arange(half, dtype=jnp.float32) * 2.0 / vectors.shape[-1]))
    angle = position[..., None] * freq
    cosine = jnp.cos(angle)
    sine = jnp.sin(angle)
    lower = vectors[..., :half]
    upper = vectors[..., half:]
    return jnp.concatenate([lower * cosine - upper * sine, upper * cosine + lower * sine], axis=-1)


def combine(first, second):
    acc_a, top_a, total_a = first
    acc_b, top_b, total_b = second
    top = jnp.maximum(top_a, top_b)
    weight_a = jnp.exp(top_a - top)
    weight_b = jnp.exp(top_b - top)
    return (
        acc_a * weight_a[..., None] + acc_b * weight_b[..., None],
        top,
        total_a * weight_a + total_b * weight_b,
    )


def local(
    hidden,
    gain,
    w_query,
    w_key,
    w_value,
    w_out,
    prefix_keys,
    prefix_values,
    suffix_keys,
    suffix_values,
    suffix_lengths,
    page_table,
):
    samples = hidden.shape[0]
    kv_local = w_key.shape[1] // HD
    query_width = kv_local * GROUP * HD
    key_width = kv_local * HD
    prompts = prefix_keys.shape[0]
    scale = 1.0 / math.sqrt(HD)
    rank = lax.axis_index(("seq", "side"))
    w_proj = jnp.concatenate([w_query, w_key, w_value], axis=1)
    pool_keys, pool_values = (suffix_keys, suffix_values)
    start = jnp.bitwise_xor(rank, 1) * SAMP_DEV
    table_rows = lax.dynamic_slice_in_dim(page_table, start, SAMP_DEV, 0)
    page_keys = pool_keys[table_rows]
    page_values = pool_values[table_rows]
    length_rows = lax.dynamic_slice_in_dim(suffix_lengths, start, SAMP_DEV, 0)
    page_count = page_keys.shape[1]
    page_size = page_keys.shape[3]
    suffix_span = page_count * page_size
    live = (jnp.arange(suffix_span, dtype=jnp.int32)[None, :] < length_rows[:, None])[
        :, None, None, :
    ]
    state = hidden
    update = jnp.zeros(hidden.shape, jnp.float32)
    new_keys = []
    new_values = []
    for step in range(STEPS):
        wide = state.astype(jnp.float32)
        scaled = (wide * gain).astype(jnp.bfloat16)
        partial_value = jnp.dot(scaled, w_proj, preferred_element_type=jnp.float32)
        squares = jnp.sum(wide * wide, axis=1)
        proj, total_sq = lax.psum((partial_value, squares), ("seq", "side"))
        inverse = lax.rsqrt(total_sq / D + 1e-05)[:, None]
        position = (PREFIX + suffix_lengths + step).astype(jnp.float32)
        query = rotate(
            (proj[:, :query_width] * inverse).reshape(samples, kv_local, GROUP, HD),
            position[:, None, None],
        ).astype(jnp.bfloat16)
        new_keys.append(
            rotate(
                (proj[:, query_width : query_width + key_width] * inverse).reshape(
                    samples, kv_local, HD
                ),
                position[:, None],
            ).astype(jnp.bfloat16)
        )
        new_values.append(
            (proj[:, query_width + key_width :] * inverse)
            .reshape(samples, kv_local, HD)
            .astype(jnp.bfloat16)
        )
        stacked_keys = jnp.stack(new_keys, axis=1)
        stacked_values = jnp.stack(new_values, axis=1)
        grouped = query.reshape(prompts, samples // prompts, kv_local, GROUP, HD)
        scores = (
            jnp.einsum(
                "pgkhd,pkld->pgkhl", grouped, prefix_keys, preferred_element_type=jnp.float32
            )
            * scale
        )
        top = jnp.max(scores, axis=-1)
        expo = jnp.exp(scores - top[..., None])
        total = jnp.sum(expo, axis=-1)
        acc = jnp.einsum(
            "pgkhl,pkld->pgkhd",
            expo.astype(jnp.bfloat16),
            prefix_values,
            preferred_element_type=jnp.float32,
        )
        acc = acc.reshape(samples, kv_local, GROUP, HD)
        top = top.reshape(samples, kv_local, GROUP)
        total = total.reshape(samples, kv_local, GROUP)
        own_query = lax.dynamic_slice_in_dim(query, start, SAMP_DEV, 0)
        own_keys = lax.dynamic_slice_in_dim(stacked_keys, start, SAMP_DEV, 0)
        own_values = lax.dynamic_slice_in_dim(stacked_values, start, SAMP_DEV, 0)
        suffix_scores = jnp.einsum(
            "skhd,spkjd->skhpj", own_query, page_keys, preferred_element_type=jnp.float32
        )
        suffix_scores = suffix_scores.reshape(SAMP_DEV, kv_local, GROUP, suffix_span) * scale
        suffix_scores = jnp.where(live, suffix_scores, -jnp.inf)
        fresh_scores = (
            jnp.einsum("skhd,sukd->skhu", own_query, own_keys, preferred_element_type=jnp.float32)
            * scale
        )
        peak = jnp.maximum(jnp.max(suffix_scores, axis=-1), jnp.max(fresh_scores, axis=-1))
        suffix_expo = jnp.exp(suffix_scores - peak[..., None])
        fresh_expo = jnp.exp(fresh_scores - peak[..., None])
        near_total = jnp.sum(suffix_expo, axis=-1) + jnp.sum(fresh_expo, axis=-1)
        near_acc = jnp.einsum(
            "skhpj,spkjd->skhd",
            suffix_expo.astype(jnp.bfloat16).reshape(
                SAMP_DEV, kv_local, GROUP, page_count, page_size
            ),
            page_values,
            preferred_element_type=jnp.float32,
        )
        near_acc = near_acc + jnp.einsum(
            "skhu,sukd->skhd",
            fresh_expo.astype(jnp.bfloat16),
            own_values,
            preferred_element_type=jnp.float32,
        )
        rows_now = (
            lax.dynamic_slice_in_dim(acc, start, SAMP_DEV, 0),
            lax.dynamic_slice_in_dim(top, start, SAMP_DEV, 0),
            lax.dynamic_slice_in_dim(total, start, SAMP_DEV, 0),
        )
        joined = combine(rows_now, (near_acc, peak, near_total))
        acc = lax.dynamic_update_slice_in_dim(acc, joined[0], start, 0)
        top = lax.dynamic_update_slice_in_dim(top, joined[1], start, 0)
        total = lax.dynamic_update_slice_in_dim(total, joined[2], start, 0)
        acc, top, total = combined_all((acc, top, total), ("seq", "side"), combine)
        mixed = (acc / total[..., None]).astype(jnp.bfloat16).reshape(samples, query_width)
        part = jnp.dot(mixed, w_out, preferred_element_type=jnp.float32)
        delta = lax.psum(part, "head")
        update = update + delta
        state = (wide + delta).astype(jnp.bfloat16)
    return (state, update)


def solution(mesh):
    placed = (
        P("groups", ("seq", "side")),
        P(("seq", "side")),
        P(("seq", "side"), "head"),
        P(("seq", "side"), "head"),
        P(("seq", "side"), "head"),
        P("head", ("seq", "side")),
        P("groups", "head", ("seq", "side"), None),
        P("groups", "head", ("seq", "side"), None),
        P(("groups", "seq", "side"), "head", None, None),
        P(("groups", "seq", "side"), "head", None, None),
        P("groups"),
        P("groups", None),
    )
    return jax.shard_map(
        local,
        mesh=mesh,
        in_specs=placed,
        out_specs=(P("groups", ("seq", "side")), P("groups", ("seq", "side"))),
        check_vma=False,
    )
```

profile of v0, /device:TPU:0, one launch (start us, length us, event | category | flops | bytes accessed | tf_op | source)
XLA Modules:
  0.0 455.7 jit_solution(1772908571731529814)
XLA Ops:
  7.3 8.0 %constant_dynamic-update-slice_fusion.8 = bf16[1024,5120]{1,0:T(8,128)(2,1)} fusion(bf16[1024,4096]{1,0:T(8,128)(2,1)} %param.20), kind=kLoop, calls=%fused_computation.277 | loop fusion | bytes 16777216
  17.6 6.2 %fusion.147 = f32[16,5120]{1,0:T(8,128)} fusion(bf16[1024,5120]{1,0:T(8,128)(2,1)} %constant_dynamic-update-slice_fusion.6, bf16[16,1024]{1,0:T(8,128)(2,1)S(1)} %copy-done.9, f32[1024]{0:T(1024)S(1)} %copy-done.8), kind=kOutput, calls=%fused_computation.190 | convolution fusion | flops 167821312 | bytes 10850304 | tf_op jit(solution)/shard_map/dot_general | solution.py:91
  24.0 18.1 %psum.64 = f32[16]{0:T(128)S(1)} all-reduce(f32[16]{0:T(128)S(1)} %fusion.135), channel_id=1, replica_groups=mesh['groups'=2,'seq'=4,'head'=2,'side'=2] {'seq','side'}, use_global_device_ids=true, to_apply=%region_2.0 | all-reduce | flops 16 | bytes 128 | tf_op jit(solution)/shard_map/psum | solution.py:93
  42.5 2.2 gather_fusion
  44.6 3.7 gather_fusion.1
  48.6 33.4 %all-reduce.7.cloned.1.call-done = f32[16,5120]{1,0:T(8,128)} async-done(((f32[16,5120]{1,0:T(8,128)}), f32[16,5120]{1,0:T(8,128)}) %all-reduce.7.cloned.1.call-update) | async-done | bytes 327696 | tf_op jit(solution)/shard_map/psum | solution.py:93
  84.4 3.7 bitcast_reduce_fusion.2
  92.6 2.0 fusion.101
  95.5 14.3 %all_gather.59 = f32[8,16,4,8]{1,3,2,0:T(8,128)S(1)} all-gather(f32[1,16,4,8]{1,3,2,0:T(8,128)S(1)} %copy.357), channel_id=1, replica_groups=mesh['groups'=2,'seq'=4,'head'=2,'side'=2] {'seq','side'}, dimensions={0}, use_global_device_ids=true | all-gather | bytes 18432 | tf_op jit(solution)/shard_map/all_gather | solution.py:17
  110.0 14.6 %all_gather.57 = f32[8,16,4,8]{1,3,2,0:T(8,128)S(1)} all-gather(f32[1,16,4,8]{1,3,2,0:T(8,128)S(1)} %copy.354), channel_id=1, replica_groups=mesh['groups'=2,'seq'=4,'head'=2,'side'=2] {'seq','side'}, dimensions={0}, use_global_device_ids=true | all-gather | bytes 18432 | tf_op jit(solution)/shard_map/all_gather | solution.py:17
  125.9 10.3 %while.57 = (s32[]{:T(128)}, f32[16,4,8,128]{3,2,1,0:T(8,128)S(1)}, f32[16,4,8]{2,1,0:T(4,128)S(1)}, f32[16,4,8]{2,1,0:T(4,128)S(1)}, f32[8,16,4,8]{1,3,2,0:T(8,...) while((s32[]{:T(128)}, f32[16,4,8,128]{3,2,1,0:T(8,128)S(1)}, ...), condition=%wide.region_8.9_spmd, body=%wide.region_7.8_spmd.sunk | while | flops 199685 | bytes 823447 | solution.py:23
  136.3 5.2 %fusion.119 = f32[16,1024]{1,0:T(8,128)} fusion(bf16[4096,1024]{1,0:T(8,128)(2,1)} %param.23, bf16[2,8,32,128]{3,2,1,0:T(8,128)(2,1)S(1)} %bitcast.325), kind=kOutput, calls=%fused_computation.139 | convolution fusion | flops 134217728 | bytes 8585216 | tf_op jit(solution)/shard_map/dot_general | solution.py:175
  141.7 20.2 %all-reduce.9.cloned.1.call-done = f32[16,1024]{1,0:T(8,128)} async-done(((f32[16,1024]{1,0:T(8,128)}), f32[16,1024]{1,0:T(8,128)}) %all-reduce.9.cloned.1.call-update) | async-done | bytes 65552 | tf_op jit(solution)/shard_map/psum | solution.py:176
  162.9 6.2 %fusion.145 = f32[16,5120]{1,0:T(8,128)} fusion(bf16[1024,5120]{1,0:T(8,128)(2,1)} %constant_dynamic-update-slice_fusion.6, bf16[16,1024]{1,0:T(8,128)(2,1)S(1)} %get-tuple-element.732, f32[1024]{0:T(1024)S(1)} %copy-done.8), kind=kOutput, calls=%fused_computation.189 | convolution fusion | flops 167821312 | bytes 10850304 | tf_op jit(solution)/shard_map/dot_general | solution.py:91
  169.2 16.0 %psum.67 = f32[16]{0:T(128)S(1)} all-reduce(f32[16]{0:T(128)S(1)} %get-tuple-element.731), channel_id=1, replica_groups=mesh['groups'=2,'seq'=4,'head'=2,'side'=2] {'seq','side'}, use_global_device_ids=true, to_apply=%region_12.13 | all-reduce | flops 16 | bytes 128 | tf_op jit(solution)/shard_map/psum | solution.py:93
  185.2 39.5 %all-reduce.11.cloned.1.call-done = f32[16,5120]{1,0:T(8,128)} async-done(((f32[16,5120]{1,0:T(8,128)}), f32[16,5120]{1,0:T(8,128)}) %all-reduce.11.cloned.1.call-update) | async-done | bytes 327696 | tf_op jit(solution)/shard_map/psum | solution.py:93
  226.1 3.7 bitcast_reduce_fusion.1
  238.3 14.3 %all_gather.65 = f32[8,16,4,8]{1,3,2,0:T(8,128)S(1)} all-gather(f32[1,16,4,8]{1,3,2,0:T(8,128)S(1)} %copy.386), channel_id=1, replica_groups=mesh['groups'=2,'seq'=4,'head'=2,'side'=2] {'seq','side'}, dimensions={0}, use_global_device_ids=true | all-gather | bytes 18432 | tf_op jit(solution)/shard_map/all_gather | solution.py:17
  252.8 14.6 %all_gather.63 = f32[8,16,4,8]{1,3,2,0:T(8,128)S(1)} all-gather(f32[1,16,4,8]{1,3,2,0:T(8,128)S(1)} %copy.383), channel_id=1, replica_groups=mesh['groups'=2,'seq'=4,'head'=2,'side'=2] {'seq','side'}, dimensions={0}, use_global_device_ids=true | all-gather | bytes 18432 | tf_op jit(solution)/shard_map/all_gather | solution.py:17
  268.7 10.3 %while.58 = (s32[]{:T(128)}, f32[16,4,8,128]{3,2,1,0:T(8,128)S(1)}, f32[16,4,8]{2,1,0:T(4,128)S(1)}, f32[16,4,8]{2,1,0:T(4,128)S(1)}, f32[8,16,4,8]{1,3,2,0:T(8,...) while((s32[]{:T(128)}, f32[16,4,8,128]{3,2,1,0:T(8,128)S(1)}, ...), condition=%wide.region_20.21_spmd, body=%wide.region_19.20_spmd.sunk | while | flops 199685 | bytes 823447 | solution.py:23
  279.2 5.2 %fusion.116 = f32[16,1024]{1,0:T(8,128)} fusion(bf16[4096,1024]{1,0:T(8,128)(2,1)} %param.23, bf16[2,8,32,128]{3,2,1,0:T(8,128)(2,1)S(1)} %bitcast.326), kind=kOutput, calls=%fused_computation.136 | convolution fusion | flops 134217728 | bytes 8585216 | tf_op jit(solution)/shard_map/dot_general | solution.py:175
  284.5 20.3 %all-reduce.13.cloned.1.call-done = f32[16,1024]{1,0:T(8,128)} async-done(((f32[16,1024]{1,0:T(8,128)}), f32[16,1024]{1,0:T(8,128)}) %all-reduce.13.cloned.1.call-update) | async-done | bytes 65552 | tf_op jit(solution)/shard_map/psum | solution.py:176
  305.7 6.2 %fusion.143 = f32[16,5120]{1,0:T(8,128)} fusion(bf16[1024,5120]{1,0:T(8,128)(2,1)} %constant_dynamic-update-slice_fusion.6, bf16[16,1024]{1,0:T(8,128)(2,1)S(1)} %get-tuple-element.725, f32[1024]{0:T(1024)S(1)} %copy-done.8), kind=kOutput, calls=%fused_computation.188 | convolution fusion | flops 167821312 | bytes 10850304 | tf_op jit(solution)/shard_map/dot_general | solution.py:91
  312.0 16.1 %psum.70 = f32[16]{0:T(128)S(1)} all-reduce(f32[16]{0:T(128)S(1)} %get-tuple-element.724), channel_id=1, replica_groups=mesh['groups'=2,'seq'=4,'head'=2,'side'=2] {'seq','side'}, use_global_device_ids=true, to_apply=%region_24.25 | all-reduce | flops 16 | bytes 128 | tf_op jit(solution)/shard_map/psum | solution.py:93
  328.0 39.4 %all-reduce.15.cloned.1.call-done = f32[16,5120]{1,0:T(8,128)} async-done(((f32[16,5120]{1,0:T(8,128)}), f32[16,5120]{1,0:T(8,128)}) %all-reduce.15.cloned.1.call-update) | async-done | bytes 327696 | tf_op jit(solution)/shard_map/psum | solution.py:93
  368.9 3.7 bitcast_reduce_fusion
  378.0 2.0 fusion.78
  381.1 14.3 %all_gather.71 = f32[8,16,4,8]{1,3,2,0:T(8,128)S(1)} all-gather(f32[1,16,4,8]{1,3,2,0:T(8,128)S(1)} %copy.414), channel_id=1, replica_groups=mesh['groups'=2,'seq'=4,'head'=2,'side'=2] {'seq','side'}, dimensions={0}, use_global_device_ids=true | all-gather | bytes 18432 | tf_op jit(solution)/shard_map/all_gather | solution.py:17
  395.6 14.4 %all_gather.69 = f32[8,16,4,8]{1,3,2,0:T(8,128)S(1)} all-gather(f32[1,16,4,8]{1,3,2,0:T(8,128)S(1)} %copy.411), channel_id=1, replica_groups=mesh['groups'=2,'seq'=4,'head'=2,'side'=2] {'seq','side'}, dimensions={0}, use_global_device_ids=true | all-gather | bytes 18432 | tf_op jit(solution)/shard_map/all_gather | solution.py:17
  411.4 10.3 %while.59 = (s32[]{:T(128)}, f32[16,4,8,128]{3,2,1,0:T(8,128)S(1)}, f32[16,4,8]{2,1,0:T(4,128)S(1)}, f32[16,4,8]{2,1,0:T(4,128)S(1)}, f32[8,16,4,8]{1,3,2,0:T(8,...) while((s32[]{:T(128)}, f32[16,4,8,128]{3,2,1,0:T(8,128)S(1)}, ...), condition=%wide.region_32.33_spmd, body=%wide.region_31.32_spmd.sunk | while | flops 199685 | bytes 823447 | solution.py:23
  421.9 5.3 %fusion.113 = f32[16,1024]{1,0:T(8,128)} fusion(bf16[4096,1024]{1,0:T(8,128)(2,1)} %param.23, bf16[2,8,32,128]{3,2,1,0:T(8,128)(2,1)S(1)} %bitcast.327), kind=kOutput, calls=%fused_computation.133 | convolution fusion | flops 134217728 | bytes 8585216 | tf_op jit(solution)/shard_map/dot_general | solution.py:175
  427.2 20.5 %all-reduce.17.cloned.1.call-done = f32[16,1024]{1,0:T(8,128)} async-done(((f32[16,1024]{1,0:T(8,128)}), f32[16,1024]{1,0:T(8,128)}) %all-reduce.17.cloned.1.call-update) | async-done | bytes 65552 | tf_op jit(solution)/shard_map/psum | solution.py:176
  (288 shorter events, 67.3 us)
Async XLA Ops:
  7.2 35.3 %copy-start = (bf16[16,4,128,128]{3,2,1,0:T(8,128)(2,1)S(1)}, bf16[16,4,128,128]{3,2,1,0:T(8,128)(2,1)}, u32[]{:S(2)}) copy-start(bf16[16,4,128,128]{3,2,1,0:T(8,128)(2,1)} %param.26) | copy-start | bytes 6291460
  7.2 8.1 %copy-start.6 = (bf16[1024,512]{1,0:T(8,128)(2,1)S(1)}, bf16[1024,512]{1,0:T(8,128)(2,1)}, u32[]{:S(2)}) copy-start(bf16[1024,512]{1,0:T(8,128)(2,1)} %param.21) | copy-start | bytes 3145732
  7.2 10.4 %copy-start.9 = (bf16[16,1024]{1,0:T(8,128)(2,1)S(1)}, bf16[16,1024]{1,0:T(8,128)(2,1)}, u32[]{:S(2)}) copy-start(bf16[16,1024]{1,0:T(8,128)(2,1)} %param.18) | copy-start | bytes 98308
  7.2 10.4 %copy-start.8 = (f32[1024]{0:T(1024)S(1)}, f32[1024]{0:T(1024)}, u32[]{:S(2)}) copy-start(f32[1024]{0:T(1024)} %param.19) | copy-start | bytes 12292
  7.2 74.8 %all-reduce.7.cloned.1.call-start = ((), (), s32[]{:S(2)}) async-start(), calls=%async_computation | async-start | bytes 655360 | tf_op jit(solution)/shard_map/psum | solution.py:93
  7.3 9.1 %copy-start.7 = (bf16[1024,512]{1,0:T(8,128)(2,1)S(1)}, bf16[1024,512]{1,0:T(8,128)(2,1)}, u32[]{:S(2)}) copy-start(bf16[1024,512]{1,0:T(8,128)(2,1)} %param.22) | copy-start | bytes 3145732
  17.6 6.4 %copy-start.13 = (s32[16]{0:T(128)S(1)}, s32[16]{0:T(128)}, u32[]{:S(2)}) copy-start(s32[16]{0:T(128)} %param.28) | copy-start | bytes 196
  17.6 24.6 %copy-start.12 = (s32[16,8]{0,1:T(8,128)S(1)}, s32[16,8]{0,1:T(8,128)}, u32[]{:S(2)}) copy-start(s32[16,8]{0,1:T(8,128)} %param.29) | copy-start | bytes 1540
  23.8 101.1 %all-gather.4.cloned.1.call-start = ((), (), s32[]{:S(2)}) async-start(), calls=%async_computation.1 | async-start | bytes 2359296 | tf_op jit(solution)/shard_map/all_gather | solution.py:17
  84.4 5.2 %copy-start.2 = (bf16[1,4,4096,128]{3,2,1,0:T(8,128)(2,1)S(1)}, bf16[1,4,4096,128]{3,2,1,0:T(8,128)(2,1)}, u32[]{:S(2)}) copy-start(bf16[1,4,4096,128]{3,2,1,0:T(8,128)(2,1)} %param.25) | copy-start | bytes 12582916
  89.7 1.8 copy-start.5
  95.3 66.6 %all-reduce.9.cloned.1.call-start = ((), (), s32[]{:S(2)}) async-start(), calls=%async_computation.2 | async-start | bytes 131072 | tf_op jit(solution)/shard_map/psum | solution.py:176
  141.6 83.1 %all-reduce.11.cloned.1.call-start = ((), (), s32[]{:S(2)}) async-start(), calls=%async_computation.3 | async-start | bytes 655360 | tf_op jit(solution)/shard_map/psum | solution.py:93
  169.1 98.6 %all-gather.6.cloned.1.call-start = ((), (), s32[]{:S(2)}) async-start(), calls=%async_computation.4 | async-start | bytes 2359296 | tf_op jit(solution)/shard_map/all_gather | solution.py:17
  226.1 5.2 %copy-start.3 = (bf16[1,4,4096,128]{3,2,1,0:T(8,128)(2,1)S(1)}, bf16[1,4,4096,128]{3,2,1,0:T(8,128)(2,1)}, u32[]{:S(2)}) copy-start(bf16[1,4,4096,128]{3,2,1,0:T(8,128)(2,1)} %param.25) | copy-start | bytes 12582916
  238.1 66.6 %all-reduce.13.cloned.1.call-start = ((), (), s32[]{:S(2)}) async-start(), calls=%async_computation.5 | async-start | bytes 131072 | tf_op jit(solution)/shard_map/psum | solution.py:176
  284.4 83.0 %all-reduce.15.cloned.1.call-start = ((), (), s32[]{:S(2)}) async-start(), calls=%async_computation.6 | async-start | bytes 655360 | tf_op jit(solution)/shard_map/psum | solution.py:93
  311.9 98.5 %all-gather.8.cloned.1.call-start = ((), (), s32[]{:S(2)}) async-start(), calls=%async_computation.7 | async-start | bytes 2359296 | tf_op jit(solution)/shard_map/all_gather | solution.py:17
  368.9 5.2 %copy-start.4 = (bf16[1,4,4096,128]{3,2,1,0:T(8,128)(2,1)S(1)}, bf16[1,4,4096,128]{3,2,1,0:T(8,128)(2,1)}, u32[]{:S(2)}) copy-start(bf16[1,4,4096,128]{3,2,1,0:T(8,128)(2,1)} %param.25) | copy-start | bytes 12582916
  381.0 66.8 %all-reduce.17.cloned.1.call-start = ((), (), s32[]{:S(2)}) async-start(), calls=%async_computation.8 | async-start | bytes 131072 | tf_op jit(solution)/shard_map/psum | solution.py:176
  421.7 26.0 %copy-start.10 = (f32[16,1024]{1,0:T(8,128)S(1)}, f32[16,1024]{1,0:T(8,128)}, u32[]{:S(2)}) copy-start(f32[16,1024]{1,0:T(8,128)} %all-reduce.9.cloned.1.call-done) | copy-start | bytes 196612
  421.7 26.0 %copy-start.11 = (f32[16,1024]{1,0:T(8,128)S(1)}, f32[16,1024]{1,0:T(8,128)}, u32[]{:S(2)}) copy-start(f32[16,1024]{1,0:T(8,128)} %all-reduce.13.cloned.1.call-done) | copy-start | bytes 196612
  421.7 27.5 %copy-start.1 = (bf16[16,4,128,128]{3,2,1,0:T(8,128)(2,1)S(1)}, bf16[16,4,128,128]{3,2,1,0:T(8,128)(2,1)}, u32[]{:S(2)}) copy-start(bf16[16,4,128,128]{3,2,1,0:T(8,128)(2,1)} %param.26) | copy-start | bytes 6291460
Sparse Core Ops, SparseCore 0:
  23.9 58.0 all-reduce.6
  95.4 29.4 all-gather.3
  141.7 20.1 all-reduce.8
  169.2 55.3 all-reduce.10
  238.3 29.4 all-gather.5
  284.5 20.1 all-reduce.12
  312.0 55.3 all-reduce.14
  381.1 29.2 all-gather.7
  427.4 20.3 all-reduce.16
where the time goes:
time: 457 us; the launch traced here: 456 us
  waiting for transfers between devices  174 us (38%)
  blocking collectives  137 us (30%)
  matrix products  59.2 us (13%)
  other arithmetic  42.5 us (9%)
  local copies, waits for them, and re-layouts  27.4 us (6%)
  between operations  14.4 us (3%)
    psum x3, waiting for transfers between devices, local(): proj, total_sq = lax.psum((partial_value, squares), ('seq', 'side'))  112 us
    all_gather x6, blocking collectives, combined_all(): everything = jax.tree.map(lambda part: lax.all_gather(part, axis), array)  86.6 us
    psum x3, waiting for transfers between devices, local(): delta = lax.psum(part, 'head')  61 us
    psum x3, blocking collectives, local(): proj, total_sq = lax.psum((partial_value, squares), ('seq', 'side'))  50.2 us
    add x21, other arithmetic, combine(): acc_a * weight_a[..., None] + acc_b * weight_b[..., None]  25.4 us
    dot_general x3, matrix products, local(): partial_value = jnp.dot(scaled, w_proj, preferred_element_type=jnp.float32)  18.6 us
    dot_general x3, matrix products, local(): part = jnp.dot(mixed, w_out, preferred_element_type=jnp.float32)  15.8 us
    dot_general x3, matrix products, local(): jnp.einsum('pgkhd,pkld->pgkhl', grouped, prefix_keys, preferred_element_t...  11.1 us
  transfers between devices with their start and end apart: 9, of which 9 were waited for; matrix products, arithmetic and copies ran while one was open for 2% of the time, Pallas kernels for 0%

commit v1 on v0

--- a/solution.py
+++ b/solution.py
@@ -1,8 +1,11 @@
+import functools
 import math
 
 import jax
 import jax.numpy as jnp
 from jax import lax
+from jax.experimental import pallas as pl
+from jax.experimental.pallas import tpu as pltpu
 from jax.sharding import PartitionSpec as P
 
 D = 8192
@@ -47,7 +50,7 @@
     )
 
 
-def local(
+def local_any(
     hidden,
     gain,
     w_query,
@@ -179,6 +182,444 @@
     return (state, update)
 
 
+LANES = 128
+LOG2E = 1.4426950408889634
+BF16 = jnp.bfloat16
+F32 = jnp.float32
+VMEM_SPEC = pl.BlockSpec(memory_space=pltpu.VMEM)
+SMEM_SPEC = pl.BlockSpec(memory_space=pltpu.SMEM)
+PARAMS = pltpu.CompilerParams(vmem_limit_bytes=20 * 1024 * 1024)
+
+
+def resident(array):
+    return pltpu.with_memory_space_constraint(array, pltpu.VMEM)
+
+
+def lanes(rows):
+    return lax.broadcasted_iota(jnp.int32, (rows, LANES), 1)
+
+
+def pieces(values):
+    high = values.astype(BF16).astype(F32)
+    middle = (values - high).astype(BF16).astype(F32)
+    return high, middle, values - high - middle
+
+
+def bias_kernel(place, lengths, table, bias):
+    pages = table.shape[1]
+    page = bias.shape[2] // (SAMP_DEV * pages)
+    row = lax.broadcasted_iota(jnp.int32, (bias.shape[1], page), 0)
+    column = lax.broadcasted_iota(jnp.int32, (bias.shape[1], page), 1)
+    for pool in range(2):
+        for j in range(SAMP_DEV):
+            sample = place[2 + pool] + j
+            mine = row % SAMP_DEV == j
+            for p in range(pages):
+                live = mine & (column < lengths[sample] - p * page)
+                spot = pl.ds(pl.multiple_of(table[sample, p] * page, page), page)
+                bias[pool, :, spot] = jnp.where(live, 0.0, -jnp.inf)
+
+
+def live_bias(place, lengths, table, page):
+    tokens = SAMP_DEV * table.shape[1] * page
+    return pl.pallas_call(
+        bias_kernel,
+        out_shape=jax.ShapeDtypeStruct((2, SAMP_DEV * GROUP, tokens), F32),
+        in_specs=[SMEM_SPEC] * 3,
+        out_specs=VMEM_SPEC,
+        compiler_params=PARAMS,
+    )(place, lengths, table)
+
+
+def project_kernel(first, place, *refs):
+    if first:
+        x_ref, gain, w_query, w_key, w_value, keep, give = refs
+        wide = x_ref[...].astype(F32)
+    else:
+        x_ref, gain, w_query, w_key, w_value, sum_ref, mine, other = refs[:8]
+        keep, give, new_x, new_sum = refs[8:]
+        delta = mine[...] + other[...]
+        new_sum[...] = sum_ref[...] + delta
+        state = (x_ref[...].astype(F32) + delta).astype(BF16)
+        new_x[...] = state
+        wide = state.astype(F32)
+    scaled = (wide * gain[...]).astype(BF16)
+    squares = jnp.sum(wide * wide, axis=1, keepdims=True)
+    column = lanes(wide.shape[0])
+    query = w_query.shape[1] // 2
+    key = w_key.shape[1] // 2
+    side = place[0]
+    for out, who in ((give, 1 - side), (keep, side)):
+        tile = min(1024, query)
+        for at in range(0, query, tile):
+            columns = pl.ds(pl.multiple_of(who * query + at, tile), tile)
+            out[:, at : at + tile] = jnp.dot(
+                scaled, w_query[:, columns], preferred_element_type=F32
+            )
+        columns = pl.ds(pl.multiple_of(who * key, key), key)
+        out[:, query : query + key] = jnp.dot(
+            scaled, w_key[:, columns], preferred_element_type=F32
+        )
+        out[:, query + key : query + 2 * key] = jnp.dot(
+            scaled, w_value[:, columns], preferred_element_type=F32
+        )
+        out[:, query + 2 * key :] = jnp.where(column == 0, squares, 0.0)
+
+
+def project(place, x, gain, weights, rest):
+    rows = x.shape[0]
+    width = sum(w.shape[1] for w in weights) // 2 + LANES
+    halves = [jax.ShapeDtypeStruct((rows, width), F32)] * 2
+    out_shape = halves if not rest else halves + [
+        jax.ShapeDtypeStruct(x.shape, BF16),
+        jax.ShapeDtypeStruct(x.shape, F32),
+    ]
+    return pl.pallas_call(
+        functools.partial(project_kernel, not rest),
+        out_shape=out_shape,
+        in_specs=[SMEM_SPEC] + [VMEM_SPEC] * (5 + len(rest)),
+        out_specs=[VMEM_SPEC] * len(out_shape),
+        compiler_params=PARAMS,
+    )(place, x, gain, *weights, *rest)
+
+
+def pair_sum_kernel(keep, got, total, sent):
+    both = keep[...] + got[...]
+    total[...] = both
+    main = both.shape[1] - LANES
+    sent[:, :main] = both[:, :main].astype(BF16)
+    column = lanes(both.shape[0])
+    high, middle, low = pieces(both[:, main : main + 1])
+    sent[:, main:] = jnp.where(
+        column == 0, high, jnp.where(column == 1, middle, jnp.where(column == 2, low, 0.0))
+    ).astype(BF16)
+
+
+def pair_sum(keep, got):
+    return pl.pallas_call(
+        pair_sum_kernel,
+        out_shape=[
+            jax.ShapeDtypeStruct(keep.shape, F32),
+            jax.ShapeDtypeStruct(keep.shape, BF16),
+        ],
+        in_specs=[VMEM_SPEC] * 2,
+        out_specs=[VMEM_SPEC] * 2,
+        compiler_params=PARAMS,
+    )(keep, got)
+
+
+def attend_kernel(features, step, others, place, *refs):
+    total_ref = refs[0]
+    got = refs[1 : 1 + others]
+    cos_ref, sin_ref, bias_ref = refs[1 + others : 4 + others]
+    pk, pv, sk, sv, got_pk, got_pv, got_sk, got_sv = refs[4 + others : 12 + others]
+    old = refs[12 + others : 12 + others + step]
+    sent, stat, fresh = refs[12 + others + step :]
+    rows = total_ref.shape[0]
+    heads = got_pk.shape[1]
+    width = total_ref.shape[1] - LANES
+    query_width = width - 2 * heads * HD
+    side, base, first_own, first_got = place[0], place[1], place[2], place[3]
+    span = 2 * SAMP_DEV
+    scale = LOG2E / math.sqrt(HD)
+
+    stats = total_ref[:, width : width + 1]
+    for ref in got:
+        stats = stats + jnp.sum(ref[:, width:].astype(F32), axis=1, keepdims=True)
+    inverse = lax.rsqrt(stats / features + 1e-05)
+    cosine = cos_ref[...]
+    sine = sin_ref[...]
+
+    def block(at):
+        value = total_ref[:, at : at + HD]
+        for ref in got:
+            value = value + ref[:, at : at + HD].astype(F32)
+        return value * inverse
+
+    def turned(at):
+        value = block(at)
+        return (value * cosine + pltpu.roll(value, HD // 2, 1) * sine).astype(BF16)
+
+    sample = lax.broadcasted_iota(jnp.int32, (rows, 1), 0)
+    owned = (sample >= base) & (sample < base + span)
+    pick_row = lax.broadcasted_iota(jnp.int32, (SAMP_DEV * GROUP, GROUP * rows), 0)
+    pick_column = lax.broadcasted_iota(jnp.int32, (SAMP_DEV * GROUP, GROUP * rows), 1)
+    spot = (pick_row // SAMP_DEV) * rows + pick_row % SAMP_DEV
+    stat_value = jnp.zeros((rows, LANES), F32)
+    column = lanes(rows)
+
+    for head in range(heads):
+        queries = [turned((head * GROUP + g) * HD) for g in range(GROUP)]
+        packed = jnp.concatenate(queries, axis=0)
+        new_key = turned(query_width + head * HD)
+        new_value = block(query_width + (heads + head) * HD).astype(BF16)
+        fresh[:, head * HD : (head + 1) * HD] = new_key
+        fresh[:, (heads + head) * HD : (heads + head + 1) * HD] = new_value
+        keys = [ref[:, head * HD : (head + 1) * HD].astype(F32) for ref in old]
+        values = [
+            ref[:, (heads + head) * HD : (heads + head + 1) * HD].astype(F32) for ref in old
+        ]
+        keys.append(new_key.astype(F32))
+        values.append(new_value.astype(F32))
+
+        near = []
+        for pool, (key_pool, value_pool, at, start) in enumerate(
+            (
+                (sk, sv, side * heads + head, first_own),
+                (got_sk, got_sv, head, first_got),
+            )
+        ):
+            tokens = key_pool.shape[0] * key_pool.shape[2]
+            pick = (pick_column == spot + start).astype(F32).astype(BF16)
+            few = jnp.dot(pick, packed, preferred_element_type=F32).astype(BF16)
+            score = lax.dot_general(
+                few,
+                key_pool[:, at].reshape(tokens, HD),
+                (((1,), (1,)), ((), ())),
+                preferred_element_type=F32,
+            )
+            score = score * scale + bias_ref[pool]
+            top = jnp.max(score, axis=1, keepdims=True)
+            expo = jnp.exp2(score - top)
+            near.append(
+                (
+                    start,
+                    top,
+                    jnp.sum(expo, axis=1, keepdims=True),
+                    jnp.dot(
+                        expo.astype(BF16),
+                        value_pool[:, at].reshape(tokens, HD),
+                        preferred_element_type=F32,
+                    ),
+                )
+            )
+        tops, totals, sums = [], [], []
+        for g in range(GROUP):
+            top = jnp.full((rows, 1), -1e30, F32)
+            total = jnp.zeros((rows, 1), F32)
+            acc = jnp.zeros((rows, HD), F32)
+            for start, near_top, near_total, near_acc in near:
+                for j in range(SAMP_DEV):
+                    line = slice(g * SAMP_DEV + j, g * SAMP_DEV + j + 1)
+                    here = sample == start + j
+                    top = jnp.where(here, near_top[line], top)
+                    total = jnp.where(here, near_total[line], total)
+                    acc = jnp.where(here, near_acc[line], acc)
+            wide_query = queries[g].astype(F32)
+            scores = [
+                jnp.sum(wide_query * key, axis=1, keepdims=True) * scale for key in keys
+            ]
+            peak = top
+            for score in scores:
+                peak = jnp.maximum(peak, score)
+            peak = jnp.where(owned, peak, top)
+            shrink = jnp.exp2(top - peak)
+            total = total * shrink
+            acc = acc * shrink
+            for score, value in zip(scores, values):
+                expo = jnp.where(owned, jnp.exp2(jnp.where(owned, score - peak, 0.0)), 0.0)
+                total = total + expo
+                acc = acc + expo.astype(BF16).astype(F32) * value
+            tops.append(peak)
+            totals.append(total)
+            sums.append(acc)
+        top = jnp.concatenate(tops, axis=0)
+        total = jnp.concatenate(totals, axis=0)
+        acc = jnp.concatenate(sums, axis=0)
+
+        length = pk.shape[2]
+        chunk = min(2048, length)
+        for key_ref, value_ref, at in ((pk, pv, side * heads + head), (got_pk, got_pv, head)):
+            for begin in range(0, length, chunk):
+                score = lax.dot_general(
+                    packed,
+                    key_ref[0, at, begin : begin + chunk],
+                    (((1,), (1,)), ((), ())),
+                    preferred_element_type=F32,
+                )
+                score = score * scale
+                peak = jnp.maximum(top, jnp.max(score, axis=1, keepdims=True))
+                shrink = jnp.exp2(top - peak)
+                expo = jnp.exp2(score - peak)
+                total = total * shrink + jnp.sum(expo, axis=1, keepdims=True)
+                acc = acc * shrink + jnp.dot(
+                    expo.astype(BF16),
+                    value_ref[0, at, begin : begin + chunk],
+                    preferred_element_type=F32,
+                )
+                top = peak
+        mean = acc / total
+        level = top + jnp.log2(total)
+        for g in range(GROUP):
+            index = head * GROUP + g
+            part = slice(g * rows, (g + 1) * rows)
+            sent[:, index * HD : (index + 1) * HD] = mean[part].astype(BF16)
+            stat_value = jnp.where(column == index, level[part], stat_value)
+    high, middle, low = pieces(stat_value)
+    many = heads * GROUP
+    stat[...] = stat_value
+    shifted = high + pltpu.roll(middle, many, 1) + pltpu.roll(low, 2 * many, 1)
+    sent[:, many * HD :] = shifted.astype(BF16)
+
+
+def attend(features, step, place, total, got, tables, pools, old):
+    rows = total.shape[0]
+    heads = pools[4].shape[1]
+    operands = [total, *got, *tables, *pools, *old]
+    return pl.pallas_call(
+        functools.partial(attend_kernel, features, step, len(got)),
+        out_shape=[
+            jax.ShapeDtypeStruct((rows, heads * GROUP * HD + LANES), BF16),
+            jax.ShapeDtypeStruct((rows, LANES), F32),
+            jax.ShapeDtypeStruct((rows, 2 * heads * HD), BF16),
+        ],
+        in_specs=[SMEM_SPEC] + [VMEM_SPEC] * len(operands),
+        out_specs=[VMEM_SPEC] * 3,
+        compiler_params=PARAMS,
+    )(place, *operands)
+
+
+def merge_kernel(own, stat, *refs):
+    got, out = refs[:-1], refs[-1]
+    many = out.shape[1] // HD
+    levels = [stat[...]]
+    for ref in got:
+        packed = ref[:, many * HD :].astype(F32)
+        levels.append(
+            packed
+            + pltpu.roll(packed, LANES - many, 1)
+            + pltpu.roll(packed, LANES - 2 * many, 1)
+        )
+    top = functools.reduce(jnp.maximum, levels)
+    weights = [jnp.exp2(level - top) for level in levels]
+    share = 1.0 / functools.reduce(jnp.add, weights)
+    weights = [weight * share for weight in weights]
+    for index in range(many):
+        part = slice(index * HD, (index + 1) * HD)
+        value = own[:, part].astype(F32) * weights[0][:, index : index + 1]
+        for ref, weight in zip(got, weights[1:]):
+            value = value + ref[:, part].astype(F32) * weight[:, index : index + 1]
+        out[:, part] = value.astype(BF16)
+
+
+def merge(own, stat, got):
+    return pl.pallas_call(
+        merge_kernel,
+        out_shape=jax.ShapeDtypeStruct((own.shape[0], own.shape[1] - LANES), BF16),
+        in_specs=[VMEM_SPEC] * (2 + len(got)),
+        out_specs=VMEM_SPEC,
+        compiler_params=PARAMS,
+    )(own, stat, *got)
+
+
+def output_kernel(place, mine, other, weight, out):
+    half = mine.shape[1]
+    side = place[0]
+    here = pl.ds(pl.multiple_of(side * half, half), half)
+    there = pl.ds(pl.multiple_of((1 - side) * half, half), half)
+    out[...] = jnp.dot(mine[...], weight[here], preferred_element_type=F32) + jnp.dot(
+        other[...], weight[there], preferred_element_type=F32
+    )
+
+
+def output(place, mine, other, weight):
+    return pl.pallas_call(
+        output_kernel,
+        out_shape=jax.ShapeDtypeStruct((mine.shape[0], weight.shape[1]), F32),
+        in_specs=[SMEM_SPEC] + [VMEM_SPEC] * 3,
+        out_specs=VMEM_SPEC,
+        compiler_params=PARAMS,
+    )(place, mine, other, weight)
+
+
+def swapped(array, axis):
+    return lax.ppermute(array, axis, [(0, 1), (1, 0)])
+
+
+def from_others(array, axis):
+    size = lax.axis_size(axis)
+    return [
+        lax.ppermute(array, axis, [(i, (i + hop) % size) for i in range(size)])
+        for hop in range(1, size)
+    ]
+
+
+def local_split(
+    hidden,
+    gain,
+    w_query,
+    w_key,
+    w_value,
+    w_out,
+    prefix_keys,
+    prefix_values,
+    suffix_keys,
+    suffix_values,
+    suffix_lengths,
+    page_table,
+):
+    samples, width = hidden.shape
+    features = width * lax.axis_size(("seq", "side"))
+    seq = lax.axis_index("seq")
+    side = lax.axis_index("side")
+    base = seq * (2 * SAMP_DEV)
+    first_own = base + (1 - side) * SAMP_DEV
+    first_got = base + side * SAMP_DEV
+    place = jnp.stack([side, base, first_own, first_got]).astype(jnp.int32)
+    own_pools = (prefix_keys, prefix_values, suffix_keys, suffix_values)
+    heads = prefix_keys.shape[1] // 2
+    got_pools = [
+        swapped(lax.dynamic_slice_in_dim(pool, (1 - side) * heads, heads, 1), "side")
+        for pool in own_pools
+    ]
+    pools = [resident(pool) for pool in (*own_pools, *got_pools)]
+    weights = [resident(weight) for weight in (w_query, w_key, w_value)]
+    out_weight = resident(w_out)
+    bias = live_bias(place, suffix_lengths, page_table, suffix_keys.shape[2])
+    half = HD // 2
+    freq = 500000.0 ** (-(jnp.arange(half, dtype=F32) * 2.0 / HD))
+    position = (
+        PREFIX + suffix_lengths[None, :] + jnp.arange(STEPS, dtype=jnp.int32)[:, None]
+    ).astype(F32)
+    angle = position[..., None] * freq
+    cosine, sine = jnp.cos(angle), jnp.sin(angle)
+    cosine = jnp.concatenate([cosine, cosine], axis=-1)
+    sine = jnp.concatenate([-sine, sine], axis=-1)
+    gain_row = gain[None, :]
+
+    state = hidden
+    update = jnp.zeros(hidden.shape, F32)
+    rest = ()
+    old = []
+    for step in range(STEPS):
+        outs = project(place, state, gain_row, weights, rest)
+        keep, give = outs[:2]
+        if rest:
+            state, update = outs[2:]
+        total, sent = pair_sum(keep, swapped(give, "side"))
+        got = from_others(sent, "seq")
+        sent, stat, fresh = attend(
+            features, step, place, total, got, (cosine[step], sine[step], bias), pools, old
+        )
+        old.append(fresh)
+        mixed = merge(sent, stat, from_others(sent, "seq"))
+        part = output(place, mixed, swapped(mixed, "side"), out_weight)
+        rest = (update, part, swapped(part, "head"))
+    delta = rest[1] + rest[2]
+    return ((state.astype(F32) + delta).astype(BF16), update + delta)
+
+
+def fits(mesh, args):
+    heads = args[4].shape[1] // HD // mesh.shape["head"]
+    return (
+        mesh.shape["head"] == 2
+        and mesh.shape["side"] == 2
+        and heads % 2 == 0
+        and args[6].shape[0] == mesh.shape["groups"]
+        and heads // 2 * GROUP * 3 <= LANES
+    )
+
+
 def solution(mesh):
     placed = (
         P("groups", ("seq", "side")),
@@ -194,10 +635,14 @@
         P("groups"),
         P("groups", None),
     )
-    return jax.shard_map(
-        local,
-        mesh=mesh,
-        in_specs=placed,
-        out_specs=(P("groups", ("seq", "side")), P("groups", ("seq", "side"))),
-        check_vma=False,
-    )
+
+    def whole(*args):
+        return jax.shard_map(
+            local_split if fits(mesh, args) else local_any,
+            mesh=mesh,
+            in_specs=placed,
+            out_specs=(P("groups", ("seq", "side")), P("groups", ("seq", "side"))),
+            check_vma=False,
+        )(*args)
+
+    return whole

time: 457 us -> 163 us (0.36)
  blocking collectives: 137 us -> 0 us
  waiting for transfers between devices: 174 us -> 54.1 us
  matrix products: 59.2 us -> 0 us
  Pallas kernels: 0 us -> 44.6 us
  other arithmetic: 42.5 us -> 1 us
  starting transfers between devices: 0.37 us -> 34.8 us
  between operations: 14.4 us -> 0.86 us
    psum x6 -> x0, waiting for transfers between devices: 173 us -> none  [the longest x3 112 us: local(): proj, total_sq = lax.psum((partial_value, squares), ('seq', 'side'))]
    all_gather x6 -> x0, blocking collectives: 86.6 us -> none  [combined_all(): everything = jax.tree.map(lambda part: lax.all_gather(part, axis), array)]
    dot_general x23 -> x0, matrix products: 59.2 us -> none  [the longest x3 18.6 us: local(): partial_value = jnp.dot(scaled, w_proj, preferred_element_type=jnp.float32)]
    ppermute x0 -> x31, waiting for transfers between devices: none -> 54.1 us  [the longest x18 38.2 us: from_others(): lax.ppermute(array, axis, [(i, (i + hop) % size) for i in range(size)])]
    psum x3 -> x0, blocking collectives: 50.2 us -> none  [local(): proj, total_sq = lax.psum((partial_value, squares), ('seq', 'side'))]
    pallas_call x0 -> x16, Pallas kernels: none -> 44.6 us  [the longest x3 30.7 us: attend(): pl.pallas_call(functools.partial(attend_kernel, features, step, len(got))...]
    ppermute x0 -> x31, starting transfers between devices: none -> 34.8 us  [the longest x18 28.3 us: from_others(): lax.ppermute(array, axis, [(i, (i + hop) % size) for i in range(size)])]
    add x46 -> x2, other arithmetic: 28.2 us -> 0.66 us  [the longest x1 0.66 us: local_split(): return ((state.astype(F32) + delta).astype(BF16), update + delta)]
  transfers between devices with their start and end apart: 9 -> 31, of which waited for: 9 -> 22; matrix products, arithmetic and copies ran while one was open for 2% -> 3% of each run, Pallas kernels for 0% -> 2%
where the time goes in v1:
time: 163 us; the launch traced here: 162 us
  waiting for transfers between devices  54.1 us (33%)
  Pallas kernels  44.6 us (27%)
  starting transfers between devices  34.8 us (21%)
  local copies, waits for them, and re-layouts  27.1 us (17%)
    ppermute x18, waiting for transfers between devices, from_others(): lax.ppermute(array, axis, [(i, (i + hop) % size) for i in range(size)])  38.2 us
    pallas_call x3, Pallas kernels, attend(): pl.pallas_call(functools.partial(attend_kernel, features, step, len(got))...  30.7 us
    ppermute x18, starting transfers between devices, from_others(): lax.ppermute(array, axis, [(i, (i + hop) % size) for i in range(size)])  28.3 us
    unnamed x59, local copies, waits for them, and re-layouts  20.1 us
    ppermute x13, waiting for transfers between devices, swapped(): return lax.ppermute(array, axis, [(0, 1), (1, 0)])  15.9 us
    dynamic_slice x4, local copies, waits for them, and re-layouts, local_split(): lax.dynamic_slice_in_dim(pool, (1 - side) * heads, heads, 1)  6.95 us
    ppermute x13, starting transfers between devices, swapped(): return lax.ppermute(array, axis, [(0, 1), (1, 0)])  6.5 us
    pallas_call x3, Pallas kernels, project(): pl.pallas_call(functools.partial(project_kernel, not rest), out_shape=out...  6.05 us
  transfers between devices with their start and end apart: 31, of which 22 were waited for; matrix products, arithmetic and copies ran while one was open for 3% of the time, Pallas kernels for 2%

profile of v1, /device:TPU:0, one launch (start us, length us, event | category | flops | bytes accessed | tf_op | source)
XLA Modules:
  0.0 162.4 jit_solution(11618088475762257122)
XLA Ops:
  0.6 3.2 %constant_dynamic-slice_fusion.3 = bf16[1,2,4096,128]{3,2,1,0:T(8,128)(2,1)} fusion(bf16[1,4,4096,128]{3,2,1,0:T(8,128)(2,1)} %refs_7_.5, s32[]{:T(128)S(6)} %select_n.2), kind=kLoop, calls=%fused_computation.29 | loop fusion | bytes 4194308 | tf_op jit(solution)/shard_map/dynamic_slice | solution.py:572
  9.1 3.4 %copy-done = bf16[1024,4096]{1,0:T(8,128)(2,1)S(1)} copy-done((bf16[1024,4096]{1,0:T(8,128)(2,1)S(1)}, bf16[1024,4096]{1,0:T(8,128)(2,1)}, u32[]{:S(2)}) %copy-start) | copy-done | bytes 8388632
  13.7 2.0 %shard_map.131 = (f32[16,2688]{1,0:T(8,128)S(1)}, f32[16,2688]{1,0:T(8,128)S(1)}) custom-call(s32[4]{0:T(128)S(1)} %pad_add_fusion.place, bf16[16,1024]{1,0:T(8,128)(2,1)S(1)} %copy-done.19, f32[1,1024]{1,0:T(1,128)S(1)} %bitcast.21, bf16[1024,4096]{1,0:T(8,128)(2,1)S(1)} %copy-done, bf16[1024,512]{1,0:T(8,128)(2,1)S(1)} %copy-done.14, ...), custom_call_target="tpu_custom_call" | custom-call | tf_op jit(solution)/shard_map/pallas_call | solution.py:277
  18.6 2.9 %collective-permute-start.1 = (bf16[16,2688]{1,0:T(8,128)(2,1)}, bf16[16,2688]{1,0:T(8,128)(2,1)S(1)}, u32[]{:S(2)}, u32[]{:S(2)}) collective-permute-start(bf16[16,2688]{1,0:T(8,128)(2,1)} %get-tuple-element.29), channel_id=1, source_target_pairs={{0,4},{4,8},{8,12},{12,0},{1,5},{5,9},{9,13},{13,1},{2,6},{6,10},{... | collective-permute-start | bytes 258056 | tf_op jit(solution)/shard_map/ppermute | solution.py:542
  21.6 5.1 %collective-permute-done.1.refs_1_ = bf16[16,2688]{1,0:T(8,128)(2,1)S(1)} collective-permute-done((bf16[16,2688]{1,0:T(8,128)(2,1)}, bf16[16,2688]{1,0:T(8,128)(2,1)S(1)}, u32[]{:S(2)}, u32[]{:S(2)}) %collective-permute-start.1) | collective-permute-done | bytes 86048 | tf_op jit(solution)/shard_map/ppermute | solution.py:542
  28.4 4.3 %collective-permute-done.2.refs_2_ = bf16[16,2688]{1,0:T(8,128)(2,1)S(1)} collective-permute-done((bf16[16,2688]{1,0:T(8,128)(2,1)}, bf16[16,2688]{1,0:T(8,128)(2,1)S(1)}, u32[]{:S(2)}, u32[]{:S(2)}) %collective-permute-start.2) | collective-permute-done | bytes 86048 | tf_op jit(solution)/shard_map/ppermute | solution.py:542
  32.7 2.2 %collective-permute-start.3 = (bf16[16,2688]{1,0:T(8,128)(2,1)}, bf16[16,2688]{1,0:T(8,128)(2,1)S(1)}, u32[]{:S(2)}, u32[]{:S(2)}) collective-permute-start(bf16[16,2688]{1,0:T(8,128)(2,1)} %get-tuple-element.29), channel_id=1, source_target_pairs={{0,12},{4,0},{8,4},{12,8},{1,13},{5,1},{9,5},{13,9},{2,14},{6,2},{... | collective-permute-start | bytes 258056 | tf_op jit(solution)/shard_map/ppermute | solution.py:542
  35.0 2.4 %collective-permute-done.3.refs_3_ = bf16[16,2688]{1,0:T(8,128)(2,1)S(1)} collective-permute-done((bf16[16,2688]{1,0:T(8,128)(2,1)}, bf16[16,2688]{1,0:T(8,128)(2,1)S(1)}, u32[]{:S(2)}, u32[]{:S(2)}) %collective-permute-start.3) | collective-permute-done | bytes 86048 | tf_op jit(solution)/shard_map/ppermute | solution.py:542
  37.5 2.3 %copy-done.2 = bf16[1,4,4096,128]{3,2,1,0:T(8,128)(2,1)S(1)} copy-done((bf16[1,4,4096,128]{3,2,1,0:T(8,128)(2,1)S(1)}, bf16[1,4,4096,128]{3,2,1,0:T(8,128)(2,1)}, u32[]{:S(2)}) %copy-start.2) | copy-done | bytes 4194328
  39.8 2.4 %copy-done.5 = bf16[1,4,4096,128]{3,2,1,0:T(8,128)(2,1)S(1)} copy-done((bf16[1,4,4096,128]{3,2,1,0:T(8,128)(2,1)S(1)}, bf16[1,4,4096,128]{3,2,1,0:T(8,128)(2,1)}, u32[]{:S(2)}) %copy-start.5) | copy-done | bytes 4194328
  45.6 10.1 %shard_map.134 = (bf16[16,2176]{1,0:T(8,128)(2,1)S(1)}, f32[16,128]{1,0:T(8,128)S(1)}, bf16[16,512]{1,0:T(8,128)(2,1)S(1)}) custom-call(s32[4]{0:T(128)S(1)} %pad_add_fusion.place, f32[16,2688]{1,0:T(8,128)S(1)} %copy-done.18, bf16[16,2688]{1,0:T(8,128)(2,1)S(1)} %collective-permute-done.1.refs_1_, bf16[16,2688]{1,0:T(8,128)(2,1)S(1)} %copy-done.21, ...), custom_call_target="tpu_custom_call" | custom-call | tf_op jit(solution)/shard_map/pallas_call | solution.py:469
  55.7 4.1 %collective-permute-start.10 = (bf16[16,2176]{1,0:T(8,128)(2,1)S(1)}, bf16[16,2176]{1,0:T(8,128)(2,1)S(1)}, u32[]{:S(2)}, u32[]{:S(2)}) collective-permute-start(bf16[16,2176]{1,0:T(8,128)(2,1)S(1)} %get-tuple-element.30.own), channel_id=1, source_target_pairs={{0,12},{4,0},{8,4},{12,8},{1,13},{5,1},{9,5},{13,9},{2,14},{6,2},{... | collective-permute-start | bytes 208904 | tf_op jit(solution)/shard_map/ppermute | solution.py:542
  61.7 4.2 %collective-permute-done.8.refs_0_ = bf16[16,2176]{1,0:T(8,128)(2,1)S(1)} collective-permute-done((bf16[16,2176]{1,0:T(8,128)(2,1)S(1)}, bf16[16,2176]{1,0:T(8,128)(2,1)S(1)}, u32[]{:S(2)}, u32[]{:S(2)}) %collective-permute-start.8) | collective-permute-done | bytes 69664 | tf_op jit(solution)/shard_map/ppermute | solution.py:542
  70.7 2.8 %collective-permute-done.12.refs_7_ = f32[16,1024]{1,0:T(8,128)S(1)} collective-permute-done((f32[16,1024]{1,0:T(8,128)S(1)}, f32[16,1024]{1,0:T(8,128)S(1)}, u32[]{:S(2)}, u32[]{:S(2)}) %collective-permute-start.12) | collective-permute-done | bytes 65568 | tf_op jit(solution)/shard_map/ppermute | solution.py:536
  73.5 3.4 %copy-done.1 = bf16[1024,4096]{1,0:T(8,128)(2,1)S(1)} copy-done((bf16[1024,4096]{1,0:T(8,128)(2,1)S(1)}, bf16[1024,4096]{1,0:T(8,128)(2,1)}, u32[]{:S(2)}) %copy-start.1) | copy-done | bytes 8388632
  76.9 2.0 %shard_map.137 = (f32[16,2688]{1,0:T(8,128)S(1)}, f32[16,2688]{1,0:T(8,128)S(1)}, bf16[16,1024]{1,0:T(8,128)(2,1)S(1)}, f32[16,1024]{1,0:T(8,128)S(1)}) custom-call(s32[4]{0:T(128)S(1)} %pad_add_fusion.place, bf16[16,1024]{1,0:T(8,128)(2,1)S(1)} %copy-done.19, f32[1,1024]{1,0:T(1,128)S(1)} %bitcast.22, bf16[1024,4096]{1,0:T(8,128)(2,1)S(1)} %copy-done.1, ...), custom_call_target="tpu_custom_call" | custom-call | tf_op jit(solution)/shard_map/pallas_call | solution.py:277
  81.7 2.2 %collective-permute-start.15 = (bf16[16,2688]{1,0:T(8,128)(2,1)S(1)}, bf16[16,2688]{1,0:T(8,128)(2,1)S(1)}, u32[]{:S(2)}, u32[]{:S(2)}) collective-permute-start(bf16[16,2688]{1,0:T(8,128)(2,1)S(1)} %get-tuple-element.37), channel_id=1, source_target_pairs={{0,8},{4,12},{8,0},{12,4},{1,9},{5,13},{9,1},{13,5},{2,10},{6,14},... | collective-permute-start | bytes 258056 | tf_op jit(solution)/shard_map/ppermute | solution.py:542
  84.3 3.4 %collective-permute-done.14.refs_1_ = bf16[16,2688]{1,0:T(8,128)(2,1)S(1)} collective-permute-done((bf16[16,2688]{1,0:T(8,128)(2,1)S(1)}, bf16[16,2688]{1,0:T(8,128)(2,1)S(1)}, u32[]{:S(2)}, u32[]{:S(2)}) %collective-permute-start.14) | collective-permute-done | bytes 86048 | tf_op jit(solution)/shard_map/ppermute | solution.py:542
  87.7 2.9 %collective-permute-done.15.refs_2_ = bf16[16,2688]{1,0:T(8,128)(2,1)S(1)} collective-permute-done((bf16[16,2688]{1,0:T(8,128)(2,1)S(1)}, bf16[16,2688]{1,0:T(8,128)(2,1)S(1)}, u32[]{:S(2)}, u32[]{:S(2)}) %collective-permute-start.15) | collective-permute-done | bytes 86048 | tf_op jit(solution)/shard_map/ppermute | solution.py:542
  93.8 10.1 %shard_map.139 = (bf16[16,2176]{1,0:T(8,128)(2,1)S(1)}, f32[16,128]{1,0:T(8,128)S(1)}, bf16[16,512]{1,0:T(8,128)(2,1)S(1)}) custom-call(s32[4]{0:T(128)S(1)} %pad_add_fusion.place, f32[16,2688]{1,0:T(8,128)S(1)} %get-tuple-element.36.refs_0_, bf16[16,2688]{1,0:T(8,128)(2,1)S(1)} %collective-permute-done.14.refs_1_, ...), custom_call_target="tpu_custom_call" | custom-call | tf_op jit(solution)/shard_map/pallas_call | solution.py:469
  103.9 2.3 %collective-permute-start.17 = (bf16[16,2176]{1,0:T(8,128)(2,1)S(1)}, bf16[16,2176]{1,0:T(8,128)(2,1)S(1)}, u32[]{:S(2)}, u32[]{:S(2)}) collective-permute-start(bf16[16,2176]{1,0:T(8,128)(2,1)S(1)} %get-tuple-element.39.own), channel_id=1, source_target_pairs={{0,4},{4,8},{8,12},{12,0},{1,5},{5,9},{9,13},{13,1},{2,6},{6,10},{... | collective-permute-start | bytes 208904 | tf_op jit(solution)/shard_map/ppermute | solution.py:542
  108.7 2.2 %collective-permute-done.17.refs_0_ = bf16[16,2176]{1,0:T(8,128)(2,1)S(1)} collective-permute-done((bf16[16,2176]{1,0:T(8,128)(2,1)S(1)}, bf16[16,2176]{1,0:T(8,128)(2,1)S(1)}, u32[]{:S(2)}, u32[]{:S(2)}) %collective-permute-start.17) | collective-permute-done | bytes 69664 | tf_op jit(solution)/shard_map/ppermute | solution.py:542
  110.9 2.2 %collective-permute-done.18.refs_1_ = bf16[16,2176]{1,0:T(8,128)(2,1)S(1)} collective-permute-done((bf16[16,2176]{1,0:T(8,128)(2,1)S(1)}, bf16[16,2176]{1,0:T(8,128)(2,1)S(1)}, u32[]{:S(2)}, u32[]{:S(2)}) %collective-permute-start.18) | collective-permute-done | bytes 69664 | tf_op jit(solution)/shard_map/ppermute | solution.py:542
  118.0 2.8 %collective-permute-done.21.refs_7_ = f32[16,1024]{1,0:T(8,128)S(1)} collective-permute-done((f32[16,1024]{1,0:T(8,128)S(1)}, f32[16,1024]{1,0:T(8,128)S(1)}, u32[]{:S(2)}, u32[]{:S(2)}) %collective-permute-start.21) | collective-permute-done | bytes 65568 | tf_op jit(solution)/shard_map/ppermute | solution.py:536
  120.8 2.0 %shard_map.142 = (f32[16,2688]{1,0:T(8,128)S(1)}, f32[16,2688]{1,0:T(8,128)S(1)}, bf16[16,1024]{1,0:T(8,128)(2,1)S(1)}, f32[16,1024]{1,0:T(8,128)S(1)}) custom-call(s32[4]{0:T(128)S(1)} %pad_add_fusion.place, bf16[16,1024]{1,0:T(8,128)(2,1)S(1)} %get-tuple-element.32.refs_0_, f32[1,1024]{1,0:T(1,128)S(1)} %bitcast.23, bf16[1024,4096]{1,0:T(8,128)(2,1)S(1)} %bitcast.18, ...), custom_call_target="tpu_custom_call" | custom-call | tf_op jit(solution)/shard_map/pallas_call | solution.py:277
  128.7 2.9 %collective-permute-done.23.refs_1_ = bf16[16,2688]{1,0:T(8,128)(2,1)S(1)} collective-permute-done((bf16[16,2688]{1,0:T(8,128)(2,1)S(1)}, bf16[16,2688]{1,0:T(8,128)(2,1)S(1)}, u32[]{:S(2)}, u32[]{:S(2)}) %collective-permute-start.23) | collective-permute-done | bytes 86048 | tf_op jit(solution)/shard_map/ppermute | solution.py:542
  131.6 2.9 %collective-permute-done.24.refs_2_ = bf16[16,2688]{1,0:T(8,128)(2,1)S(1)} collective-permute-done((bf16[16,2688]{1,0:T(8,128)(2,1)S(1)}, bf16[16,2688]{1,0:T(8,128)(2,1)S(1)}, u32[]{:S(2)}, u32[]{:S(2)}) %collective-permute-start.24) | collective-permute-done | bytes 86048 | tf_op jit(solution)/shard_map/ppermute | solution.py:542
  134.5 10.5 %shard_map.144 = (bf16[16,2176]{1,0:T(8,128)(2,1)S(1)}, f32[16,128]{1,0:T(8,128)S(1)}, bf16[16,512]{1,0:T(8,128)(2,1)}) custom-call(s32[4]{0:T(128)S(1)} %pad_add_fusion.place, f32[16,2688]{1,0:T(8,128)S(1)} %get-tuple-element.44.refs_0_, bf16[16,2688]{1,0:T(8,128)(2,1)S(1)} %collective-permute-done.23.refs_1_, ...), custom_call_target="tpu_custom_call" | custom-call | tf_op jit(solution)/shard_map/pallas_call | solution.py:469
  145.0 2.3 %collective-permute-start.26 = (bf16[16,2176]{1,0:T(8,128)(2,1)S(1)}, bf16[16,2176]{1,0:T(8,128)(2,1)S(1)}, u32[]{:S(2)}, u32[]{:S(2)}) collective-permute-start(bf16[16,2176]{1,0:T(8,128)(2,1)S(1)} %get-tuple-element.47.own), channel_id=1, source_target_pairs={{0,4},{4,8},{8,12},{12,0},{1,5},{5,9},{9,13},{13,1},{2,6},{6,10},{... | collective-permute-start | bytes 208904 | tf_op jit(solution)/shard_map/ppermute | solution.py:542
  149.7 2.2 %collective-permute-done.26.refs_0_ = bf16[16,2176]{1,0:T(8,128)(2,1)S(1)} collective-permute-done((bf16[16,2176]{1,0:T(8,128)(2,1)S(1)}, bf16[16,2176]{1,0:T(8,128)(2,1)S(1)}, u32[]{:S(2)}, u32[]{:S(2)}) %collective-permute-start.26) | collective-permute-done | bytes 69664 | tf_op jit(solution)/shard_map/ppermute | solution.py:542
  151.9 2.2 %collective-permute-done.27.refs_1_ = bf16[16,2176]{1,0:T(8,128)(2,1)S(1)} collective-permute-done((bf16[16,2176]{1,0:T(8,128)(2,1)S(1)}, bf16[16,2176]{1,0:T(8,128)(2,1)S(1)}, u32[]{:S(2)}, u32[]{:S(2)}) %collective-permute-start.27) | collective-permute-done | bytes 69664 | tf_op jit(solution)/shard_map/ppermute | solution.py:542
  159.0 2.8 %collective-permute-done.30 = f32[16,1024]{1,0:T(8,128)S(1)} collective-permute-done((f32[16,1024]{1,0:T(8,128)S(1)}, f32[16,1024]{1,0:T(8,128)S(1)}, u32[]{:S(2)}, u32[]{:S(2)}) %collective-permute-start.30) | collective-permute-done | bytes 65568 | tf_op jit(solution)/shard_map/ppermute | solution.py:536
  (119 shorter events, 48.9 us)
Async XLA Ops:
  3.9 33.6 %collective-permute-start.4 = (bf16[1,2,4096,128]{3,2,1,0:T(8,128)(2,1)}, bf16[1,2,4096,128]{3,2,1,0:T(8,128)(2,1)}, u32[]{:S(2)}, u32[]{:S(2)}) collective-permute-start(bf16[1,2,4096,128]{3,2,1,0:T(8,128)(2,1)} %constant_dynamic-slice_fusion.3), channel_id=1, source_target_pairs={{0,1},{1,0},{2,3},{3,2},{4,5},{5,4},{6,7},{7,6},{8,9},{9,8},{10,11... | collective-permute-start | bytes 6291464 | tf_op jit(solution)/shard_map/ppermute | solution.py:536
  5.9 31.6 %collective-permute-start.5 = (bf16[1,2,4096,128]{3,2,1,0:T(8,128)(2,1)}, bf16[1,2,4096,128]{3,2,1,0:T(8,128)(2,1)}, u32[]{:S(2)}, u32[]{:S(2)}) collective-permute-start(bf16[1,2,4096,128]{3,2,1,0:T(8,128)(2,1)} %constant_dynamic-slice_fusion.2), channel_id=1, source_target_pairs={{0,1},{1,0},{2,3},{3,2},{4,5},{5,4},{6,7},{7,6},{8,9},{9,8},{10,11... | collective-permute-start | bytes 6291464 | tf_op jit(solution)/shard_map/ppermute | solution.py:536
  7.1 30.4 %collective-permute-start.6 = (bf16[16,2,128,128]{3,2,1,0:T(8,128)(2,1)}, bf16[16,2,128,128]{3,2,1,0:T(8,128)(2,1)}, u32[]{:S(2)}, u32[]{:S(2)}) collective-permute-start(bf16[16,2,128,128]{3,2,1,0:T(8,128)(2,1)} %constant_dynamic-slice_fusion.1), channel_id=1, source_target_pairs={{0,1},{1,0},{2,3},{3,2},{4,5},{5,4},{6,7},{7,6},{8,9},{9,8},{10,11... | collective-permute-start | bytes 3145736 | tf_op jit(solution)/shard_map/ppermute | solution.py:536
  9.0 28.5 %collective-permute-start.7 = (bf16[16,2,128,128]{3,2,1,0:T(8,128)(2,1)}, bf16[16,2,128,128]{3,2,1,0:T(8,128)(2,1)}, u32[]{:S(2)}, u32[]{:S(2)}) collective-permute-start(bf16[16,2,128,128]{3,2,1,0:T(8,128)(2,1)} %constant_dynamic-slice_fusion), channel_id=1, source_target_pairs={{0,1},{1,0},{2,3},{3,2},{4,5},{5,4},{6,7},{7,6},{8,9},{9,8},{10,11... | collective-permute-start | bytes 3145736 | tf_op jit(solution)/shard_map/ppermute | solution.py:536
  15.7 1.6 collective-permute-start
  18.6 8.0 %collective-permute-start.1 = (bf16[16,2688]{1,0:T(8,128)(2,1)}, bf16[16,2688]{1,0:T(8,128)(2,1)S(1)}, u32[]{:S(2)}, u32[]{:S(2)}) collective-permute-start(bf16[16,2688]{1,0:T(8,128)(2,1)} %get-tuple-element.29), channel_id=1, source_target_pairs={{0,4},{4,8},{8,12},{12,0},{1,5},{5,9},{9,13},{13,1},{2,6},{6,10},{... | collective-permute-start | bytes 258056 | tf_op jit(solution)/shard_map/ppermute | solution.py:542
  26.6 6.1 %collective-permute-start.2 = (bf16[16,2688]{1,0:T(8,128)(2,1)}, bf16[16,2688]{1,0:T(8,128)(2,1)S(1)}, u32[]{:S(2)}, u32[]{:S(2)}) collective-permute-start(bf16[16,2688]{1,0:T(8,128)(2,1)} %get-tuple-element.29), channel_id=1, source_target_pairs={{0,8},{4,12},{8,0},{12,4},{1,9},{5,13},{9,1},{13,5},{2,10},{6,14},... | collective-permute-start | bytes 258056 | tf_op jit(solution)/shard_map/ppermute | solution.py:542
  32.7 4.7 %collective-permute-start.3 = (bf16[16,2688]{1,0:T(8,128)(2,1)}, bf16[16,2688]{1,0:T(8,128)(2,1)S(1)}, u32[]{:S(2)}, u32[]{:S(2)}) collective-permute-start(bf16[16,2688]{1,0:T(8,128)(2,1)} %get-tuple-element.29), channel_id=1, source_target_pairs={{0,12},{4,0},{8,4},{12,8},{1,13},{5,1},{9,5},{13,9},{2,14},{6,2},{... | collective-permute-start | bytes 258056 | tf_op jit(solution)/shard_map/ppermute | solution.py:542
  55.7 6.0 %collective-permute-start.10 = (bf16[16,2176]{1,0:T(8,128)(2,1)S(1)}, bf16[16,2176]{1,0:T(8,128)(2,1)S(1)}, u32[]{:S(2)}, u32[]{:S(2)}) collective-permute-start(bf16[16,2176]{1,0:T(8,128)(2,1)S(1)} %get-tuple-element.30.own), channel_id=1, source_target_pairs={{0,12},{4,0},{8,4},{12,8},{1,13},{5,1},{9,5},{13,9},{2,14},{6,2},{... | collective-permute-start | bytes 208904 | tf_op jit(solution)/shard_map/ppermute | solution.py:542
  59.7 6.1 %collective-permute-start.8 = (bf16[16,2176]{1,0:T(8,128)(2,1)S(1)}, bf16[16,2176]{1,0:T(8,128)(2,1)S(1)}, u32[]{:S(2)}, u32[]{:S(2)}) collective-permute-start(bf16[16,2176]{1,0:T(8,128)(2,1)S(1)} %get-tuple-element.30.own), channel_id=1, source_target_pairs={{0,4},{4,8},{8,12},{12,0},{1,5},{5,9},{9,13},{13,1},{2,6},{6,10},{... | collective-permute-start | bytes 208904 | tf_op jit(solution)/shard_map/ppermute | solution.py:542
  59.7 6.1 %collective-permute-start.9 = (bf16[16,2176]{1,0:T(8,128)(2,1)S(1)}, bf16[16,2176]{1,0:T(8,128)(2,1)S(1)}, u32[]{:S(2)}, u32[]{:S(2)}) collective-permute-start(bf16[16,2176]{1,0:T(8,128)(2,1)S(1)} %get-tuple-element.30.own), channel_id=1, source_target_pairs={{0,8},{4,12},{8,0},{12,4},{1,9},{5,13},{9,1},{13,5},{2,10},{6,14},... | collective-permute-start | bytes 208904 | tf_op jit(solution)/shard_map/ppermute | solution.py:542
  66.2 1.3 collective-permute-start.11
  69.2 4.3 %collective-permute-start.12 = (f32[16,1024]{1,0:T(8,128)S(1)}, f32[16,1024]{1,0:T(8,128)S(1)}, u32[]{:S(2)}, u32[]{:S(2)}) collective-permute-start(f32[16,1024]{1,0:T(8,128)S(1)} %shard_map.136.refs_6_), channel_id=1, source_target_pairs={{0,2},{2,0},{1,3},{3,1},{4,6},{6,4},{5,7},{7,5},{8,10},{10,8},{9,1... | collective-permute-start | bytes 196616 | tf_op jit(solution)/shard_map/ppermute | solution.py:536
  76.9 43.8 %slice-start = ((s8[8388608]{0:T(1024)(128)(4,1)}), s8[4194304]{0:T(1024)(128)(4,1)S(1)}, s32[]{:S(2)}) async-start(s8[8388608]{0:T(1024)(128)(4,1)} %bitcast.17), calls=%async_computation | async-start | bytes 8388608
  78.9 1.4 collective-permute-start.13
  80.4 7.3 %collective-permute-start.14 = (bf16[16,2688]{1,0:T(8,128)(2,1)S(1)}, bf16[16,2688]{1,0:T(8,128)(2,1)S(1)}, u32[]{:S(2)}, u32[]{:S(2)}) collective-permute-start(bf16[16,2688]{1,0:T(8,128)(2,1)S(1)} %get-tuple-element.37), channel_id=1, source_target_pairs={{0,4},{4,8},{8,12},{12,0},{1,5},{5,9},{9,13},{13,1},{2,6},{6,10},{... | collective-permute-start | bytes 258056 | tf_op jit(solution)/shard_map/ppermute | solution.py:542
  81.7 8.9 %collective-permute-start.15 = (bf16[16,2688]{1,0:T(8,128)(2,1)S(1)}, bf16[16,2688]{1,0:T(8,128)(2,1)S(1)}, u32[]{:S(2)}, u32[]{:S(2)}) collective-permute-start(bf16[16,2688]{1,0:T(8,128)(2,1)S(1)} %get-tuple-element.37), channel_id=1, source_target_pairs={{0,8},{4,12},{8,0},{12,4},{1,9},{5,13},{9,1},{13,5},{2,10},{6,14},... | collective-permute-start | bytes 258056 | tf_op jit(solution)/shard_map/ppermute | solution.py:542
  83.9 6.7 %collective-permute-start.16 = (bf16[16,2688]{1,0:T(8,128)(2,1)S(1)}, bf16[16,2688]{1,0:T(8,128)(2,1)S(1)}, u32[]{:S(2)}, u32[]{:S(2)}) collective-permute-start(bf16[16,2688]{1,0:T(8,128)(2,1)S(1)} %get-tuple-element.37), channel_id=1, source_target_pairs={{0,12},{4,0},{8,4},{12,8},{1,13},{5,1},{9,5},{13,9},{2,14},{6,2},{... | collective-permute-start | bytes 258056 | tf_op jit(solution)/shard_map/ppermute | solution.py:542
  103.9 7.0 %collective-permute-start.17 = (bf16[16,2176]{1,0:T(8,128)(2,1)S(1)}, bf16[16,2176]{1,0:T(8,128)(2,1)S(1)}, u32[]{:S(2)}, u32[]{:S(2)}) collective-permute-start(bf16[16,2176]{1,0:T(8,128)(2,1)S(1)} %get-tuple-element.39.own), channel_id=1, source_target_pairs={{0,4},{4,8},{8,12},{12,0},{1,5},{5,9},{9,13},{13,1},{2,6},{6,10},{... | collective-permute-start | bytes 208904 | tf_op jit(solution)/shard_map/ppermute | solution.py:542
  106.2 6.9 %collective-permute-start.18 = (bf16[16,2176]{1,0:T(8,128)(2,1)S(1)}, bf16[16,2176]{1,0:T(8,128)(2,1)S(1)}, u32[]{:S(2)}, u32[]{:S(2)}) collective-permute-start(bf16[16,2176]{1,0:T(8,128)(2,1)S(1)} %get-tuple-element.39.own), channel_id=1, source_target_pairs={{0,8},{4,12},{8,0},{12,4},{1,9},{5,13},{9,1},{13,5},{2,10},{6,14},... | collective-permute-start | bytes 208904 | tf_op jit(solution)/shard_map/ppermute | solution.py:542
  107.0 6.0 %collective-permute-start.19 = (bf16[16,2176]{1,0:T(8,128)(2,1)S(1)}, bf16[16,2176]{1,0:T(8,128)(2,1)S(1)}, u32[]{:S(2)}, u32[]{:S(2)}) collective-permute-start(bf16[16,2176]{1,0:T(8,128)(2,1)S(1)} %get-tuple-element.39.own), channel_id=1, source_target_pairs={{0,12},{4,0},{8,4},{12,8},{1,13},{5,1},{9,5},{13,9},{2,14},{6,2},{... | collective-permute-start | bytes 208904 | tf_op jit(solution)/shard_map/ppermute | solution.py:542
  113.4 1.3 collective-permute-start.20
  116.5 4.3 %collective-permute-start.21 = (f32[16,1024]{1,0:T(8,128)S(1)}, f32[16,1024]{1,0:T(8,128)S(1)}, u32[]{:S(2)}, u32[]{:S(2)}) collective-permute-start(f32[16,1024]{1,0:T(8,128)S(1)} %shard_map.141.refs_6_), channel_id=1, source_target_pairs={{0,2},{2,0},{1,3},{3,1},{4,6},{6,4},{5,7},{7,5},{8,10},{10,8},{9,1... | collective-permute-start | bytes 196616 | tf_op jit(solution)/shard_map/ppermute | solution.py:536
  122.8 1.4 collective-permute-start.22
  124.3 7.3 %collective-permute-start.23 = (bf16[16,2688]{1,0:T(8,128)(2,1)S(1)}, bf16[16,2688]{1,0:T(8,128)(2,1)S(1)}, u32[]{:S(2)}, u32[]{:S(2)}) collective-permute-start(bf16[16,2688]{1,0:T(8,128)(2,1)S(1)} %get-tuple-element.45), channel_id=1, source_target_pairs={{0,4},{4,8},{8,12},{12,0},{1,5},{5,9},{9,13},{13,1},{2,6},{6,10},{... | collective-permute-start | bytes 258056 | tf_op jit(solution)/shard_map/ppermute | solution.py:542
  126.3 8.2 %collective-permute-start.24 = (bf16[16,2688]{1,0:T(8,128)(2,1)S(1)}, bf16[16,2688]{1,0:T(8,128)(2,1)S(1)}, u32[]{:S(2)}, u32[]{:S(2)}) collective-permute-start(bf16[16,2688]{1,0:T(8,128)(2,1)S(1)} %get-tuple-element.45), channel_id=1, source_target_pairs={{0,8},{4,12},{8,0},{12,4},{1,9},{5,13},{9,1},{13,5},{2,10},{6,14},... | collective-permute-start | bytes 258056 | tf_op jit(solution)/shard_map/ppermute | solution.py:542
  127.2 7.2 %collective-permute-start.25 = (bf16[16,2688]{1,0:T(8,128)(2,1)S(1)}, bf16[16,2688]{1,0:T(8,128)(2,1)S(1)}, u32[]{:S(2)}, u32[]{:S(2)}) collective-permute-start(bf16[16,2688]{1,0:T(8,128)(2,1)S(1)} %get-tuple-element.45), channel_id=1, source_target_pairs={{0,12},{4,0},{8,4},{12,8},{1,13},{5,1},{9,5},{13,9},{2,14},{6,2},{... | collective-permute-start | bytes 258056 | tf_op jit(solution)/shard_map/ppermute | solution.py:542
  145.0 6.9 %collective-permute-start.26 = (bf16[16,2176]{1,0:T(8,128)(2,1)S(1)}, bf16[16,2176]{1,0:T(8,128)(2,1)S(1)}, u32[]{:S(2)}, u32[]{:S(2)}) collective-permute-start(bf16[16,2176]{1,0:T(8,128)(2,1)S(1)} %get-tuple-element.47.own), channel_id=1, source_target_pairs={{0,4},{4,8},{8,12},{12,0},{1,5},{5,9},{9,13},{13,1},{2,6},{6,10},{... | collective-permute-start | bytes 208904 | tf_op jit(solution)/shard_map/ppermute | solution.py:542
  147.3 6.8 %collective-permute-start.27 = (bf16[16,2176]{1,0:T(8,128)(2,1)S(1)}, bf16[16,2176]{1,0:T(8,128)(2,1)S(1)}, u32[]{:S(2)}, u32[]{:S(2)}) collective-permute-start(bf16[16,2176]{1,0:T(8,128)(2,1)S(1)} %get-tuple-element.47.own), channel_id=1, source_target_pairs={{0,8},{4,12},{8,0},{12,4},{1,9},{5,13},{9,1},{13,5},{2,10},{6,14},... | collective-permute-start | bytes 208904 | tf_op jit(solution)/shard_map/ppermute | solution.py:542
  148.1 6.0 %collective-permute-start.28 = (bf16[16,2176]{1,0:T(8,128)(2,1)S(1)}, bf16[16,2176]{1,0:T(8,128)(2,1)S(1)}, u32[]{:S(2)}, u32[]{:S(2)}) collective-permute-start(bf16[16,2176]{1,0:T(8,128)(2,1)S(1)} %get-tuple-element.47.own), channel_id=1, source_target_pairs={{0,12},{4,0},{8,4},{12,8},{1,13},{5,1},{9,5},{13,9},{2,14},{6,2},{... | collective-permute-start | bytes 208904 | tf_op jit(solution)/shard_map/ppermute | solution.py:542
  154.4 1.3 collective-permute-start.29
  157.5 4.3 %collective-permute-start.30 = (f32[16,1024]{1,0:T(8,128)S(1)}, f32[16,1024]{1,0:T(8,128)S(1)}, u32[]{:S(2)}, u32[]{:S(2)}) collective-permute-start(f32[16,1024]{1,0:T(8,128)S(1)} %shard_map.146), channel_id=1, source_target_pairs={{0,2},{2,0},{1,3},{3,1},{4,6},{6,4},{5,7},{7,5},{8,10},{10,8},{9,1... | collective-permute-start | bytes 196616 | tf_op jit(solution)/shard_map/ppermute | solution.py:536
  (28 other events, 208.9 us)

commit v2 on v1

--- a/solution.py
+++ b/solution.py
@@ -188,11 +188,16 @@
 F32 = jnp.float32
 VMEM_SPEC = pl.BlockSpec(memory_space=pltpu.VMEM)
 SMEM_SPEC = pl.BlockSpec(memory_space=pltpu.SMEM)
-PARAMS = pltpu.CompilerParams(vmem_limit_bytes=20 * 1024 * 1024)
+HBM_SPEC = pl.BlockSpec(memory_space=pltpu.HBM)
+PARAMS = pltpu.CompilerParams(vmem_limit_bytes=13 * 1024 * 1024)
 
 
 def resident(array):
     return pltpu.with_memory_space_constraint(array, pltpu.VMEM)
+
+
+def in_hbm(array):
+    return pltpu.with_memory_space_constraint(array, pltpu.HBM)
 
 
 def lanes(rows):
@@ -203,6 +208,41 @@
     high = values.astype(BF16).astype(F32)
     middle = (values - high).astype(BF16).astype(F32)
     return high, middle, values - high - middle
+
+
+def move(copies):
+    for copy in copies:
+        copy.start()
+    for copy in copies:
+        copy.wait()
+
+
+def split_kernel(place, pk, pv, sk, sv, prefix, suffix, sems):
+    heads = prefix.shape[1]
+    away = pl.ds((1 - place[0]) * heads, heads)
+    move(
+        [
+            pltpu.make_async_copy(pk.at[0, away], prefix.at[0], sems.at[0]),
+            pltpu.make_async_copy(pv.at[0, away], prefix.at[1], sems.at[1]),
+            pltpu.make_async_copy(sk.at[:, away], suffix.at[0], sems.at[2]),
+            pltpu.make_async_copy(sv.at[:, away], suffix.at[1], sems.at[3]),
+        ]
+    )
+
+
+def split_heads(place, pools):
+    pk, sk = pools[0], pools[2]
+    return pl.pallas_call(
+        split_kernel,
+        out_shape=[
+            pltpu.VMEM((2, pk.shape[1] // 2) + pk.shape[2:], pk.dtype),
+            pltpu.VMEM((2, sk.shape[0], sk.shape[1] // 2) + sk.shape[2:], sk.dtype),
+        ],
+        in_specs=[SMEM_SPEC] + [HBM_SPEC] * 4,
+        out_specs=[VMEM_SPEC] * 2,
+        scratch_shapes=[pltpu.SemaphoreType.DMA((4,))],
+        compiler_params=PARAMS,
+    )(place, *pools)
 
 
 def bias_kernel(place, lengths, table, bias):
@@ -308,19 +348,65 @@
     )(keep, got)
 
 
+def lane_fold(fold, array):
+    parts = [array[:, at : at + LANES] for at in range(0, array.shape[1], LANES)]
+    return functools.reduce(fold, parts)
+
+
+def row_max(arrays):
+    folded = [lane_fold(jnp.maximum, array) for array in arrays]
+    return jnp.max(functools.reduce(jnp.maximum, folded), axis=1, keepdims=True)
+
+
+def against(rows, keys):
+    return lax.dot_general(
+        rows, keys, (((1,), (1,)), ((), ())), preferred_element_type=F32
+    )
+
+
+def weigh(scores, top, values, scale):
+    total, acc = None, None
+    for score, value in zip(scores, values):
+        expo = jnp.exp2((score - top) * scale)
+        part = lane_fold(jnp.add, expo)
+        term = jnp.dot(expo.astype(BF16), value, preferred_element_type=F32)
+        total = part if total is None else total + part
+        acc = term if acc is None else acc + term
+    return jnp.sum(total, axis=1, keepdims=True), acc
+
+
 def attend_kernel(features, step, others, place, *refs):
     total_ref = refs[0]
     got = refs[1 : 1 + others]
     cos_ref, sin_ref, bias_ref = refs[1 + others : 4 + others]
-    pk, pv, sk, sv, got_pk, got_pv, got_sk, got_sv = refs[4 + others : 12 + others]
-    old = refs[12 + others : 12 + others + step]
-    sent, stat, fresh = refs[12 + others + step :]
+    if step == 0:
+        pk, pv, sk, sv, got_prefix, got_suffix = refs[4 + others : 10 + others]
+        sent, stat, fresh, prefix, suffix, sems = refs[10 + others :]
+        old = ()
+        heads = got_prefix.shape[1]
+        own = pl.ds(place[0] * heads, heads)
+        waits = [
+            pltpu.make_async_copy(got_suffix.at[0], suffix.at[0, 1], sems.at[0]),
+            pltpu.make_async_copy(sk.at[:, own], suffix.at[0, 0], sems.at[1]),
+            pltpu.make_async_copy(got_prefix.at[0], prefix.at[0, 1], sems.at[2]),
+            pltpu.make_async_copy(pk.at[0, own], prefix.at[0, 0], sems.at[3]),
+            pltpu.make_async_copy(got_suffix.at[1], suffix.at[1, 1], sems.at[4]),
+            pltpu.make_async_copy(sv.at[:, own], suffix.at[1, 0], sems.at[5]),
+            pltpu.make_async_copy(got_prefix.at[1], prefix.at[1, 1], sems.at[6]),
+            pltpu.make_async_copy(pv.at[0, own], prefix.at[1, 0], sems.at[7]),
+        ]
+        for copy in waits:
+            copy.start()
+    else:
+        prefix, suffix = refs[4 + others : 6 + others]
+        old = refs[6 + others : 6 + others + step]
+        sent, stat, fresh = refs[6 + others + step :]
+        waits = []
     rows = total_ref.shape[0]
-    heads = got_pk.shape[1]
+    heads = prefix.shape[2]
     width = total_ref.shape[1] - LANES
     query_width = width - 2 * heads * HD
-    side, base, first_own, first_got = place[0], place[1], place[2], place[3]
-    span = 2 * SAMP_DEV
+    base, starts = place[1], (place[2], place[3])
     scale = LOG2E / math.sqrt(HD)
 
     stats = total_ref[:, width : width + 1]
@@ -341,120 +427,113 @@
         return (value * cosine + pltpu.roll(value, HD // 2, 1) * sine).astype(BF16)
 
     sample = lax.broadcasted_iota(jnp.int32, (rows, 1), 0)
-    owned = (sample >= base) & (sample < base + span)
-    pick_row = lax.broadcasted_iota(jnp.int32, (SAMP_DEV * GROUP, GROUP * rows), 0)
-    pick_column = lax.broadcasted_iota(jnp.int32, (SAMP_DEV * GROUP, GROUP * rows), 1)
+    owned = (sample >= base) & (sample < base + 2 * SAMP_DEV)
+    few_rows = SAMP_DEV * GROUP
+    pick_row = lax.broadcasted_iota(jnp.int32, (few_rows, GROUP * rows), 0)
+    pick_column = lax.broadcasted_iota(jnp.int32, (few_rows, GROUP * rows), 1)
     spot = (pick_row // SAMP_DEV) * rows + pick_row % SAMP_DEV
-    stat_value = jnp.zeros((rows, LANES), F32)
+    picks = [(pick_column == spot + start).astype(F32).astype(BF16) for start in starts]
     column = lanes(rows)
 
+    queries = [
+        [turned((head * GROUP + g) * HD) for g in range(GROUP)] for head in range(heads)
+    ]
+    packed = [jnp.concatenate(query, axis=0) for query in queries]
+    keys, values = [], []
     for head in range(heads):
-        queries = [turned((head * GROUP + g) * HD) for g in range(GROUP)]
-        packed = jnp.concatenate(queries, axis=0)
         new_key = turned(query_width + head * HD)
         new_value = block(query_width + (heads + head) * HD).astype(BF16)
-        fresh[:, head * HD : (head + 1) * HD] = new_key
-        fresh[:, (heads + head) * HD : (heads + head + 1) * HD] = new_value
-        keys = [ref[:, head * HD : (head + 1) * HD].astype(F32) for ref in old]
-        values = [
-            ref[:, (heads + head) * HD : (heads + head + 1) * HD].astype(F32) for ref in old
+        key_part = slice(head * HD, (head + 1) * HD)
+        value_part = slice((heads + head) * HD, (heads + head + 1) * HD)
+        fresh[:, key_part] = new_key
+        fresh[:, value_part] = new_value
+        keys.append([ref[:, key_part].astype(F32) for ref in old] + [new_key.astype(F32)])
+        values.append([ref[:, value_part].astype(F32) for ref in old] + [new_value.astype(F32)])
+    few = [
+        [jnp.dot(pick, packed[head], preferred_element_type=F32).astype(BF16) for pick in picks]
+        for head in range(heads)
+    ]
+    fresh_scores = [
+        [
+            [
+                jnp.sum(query.astype(F32) * key, axis=1, keepdims=True)
+                for key in keys[head]
+            ]
+            for query in queries[head]
         ]
-        keys.append(new_key.astype(F32))
-        values.append(new_value.astype(F32))
-
-        near = []
-        for pool, (key_pool, value_pool, at, start) in enumerate(
-            (
-                (sk, sv, side * heads + head, first_own),
-                (got_sk, got_sv, head, first_got),
-            )
-        ):
-            tokens = key_pool.shape[0] * key_pool.shape[2]
-            pick = (pick_column == spot + start).astype(F32).astype(BF16)
-            few = jnp.dot(pick, packed, preferred_element_type=F32).astype(BF16)
-            score = lax.dot_general(
-                few,
-                key_pool[:, at].reshape(tokens, HD),
-                (((1,), (1,)), ((), ())),
-                preferred_element_type=F32,
-            )
-            score = score * scale + bias_ref[pool]
-            top = jnp.max(score, axis=1, keepdims=True)
-            expo = jnp.exp2(score - top)
-            near.append(
-                (
-                    start,
-                    top,
-                    jnp.sum(expo, axis=1, keepdims=True),
-                    jnp.dot(
-                        expo.astype(BF16),
-                        value_pool[:, at].reshape(tokens, HD),
-                        preferred_element_type=F32,
-                    ),
-                )
-            )
-        tops, totals, sums = [], [], []
+        for head in range(heads)
+    ]
+
+    slots, page = suffix.shape[2], suffix.shape[4]
+    length = prefix.shape[3]
+    chunk = min(2048, length)
+    pieces_of = [(src, at) for src in range(2) for at in range(0, length, chunk)]
+
+    def pool(kind, src, head):
+        return suffix[kind, src, :, head].reshape(slots * page, HD)
+
+    for copy in waits[:4]:
+        copy.wait()
+    near_scores = [
+        [against(few[head][src], pool(0, src, head)) + bias_ref[src] for src in range(2)]
+        for head in range(heads)
+    ]
+    far_scores = [
+        [
+            against(packed[head], prefix[0, src, head, at : at + chunk])
+            for src, at in pieces_of
+        ]
+        for head in range(heads)
+    ]
+    near_tops = [[row_max([score]) for score in scores] for scores in near_scores]
+    far_tops = [row_max(scores) for scores in far_scores]
+    for copy in waits[4:]:
+        copy.wait()
+    near = [
+        [
+            weigh([near_scores[head][src]], near_tops[head][src], [pool(1, src, head)], scale)
+            for src in range(2)
+        ]
+        for head in range(heads)
+    ]
+
+    stat_value = jnp.zeros((rows, LANES), F32)
+    for head in range(heads):
+        far_total, far_acc = weigh(
+            far_scores[head],
+            far_tops[head],
+            [prefix[1, src, head, at : at + chunk] for src, at in pieces_of],
+            scale,
+        )
         for g in range(GROUP):
-            top = jnp.full((rows, 1), -1e30, F32)
+            part = slice(g * rows, (g + 1) * rows)
+            far_top = far_tops[head][part]
+            near_top = jnp.full((rows, 1), -1e30, F32)
             total = jnp.zeros((rows, 1), F32)
             acc = jnp.zeros((rows, HD), F32)
-            for start, near_top, near_total, near_acc in near:
+            for src in range(2):
                 for j in range(SAMP_DEV):
                     line = slice(g * SAMP_DEV + j, g * SAMP_DEV + j + 1)
-                    here = sample == start + j
-                    top = jnp.where(here, near_top[line], top)
-                    total = jnp.where(here, near_total[line], total)
-                    acc = jnp.where(here, near_acc[line], acc)
-            wide_query = queries[g].astype(F32)
-            scores = [
-                jnp.sum(wide_query * key, axis=1, keepdims=True) * scale for key in keys
-            ]
-            peak = top
+                    here = sample == starts[src] + j
+                    near_top = jnp.where(here, near_tops[head][src][line], near_top)
+                    total = jnp.where(here, near[head][src][0][line], total)
+                    acc = jnp.where(here, near[head][src][1][line], acc)
+            top = jnp.maximum(far_top, near_top)
+            scores = fresh_scores[head][g]
             for score in scores:
-                peak = jnp.maximum(peak, score)
-            peak = jnp.where(owned, peak, top)
-            shrink = jnp.exp2(top - peak)
-            total = total * shrink
-            acc = acc * shrink
-            for score, value in zip(scores, values):
-                expo = jnp.where(owned, jnp.exp2(jnp.where(owned, score - peak, 0.0)), 0.0)
+                top = jnp.where(owned, jnp.maximum(top, score), top)
+            far_weight = jnp.exp2((far_top - top) * scale)
+            near_weight = jnp.exp2((near_top - top) * scale)
+            total = total * near_weight + far_total[part] * far_weight
+            acc = acc * near_weight + far_acc[part] * far_weight
+            for score, value in zip(scores, values[head]):
+                expo = jnp.where(owned, jnp.exp2(jnp.where(owned, score - top, 0.0) * scale), 0.0)
                 total = total + expo
                 acc = acc + expo.astype(BF16).astype(F32) * value
-            tops.append(peak)
-            totals.append(total)
-            sums.append(acc)
-        top = jnp.concatenate(tops, axis=0)
-        total = jnp.concatenate(totals, axis=0)
-        acc = jnp.concatenate(sums, axis=0)
-
-        length = pk.shape[2]
-        chunk = min(2048, length)
-        for key_ref, value_ref, at in ((pk, pv, side * heads + head), (got_pk, got_pv, head)):
-            for begin in range(0, length, chunk):
-                score = lax.dot_general(
-                    packed,
-                    key_ref[0, at, begin : begin + chunk],
-                    (((1,), (1,)), ((), ())),
-                    preferred_element_type=F32,
-                )
-                score = score * scale
-                peak = jnp.maximum(top, jnp.max(score, axis=1, keepdims=True))
-                shrink = jnp.exp2(top - peak)
-                expo = jnp.exp2(score - peak)
-                total = total * shrink + jnp.sum(expo, axis=1, keepdims=True)
-                acc = acc * shrink + jnp.dot(
-                    expo.astype(BF16),
-                    value_ref[0, at, begin : begin + chunk],
-                    preferred_element_type=F32,
-                )
-                top = peak
-        mean = acc / total
-        level = top + jnp.log2(total)
-        for g in range(GROUP):
             index = head * GROUP + g
-            part = slice(g * rows, (g + 1) * rows)
-            sent[:, index * HD : (index + 1) * HD] = mean[part].astype(BF16)
-            stat_value = jnp.where(column == index, level[part], stat_value)
+            sent[:, index * HD : (index + 1) * HD] = (acc / total).astype(BF16)
+            level = top * scale + jnp.log2(total)
+            stat_value = jnp.where(column == index, level, stat_value)
     high, middle, low = pieces(stat_value)
     many = heads * GROUP
     stat[...] = stat_value
@@ -462,21 +541,36 @@
     sent[:, many * HD :] = shifted.astype(BF16)
 
 
-def attend(features, step, place, total, got, tables, pools, old):
+def attend(features, step, place, total, got, tables, caches, old):
     rows = total.shape[0]
-    heads = pools[4].shape[1]
-    operands = [total, *got, *tables, *pools, *old]
+    out_shape, scratch = [], []
+    if step == 0:
+        pools, (got_prefix, got_suffix) = caches
+        heads = got_prefix.shape[1]
+        out_shape = [
+            pltpu.VMEM((2, 2) + part.shape[1:], BF16) for part in (got_prefix, got_suffix)
+        ]
+        scratch = [pltpu.SemaphoreType.DMA((8,))]
+        inputs = [in_hbm(array) for array in (*pools, got_prefix, got_suffix)]
+        specs = [HBM_SPEC] * len(inputs)
+    else:
+        heads = caches[0].shape[2]
+        inputs = [resident(array) for array in caches]
+        specs = [VMEM_SPEC] * len(inputs)
+    small = [total, *got, *tables]
     return pl.pallas_call(
         functools.partial(attend_kernel, features, step, len(got)),
         out_shape=[
             jax.ShapeDtypeStruct((rows, heads * GROUP * HD + LANES), BF16),
             jax.ShapeDtypeStruct((rows, LANES), F32),
             jax.ShapeDtypeStruct((rows, 2 * heads * HD), BF16),
+            *out_shape,
         ],
-        in_specs=[SMEM_SPEC] + [VMEM_SPEC] * len(operands),
-        out_specs=[VMEM_SPEC] * 3,
+        in_specs=[SMEM_SPEC] + [VMEM_SPEC] * len(small) + specs + [VMEM_SPEC] * len(old),
+        out_specs=[VMEM_SPEC] * (3 + len(out_shape)),
+        scratch_shapes=scratch,
         compiler_params=PARAMS,
-    )(place, *operands)
+    )(place, *small, *inputs, *old)
 
 
 def merge_kernel(own, stat, *refs):
@@ -566,13 +660,9 @@
     first_own = base + (1 - side) * SAMP_DEV
     first_got = base + side * SAMP_DEV
     place = jnp.stack([side, base, first_own, first_got]).astype(jnp.int32)
-    own_pools = (prefix_keys, prefix_values, suffix_keys, suffix_values)
-    heads = prefix_keys.shape[1] // 2
-    got_pools = [
-        swapped(lax.dynamic_slice_in_dim(pool, (1 - side) * heads, heads, 1), "side")
-        for pool in own_pools
-    ]
-    pools = [resident(pool) for pool in (*own_pools, *got_pools)]
+    pools = (prefix_keys, prefix_values, suffix_keys, suffix_values)
+    given = split_heads(place, [in_hbm(pool) for pool in pools])
+    caches = (pools, [swapped(part, "side") for part in given])
     weights = [resident(weight) for weight in (w_query, w_key, w_value)]
     out_weight = resident(w_out)
     bias = live_bias(place, suffix_lengths, page_table, suffix_keys.shape[2])
@@ -598,9 +688,10 @@
             state, update = outs[2:]
         total, sent = pair_sum(keep, swapped(give, "side"))
         got = from_others(sent, "seq")
-        sent, stat, fresh = attend(
-            features, step, place, total, got, (cosine[step], sine[step], bias), pools, old
-        )
+        sent, stat, fresh, *kept = attend(
+            features, step, place, total, got, (cosine[step], sine[step], bias), caches, old
+        )
+        caches = kept or caches
         old.append(fresh)
         mixed = merge(sent, stat, from_others(sent, "seq"))
         part = output(place, mixed, swapped(mixed, "side"), out_weight)

time: 163 us -> 129 us (0.79)
  local copies, waits for them, and re-layouts: 27.1 us -> 4.12 us
  waiting for transfers between devices: 54.1 us -> 47.8 us
  Pallas kernels: 44.6 us -> 39.7 us
    unnamed x59 -> x25, local copies, waits for them, and re-layouts: 20.1 us -> 4.12 us
    pallas_call x3, Pallas kernels: 30.7 us -> 19.7 us  [attend(): pl.pallas_call(functools.partial(attend_kernel, features, step, len(got))...]
    ppermute x18, waiting for transfers between devices: 38.2 us -> 29.9 us  [from_others(): lax.ppermute(array, axis, [(i, (i + hop) % size) for i in range(size)])]
    dynamic_slice x4 -> x0, local copies, waits for them, and re-layouts: 6.95 us -> none  [local_split(): lax.dynamic_slice_in_dim(pool, (1 - side) * heads, heads, 1)]
    pallas_call x0 -> x1, Pallas kernels: none -> 6.75 us  [split_heads(): pl.pallas_call(split_kernel, out_shape=[pltpu.VMEM((2, pk.shape[1] // 2)...]
    ppermute x13 -> x11, waiting for transfers between devices: 15.9 us -> 17.9 us  [swapped(): return lax.ppermute(array, axis, [(0, 1), (1, 0)])]
    ppermute x13 -> x11, starting transfers between devices: 6.5 us -> 5.82 us  [swapped(): return lax.ppermute(array, axis, [(0, 1), (1, 0)])]
  transfers between devices with their start and end apart: 31 -> 29, of which waited for: 22 -> 23; matrix products, arithmetic and copies ran while one was open for 3% -> 0% of each run, Pallas kernels for 2% -> 2%
where the time goes in v2:
time: 129 us
  waiting for transfers between devices  47.8 us (37%)
  Pallas kernels  39.7 us (31%)
  starting transfers between devices  35.5 us (28%)
  local copies, waits for them, and re-layouts  4.12 us (3%)
    ppermute x18, waiting for transfers between devices, from_others(): lax.ppermute(array, axis, [(i, (i + hop) % size) for i in range(size)])  29.9 us
    ppermute x18, starting transfers between devices, from_others(): lax.ppermute(array, axis, [(i, (i + hop) % size) for i in range(size)])  29.7 us
    pallas_call x3, Pallas kernels, attend(): pl.pallas_call(functools.partial(attend_kernel, features, step, len(got))...  19.7 us
    ppermute x11, waiting for transfers between devices, swapped(): return lax.ppermute(array, axis, [(0, 1), (1, 0)])  17.9 us
    pallas_call x1, Pallas kernels, split_heads(): pl.pallas_call(split_kernel, out_shape=[pltpu.VMEM((2, pk.shape[1] // 2)...  6.75 us
    pallas_call x3, Pallas kernels, project(): pl.pallas_call(functools.partial(project_kernel, not rest), out_shape=out...  6.05 us
    ppermute x11, starting transfers between devices, swapped(): return lax.ppermute(array, axis, [(0, 1), (1, 0)])  5.82 us
    pallas_call x3, Pallas kernels, output(): pl.pallas_call(output_kernel, out_shape=jax.ShapeDtypeStruct((mine.shape[...  5.19 us
  transfers between devices with their start and end apart: 29, of which 23 were waited for; matrix products, arithmetic and copies ran while one was open for 0% of the time, Pallas kernels for 2%

profile of v2, /device:TPU:0, one launch (start us, length us, event | category | flops | bytes accessed | tf_op | source)
XLA Modules:
  0.0 128.9 jit_solution(3358638335164764309)
XLA Ops:
  0.7 6.7 %shard_map.134 = (bf16[2,2,4096,128]{3,2,1,0:T(8,128)(2,1)}, bf16[2,16,2,128,128]{4,3,2,1,0:T(8,128)(2,1)}) custom-call(s32[4]{0:T(128)S(1)} %pad_add_fusion.place, bf16[1,4,4096,128]{3,2,1,0:T(8,128)(2,1)} %refs_7_.1, bf16[1,4,4096,128]{3,2,1,0:T(8,128)(2,1)} %refs_8_.1, bf16[16,4,128,128]{3,2,1,0:T(8,128)(2,1)} %refs_9_.1, bf16[16,4,128,128]{3,2,1,0:T(8,128)(2,1)} %refs_10_.1), custom_call_target="tpu_custom_call" | custom-call | tf_op jit(solution)/shard_map/pallas_call | solution.py:235
  8.7 2.0 %shard_map.131 = (f32[16,2688]{1,0:T(8,128)S(1)}, f32[16,2688]{1,0:T(8,128)S(1)}) custom-call(s32[4]{0:T(128)S(1)} %pad_add_fusion.place, bf16[16,1024]{1,0:T(8,128)(2,1)S(1)} %copy-done.4, f32[1,1024]{1,0:T(1,128)S(1)} %bitcast.21, bf16[1024,4096]{1,0:T(8,128)(2,1)S(1)} %copy-done, bf16[1024,512]{1,0:T(8,128)(2,1)S(1)} %copy-done.2, ...), custom_call_target="tpu_custom_call" | custom-call | tf_op jit(solution)/shard_map/pallas_call | solution.py:317
  12.3 3.0 %collective-permute-done.got = f32[16,2688]{1,0:T(8,128)S(1)} collective-permute-done((f32[16,2688]{1,0:T(8,128)S(1)}, f32[16,2688]{1,0:T(8,128)S(1)}, u32[]{:S(2)}, u32[]{:S(2)}) %collective-permute-start) | collective-permute-done | bytes 172064 | tf_op jit(solution)/shard_map/ppermute | solution.py:630
  15.4 2.9 %collective-permute-start.1 = (bf16[16,2688]{1,0:T(8,128)(2,1)S(1)}, bf16[16,2688]{1,0:T(8,128)(2,1)S(1)}, u32[]{:S(2)}, u32[]{:S(2)}) collective-permute-start(bf16[16,2688]{1,0:T(8,128)(2,1)S(1)} %get-tuple-element.33), channel_id=1, source_target_pairs={{0,4},{4,8},{8,12},{12,0},{1,5},{5,9},{9,13},{13,1},{2,6},{6,10},{... | collective-permute-start | bytes 258056 | tf_op jit(solution)/shard_map/ppermute | solution.py:636
  18.3 2.6 %collective-permute-start.2 = (bf16[16,2688]{1,0:T(8,128)(2,1)S(1)}, bf16[16,2688]{1,0:T(8,128)(2,1)S(1)}, u32[]{:S(2)}, u32[]{:S(2)}) collective-permute-start(bf16[16,2688]{1,0:T(8,128)(2,1)S(1)} %get-tuple-element.33), channel_id=1, source_target_pairs={{0,8},{4,12},{8,0},{12,4},{1,9},{5,13},{9,1},{13,5},{2,10},{6,14},... | collective-permute-start | bytes 258056 | tf_op jit(solution)/shard_map/ppermute | solution.py:636
  23.8 3.2 %collective-permute-done.2.refs_2_ = bf16[16,2688]{1,0:T(8,128)(2,1)S(1)} collective-permute-done((bf16[16,2688]{1,0:T(8,128)(2,1)S(1)}, bf16[16,2688]{1,0:T(8,128)(2,1)S(1)}, u32[]{:S(2)}, u32[]{:S(2)}) %collective-permute-start.2) | collective-permute-done | bytes 86048 | tf_op jit(solution)/shard_map/ppermute | solution.py:636
  27.2 8.4 %shard_map.135 = (bf16[16,2176]{1,0:T(8,128)(2,1)S(1)}, f32[16,128]{1,0:T(8,128)S(1)}, bf16[16,512]{1,0:T(8,128)(2,1)S(1)}, bf16[2,2,2,4096,128]{4,3,2,1,0:T(8,1...) custom-call(s32[4]{0:T(128)S(1)} %pad_add_fusion.place, f32[16,2688]{1,0:T(8,128)S(1)} %get-tuple-element.32.refs_0_, ...), custom_call_target="tpu_custom_call" | custom-call | tf_op jit(solution)/shard_map/pallas_call | solution.py:561
  35.6 2.2 %collective-permute-start.6 = (bf16[16,2176]{1,0:T(8,128)(2,1)S(1)}, bf16[16,2176]{1,0:T(8,128)(2,1)S(1)}, u32[]{:S(2)}, u32[]{:S(2)}) collective-permute-start(bf16[16,2176]{1,0:T(8,128)(2,1)S(1)} %get-tuple-element.36.own), channel_id=1, source_target_pairs={{0,4},{4,8},{8,12},{12,0},{1,5},{5,9},{9,13},{13,1},{2,6},{6,10},{... | collective-permute-start | bytes 208904 | tf_op jit(solution)/shard_map/ppermute | solution.py:636
  40.2 2.2 %collective-permute-done.6.refs_0_ = bf16[16,2176]{1,0:T(8,128)(2,1)S(1)} collective-permute-done((bf16[16,2176]{1,0:T(8,128)(2,1)S(1)}, bf16[16,2176]{1,0:T(8,128)(2,1)S(1)}, u32[]{:S(2)}, u32[]{:S(2)}) %collective-permute-start.6) | collective-permute-done | bytes 69664 | tf_op jit(solution)/shard_map/ppermute | solution.py:636
  42.4 2.2 %collective-permute-done.7.refs_1_ = bf16[16,2176]{1,0:T(8,128)(2,1)S(1)} collective-permute-done((bf16[16,2176]{1,0:T(8,128)(2,1)S(1)}, bf16[16,2176]{1,0:T(8,128)(2,1)S(1)}, u32[]{:S(2)}, u32[]{:S(2)}) %collective-permute-start.7) | collective-permute-done | bytes 69664 | tf_op jit(solution)/shard_map/ppermute | solution.py:636
  46.5 3.4 %copy-done.1 = bf16[4096,1024]{1,0:T(8,128)(2,1)S(1)} copy-done((bf16[4096,1024]{1,0:T(8,128)(2,1)S(1)}, bf16[4096,1024]{1,0:T(8,128)(2,1)}, u32[]{:S(2)}) %copy-start.1) | copy-done | bytes 8388632
  53.1 2.8 %collective-permute-done.10.refs_7_ = f32[16,1024]{1,0:T(8,128)S(1)} collective-permute-done((f32[16,1024]{1,0:T(8,128)S(1)}, f32[16,1024]{1,0:T(8,128)S(1)}, u32[]{:S(2)}, u32[]{:S(2)}) %collective-permute-start.10) | collective-permute-done | bytes 65568 | tf_op jit(solution)/shard_map/ppermute | solution.py:630
  55.9 2.0 %shard_map.138 = (f32[16,2688]{1,0:T(8,128)S(1)}, f32[16,2688]{1,0:T(8,128)S(1)}, bf16[16,1024]{1,0:T(8,128)(2,1)S(1)}, f32[16,1024]{1,0:T(8,128)S(1)}) custom-call(s32[4]{0:T(128)S(1)} %pad_add_fusion.place, bf16[16,1024]{1,0:T(8,128)(2,1)S(1)} %copy-done.4, f32[1,1024]{1,0:T(1,128)S(1)} %bitcast.22, bf16[1024,4096]{1,0:T(8,128)(2,1)S(1)} %bitcast.18, ...), custom_call_target="tpu_custom_call" | custom-call | tf_op jit(solution)/shard_map/pallas_call | solution.py:317
  59.5 1.8 %collective-permute-start.12 = (bf16[16,2688]{1,0:T(8,128)(2,1)S(1)}, bf16[16,2688]{1,0:T(8,128)(2,1)S(1)}, u32[]{:S(2)}, u32[]{:S(2)}) collective-permute-start(bf16[16,2688]{1,0:T(8,128)(2,1)S(1)} %get-tuple-element.43), channel_id=1, source_target_pairs={{0,4},{4,8},{8,12},{12,0},{1,5},{5,9},{9,13},{13,1},{2,6},{6,10},{... | collective-permute-start | bytes 258056 | tf_op jit(solution)/shard_map/ppermute | solution.py:636
  63.7 3.1 %collective-permute-done.12.refs_1_ = bf16[16,2688]{1,0:T(8,128)(2,1)S(1)} collective-permute-done((bf16[16,2688]{1,0:T(8,128)(2,1)S(1)}, bf16[16,2688]{1,0:T(8,128)(2,1)S(1)}, u32[]{:S(2)}, u32[]{:S(2)}) %collective-permute-start.12) | collective-permute-done | bytes 86048 | tf_op jit(solution)/shard_map/ppermute | solution.py:636
  66.7 2.9 %collective-permute-done.13.refs_2_ = bf16[16,2688]{1,0:T(8,128)(2,1)S(1)} collective-permute-done((bf16[16,2688]{1,0:T(8,128)(2,1)S(1)}, bf16[16,2688]{1,0:T(8,128)(2,1)S(1)}, u32[]{:S(2)}, u32[]{:S(2)}) %collective-permute-start.13) | collective-permute-done | bytes 86048 | tf_op jit(solution)/shard_map/ppermute | solution.py:636
  69.6 5.4 %shard_map.140 = (bf16[16,2176]{1,0:T(8,128)(2,1)S(1)}, f32[16,128]{1,0:T(8,128)S(1)}, bf16[16,512]{1,0:T(8,128)(2,1)S(1)}) custom-call(s32[4]{0:T(128)S(1)} %pad_add_fusion.place, f32[16,2688]{1,0:T(8,128)S(1)} %get-tuple-element.42.refs_0_, bf16[16,2688]{1,0:T(8,128)(2,1)S(1)} %collective-permute-done.12.refs_1_, ...), custom_call_target="tpu_custom_call" | custom-call | tf_op jit(solution)/shard_map/pallas_call | solution.py:561
  75.0 2.4 %collective-permute-start.15 = (bf16[16,2176]{1,0:T(8,128)(2,1)S(1)}, bf16[16,2176]{1,0:T(8,128)(2,1)S(1)}, u32[]{:S(2)}, u32[]{:S(2)}) collective-permute-start(bf16[16,2176]{1,0:T(8,128)(2,1)S(1)} %get-tuple-element.47.own), channel_id=1, source_target_pairs={{0,4},{4,8},{8,12},{12,0},{1,5},{5,9},{9,13},{13,1},{2,6},{6,10},{... | collective-permute-start | bytes 208904 | tf_op jit(solution)/shard_map/ppermute | solution.py:636
  79.8 2.2 %collective-permute-done.15.refs_0_ = bf16[16,2176]{1,0:T(8,128)(2,1)S(1)} collective-permute-done((bf16[16,2176]{1,0:T(8,128)(2,1)S(1)}, bf16[16,2176]{1,0:T(8,128)(2,1)S(1)}, u32[]{:S(2)}, u32[]{:S(2)}) %collective-permute-start.15) | collective-permute-done | bytes 69664 | tf_op jit(solution)/shard_map/ppermute | solution.py:636
  82.0 2.2 %collective-permute-done.16.refs_1_ = bf16[16,2176]{1,0:T(8,128)(2,1)S(1)} collective-permute-done((bf16[16,2176]{1,0:T(8,128)(2,1)S(1)}, bf16[16,2176]{1,0:T(8,128)(2,1)S(1)}, u32[]{:S(2)}, u32[]{:S(2)}) %collective-permute-start.16) | collective-permute-done | bytes 69664 | tf_op jit(solution)/shard_map/ppermute | solution.py:636
  85.9 1.7 %shard_map.142.refs_6_ = f32[16,1024]{1,0:T(8,128)S(1)} custom-call(s32[4]{0:T(128)S(1)} %pad_add_fusion.place, bf16[16,2048]{1,0:T(8,128)(2,1)S(1)} %shard_map.141.mine, bf16[16,2048]{1,0:T(8,128)(2,1)S(1)} %collective-permute-done.18.other, bf16[4096,1024]{1,0:T(8,128)(2,1)S(1)} %bitcast.20), custom_call_target="tpu_custom_call" | custom-call | tf_op jit(solution)/shard_map/pallas_call | solution.py:620
  89.1 2.8 %collective-permute-done.19.refs_7_ = f32[16,1024]{1,0:T(8,128)S(1)} collective-permute-done((f32[16,1024]{1,0:T(8,128)S(1)}, f32[16,1024]{1,0:T(8,128)S(1)}, u32[]{:S(2)}, u32[]{:S(2)}) %collective-permute-start.19) | collective-permute-done | bytes 65568 | tf_op jit(solution)/shard_map/ppermute | solution.py:630
  91.9 2.0 %shard_map.143 = (f32[16,2688]{1,0:T(8,128)S(1)}, f32[16,2688]{1,0:T(8,128)S(1)}, bf16[16,1024]{1,0:T(8,128)(2,1)S(1)}, f32[16,1024]{1,0:T(8,128)S(1)}) custom-call(s32[4]{0:T(128)S(1)} %pad_add_fusion.place, bf16[16,1024]{1,0:T(8,128)(2,1)S(1)} %get-tuple-element.38.refs_0_, f32[1,1024]{1,0:T(1,128)S(1)} %bitcast.23, bf16[1024,4096]{1,0:T(8,128)(2,1)S(1)} %bitcast.18, ...), custom_call_target="tpu_custom_call" | custom-call | tf_op jit(solution)/shard_map/pallas_call | solution.py:317
  95.4 2.0 %collective-permute-start.21 = (bf16[16,2688]{1,0:T(8,128)(2,1)S(1)}, bf16[16,2688]{1,0:T(8,128)(2,1)S(1)}, u32[]{:S(2)}, u32[]{:S(2)}) collective-permute-start(bf16[16,2688]{1,0:T(8,128)(2,1)S(1)} %get-tuple-element.53), channel_id=1, source_target_pairs={{0,4},{4,8},{8,12},{12,0},{1,5},{5,9},{9,13},{13,1},{2,6},{6,10},{... | collective-permute-start | bytes 258056 | tf_op jit(solution)/shard_map/ppermute | solution.py:636
  99.8 2.9 %collective-permute-done.21.refs_1_ = bf16[16,2688]{1,0:T(8,128)(2,1)S(1)} collective-permute-done((bf16[16,2688]{1,0:T(8,128)(2,1)S(1)}, bf16[16,2688]{1,0:T(8,128)(2,1)S(1)}, u32[]{:S(2)}, u32[]{:S(2)}) %collective-permute-start.21) | collective-permute-done | bytes 86048 | tf_op jit(solution)/shard_map/ppermute | solution.py:636
  102.7 2.9 %collective-permute-done.22.refs_2_ = bf16[16,2688]{1,0:T(8,128)(2,1)S(1)} collective-permute-done((bf16[16,2688]{1,0:T(8,128)(2,1)S(1)}, bf16[16,2688]{1,0:T(8,128)(2,1)S(1)}, u32[]{:S(2)}, u32[]{:S(2)}) %collective-permute-start.22) | collective-permute-done | bytes 86048 | tf_op jit(solution)/shard_map/ppermute | solution.py:636
  105.6 5.9 %shard_map.145 = (bf16[16,2176]{1,0:T(8,128)(2,1)S(1)}, f32[16,128]{1,0:T(8,128)S(1)}, bf16[16,512]{1,0:T(8,128)(2,1)}) custom-call(s32[4]{0:T(128)S(1)} %pad_add_fusion.place, f32[16,2688]{1,0:T(8,128)S(1)} %get-tuple-element.52.refs_0_, bf16[16,2688]{1,0:T(8,128)(2,1)S(1)} %collective-permute-done.21.refs_1_, ...), custom_call_target="tpu_custom_call" | custom-call | tf_op jit(solution)/shard_map/pallas_call | solution.py:561
  111.5 2.3 %collective-permute-start.24 = (bf16[16,2176]{1,0:T(8,128)(2,1)S(1)}, bf16[16,2176]{1,0:T(8,128)(2,1)S(1)}, u32[]{:S(2)}, u32[]{:S(2)}) collective-permute-start(bf16[16,2176]{1,0:T(8,128)(2,1)S(1)} %get-tuple-element.55.own), channel_id=1, source_target_pairs={{0,4},{4,8},{8,12},{12,0},{1,5},{5,9},{9,13},{13,1},{2,6},{6,10},{... | collective-permute-start | bytes 208904 | tf_op jit(solution)/shard_map/ppermute | solution.py:636
  116.1 2.2 %collective-permute-done.24.refs_0_ = bf16[16,2176]{1,0:T(8,128)(2,1)S(1)} collective-permute-done((bf16[16,2176]{1,0:T(8,128)(2,1)S(1)}, bf16[16,2176]{1,0:T(8,128)(2,1)S(1)}, u32[]{:S(2)}, u32[]{:S(2)}) %collective-permute-start.24) | collective-permute-done | bytes 69664 | tf_op jit(solution)/shard_map/ppermute | solution.py:636
  118.3 2.2 %collective-permute-done.25.refs_1_ = bf16[16,2176]{1,0:T(8,128)(2,1)S(1)} collective-permute-done((bf16[16,2176]{1,0:T(8,128)(2,1)S(1)}, bf16[16,2176]{1,0:T(8,128)(2,1)S(1)}, u32[]{:S(2)}, u32[]{:S(2)}) %collective-permute-start.25) | collective-permute-done | bytes 69664 | tf_op jit(solution)/shard_map/ppermute | solution.py:636
  122.2 1.7 %shard_map.147 = f32[16,1024]{1,0:T(8,128)S(1)} custom-call(s32[4]{0:T(128)S(1)} %pad_add_fusion.place, bf16[16,2048]{1,0:T(8,128)(2,1)S(1)} %shard_map.146.mine, bf16[16,2048]{1,0:T(8,128)(2,1)S(1)} %collective-permute-done.27.other, bf16[4096,1024]{1,0:T(8,128)(2,1)S(1)} %bitcast.20), custom_call_target="tpu_custom_call" | custom-call | tf_op jit(solution)/shard_map/pallas_call | solution.py:620
  125.4 2.8 %collective-permute-done.28 = f32[16,1024]{1,0:T(8,128)S(1)} collective-permute-done((f32[16,1024]{1,0:T(8,128)S(1)}, f32[16,1024]{1,0:T(8,128)S(1)}, u32[]{:S(2)}, u32[]{:S(2)}) %collective-permute-start.28) | collective-permute-done | bytes 65568 | tf_op jit(solution)/shard_map/ppermute | solution.py:630
  (78 shorter events, 33.1 us)
Async XLA Ops:
  7.5 19.7 %collective-permute-start.4 = (bf16[2,2,4096,128]{3,2,1,0:T(8,128)(2,1)}, bf16[2,2,4096,128]{3,2,1,0:T(8,128)(2,1)}, u32[]{:S(2)}, u32[]{:S(2)}) collective-permute-start(bf16[2,2,4096,128]{3,2,1,0:T(8,128)(2,1)} %get-tuple-element.34), channel_id=1, source_target_pairs={{0,1},{1,0},{2,3},{3,2},{4,5},{5,4},{6,7},{7,6},{8,9},{9,8},{10,11... | collective-permute-start | bytes 12582920 | tf_op jit(solution)/shard_map/ppermute | solution.py:630
  8.0 19.1 %collective-permute-start.5 = (bf16[2,16,2,128,128]{4,3,2,1,0:T(8,128)(2,1)}, bf16[2,16,2,128,128]{4,3,2,1,0:T(8,128)(2,1)}, u32[]{:S(2)}, u32[]{:S(2)}) collective-permute-start(bf16[2,16,2,128,128]{4,3,2,1,0:T(8,128)(2,1)} %get-tuple-element.35), channel_id=1, source_target_pairs={{0,1},{1,0},{2,3},{3,2},{4,5},{5,4},{6,7},{7,6},{8,9},{9,8},{10,11... | collective-permute-start | bytes 6291464 | tf_op jit(solution)/shard_map/ppermute | solution.py:630
  10.7 4.5 %collective-permute-start = (f32[16,2688]{1,0:T(8,128)S(1)}, f32[16,2688]{1,0:T(8,128)S(1)}, u32[]{:S(2)}, u32[]{:S(2)}) collective-permute-start(f32[16,2688]{1,0:T(8,128)S(1)} %get-tuple-element.31), channel_id=1, source_target_pairs={{0,1},{1,0},{2,3},{3,2},{4,5},{5,4},{6,7},{7,6},{8,9},{9,8},{10,11... | collective-permute-start | bytes 516104 | tf_op jit(solution)/shard_map/ppermute | solution.py:630
  12.1 43.8 %slice-start = ((s8[8388608]{0:T(1024)(128)(4,1)}), s8[4194304]{0:T(1024)(128)(4,1)S(1)}, s32[]{:S(2)}) async-start(s8[8388608]{0:T(1024)(128)(4,1)} %bitcast.17), calls=%async_computation | async-start | bytes 8388608
  15.4 8.4 %collective-permute-start.1 = (bf16[16,2688]{1,0:T(8,128)(2,1)S(1)}, bf16[16,2688]{1,0:T(8,128)(2,1)S(1)}, u32[]{:S(2)}, u32[]{:S(2)}) collective-permute-start(bf16[16,2688]{1,0:T(8,128)(2,1)S(1)} %get-tuple-element.33), channel_id=1, source_target_pairs={{0,4},{4,8},{8,12},{12,0},{1,5},{5,9},{9,13},{13,1},{2,6},{6,10},{... | collective-permute-start | bytes 258056 | tf_op jit(solution)/shard_map/ppermute | solution.py:636
  18.3 8.7 %collective-permute-start.2 = (bf16[16,2688]{1,0:T(8,128)(2,1)S(1)}, bf16[16,2688]{1,0:T(8,128)(2,1)S(1)}, u32[]{:S(2)}, u32[]{:S(2)}) collective-permute-start(bf16[16,2688]{1,0:T(8,128)(2,1)S(1)} %get-tuple-element.33), channel_id=1, source_target_pairs={{0,8},{4,12},{8,0},{12,4},{1,9},{5,13},{9,1},{13,5},{2,10},{6,14},... | collective-permute-start | bytes 258056 | tf_op jit(solution)/shard_map/ppermute | solution.py:636
  20.9 6.2 %collective-permute-start.3 = (bf16[16,2688]{1,0:T(8,128)(2,1)S(1)}, bf16[16,2688]{1,0:T(8,128)(2,1)S(1)}, u32[]{:S(2)}, u32[]{:S(2)}) collective-permute-start(bf16[16,2688]{1,0:T(8,128)(2,1)S(1)} %get-tuple-element.33), channel_id=1, source_target_pairs={{0,12},{4,0},{8,4},{12,8},{1,13},{5,1},{9,5},{13,9},{2,14},{6,2},{... | collective-permute-start | bytes 258056 | tf_op jit(solution)/shard_map/ppermute | solution.py:636
  27.2 28.7 %slice-start.1 = ((s8[8388608]{0:T(1024)(128)(4,1)}), s8[4194304]{0:T(1024)(128)(4,1)S(1)}, s32[]{:S(2)}) async-start(s8[8388608]{0:T(1024)(128)(4,1)} %bitcast.17), calls=%async_computation.1 | async-start | bytes 8388608
  35.6 6.8 %collective-permute-start.6 = (bf16[16,2176]{1,0:T(8,128)(2,1)S(1)}, bf16[16,2176]{1,0:T(8,128)(2,1)S(1)}, u32[]{:S(2)}, u32[]{:S(2)}) collective-permute-start(bf16[16,2176]{1,0:T(8,128)(2,1)S(1)} %get-tuple-element.36.own), channel_id=1, source_target_pairs={{0,4},{4,8},{8,12},{12,0},{1,5},{5,9},{9,13},{13,1},{2,6},{6,10},{... | collective-permute-start | bytes 208904 | tf_op jit(solution)/shard_map/ppermute | solution.py:636
  37.8 6.8 %collective-permute-start.7 = (bf16[16,2176]{1,0:T(8,128)(2,1)S(1)}, bf16[16,2176]{1,0:T(8,128)(2,1)S(1)}, u32[]{:S(2)}, u32[]{:S(2)}) collective-permute-start(bf16[16,2176]{1,0:T(8,128)(2,1)S(1)} %get-tuple-element.36.own), channel_id=1, source_target_pairs={{0,8},{4,12},{8,0},{12,4},{1,9},{5,13},{9,1},{13,5},{2,10},{6,14},... | collective-permute-start | bytes 208904 | tf_op jit(solution)/shard_map/ppermute | solution.py:636
  39.4 5.4 %collective-permute-start.8 = (bf16[16,2176]{1,0:T(8,128)(2,1)S(1)}, bf16[16,2176]{1,0:T(8,128)(2,1)S(1)}, u32[]{:S(2)}, u32[]{:S(2)}) collective-permute-start(bf16[16,2176]{1,0:T(8,128)(2,1)S(1)} %get-tuple-element.36.own), channel_id=1, source_target_pairs={{0,12},{4,0},{8,4},{12,8},{1,13},{5,1},{9,5},{13,9},{2,14},{6,2},{... | collective-permute-start | bytes 208904 | tf_op jit(solution)/shard_map/ppermute | solution.py:636
  45.2 1.3 %collective-permute-start.9 = (bf16[16,2048]{1,0:T(8,128)(2,1)S(1)}, bf16[16,2048]{1,0:T(8,128)(2,1)S(1)}, u32[]{:S(2)}, u32[]{:S(2)}) collective-permute-start(bf16[16,2048]{1,0:T(8,128)(2,1)S(1)} %shard_map.136.mine), channel_id=1, source_target_pairs={{0,1},{1,0},{2,3},{3,2},{4,5},{5,4},{6,7},{7,6},{8,9},{9,8},{10,11... | collective-permute-start | bytes 196616 | tf_op jit(solution)/shard_map/ppermute | solution.py:630
  51.6 4.3 %collective-permute-start.10 = (f32[16,1024]{1,0:T(8,128)S(1)}, f32[16,1024]{1,0:T(8,128)S(1)}, u32[]{:S(2)}, u32[]{:S(2)}) collective-permute-start(f32[16,1024]{1,0:T(8,128)S(1)} %shard_map.137.refs_6_), channel_id=1, source_target_pairs={{0,2},{2,0},{1,3},{3,1},{4,6},{6,4},{5,7},{7,5},{8,10},{10,8},{9,1... | collective-permute-start | bytes 196616 | tf_op jit(solution)/shard_map/ppermute | solution.py:630
  55.9 30.0 %slice-start.2 = ((s8[8388608]{0:T(1024)(128)(4,1)}), s8[4194304]{0:T(1024)(128)(4,1)S(1)}, s32[]{:S(2)}) async-start(s8[8388608]{0:T(1024)(128)(4,1)} %bitcast.19), calls=%async_computation.2 | async-start | bytes 8388608
  57.9 1.4 %collective-permute-start.11 = (f32[16,2688]{1,0:T(8,128)S(1)}, f32[16,2688]{1,0:T(8,128)S(1)}, u32[]{:S(2)}, u32[]{:S(2)}) collective-permute-start(f32[16,2688]{1,0:T(8,128)S(1)} %get-tuple-element.41), channel_id=1, source_target_pairs={{0,1},{1,0},{2,3},{3,2},{4,5},{5,4},{6,7},{7,6},{8,9},{9,8},{10,11... | collective-permute-start | bytes 516104 | tf_op jit(solution)/shard_map/ppermute | solution.py:630
  59.5 7.3 %collective-permute-start.12 = (bf16[16,2688]{1,0:T(8,128)(2,1)S(1)}, bf16[16,2688]{1,0:T(8,128)(2,1)S(1)}, u32[]{:S(2)}, u32[]{:S(2)}) collective-permute-start(bf16[16,2688]{1,0:T(8,128)(2,1)S(1)} %get-tuple-element.43), channel_id=1, source_target_pairs={{0,4},{4,8},{8,12},{12,0},{1,5},{5,9},{9,13},{13,1},{2,6},{6,10},{... | collective-permute-start | bytes 258056 | tf_op jit(solution)/shard_map/ppermute | solution.py:636
  61.2 8.4 %collective-permute-start.13 = (bf16[16,2688]{1,0:T(8,128)(2,1)S(1)}, bf16[16,2688]{1,0:T(8,128)(2,1)S(1)}, u32[]{:S(2)}, u32[]{:S(2)}) collective-permute-start(bf16[16,2688]{1,0:T(8,128)(2,1)S(1)} %get-tuple-element.43), channel_id=1, source_target_pairs={{0,8},{4,12},{8,0},{12,4},{1,9},{5,13},{9,1},{13,5},{2,10},{6,14},... | collective-permute-start | bytes 258056 | tf_op jit(solution)/shard_map/ppermute | solution.py:636
  62.2 7.4 %collective-permute-start.14 = (bf16[16,2688]{1,0:T(8,128)(2,1)S(1)}, bf16[16,2688]{1,0:T(8,128)(2,1)S(1)}, u32[]{:S(2)}, u32[]{:S(2)}) collective-permute-start(bf16[16,2688]{1,0:T(8,128)(2,1)S(1)} %get-tuple-element.43), channel_id=1, source_target_pairs={{0,12},{4,0},{8,4},{12,8},{1,13},{5,1},{9,5},{13,9},{2,14},{6,2},{... | collective-permute-start | bytes 258056 | tf_op jit(solution)/shard_map/ppermute | solution.py:636
  75.0 7.0 %collective-permute-start.15 = (bf16[16,2176]{1,0:T(8,128)(2,1)S(1)}, bf16[16,2176]{1,0:T(8,128)(2,1)S(1)}, u32[]{:S(2)}, u32[]{:S(2)}) collective-permute-start(bf16[16,2176]{1,0:T(8,128)(2,1)S(1)} %get-tuple-element.47.own), channel_id=1, source_target_pairs={{0,4},{4,8},{8,12},{12,0},{1,5},{5,9},{9,13},{13,1},{2,6},{6,10},{... | collective-permute-start | bytes 208904 | tf_op jit(solution)/shard_map/ppermute | solution.py:636
  77.4 6.8 %collective-permute-start.16 = (bf16[16,2176]{1,0:T(8,128)(2,1)S(1)}, bf16[16,2176]{1,0:T(8,128)(2,1)S(1)}, u32[]{:S(2)}, u32[]{:S(2)}) collective-permute-start(bf16[16,2176]{1,0:T(8,128)(2,1)S(1)} %get-tuple-element.47.own), channel_id=1, source_target_pairs={{0,8},{4,12},{8,0},{12,4},{1,9},{5,13},{9,1},{13,5},{2,10},{6,14},... | collective-permute-start | bytes 208904 | tf_op jit(solution)/shard_map/ppermute | solution.py:636
  78.2 6.0 %collective-permute-start.17 = (bf16[16,2176]{1,0:T(8,128)(2,1)S(1)}, bf16[16,2176]{1,0:T(8,128)(2,1)S(1)}, u32[]{:S(2)}, u32[]{:S(2)}) collective-permute-start(bf16[16,2176]{1,0:T(8,128)(2,1)S(1)} %get-tuple-element.47.own), channel_id=1, source_target_pairs={{0,12},{4,0},{8,4},{12,8},{1,13},{5,1},{9,5},{13,9},{2,14},{6,2},{... | collective-permute-start | bytes 208904 | tf_op jit(solution)/shard_map/ppermute | solution.py:636
  84.5 1.3 %collective-permute-start.18 = (bf16[16,2048]{1,0:T(8,128)(2,1)S(1)}, bf16[16,2048]{1,0:T(8,128)(2,1)S(1)}, u32[]{:S(2)}, u32[]{:S(2)}) collective-permute-start(bf16[16,2048]{1,0:T(8,128)(2,1)S(1)} %shard_map.141.mine), channel_id=1, source_target_pairs={{0,1},{1,0},{2,3},{3,2},{4,5},{5,4},{6,7},{7,6},{8,9},{9,8},{10,11... | collective-permute-start | bytes 196616 | tf_op jit(solution)/shard_map/ppermute | solution.py:630
  87.6 4.3 %collective-permute-start.19 = (f32[16,1024]{1,0:T(8,128)S(1)}, f32[16,1024]{1,0:T(8,128)S(1)}, u32[]{:S(2)}, u32[]{:S(2)}) collective-permute-start(f32[16,1024]{1,0:T(8,128)S(1)} %shard_map.142.refs_6_), channel_id=1, source_target_pairs={{0,2},{2,0},{1,3},{3,1},{4,6},{6,4},{5,7},{7,5},{8,10},{10,8},{9,1... | collective-permute-start | bytes 196616 | tf_op jit(solution)/shard_map/ppermute | solution.py:630
  93.9 1.4 %collective-permute-start.20 = (f32[16,2688]{1,0:T(8,128)S(1)}, f32[16,2688]{1,0:T(8,128)S(1)}, u32[]{:S(2)}, u32[]{:S(2)}) collective-permute-start(f32[16,2688]{1,0:T(8,128)S(1)} %get-tuple-element.51), channel_id=1, source_target_pairs={{0,1},{1,0},{2,3},{3,2},{4,5},{5,4},{6,7},{7,6},{8,9},{9,8},{10,11... | collective-permute-start | bytes 516104 | tf_op jit(solution)/shard_map/ppermute | solution.py:630
  95.4 7.3 %collective-permute-start.21 = (bf16[16,2688]{1,0:T(8,128)(2,1)S(1)}, bf16[16,2688]{1,0:T(8,128)(2,1)S(1)}, u32[]{:S(2)}, u32[]{:S(2)}) collective-permute-start(bf16[16,2688]{1,0:T(8,128)(2,1)S(1)} %get-tuple-element.53), channel_id=1, source_target_pairs={{0,4},{4,8},{8,12},{12,0},{1,5},{5,9},{9,13},{13,1},{2,6},{6,10},{... | collective-permute-start | bytes 258056 | tf_op jit(solution)/shard_map/ppermute | solution.py:636
  97.4 8.2 %collective-permute-start.22 = (bf16[16,2688]{1,0:T(8,128)(2,1)S(1)}, bf16[16,2688]{1,0:T(8,128)(2,1)S(1)}, u32[]{:S(2)}, u32[]{:S(2)}) collective-permute-start(bf16[16,2688]{1,0:T(8,128)(2,1)S(1)} %get-tuple-element.53), channel_id=1, source_target_pairs={{0,8},{4,12},{8,0},{12,4},{1,9},{5,13},{9,1},{13,5},{2,10},{6,14},... | collective-permute-start | bytes 258056 | tf_op jit(solution)/shard_map/ppermute | solution.py:636
  98.3 7.2 %collective-permute-start.23 = (bf16[16,2688]{1,0:T(8,128)(2,1)S(1)}, bf16[16,2688]{1,0:T(8,128)(2,1)S(1)}, u32[]{:S(2)}, u32[]{:S(2)}) collective-permute-start(bf16[16,2688]{1,0:T(8,128)(2,1)S(1)} %get-tuple-element.53), channel_id=1, source_target_pairs={{0,12},{4,0},{8,4},{12,8},{1,13},{5,1},{9,5},{13,9},{2,14},{6,2},{... | collective-permute-start | bytes 258056 | tf_op jit(solution)/shard_map/ppermute | solution.py:636
  111.5 6.9 %collective-permute-start.24 = (bf16[16,2176]{1,0:T(8,128)(2,1)S(1)}, bf16[16,2176]{1,0:T(8,128)(2,1)S(1)}, u32[]{:S(2)}, u32[]{:S(2)}) collective-permute-start(bf16[16,2176]{1,0:T(8,128)(2,1)S(1)} %get-tuple-element.55.own), channel_id=1, source_target_pairs={{0,4},{4,8},{8,12},{12,0},{1,5},{5,9},{9,13},{13,1},{2,6},{6,10},{... | collective-permute-start | bytes 208904 | tf_op jit(solution)/shard_map/ppermute | solution.py:636
  113.8 6.8 %collective-permute-start.25 = (bf16[16,2176]{1,0:T(8,128)(2,1)S(1)}, bf16[16,2176]{1,0:T(8,128)(2,1)S(1)}, u32[]{:S(2)}, u32[]{:S(2)}) collective-permute-start(bf16[16,2176]{1,0:T(8,128)(2,1)S(1)} %get-tuple-element.55.own), channel_id=1, source_target_pairs={{0,8},{4,12},{8,0},{12,4},{1,9},{5,13},{9,1},{13,5},{2,10},{6,14},... | collective-permute-start | bytes 208904 | tf_op jit(solution)/shard_map/ppermute | solution.py:636
  114.6 6.0 %collective-permute-start.26 = (bf16[16,2176]{1,0:T(8,128)(2,1)S(1)}, bf16[16,2176]{1,0:T(8,128)(2,1)S(1)}, u32[]{:S(2)}, u32[]{:S(2)}) collective-permute-start(bf16[16,2176]{1,0:T(8,128)(2,1)S(1)} %get-tuple-element.55.own), channel_id=1, source_target_pairs={{0,12},{4,0},{8,4},{12,8},{1,13},{5,1},{9,5},{13,9},{2,14},{6,2},{... | collective-permute-start | bytes 208904 | tf_op jit(solution)/shard_map/ppermute | solution.py:636
  120.9 1.3 %collective-permute-start.27 = (bf16[16,2048]{1,0:T(8,128)(2,1)S(1)}, bf16[16,2048]{1,0:T(8,128)(2,1)S(1)}, u32[]{:S(2)}, u32[]{:S(2)}) collective-permute-start(bf16[16,2048]{1,0:T(8,128)(2,1)S(1)} %shard_map.146.mine), channel_id=1, source_target_pairs={{0,1},{1,0},{2,3},{3,2},{4,5},{5,4},{6,7},{7,6},{8,9},{9,8},{10,11... | collective-permute-start | bytes 196616 | tf_op jit(solution)/shard_map/ppermute | solution.py:630
  123.9 4.3 %collective-permute-start.28 = (f32[16,1024]{1,0:T(8,128)S(1)}, f32[16,1024]{1,0:T(8,128)S(1)}, u32[]{:S(2)}, u32[]{:S(2)}) collective-permute-start(f32[16,1024]{1,0:T(8,128)S(1)} %shard_map.147), channel_id=1, source_target_pairs={{0,2},{2,0},{1,3},{3,1},{4,6},{6,4},{5,7},{7,5},{8,10},{10,8},{9,1... | collective-permute-start | bytes 196616 | tf_op jit(solution)/shard_map/ppermute | solution.py:630
  (9 other events, 63.7 us)

commit v3 on v2

--- a/solution.py
+++ b/solution.py
@@ -189,7 +189,8 @@
 VMEM_SPEC = pl.BlockSpec(memory_space=pltpu.VMEM)
 SMEM_SPEC = pl.BlockSpec(memory_space=pltpu.SMEM)
 HBM_SPEC = pl.BlockSpec(memory_space=pltpu.HBM)
-PARAMS = pltpu.CompilerParams(vmem_limit_bytes=13 * 1024 * 1024)
+PARAMS = pltpu.CompilerParams(vmem_limit_bytes=4 * 1024 * 1024)
+LARGE_PARAMS = pltpu.CompilerParams(vmem_limit_bytes=13 * 1024 * 1024)
 
 
 def resident(array):
@@ -217,32 +218,59 @@
         copy.wait()
 
 
-def split_kernel(place, pk, pv, sk, sv, prefix, suffix, sems):
+def copied(pairs, sems):
+    copies = [
+        pltpu.make_async_copy(source, target, sems.at[n])
+        for n, (source, target) in enumerate(pairs)
+    ]
+    for copy in copies:
+        copy.start()
+    return copies
+
+
+def halves(place, pools, prefix, suffix):
     heads = prefix.shape[1]
-    away = pl.ds((1 - place[0]) * heads, heads)
-    move(
-        [
-            pltpu.make_async_copy(pk.at[0, away], prefix.at[0], sems.at[0]),
-            pltpu.make_async_copy(pv.at[0, away], prefix.at[1], sems.at[1]),
-            pltpu.make_async_copy(sk.at[:, away], suffix.at[0], sems.at[2]),
-            pltpu.make_async_copy(sv.at[:, away], suffix.at[1], sems.at[3]),
-        ]
-    )
-
-
-def split_heads(place, pools):
+    part = pl.ds(place[0] * heads, heads)
+    pk, pv, sk, sv = pools
+    return [
+        (sk.at[:, part], suffix.at[0]),
+        (pk.at[0, part], prefix.at[0]),
+        (sv.at[:, part], suffix.at[1]),
+        (pv.at[0, part], prefix.at[1]),
+    ]
+
+
+def half_shapes(pools):
     pk, sk = pools[0], pools[2]
+    return [
+        pltpu.VMEM((2, pk.shape[1] // 2) + pk.shape[2:], pk.dtype),
+        pltpu.VMEM((2, sk.shape[0], sk.shape[1] // 2) + sk.shape[2:], sk.dtype),
+    ]
+
+
+def load_kernel(pools, place, *refs):
+    count = (len(refs) - 2 + 2 * (pools > 0)) // 2
+    sources, outs, sems = refs[:count], refs[count + 1 : -1], refs[-1]
+    pairs = list(zip(sources[pools:], outs[2 * (pools > 0) :]))
+    if pools:
+        pairs = halves(place, sources[:pools], *outs[:2]) + pairs
+    for copy in copied(pairs, sems):
+        copy.wait()
+
+
+def load(place, pools, weights, after):
+    sources = [in_hbm(array) for array in (*pools, *weights)]
+    shapes = half_shapes(pools) if pools else []
+    shapes = shapes + [pltpu.VMEM(w.shape, w.dtype) for w in weights]
     return pl.pallas_call(
-        split_kernel,
-        out_shape=[
-            pltpu.VMEM((2, pk.shape[1] // 2) + pk.shape[2:], pk.dtype),
-            pltpu.VMEM((2, sk.shape[0], sk.shape[1] // 2) + sk.shape[2:], sk.dtype),
-        ],
-        in_specs=[SMEM_SPEC] + [HBM_SPEC] * 4,
-        out_specs=[VMEM_SPEC] * 2,
-        scratch_shapes=[pltpu.SemaphoreType.DMA((4,))],
+        functools.partial(load_kernel, len(pools)),
+        out_shape=shapes,
+        in_specs=[SMEM_SPEC] + [HBM_SPEC] * len(sources) + [VMEM_SPEC],
+        out_specs=[VMEM_SPEC] * len(shapes),
+        scratch_shapes=[pltpu.SemaphoreType.DMA((len(sources),))],
         compiler_params=PARAMS,
-    )(place, *pools)
+        cost_estimate=pl.CostEstimate(flops=0, bytes_accessed=1 << 25, transcendentals=0),
+    )(place, *sources, after)
 
 
 def bias_kernel(place, lengths, table, bias):
@@ -272,54 +300,80 @@
 
 
 def project_kernel(first, place, *refs):
+    x_ref, gain, *weights = refs[:5]
     if first:
-        x_ref, gain, w_query, w_key, w_value, keep, give = refs
-        wide = x_ref[...].astype(F32)
+        keep, give, *buffers, sems = refs[5:]
     else:
-        x_ref, gain, w_query, w_key, w_value, sum_ref, mine, other = refs[:8]
-        keep, give, new_x, new_sum = refs[8:]
+        sum_ref, mine, other, keep, give, new_x, new_sum = refs[5:]
         delta = mine[...] + other[...]
         new_sum[...] = sum_ref[...] + delta
         state = (x_ref[...].astype(F32) + delta).astype(BF16)
         new_x[...] = state
         wide = state.astype(F32)
+    tiles = []
+    for out, who in ((give, 1 - place[0]), (keep, place[0])):
+        at = 0
+        for index, weight in enumerate(weights):
+            half = weight.shape[1] // 2
+            tile = min(1024, half)
+            for begin in range(0, half, tile):
+                columns = pl.ds(pl.multiple_of(who * half + begin, tile), tile)
+                tiles.append((out, at + begin, tile, index, columns))
+            at += half
+    copies = []
+    if first:
+        copies = copied(
+            [(x_ref, buffers[3]), (gain, buffers[4])]
+            + [
+                (weights[index].at[:, columns], buffers[index].at[:, columns])
+                for _, _, _, index, columns in tiles
+            ],
+            sems,
+        )
+        weights = buffers
+        copies[0].wait()
+        copies[1].wait()
+        wide = buffers[3][...].astype(F32)
+        gain = buffers[4]
     scaled = (wide * gain[...]).astype(BF16)
     squares = jnp.sum(wide * wide, axis=1, keepdims=True)
     column = lanes(wide.shape[0])
-    query = w_query.shape[1] // 2
-    key = w_key.shape[1] // 2
-    side = place[0]
-    for out, who in ((give, 1 - side), (keep, side)):
-        tile = min(1024, query)
-        for at in range(0, query, tile):
-            columns = pl.ds(pl.multiple_of(who * query + at, tile), tile)
-            out[:, at : at + tile] = jnp.dot(
-                scaled, w_query[:, columns], preferred_element_type=F32
-            )
-        columns = pl.ds(pl.multiple_of(who * key, key), key)
-        out[:, query : query + key] = jnp.dot(
-            scaled, w_key[:, columns], preferred_element_type=F32
-        )
-        out[:, query + key : query + 2 * key] = jnp.dot(
-            scaled, w_value[:, columns], preferred_element_type=F32
-        )
-        out[:, query + 2 * key :] = jnp.where(column == 0, squares, 0.0)
+    for out in (give, keep):
+        out[:, out.shape[1] - LANES :] = jnp.where(column == 0, squares, 0.0)
+    for n, (out, at, tile, index, columns) in enumerate(tiles):
+        if copies:
+            copies[n + 2].wait()
+        out[:, at : at + tile] = jnp.dot(
+            scaled, weights[index][:, columns], preferred_element_type=F32
+        )
 
 
 def project(place, x, gain, weights, rest):
     rows = x.shape[0]
     width = sum(w.shape[1] for w in weights) // 2 + LANES
-    halves = [jax.ShapeDtypeStruct((rows, width), F32)] * 2
-    out_shape = halves if not rest else halves + [
-        jax.ShapeDtypeStruct(x.shape, BF16),
-        jax.ShapeDtypeStruct(x.shape, F32),
-    ]
+    out_shape = [jax.ShapeDtypeStruct((rows, width), F32)] * 2
+    if rest:
+        weights = [resident(weight) for weight in weights]
+        scratch = []
+        out_shape = out_shape + [
+            jax.ShapeDtypeStruct(x.shape, BF16),
+            jax.ShapeDtypeStruct(x.shape, F32),
+        ]
+    else:
+        weights = [in_hbm(weight) for weight in weights]
+        x, gain = in_hbm(x), in_hbm(gain)
+        count = 2 + 2 * sum(max(1, w.shape[1] // 2048) for w in weights)
+        scratch = [pltpu.VMEM(w.shape, w.dtype) for w in (*weights, x, gain)]
+        scratch.append(pltpu.SemaphoreType.DMA((count,)))
     return pl.pallas_call(
         functools.partial(project_kernel, not rest),
         out_shape=out_shape,
-        in_specs=[SMEM_SPEC] + [VMEM_SPEC] * (5 + len(rest)),
+        in_specs=[SMEM_SPEC]
+        + [VMEM_SPEC if rest else HBM_SPEC] * 5
+        + [VMEM_SPEC] * len(rest),
         out_specs=[VMEM_SPEC] * len(out_shape),
-        compiler_params=PARAMS,
+        scratch_shapes=scratch,
+        compiler_params=PARAMS if rest else LARGE_PARAMS,
     )(place, x, gain, *weights, *rest)
 
 
@@ -379,31 +433,19 @@
     total_ref = refs[0]
     got = refs[1 : 1 + others]
     cos_ref, sin_ref, bias_ref = refs[1 + others : 4 + others]
+    own_prefix, own_suffix, *far = refs[4 + others : (10 if step == 0 else 8) + others]
+    refs = refs[(10 if step == 0 else 8) + others :]
+    old, (sent, stat, fresh) = refs[:step], refs[step : 3 + step]
+    heads = own_prefix.shape[1]
+    waits = []
     if step == 0:
-        pk, pv, sk, sv, got_prefix, got_suffix = refs[4 + others : 10 + others]
-        sent, stat, fresh, prefix, suffix, sems = refs[10 + others :]
-        old = ()
-        heads = got_prefix.shape[1]
-        own = pl.ds(place[0] * heads, heads)
-        waits = [
-            pltpu.make_async_copy(got_suffix.at[0], suffix.at[0, 1], sems.at[0]),
-            pltpu.make_async_copy(sk.at[:, own], suffix.at[0, 0], sems.at[1]),
-            pltpu.make_async_copy(got_prefix.at[0], prefix.at[0, 1], sems.at[2]),
-            pltpu.make_async_copy(pk.at[0, own], prefix.at[0, 0], sems.at[3]),
-            pltpu.make_async_copy(got_suffix.at[1], suffix.at[1, 1], sems.at[4]),
-            pltpu.make_async_copy(sv.at[:, own], suffix.at[1, 0], sems.at[5]),
-            pltpu.make_async_copy(got_prefix.at[1], prefix.at[1, 1], sems.at[6]),
-            pltpu.make_async_copy(pv.at[0, own], prefix.at[1, 0], sems.at[7]),
-        ]
-        for copy in waits:
-            copy.start()
+        got_prefix, got_suffix, sems = refs[3:]
+        waits = copied(halves(place, far, got_prefix, got_suffix), sems)
     else:
-        prefix, suffix = refs[4 + others : 6 + others]
-        old = refs[6 + others : 6 + others + step]
-        sent, stat, fresh = refs[6 + others + step :]
-        waits = []
+        got_prefix, got_suffix = far
+    prefix = (own_prefix, got_prefix)
+    suffix = (own_suffix, got_suffix)
     rows = total_ref.shape[0]
-    heads = prefix.shape[2]
     width = total_ref.shape[1] - LANES
     query_width = width - 2 * heads * HD
     base, starts = place[1], (place[2], place[3])
@@ -464,30 +506,30 @@
         for head in range(heads)
     ]
 
-    slots, page = suffix.shape[2], suffix.shape[4]
-    length = prefix.shape[3]
+    slots, page = own_suffix.shape[1], own_suffix.shape[3]
+    length = own_prefix.shape[2]
     chunk = min(2048, length)
     pieces_of = [(src, at) for src in range(2) for at in range(0, length, chunk)]
 
     def pool(kind, src, head):
-        return suffix[kind, src, :, head].reshape(slots * page, HD)
-
-    for copy in waits[:4]:
-        copy.wait()
-    near_scores = [
-        [against(few[head][src], pool(0, src, head)) + bias_ref[src] for src in range(2)]
-        for head in range(heads)
-    ]
-    far_scores = [
-        [
-            against(packed[head], prefix[0, src, head, at : at + chunk])
-            for src, at in pieces_of
-        ]
-        for head in range(heads)
-    ]
+        return suffix[src][kind, :, head].reshape(slots * page, HD)
+
+    near_scores = [[None] * 2 for _ in range(heads)]
+    far_scores = [[None] * len(pieces_of) for _ in range(heads)]
+    for src in range(2):
+        if src == 1:
+            for copy in waits[:2]:
+                copy.wait()
+        for head in range(heads):
+            near_scores[head][src] = against(few[head][src], pool(0, src, head)) + bias_ref[src]
+            for n, (whose, at) in enumerate(pieces_of):
+                if whose == src:
+                    far_scores[head][n] = against(
+                        packed[head], prefix[src][0, head, at : at + chunk]
+                    )
     near_tops = [[row_max([score]) for score in scores] for scores in near_scores]
     far_tops = [row_max(scores) for scores in far_scores]
-    for copy in waits[4:]:
+    for copy in waits[2:]:
         copy.wait()
     near = [
         [
@@ -502,7 +544,7 @@
         far_total, far_acc = weigh(
             far_scores[head],
             far_tops[head],
-            [prefix[1, src, head, at : at + chunk] for src, at in pieces_of],
+            [prefix[src][1, head, at : at + chunk] for src, at in pieces_of],
             scale,
         )
         for g in range(GROUP):
@@ -543,20 +585,17 @@
 
 def attend(features, step, place, total, got, tables, caches, old):
     rows = total.shape[0]
-    out_shape, scratch = [], []
+    own, far = caches
+    heads = own[0].shape[1]
     if step == 0:
-        pools, (got_prefix, got_suffix) = caches
-        heads = got_prefix.shape[1]
-        out_shape = [
-            pltpu.VMEM((2, 2) + part.shape[1:], BF16) for part in (got_prefix, got_suffix)
-        ]
-        scratch = [pltpu.SemaphoreType.DMA((8,))]
-        inputs = [in_hbm(array) for array in (*pools, got_prefix, got_suffix)]
-        specs = [HBM_SPEC] * len(inputs)
+        inputs = [resident(array) for array in own] + [in_hbm(array) for array in far]
+        specs = [VMEM_SPEC] * 2 + [HBM_SPEC] * 4
+        out_shape = [pltpu.VMEM(part.shape, BF16) for part in own]
+        scratch = [pltpu.SemaphoreType.DMA((4,))]
     else:
-        heads = caches[0].shape[2]
-        inputs = [resident(array) for array in caches]
-        specs = [VMEM_SPEC] * len(inputs)
+        inputs = [resident(array) for array in (*own, *far)]
+        specs = [VMEM_SPEC] * 4
+        out_shape, scratch = [], []
     small = [total, *got, *tables]
     return pl.pallas_call(
         functools.partial(attend_kernel, features, step, len(got)),
@@ -569,7 +608,7 @@
         in_specs=[SMEM_SPEC] + [VMEM_SPEC] * len(small) + specs + [VMEM_SPEC] * len(old),
         out_specs=[VMEM_SPEC] * (3 + len(out_shape)),
         scratch_shapes=scratch,
-        compiler_params=PARAMS,
+        compiler_params=LARGE_PARAMS,
     )(place, *small, *inputs, *old)
 
 
@@ -661,10 +700,8 @@
     first_got = base + side * SAMP_DEV
     place = jnp.stack([side, base, first_own, first_got]).astype(jnp.int32)
     pools = (prefix_keys, prefix_values, suffix_keys, suffix_values)
-    given = split_heads(place, [in_hbm(pool) for pool in pools])
-    caches = (pools, [swapped(part, "side") for part in given])
-    weights = [resident(weight) for weight in (w_query, w_key, w_value)]
-    out_weight = resident(w_out)
+    weights = (w_query, w_key, w_value)
+    far = [swapped(pool, "side") for pool in pools[2:]]
     bias = live_bias(place, suffix_lengths, page_table, suffix_keys.shape[2])
     half = HD // 2
     freq = 500000.0 ** (-(jnp.arange(half, dtype=F32) * 2.0 / HD))
@@ -682,19 +719,28 @@
     rest = ()
     old = []
     for step in range(STEPS):
-        outs = project(place, state, gain_row, weights, rest)
-        keep, give = outs[:2]
+        keep, give, *more = project(place, state, gain_row, weights, rest)
+        got_sum = swapped(give, "side")
         if rest:
-            state, update = outs[2:]
-        total, sent = pair_sum(keep, swapped(give, "side"))
+            state, update = more
+        else:
+            got_sum, *given = lax.optimization_barrier((got_sum, *far, *pools[:2]))
+            far = [swapped(pool, "side") for pool in given[2:]] + given[:2]
+        total, sent = pair_sum(keep, got_sum)
+        if not rest:
+            *own, out_weight = load(place, pools, [w_out], sent)
         got = from_others(sent, "seq")
         sent, stat, fresh, *kept = attend(
-            features, step, place, total, got, (cosine[step], sine[step], bias), caches, old
-        )
-        caches = kept or caches
+            features, step, place, total, got, (cosine[step], sine[step], bias), (own, far), old
+        )
+        far = kept or far
+        got = from_others(sent, "seq")
+        if not rest:
+            weights = load(place, (), weights, stat)
+            got, weights = lax.optimization_barrier((got, weights))
         old.append(fresh)
-        mixed = merge(sent, stat, from_others(sent, "seq"))
-        part = output(place, mixed, swapped(mixed, "side"), out_weight)
+        mixed = merge(sent, stat, got)
+        part = output(place, mixed, swapped(mixed, "side"), resident(out_weight))
         rest = (update, part, swapped(part, "head"))
     delta = rest[1] + rest[2]
     return ((state.astype(F32) + delta).astype(BF16), update + delta)

time: 129 us -> 122 us (0.946)
  waiting for transfers between devices: 47.8 us -> 39.3 us
  Pallas kernels: 39.7 us -> 44.8 us
  local copies, waits for them, and re-layouts: 4.12 us -> 0.09 us
    ppermute x18, waiting for transfers between devices: 29.9 us -> 23.3 us  [from_others(): lax.ppermute(array, axis, [(i, (i + hop) % size) for i in range(size)])]
    unnamed x25 -> x11, local copies, waits for them, and re-layouts: 4.12 us -> 0.09 us
    pallas_call x1 -> x2, Pallas kernels: 6.75 us -> 10.3 us  [load(): pl.pallas_call(functools.partial(load_kernel, len(pools)), out_shape=shap...]
    pallas_call x3, Pallas kernels: 6.05 us -> 9.38 us  [project(): pl.pallas_call(functools.partial(project_kernel, not rest), out_shape=out...]
    ppermute x11 -> x13, waiting for transfers between devices: 17.9 us -> 16 us  [swapped(): return lax.ppermute(array, axis, [(0, 1), (1, 0)])]
    pallas_call x3, Pallas kernels: 19.7 us -> 17.9 us  [attend(): pl.pallas_call(functools.partial(attend_kernel, features, step, len(got))...]
    ppermute x11 -> x13, starting transfers between devices: 5.82 us -> 6.32 us  [swapped(): return lax.ppermute(array, axis, [(0, 1), (1, 0)])]
  transfers between devices with their start and end apart: 29 -> 31, of which waited for: 23 -> 20; matrix products, arithmetic and copies ran while one was open for 0% -> 0% of each run, Pallas kernels for 2% -> 14%
where the time goes in v3:
time: 122 us
  Pallas kernels  44.8 us (37%)
  waiting for transfers between devices  39.3 us (32%)
  starting transfers between devices  35.5 us (29%)
    ppermute x18, starting transfers between devices, from_others(): lax.ppermute(array, axis, [(i, (i + hop) % size) for i in range(size)])  29.2 us
    ppermute x18, waiting for transfers between devices, from_others(): lax.ppermute(array, axis, [(i, (i + hop) % size) for i in range(size)])  23.3 us
    pallas_call x3, Pallas kernels, attend(): pl.pallas_call(functools.partial(attend_kernel, features, step, len(got))...  17.9 us
    ppermute x13, waiting for transfers between devices, swapped(): return lax.ppermute(array, axis, [(0, 1), (1, 0)])  16 us
    pallas_call x2, Pallas kernels, load(): pl.pallas_call(functools.partial(load_kernel, len(pools)), out_shape=shap...  10.3 us
    pallas_call x3, Pallas kernels, project(): pl.pallas_call(functools.partial(project_kernel, not rest), out_shape=out...  9.38 us
    ppermute x13, starting transfers between devices, swapped(): return lax.ppermute(array, axis, [(0, 1), (1, 0)])  6.32 us
    pallas_call x3, Pallas kernels, output(): pl.pallas_call(output_kernel, out_shape=jax.ShapeDtypeStruct((mine.shape[...  5.19 us
  transfers between devices with their start and end apart: 31, of which 20 were waited for; matrix products, arithmetic and copies ran while one was open for 0% of the time, Pallas kernels for 14%

profile of v3, /device:TPU:0, one launch (start us, length us, event | category | flops | bytes accessed | tf_op | source)
XLA Modules:
  0.0 121.6 jit_solution(548464578935908905)
XLA Ops:
  1.3 5.3 %shard_map.131 = (f32[16,2688]{1,0:T(8,128)S(1)}, f32[16,2688]{1,0:T(8,128)S(1)}) custom-call(s32[4]{0:T(128)S(1)} %pad_add_fusion.place, bf16[16,1024]{1,0:T(8,128)(2,1)} %refs_0_.7, f32[1,1024]{1,0:T(1,128)} %bitcast.17, bf16[1024,4096]{1,0:T(8,128)(2,1)} %refs_0_.6, bf16[1024,512]{1,0:T(8,128)(2,1)} %refs_1_.3, bf16[1024,512]{1,0:T(8,128)(2,1)} %refs_2_.5), custom_call_target="tpu_custom_call" | custom-call | tf_op jit(solution)/shard_map/pallas_call | solution.py:368
  9.9 2.9 %collective-permute-start.3 = (bf16[16,2688]{1,0:T(8,128)(2,1)S(1)}, bf16[16,2688]{1,0:T(8,128)(2,1)S(1)}, u32[]{:S(2)}, u32[]{:S(2)}) collective-permute-start(bf16[16,2688]{1,0:T(8,128)(2,1)S(1)} %get-tuple-element.49.refs_5_), channel_id=1, source_target_pairs={{0,4},{4,8},{8,12},{12,0},{1,5},{5,9},{9,13},{13,1},{2,6},{6,10},{... | collective-permute-start | bytes 258056 | tf_op jit(solution)/shard_map/ppermute | solution.py:675
  12.9 2.6 %collective-permute-start.4 = (bf16[16,2688]{1,0:T(8,128)(2,1)S(1)}, bf16[16,2688]{1,0:T(8,128)(2,1)S(1)}, u32[]{:S(2)}, u32[]{:S(2)}) collective-permute-start(bf16[16,2688]{1,0:T(8,128)(2,1)S(1)} %get-tuple-element.49.refs_5_), channel_id=1, source_target_pairs={{0,8},{4,12},{8,0},{12,4},{1,9},{5,13},{9,1},{13,5},{2,10},{6,14},... | collective-permute-start | bytes 258056 | tf_op jit(solution)/shard_map/ppermute | solution.py:675
  16.9 5.9 %shard_map.134 = (bf16[2,2,4096,128]{3,2,1,0:T(8,128)(2,1)S(1)}, bf16[2,16,2,128,128]{4,3,2,1,0:T(8,128)(2,1)S(1)}, bf16[4096,1024]{1,0:T(8,128)(2,1)S(1)}) custom-call(s32[4]{0:T(128)S(1)} %pad_add_fusion.place, bf16[1,4,4096,128]{3,2,1,0:T(8,128)(2,1)} %refs_0_.5, bf16[1,4,4096,128]{3,2,1,0:T(8,128)(2,1)} %refs_1_.2, bf16[16,4,128,128]{3,2,1,0:T(8,128)(2,1)} %refs_2_.4, ...), custom_call_target="tpu_custom_call" | custom-call | bytes 33554432 | tf_op jit(solution)/shard_map/pallas_call | solution.py:265
  22.8 6.4 %shard_map.135 = (bf16[16,2176]{1,0:T(8,128)(2,1)S(1)}, f32[16,128]{1,0:T(8,128)S(1)}, bf16[16,512]{1,0:T(8,128)(2,1)S(1)}, bf16[2,2,4096,128]{3,2,1,0:T(8,128)(2,1)S(1)}, bf16[2,16,2,128,128]{4,3,2,1,0:T(8,128)(2,1)S(1)}) custom-call(s32[4]{0:T(128)S(1)} %pad_add_fusion.place, f32[16,2688]{1,0:T(8,128)S(1)} %get-tuple-element.48.refs_0_, ...), custom_call_target="tpu_custom_call" | custom-call | tf_op jit(solution)/shard_map/pallas_call | solution.py:600
  29.3 4.0 %collective-permute-start.10 = (bf16[16,2176]{1,0:T(8,128)(2,1)S(1)}, bf16[16,2176]{1,0:T(8,128)(2,1)S(1)}, u32[]{:S(2)}, u32[]{:S(2)}) collective-permute-start(bf16[16,2176]{1,0:T(8,128)(2,1)S(1)} %get-tuple-element.56.own), channel_id=1, source_target_pairs={{0,12},{4,0},{8,4},{12,8},{1,13},{5,1},{9,5},{13,9},{2,14},{6,2},{... | collective-permute-start | bytes 208904 | tf_op jit(solution)/shard_map/ppermute | solution.py:675
  34.2 4.5 %shard_map.136 = (bf16[1024,4096]{1,0:T(8,128)(2,1)S(1)}, bf16[1024,512]{1,0:T(8,128)(2,1)S(1)}, bf16[1024,512]{1,0:T(8,128)(2,1)S(1)}) custom-call(s32[4]{0:T(128)S(1)} %pad_add_fusion.place, bf16[1024,4096]{1,0:T(8,128)(2,1)} %refs_0_.6, bf16[1024,512]{1,0:T(8,128)(2,1)} %refs_1_.3, bf16[1024,512]{1,0:T(8,128)(2,1)} %refs_2_.5, ...), custom_call_target="tpu_custom_call" | custom-call | bytes 33554432 | tf_op jit(solution)/shard_map/pallas_call | solution.py:265
  42.9 1.7 %shard_map.138.refs_6_ = f32[16,1024]{1,0:T(8,128)S(1)} custom-call(s32[4]{0:T(128)S(1)} %pad_add_fusion.place, bf16[16,2048]{1,0:T(8,128)(2,1)S(1)} %shard_map.137.mine, bf16[16,2048]{1,0:T(8,128)(2,1)S(1)} %collective-permute-done.11.other, bf16[4096,1024]{1,0:T(8,128)(2,1)S(1)} %get-tuple-element.67.weight), custom_call_target="tpu_custom_call" | custom-call | tf_op jit(solution)/shard_map/pallas_call | solution.py:659
  44.6 1.5 %collective-permute-start.12 = (f32[16,1024]{1,0:T(8,128)S(1)}, f32[16,1024]{1,0:T(8,128)S(1)}, u32[]{:S(2)}, u32[]{:S(2)}) collective-permute-start(f32[16,1024]{1,0:T(8,128)S(1)} %shard_map.138.refs_6_), channel_id=1, source_target_pairs={{0,2},{2,0},{1,3},{3,1},{4,6},{6,4},{5,7},{7,5},{8,10},{10,8},{9,1... | collective-permute-start | bytes 196616 | tf_op jit(solution)/shard_map/ppermute | solution.py:669
  46.1 2.8 %collective-permute-done.12.refs_7_ = f32[16,1024]{1,0:T(8,128)S(1)} collective-permute-done((f32[16,1024]{1,0:T(8,128)S(1)}, f32[16,1024]{1,0:T(8,128)S(1)}, u32[]{:S(2)}, u32[]{:S(2)}) %collective-permute-start.12) | collective-permute-done | bytes 65568 | tf_op jit(solution)/shard_map/ppermute | solution.py:669
  48.9 2.0 %shard_map.139 = (f32[16,2688]{1,0:T(8,128)S(1)}, f32[16,2688]{1,0:T(8,128)S(1)}, bf16[16,1024]{1,0:T(8,128)(2,1)S(1)}, f32[16,1024]{1,0:T(8,128)S(1)}) custom-call(s32[4]{0:T(128)S(1)} %pad_add_fusion.place, bf16[16,1024]{1,0:T(8,128)(2,1)S(1)} %copy-done, f32[1,1024]{1,0:T(1,128)S(1)} %bitcast.18, bf16[1024,4096]{1,0:T(8,128)(2,1)S(1)} %get-tuple-element.61.refs_2_, ...), custom_call_target="tpu_custom_call" | custom-call | tf_op jit(solution)/shard_map/pallas_call | solution.py:368
  56.2 3.4 %collective-permute-done.14.refs_1_ = bf16[16,2688]{1,0:T(8,128)(2,1)S(1)} collective-permute-done((bf16[16,2688]{1,0:T(8,128)(2,1)S(1)}, bf16[16,2688]{1,0:T(8,128)(2,1)S(1)}, u32[]{:S(2)}, u32[]{:S(2)}) %collective-permute-start.14) | collective-permute-done | bytes 86048 | tf_op jit(solution)/shard_map/ppermute | solution.py:675
  59.7 2.9 %collective-permute-done.15.refs_2_ = bf16[16,2688]{1,0:T(8,128)(2,1)S(1)} collective-permute-done((bf16[16,2688]{1,0:T(8,128)(2,1)S(1)}, bf16[16,2688]{1,0:T(8,128)(2,1)S(1)}, u32[]{:S(2)}, u32[]{:S(2)}) %collective-permute-start.15) | collective-permute-done | bytes 86048 | tf_op jit(solution)/shard_map/ppermute | solution.py:675
  62.6 5.5 %shard_map.141 = (bf16[16,2176]{1,0:T(8,128)(2,1)S(1)}, f32[16,128]{1,0:T(8,128)S(1)}, bf16[16,512]{1,0:T(8,128)(2,1)S(1)}) custom-call(s32[4]{0:T(128)S(1)} %pad_add_fusion.place, f32[16,2688]{1,0:T(8,128)S(1)} %get-tuple-element.72.refs_0_, bf16[16,2688]{1,0:T(8,128)(2,1)S(1)} %collective-permute-done.14.refs_1_, ...), custom_call_target="tpu_custom_call" | custom-call | tf_op jit(solution)/shard_map/pallas_call | solution.py:600
  68.1 2.1 %collective-permute-start.17 = (bf16[16,2176]{1,0:T(8,128)(2,1)S(1)}, bf16[16,2176]{1,0:T(8,128)(2,1)S(1)}, u32[]{:S(2)}, u32[]{:S(2)}) collective-permute-start(bf16[16,2176]{1,0:T(8,128)(2,1)S(1)} %get-tuple-element.77.own), channel_id=1, source_target_pairs={{0,4},{4,8},{8,12},{12,0},{1,5},{5,9},{9,13},{13,1},{2,6},{6,10},{... | collective-permute-start | bytes 208904 | tf_op jit(solution)/shard_map/ppermute | solution.py:675
  71.0 1.7 %collective-permute-start.19 = (bf16[16,2176]{1,0:T(8,128)(2,1)S(1)}, bf16[16,2176]{1,0:T(8,128)(2,1)S(1)}, u32[]{:S(2)}, u32[]{:S(2)}) collective-permute-start(bf16[16,2176]{1,0:T(8,128)(2,1)S(1)} %get-tuple-element.77.own), channel_id=1, source_target_pairs={{0,12},{4,0},{8,4},{12,8},{1,13},{5,1},{9,5},{13,9},{2,14},{6,2},{... | collective-permute-start | bytes 208904 | tf_op jit(solution)/shard_map/ppermute | solution.py:675
  72.6 1.9 %collective-permute-done.17.refs_0_ = bf16[16,2176]{1,0:T(8,128)(2,1)S(1)} collective-permute-done((bf16[16,2176]{1,0:T(8,128)(2,1)S(1)}, bf16[16,2176]{1,0:T(8,128)(2,1)S(1)}, u32[]{:S(2)}, u32[]{:S(2)}) %collective-permute-start.17) | collective-permute-done | bytes 69664 | tf_op jit(solution)/shard_map/ppermute | solution.py:675
  74.6 2.3 %collective-permute-done.18.refs_1_ = bf16[16,2176]{1,0:T(8,128)(2,1)S(1)} collective-permute-done((bf16[16,2176]{1,0:T(8,128)(2,1)S(1)}, bf16[16,2176]{1,0:T(8,128)(2,1)S(1)}, u32[]{:S(2)}, u32[]{:S(2)}) %collective-permute-start.18) | collective-permute-done | bytes 69664 | tf_op jit(solution)/shard_map/ppermute | solution.py:675
  78.5 1.7 %shard_map.143.refs_6_ = f32[16,1024]{1,0:T(8,128)S(1)} custom-call(s32[4]{0:T(128)S(1)} %pad_add_fusion.place, bf16[16,2048]{1,0:T(8,128)(2,1)S(1)} %shard_map.142.mine, bf16[16,2048]{1,0:T(8,128)(2,1)S(1)} %collective-permute-done.20.other, bf16[4096,1024]{1,0:T(8,128)(2,1)S(1)} %get-tuple-element.67.weight), custom_call_target="tpu_custom_call" | custom-call | tf_op jit(solution)/shard_map/pallas_call | solution.py:659
  80.2 1.5 %collective-permute-start.21 = (f32[16,1024]{1,0:T(8,128)S(1)}, f32[16,1024]{1,0:T(8,128)S(1)}, u32[]{:S(2)}, u32[]{:S(2)}) collective-permute-start(f32[16,1024]{1,0:T(8,128)S(1)} %shard_map.143.refs_6_), channel_id=1, source_target_pairs={{0,2},{2,0},{1,3},{3,1},{4,6},{6,4},{5,7},{7,5},{8,10},{10,8},{9,1... | collective-permute-start | bytes 196616 | tf_op jit(solution)/shard_map/ppermute | solution.py:669
  81.7 2.8 %collective-permute-done.21.refs_7_ = f32[16,1024]{1,0:T(8,128)S(1)} collective-permute-done((f32[16,1024]{1,0:T(8,128)S(1)}, f32[16,1024]{1,0:T(8,128)S(1)}, u32[]{:S(2)}, u32[]{:S(2)}) %collective-permute-start.21) | collective-permute-done | bytes 65568 | tf_op jit(solution)/shard_map/ppermute | solution.py:669
  84.5 2.0 %shard_map.144 = (f32[16,2688]{1,0:T(8,128)S(1)}, f32[16,2688]{1,0:T(8,128)S(1)}, bf16[16,1024]{1,0:T(8,128)(2,1)S(1)}, f32[16,1024]{1,0:T(8,128)S(1)}) custom-call(s32[4]{0:T(128)S(1)} %pad_add_fusion.place, bf16[16,1024]{1,0:T(8,128)(2,1)S(1)} %get-tuple-element.68.refs_0_, f32[1,1024]{1,0:T(1,128)S(1)} %bitcast.19, ...), custom_call_target="tpu_custom_call" | custom-call | tf_op jit(solution)/shard_map/pallas_call | solution.py:368
  88.0 1.9 %collective-permute-start.23 = (bf16[16,2688]{1,0:T(8,128)(2,1)S(1)}, bf16[16,2688]{1,0:T(8,128)(2,1)S(1)}, u32[]{:S(2)}, u32[]{:S(2)}) collective-permute-start(bf16[16,2688]{1,0:T(8,128)(2,1)S(1)} %get-tuple-element.83), channel_id=1, source_target_pairs={{0,4},{4,8},{8,12},{12,0},{1,5},{5,9},{9,13},{13,1},{2,6},{6,10},{... | collective-permute-start | bytes 258056 | tf_op jit(solution)/shard_map/ppermute | solution.py:675
  92.3 2.9 %collective-permute-done.23.refs_1_ = bf16[16,2688]{1,0:T(8,128)(2,1)S(1)} collective-permute-done((bf16[16,2688]{1,0:T(8,128)(2,1)S(1)}, bf16[16,2688]{1,0:T(8,128)(2,1)S(1)}, u32[]{:S(2)}, u32[]{:S(2)}) %collective-permute-start.23) | collective-permute-done | bytes 86048 | tf_op jit(solution)/shard_map/ppermute | solution.py:675
  95.3 2.9 %collective-permute-done.24.refs_2_ = bf16[16,2688]{1,0:T(8,128)(2,1)S(1)} collective-permute-done((bf16[16,2688]{1,0:T(8,128)(2,1)S(1)}, bf16[16,2688]{1,0:T(8,128)(2,1)S(1)}, u32[]{:S(2)}, u32[]{:S(2)}) %collective-permute-start.24) | collective-permute-done | bytes 86048 | tf_op jit(solution)/shard_map/ppermute | solution.py:675
  98.2 6.0 %shard_map.146 = (bf16[16,2176]{1,0:T(8,128)(2,1)S(1)}, f32[16,128]{1,0:T(8,128)S(1)}, bf16[16,512]{1,0:T(8,128)(2,1)}) custom-call(s32[4]{0:T(128)S(1)} %pad_add_fusion.place, f32[16,2688]{1,0:T(8,128)S(1)} %get-tuple-element.82.refs_0_, bf16[16,2688]{1,0:T(8,128)(2,1)S(1)} %collective-permute-done.23.refs_1_, ...), custom_call_target="tpu_custom_call" | custom-call | tf_op jit(solution)/shard_map/pallas_call | solution.py:600
  104.2 2.3 %collective-permute-start.26 = (bf16[16,2176]{1,0:T(8,128)(2,1)S(1)}, bf16[16,2176]{1,0:T(8,128)(2,1)S(1)}, u32[]{:S(2)}, u32[]{:S(2)}) collective-permute-start(bf16[16,2176]{1,0:T(8,128)(2,1)S(1)} %get-tuple-element.85.own), channel_id=1, source_target_pairs={{0,4},{4,8},{8,12},{12,0},{1,5},{5,9},{9,13},{13,1},{2,6},{6,10},{... | collective-permute-start | bytes 208904 | tf_op jit(solution)/shard_map/ppermute | solution.py:675
  107.3 1.6 %collective-permute-start.28 = (bf16[16,2176]{1,0:T(8,128)(2,1)S(1)}, bf16[16,2176]{1,0:T(8,128)(2,1)S(1)}, u32[]{:S(2)}, u32[]{:S(2)}) collective-permute-start(bf16[16,2176]{1,0:T(8,128)(2,1)S(1)} %get-tuple-element.85.own), channel_id=1, source_target_pairs={{0,12},{4,0},{8,4},{12,8},{1,13},{5,1},{9,5},{13,9},{2,14},{6,2},{... | collective-permute-start | bytes 208904 | tf_op jit(solution)/shard_map/ppermute | solution.py:675
  108.9 2.2 %collective-permute-done.26.refs_0_ = bf16[16,2176]{1,0:T(8,128)(2,1)S(1)} collective-permute-done((bf16[16,2176]{1,0:T(8,128)(2,1)S(1)}, bf16[16,2176]{1,0:T(8,128)(2,1)S(1)}, u32[]{:S(2)}, u32[]{:S(2)}) %collective-permute-start.26) | collective-permute-done | bytes 69664 | tf_op jit(solution)/shard_map/ppermute | solution.py:675
  111.0 2.2 %collective-permute-done.27.refs_1_ = bf16[16,2176]{1,0:T(8,128)(2,1)S(1)} collective-permute-done((bf16[16,2176]{1,0:T(8,128)(2,1)S(1)}, bf16[16,2176]{1,0:T(8,128)(2,1)S(1)}, u32[]{:S(2)}, u32[]{:S(2)}) %collective-permute-start.27) | collective-permute-done | bytes 69664 | tf_op jit(solution)/shard_map/ppermute | solution.py:675
  114.9 1.7 %shard_map.148 = f32[16,1024]{1,0:T(8,128)S(1)} custom-call(s32[4]{0:T(128)S(1)} %pad_add_fusion.place, bf16[16,2048]{1,0:T(8,128)(2,1)S(1)} %shard_map.147.mine, bf16[16,2048]{1,0:T(8,128)(2,1)S(1)} %collective-permute-done.29.other, bf16[4096,1024]{1,0:T(8,128)(2,1)S(1)} %get-tuple-element.67.weight), custom_call_target="tpu_custom_call" | custom-call | tf_op jit(solution)/shard_map/pallas_call | solution.py:659
  118.2 2.8 %collective-permute-done.30 = f32[16,1024]{1,0:T(8,128)S(1)} collective-permute-done((f32[16,1024]{1,0:T(8,128)S(1)}, f32[16,1024]{1,0:T(8,128)S(1)}, u32[]{:S(2)}, u32[]{:S(2)}) %collective-permute-start.30) | collective-permute-done | bytes 65568 | tf_op jit(solution)/shard_map/ppermute | solution.py:669
  (67 shorter events, 26.8 us)
Async XLA Ops:
  0.6 7.6 %collective-permute-start.1 = (bf16[16,4,128,128]{3,2,1,0:T(8,128)(2,1)}, bf16[16,4,128,128]{3,2,1,0:T(8,128)(2,1)S(1)}, u32[]{:S(2)}, u32[]{:S(2)}) collective-permute-start(bf16[16,4,128,128]{3,2,1,0:T(8,128)(2,1)} %refs_2_.4), channel_id=1, source_target_pairs={{0,1},{1,0},{2,3},{3,2},{4,5},{5,4},{6,7},{7,6},{8,9},{9,8},{10,11... | collective-permute-start | bytes 6291464 | tf_op jit(solution)/shard_map/ppermute | solution.py:669
  1.1 7.1 %collective-permute-start.2 = (bf16[16,4,128,128]{3,2,1,0:T(8,128)(2,1)}, bf16[16,4,128,128]{3,2,1,0:T(8,128)(2,1)}, u32[]{:S(2)}, u32[]{:S(2)}) collective-permute-start(bf16[16,4,128,128]{3,2,1,0:T(8,128)(2,1)} %refs_3_.3), channel_id=1, source_target_pairs={{0,1},{1,0},{2,3},{3,2},{4,5},{5,4},{6,7},{7,6},{8,9},{9,8},{10,11... | collective-permute-start | bytes 6291464 | tf_op jit(solution)/shard_map/ppermute | solution.py:669
  6.7 1.5 %collective-permute-start = (f32[16,2688]{1,0:T(8,128)S(1)}, f32[16,2688]{1,0:T(8,128)S(1)}, u32[]{:S(2)}, u32[]{:S(2)}) collective-permute-start(f32[16,2688]{1,0:T(8,128)S(1)} %get-tuple-element.46), channel_id=1, source_target_pairs={{0,1},{1,0},{2,3},{3,2},{4,5},{5,4},{6,7},{7,6},{8,9},{9,8},{10,11... | collective-permute-start | bytes 516104 | tf_op jit(solution)/shard_map/ppermute | solution.py:669
  8.2 14.6 %copy-start.3 = (bf16[16,4,128,128]{3,2,1,0:T(8,128)(2,1)}, bf16[16,4,128,128]{3,2,1,0:T(8,128)(2,1)S(1)}, u32[]{:S(2)}) copy-start(bf16[16,4,128,128]{3,2,1,0:T(8,128)(2,1)S(1)} %collective-permute-done.1.refs_11_) | copy-start | bytes 6291460
  8.3 14.5 %collective-permute-start.6 = (bf16[1,4,4096,128]{3,2,1,0:T(8,128)(2,1)}, bf16[1,4,4096,128]{3,2,1,0:T(8,128)(2,1)}, u32[]{:S(2)}, u32[]{:S(2)}) collective-permute-start(bf16[1,4,4096,128]{3,2,1,0:T(8,128)(2,1)} %refs_0_.5), channel_id=1, source_target_pairs={{0,1},{1,0},{2,3},{3,2},{4,5},{5,4},{6,7},{7,6},{8,9},{9,8},{10,11... | collective-permute-start | bytes 12582920 | tf_op jit(solution)/shard_map/ppermute | solution.py:669
  8.6 14.2 %collective-permute-start.7 = (bf16[1,4,4096,128]{3,2,1,0:T(8,128)(2,1)}, bf16[1,4,4096,128]{3,2,1,0:T(8,128)(2,1)}, u32[]{:S(2)}, u32[]{:S(2)}) collective-permute-start(bf16[1,4,4096,128]{3,2,1,0:T(8,128)(2,1)} %refs_1_.2), channel_id=1, source_target_pairs={{0,1},{1,0},{2,3},{3,2},{4,5},{5,4},{6,7},{7,6},{8,9},{9,8},{10,11... | collective-permute-start | bytes 12582920 | tf_op jit(solution)/shard_map/ppermute | solution.py:669
  9.9 12.9 %collective-permute-start.3 = (bf16[16,2688]{1,0:T(8,128)(2,1)S(1)}, bf16[16,2688]{1,0:T(8,128)(2,1)S(1)}, u32[]{:S(2)}, u32[]{:S(2)}) collective-permute-start(bf16[16,2688]{1,0:T(8,128)(2,1)S(1)} %get-tuple-element.49.refs_5_), channel_id=1, source_target_pairs={{0,4},{4,8},{8,12},{12,0},{1,5},{5,9},{9,13},{13,1},{2,6},{6,10},{... | collective-permute-start | bytes 258056 | tf_op jit(solution)/shard_map/ppermute | solution.py:675
  12.9 9.9 %collective-permute-start.4 = (bf16[16,2688]{1,0:T(8,128)(2,1)S(1)}, bf16[16,2688]{1,0:T(8,128)(2,1)S(1)}, u32[]{:S(2)}, u32[]{:S(2)}) collective-permute-start(bf16[16,2688]{1,0:T(8,128)(2,1)S(1)} %get-tuple-element.49.refs_5_), channel_id=1, source_target_pairs={{0,8},{4,12},{8,0},{12,4},{1,9},{5,13},{9,1},{13,5},{2,10},{6,14},... | collective-permute-start | bytes 258056 | tf_op jit(solution)/shard_map/ppermute | solution.py:675
  15.5 7.3 %collective-permute-start.5 = (bf16[16,2688]{1,0:T(8,128)(2,1)S(1)}, bf16[16,2688]{1,0:T(8,128)(2,1)S(1)}, u32[]{:S(2)}, u32[]{:S(2)}) collective-permute-start(bf16[16,2688]{1,0:T(8,128)(2,1)S(1)} %get-tuple-element.49.refs_5_), channel_id=1, source_target_pairs={{0,12},{4,0},{8,4},{12,8},{1,13},{5,1},{9,5},{13,9},{2,14},{6,2},{... | collective-permute-start | bytes 258056 | tf_op jit(solution)/shard_map/ppermute | solution.py:675
  29.3 9.4 %collective-permute-start.10 = (bf16[16,2176]{1,0:T(8,128)(2,1)S(1)}, bf16[16,2176]{1,0:T(8,128)(2,1)S(1)}, u32[]{:S(2)}, u32[]{:S(2)}) collective-permute-start(bf16[16,2176]{1,0:T(8,128)(2,1)S(1)} %get-tuple-element.56.own), channel_id=1, source_target_pairs={{0,12},{4,0},{8,4},{12,8},{1,13},{5,1},{9,5},{13,9},{2,14},{6,2},{... | collective-permute-start | bytes 208904 | tf_op jit(solution)/shard_map/ppermute | solution.py:675
  33.2 6.6 %collective-permute-start.8 = (bf16[16,2176]{1,0:T(8,128)(2,1)S(1)}, bf16[16,2176]{1,0:T(8,128)(2,1)S(1)}, u32[]{:S(2)}, u32[]{:S(2)}) collective-permute-start(bf16[16,2176]{1,0:T(8,128)(2,1)S(1)} %get-tuple-element.56.own), channel_id=1, source_target_pairs={{0,4},{4,8},{8,12},{12,0},{1,5},{5,9},{9,13},{13,1},{2,6},{6,10},{... | collective-permute-start | bytes 208904 | tf_op jit(solution)/shard_map/ppermute | solution.py:675
  33.2 8.0 %collective-permute-start.9 = (bf16[16,2176]{1,0:T(8,128)(2,1)S(1)}, bf16[16,2176]{1,0:T(8,128)(2,1)S(1)}, u32[]{:S(2)}, u32[]{:S(2)}) collective-permute-start(bf16[16,2176]{1,0:T(8,128)(2,1)S(1)} %get-tuple-element.56.own), channel_id=1, source_target_pairs={{0,8},{4,12},{8,0},{12,4},{1,9},{5,13},{9,1},{13,5},{2,10},{6,14},... | collective-permute-start | bytes 208904 | tf_op jit(solution)/shard_map/ppermute | solution.py:675
  41.5 1.3 %collective-permute-start.11 = (bf16[16,2048]{1,0:T(8,128)(2,1)S(1)}, bf16[16,2048]{1,0:T(8,128)(2,1)S(1)}, u32[]{:S(2)}, u32[]{:S(2)}) collective-permute-start(bf16[16,2048]{1,0:T(8,128)(2,1)S(1)} %shard_map.137.mine), channel_id=1, source_target_pairs={{0,1},{1,0},{2,3},{3,2},{4,5},{5,4},{6,7},{7,6},{8,9},{9,8},{10,11... | collective-permute-start | bytes 196616 | tf_op jit(solution)/shard_map/ppermute | solution.py:669
  44.6 4.3 %collective-permute-start.12 = (f32[16,1024]{1,0:T(8,128)S(1)}, f32[16,1024]{1,0:T(8,128)S(1)}, u32[]{:S(2)}, u32[]{:S(2)}) collective-permute-start(f32[16,1024]{1,0:T(8,128)S(1)} %shard_map.138.refs_6_), channel_id=1, source_target_pairs={{0,2},{2,0},{1,3},{3,1},{4,6},{6,4},{5,7},{7,5},{8,10},{10,8},{9,1... | collective-permute-start | bytes 196616 | tf_op jit(solution)/shard_map/ppermute | solution.py:669
  50.9 1.4 %collective-permute-start.13 = (f32[16,2688]{1,0:T(8,128)S(1)}, f32[16,2688]{1,0:T(8,128)S(1)}, u32[]{:S(2)}, u32[]{:S(2)}) collective-permute-start(f32[16,2688]{1,0:T(8,128)S(1)} %get-tuple-element.71), channel_id=1, source_target_pairs={{0,1},{1,0},{2,3},{3,2},{4,5},{5,4},{6,7},{7,6},{8,9},{9,8},{10,11... | collective-permute-start | bytes 516104 | tf_op jit(solution)/shard_map/ppermute | solution.py:669
  52.4 7.3 %collective-permute-start.14 = (bf16[16,2688]{1,0:T(8,128)(2,1)S(1)}, bf16[16,2688]{1,0:T(8,128)(2,1)S(1)}, u32[]{:S(2)}, u32[]{:S(2)}) collective-permute-start(bf16[16,2688]{1,0:T(8,128)(2,1)S(1)} %get-tuple-element.73), channel_id=1, source_target_pairs={{0,4},{4,8},{8,12},{12,0},{1,5},{5,9},{9,13},{13,1},{2,6},{6,10},{... | collective-permute-start | bytes 258056 | tf_op jit(solution)/shard_map/ppermute | solution.py:675
  53.3 9.2 %collective-permute-start.15 = (bf16[16,2688]{1,0:T(8,128)(2,1)S(1)}, bf16[16,2688]{1,0:T(8,128)(2,1)S(1)}, u32[]{:S(2)}, u32[]{:S(2)}) collective-permute-start(bf16[16,2688]{1,0:T(8,128)(2,1)S(1)} %get-tuple-element.73), channel_id=1, source_target_pairs={{0,8},{4,12},{8,0},{12,4},{1,9},{5,13},{9,1},{13,5},{2,10},{6,14},... | collective-permute-start | bytes 258056 | tf_op jit(solution)/shard_map/ppermute | solution.py:675
  54.8 7.8 %collective-permute-start.16 = (bf16[16,2688]{1,0:T(8,128)(2,1)S(1)}, bf16[16,2688]{1,0:T(8,128)(2,1)S(1)}, u32[]{:S(2)}, u32[]{:S(2)}) collective-permute-start(bf16[16,2688]{1,0:T(8,128)(2,1)S(1)} %get-tuple-element.73), channel_id=1, source_target_pairs={{0,12},{4,0},{8,4},{12,8},{1,13},{5,1},{9,5},{13,9},{2,14},{6,2},{... | collective-permute-start | bytes 258056 | tf_op jit(solution)/shard_map/ppermute | solution.py:675
  68.1 6.5 %collective-permute-start.17 = (bf16[16,2176]{1,0:T(8,128)(2,1)S(1)}, bf16[16,2176]{1,0:T(8,128)(2,1)S(1)}, u32[]{:S(2)}, u32[]{:S(2)}) collective-permute-start(bf16[16,2176]{1,0:T(8,128)(2,1)S(1)} %get-tuple-element.77.own), channel_id=1, source_target_pairs={{0,4},{4,8},{8,12},{12,0},{1,5},{5,9},{9,13},{13,1},{2,6},{6,10},{... | collective-permute-start | bytes 208904 | tf_op jit(solution)/shard_map/ppermute | solution.py:675
  70.2 6.7 %collective-permute-start.18 = (bf16[16,2176]{1,0:T(8,128)(2,1)S(1)}, bf16[16,2176]{1,0:T(8,128)(2,1)S(1)}, u32[]{:S(2)}, u32[]{:S(2)}) collective-permute-start(bf16[16,2176]{1,0:T(8,128)(2,1)S(1)} %get-tuple-element.77.own), channel_id=1, source_target_pairs={{0,8},{4,12},{8,0},{12,4},{1,9},{5,13},{9,1},{13,5},{2,10},{6,14},... | collective-permute-start | bytes 208904 | tf_op jit(solution)/shard_map/ppermute | solution.py:675
  71.0 5.9 %collective-permute-start.19 = (bf16[16,2176]{1,0:T(8,128)(2,1)S(1)}, bf16[16,2176]{1,0:T(8,128)(2,1)S(1)}, u32[]{:S(2)}, u32[]{:S(2)}) collective-permute-start(bf16[16,2176]{1,0:T(8,128)(2,1)S(1)} %get-tuple-element.77.own), channel_id=1, source_target_pairs={{0,12},{4,0},{8,4},{12,8},{1,13},{5,1},{9,5},{13,9},{2,14},{6,2},{... | collective-permute-start | bytes 208904 | tf_op jit(solution)/shard_map/ppermute | solution.py:675
  77.2 1.3 %collective-permute-start.20 = (bf16[16,2048]{1,0:T(8,128)(2,1)S(1)}, bf16[16,2048]{1,0:T(8,128)(2,1)S(1)}, u32[]{:S(2)}, u32[]{:S(2)}) collective-permute-start(bf16[16,2048]{1,0:T(8,128)(2,1)S(1)} %shard_map.142.mine), channel_id=1, source_target_pairs={{0,1},{1,0},{2,3},{3,2},{4,5},{5,4},{6,7},{7,6},{8,9},{9,8},{10,11... | collective-permute-start | bytes 196616 | tf_op jit(solution)/shard_map/ppermute | solution.py:669
  80.2 4.3 %collective-permute-start.21 = (f32[16,1024]{1,0:T(8,128)S(1)}, f32[16,1024]{1,0:T(8,128)S(1)}, u32[]{:S(2)}, u32[]{:S(2)}) collective-permute-start(f32[16,1024]{1,0:T(8,128)S(1)} %shard_map.143.refs_6_), channel_id=1, source_target_pairs={{0,2},{2,0},{1,3},{3,1},{4,6},{6,4},{5,7},{7,5},{8,10},{10,8},{9,1... | collective-permute-start | bytes 196616 | tf_op jit(solution)/shard_map/ppermute | solution.py:669
  86.5 1.4 %collective-permute-start.22 = (f32[16,2688]{1,0:T(8,128)S(1)}, f32[16,2688]{1,0:T(8,128)S(1)}, u32[]{:S(2)}, u32[]{:S(2)}) collective-permute-start(f32[16,2688]{1,0:T(8,128)S(1)} %get-tuple-element.81), channel_id=1, source_target_pairs={{0,1},{1,0},{2,3},{3,2},{4,5},{5,4},{6,7},{7,6},{8,9},{9,8},{10,11... | collective-permute-start | bytes 516104 | tf_op jit(solution)/shard_map/ppermute | solution.py:669
  88.0 7.3 %collective-permute-start.23 = (bf16[16,2688]{1,0:T(8,128)(2,1)S(1)}, bf16[16,2688]{1,0:T(8,128)(2,1)S(1)}, u32[]{:S(2)}, u32[]{:S(2)}) collective-permute-start(bf16[16,2688]{1,0:T(8,128)(2,1)S(1)} %get-tuple-element.83), channel_id=1, source_target_pairs={{0,4},{4,8},{8,12},{12,0},{1,5},{5,9},{9,13},{13,1},{2,6},{6,10},{... | collective-permute-start | bytes 258056 | tf_op jit(solution)/shard_map/ppermute | solution.py:675
  89.9 8.3 %collective-permute-start.24 = (bf16[16,2688]{1,0:T(8,128)(2,1)S(1)}, bf16[16,2688]{1,0:T(8,128)(2,1)S(1)}, u32[]{:S(2)}, u32[]{:S(2)}) collective-permute-start(bf16[16,2688]{1,0:T(8,128)(2,1)S(1)} %get-tuple-element.83), channel_id=1, source_target_pairs={{0,8},{4,12},{8,0},{12,4},{1,9},{5,13},{9,1},{13,5},{2,10},{6,14},... | collective-permute-start | bytes 258056 | tf_op jit(solution)/shard_map/ppermute | solution.py:675
  91.2 7.0 %collective-permute-start.25 = (bf16[16,2688]{1,0:T(8,128)(2,1)S(1)}, bf16[16,2688]{1,0:T(8,128)(2,1)S(1)}, u32[]{:S(2)}, u32[]{:S(2)}) collective-permute-start(bf16[16,2688]{1,0:T(8,128)(2,1)S(1)} %get-tuple-element.83), channel_id=1, source_target_pairs={{0,12},{4,0},{8,4},{12,8},{1,13},{5,1},{9,5},{13,9},{2,14},{6,2},{... | collective-permute-start | bytes 258056 | tf_op jit(solution)/shard_map/ppermute | solution.py:675
  104.2 6.9 %collective-permute-start.26 = (bf16[16,2176]{1,0:T(8,128)(2,1)S(1)}, bf16[16,2176]{1,0:T(8,128)(2,1)S(1)}, u32[]{:S(2)}, u32[]{:S(2)}) collective-permute-start(bf16[16,2176]{1,0:T(8,128)(2,1)S(1)} %get-tuple-element.85.own), channel_id=1, source_target_pairs={{0,4},{4,8},{8,12},{12,0},{1,5},{5,9},{9,13},{13,1},{2,6},{6,10},{... | collective-permute-start | bytes 208904 | tf_op jit(solution)/shard_map/ppermute | solution.py:675
  106.5 6.8 %collective-permute-start.27 = (bf16[16,2176]{1,0:T(8,128)(2,1)S(1)}, bf16[16,2176]{1,0:T(8,128)(2,1)S(1)}, u32[]{:S(2)}, u32[]{:S(2)}) collective-permute-start(bf16[16,2176]{1,0:T(8,128)(2,1)S(1)} %get-tuple-element.85.own), channel_id=1, source_target_pairs={{0,8},{4,12},{8,0},{12,4},{1,9},{5,13},{9,1},{13,5},{2,10},{6,14},... | collective-permute-start | bytes 208904 | tf_op jit(solution)/shard_map/ppermute | solution.py:675
  107.3 6.0 %collective-permute-start.28 = (bf16[16,2176]{1,0:T(8,128)(2,1)S(1)}, bf16[16,2176]{1,0:T(8,128)(2,1)S(1)}, u32[]{:S(2)}, u32[]{:S(2)}) collective-permute-start(bf16[16,2176]{1,0:T(8,128)(2,1)S(1)} %get-tuple-element.85.own), channel_id=1, source_target_pairs={{0,12},{4,0},{8,4},{12,8},{1,13},{5,1},{9,5},{13,9},{2,14},{6,2},{... | collective-permute-start | bytes 208904 | tf_op jit(solution)/shard_map/ppermute | solution.py:675
  113.6 1.3 %collective-permute-start.29 = (bf16[16,2048]{1,0:T(8,128)(2,1)S(1)}, bf16[16,2048]{1,0:T(8,128)(2,1)S(1)}, u32[]{:S(2)}, u32[]{:S(2)}) collective-permute-start(bf16[16,2048]{1,0:T(8,128)(2,1)S(1)} %shard_map.147.mine), channel_id=1, source_target_pairs={{0,1},{1,0},{2,3},{3,2},{4,5},{5,4},{6,7},{7,6},{8,9},{9,8},{10,11... | collective-permute-start | bytes 196616 | tf_op jit(solution)/shard_map/ppermute | solution.py:669
  116.7 4.3 %collective-permute-start.30 = (f32[16,1024]{1,0:T(8,128)S(1)}, f32[16,1024]{1,0:T(8,128)S(1)}, u32[]{:S(2)}, u32[]{:S(2)}) collective-permute-start(f32[16,1024]{1,0:T(8,128)S(1)} %shard_map.148), channel_id=1, source_target_pairs={{0,2},{2,0},{1,3},{3,1},{4,6},{6,4},{5,7},{7,5},{8,10},{10,8},{9,1... | collective-permute-start | bytes 196616 | tf_op jit(solution)/shard_map/ppermute | solution.py:669
  (4 other events, 27.1 us)

commit v4 on v3

--- a/solution.py
+++ b/solution.py
@@ -191,6 +191,7 @@
 HBM_SPEC = pl.BlockSpec(memory_space=pltpu.HBM)
 PARAMS = pltpu.CompilerParams(vmem_limit_bytes=4 * 1024 * 1024)
 LARGE_PARAMS = pltpu.CompilerParams(vmem_limit_bytes=13 * 1024 * 1024)
+COST = pl.CostEstimate(flops=1 << 28, bytes_accessed=1 << 22, transcendentals=0)
 
 
 def resident(array):
@@ -248,32 +249,7 @@
     ]
 
 
-def load_kernel(pools, place, *refs):
-    count = (len(refs) - 2 + 2 * (pools > 0)) // 2
-    sources, outs, sems = refs[:count], refs[count + 1 : -1], refs[-1]
-    pairs = list(zip(sources[pools:], outs[2 * (pools > 0) :]))
-    if pools:
-        pairs = halves(place, sources[:pools], *outs[:2]) + pairs
-    for copy in copied(pairs, sems):
-        copy.wait()
-
-
-def load(place, pools, weights, after):
-    sources = [in_hbm(array) for array in (*pools, *weights)]
-    shapes = half_shapes(pools) if pools else []
-    shapes = shapes + [pltpu.VMEM(w.shape, w.dtype) for w in weights]
-    return pl.pallas_call(
-        functools.partial(load_kernel, len(pools)),
-        out_shape=shapes,
-        in_specs=[SMEM_SPEC] + [HBM_SPEC] * len(sources) + [VMEM_SPEC],
-        out_specs=[VMEM_SPEC] * len(shapes),
-        scratch_shapes=[pltpu.SemaphoreType.DMA((len(sources),))],
-        compiler_params=PARAMS,
-        cost_estimate=pl.CostEstimate(flops=0, bytes_accessed=1 << 25, transcendentals=0),
-    )(place, *sources, after)
-
-
-def bias_kernel(place, lengths, table, bias):
+def live_bias(place, lengths, table, bias):
     pages = table.shape[1]
     page = bias.shape[2] // (SAMP_DEV * pages)
     row = lax.broadcasted_iota(jnp.int32, (bias.shape[1], page), 0)
@@ -288,93 +264,163 @@
                 bias[pool, :, spot] = jnp.where(live, 0.0, -jnp.inf)
 
 
-def live_bias(place, lengths, table, page):
+def load_caches_kernel(
+    place, lengths, table, pk, pv, sk, sv, w_out, after, prefix, suffix, kept_out, bias, sems
+):
+    pairs = halves(place, (pk, pv, sk, sv), prefix, suffix) + [(w_out, kept_out)]
+    copies = copied(pairs, sems)
+    live_bias(place, lengths, table, bias)
+    for copy in copies:
+        copy.wait()
+
+
+def load_caches(place, lengths, table, pools, w_out, after):
+    page = pools[2].shape[2]
     tokens = SAMP_DEV * table.shape[1] * page
+    sources = [in_hbm(array) for array in (*pools, w_out)]
     return pl.pallas_call(
-        bias_kernel,
-        out_shape=jax.ShapeDtypeStruct((2, SAMP_DEV * GROUP, tokens), F32),
-        in_specs=[SMEM_SPEC] * 3,
-        out_specs=VMEM_SPEC,
+        load_caches_kernel,
+        out_shape=half_shapes(pools)
+        + [
+            pltpu.VMEM(w_out.shape, w_out.dtype),
+            jax.ShapeDtypeStruct((2, SAMP_DEV * GROUP, tokens), F32),
+        ],
+        in_specs=[SMEM_SPEC] * 3 + [HBM_SPEC] * 5 + [VMEM_SPEC],
+        out_specs=[VMEM_SPEC] * 4,
+        scratch_shapes=[pltpu.SemaphoreType.DMA((5,))],
         compiler_params=PARAMS,
-    )(place, lengths, table)
-
-
-def project_kernel(first, place, *refs):
-    x_ref, gain, *weights = refs[:5]
-    if first:
-        keep, give, *buffers, sems = refs[5:]
-    else:
-        sum_ref, mine, other, keep, give, new_x, new_sum = refs[5:]
-        delta = mine[...] + other[...]
-        new_sum[...] = sum_ref[...] + delta
-        state = (x_ref[...].astype(F32) + delta).astype(BF16)
-        new_x[...] = state
-        wide = state.astype(F32)
-    tiles = []
-    for out, who in ((give, 1 - place[0]), (keep, place[0])):
-        at = 0
-        for index, weight in enumerate(weights):
-            half = weight.shape[1] // 2
-            tile = min(1024, half)
-            for begin in range(0, half, tile):
-                columns = pl.ds(pl.multiple_of(who * half + begin, tile), tile)
-                tiles.append((out, at + begin, tile, index, columns))
-            at += half
-    copies = []
-    if first:
-        copies = copied(
-            [(x_ref, buffers[3]), (gain, buffers[4])]
-            + [
-                (weights[index].at[:, columns], buffers[index].at[:, columns])
-                for _, _, _, index, columns in tiles
-            ],
-            sems,
-        )
-        weights = buffers
-        copies[0].wait()
-        copies[1].wait()
-        wide = buffers[3][...].astype(F32)
-        gain = buffers[4]
+        cost_estimate=pl.CostEstimate(flops=0, bytes_accessed=1 << 25, transcendentals=0),
+    )(place, lengths, table, *sources, after)
+
+
+def load_kernel(*refs):
+    count = len(refs) // 2 - 1
+    for copy in copied(zip(refs[:count], refs[count + 1 : -1]), refs[-1]):
+        copy.wait()
+
+
+def load(weights, after):
+    return pl.pallas_call(
+        load_kernel,
+        out_shape=[pltpu.VMEM(w.shape, w.dtype) for w in weights],
+        in_specs=[HBM_SPEC] * len(weights) + [VMEM_SPEC],
+        out_specs=[VMEM_SPEC] * len(weights),
+        scratch_shapes=[pltpu.SemaphoreType.DMA((len(weights),))],
+        compiler_params=PARAMS,
+        cost_estimate=pl.CostEstimate(flops=0, bytes_accessed=1 << 25, transcendentals=0),
+    )(*[in_hbm(weight) for weight in weights], after)
+
+
+def column_tiles(place, weights, who):
+    tiles, at = [], 0
+    for index, weight in enumerate(weights):
+        half = weight.shape[1] // 2
+        tile = min(1024, half)
+        for begin in range(0, half, tile):
+            columns = pl.ds(pl.multiple_of(who * half + begin, tile), tile)
+            tiles.append((index, columns, slice(at + begin, at + begin + tile)))
+        at += half
+    return tiles
+
+
+def first_project_kernel(place, *refs):
+    sources, (keep, give, *buffers, sems) = refs[:5], refs[5:]
+    weights, (x_ref, gain) = buffers[:3], buffers[3:]
+    outs = ((give, 1 - place[0]), (keep, place[0]))
+    tiles = [
+        (out, *tile) for out, who in outs for tile in column_tiles(place, weights, who)
+    ]
+    pairs = list(zip(sources[3:], buffers[3:]))
+    for _, index, columns, _ in tiles:
+        pairs.append((sources[index].at[:, columns], weights[index].at[:, columns]))
+    copies = copied(pairs, sems)
+    copies[0].wait()
+    copies[1].wait()
+    wide = x_ref[...].astype(F32)
     scaled = (wide * gain[...]).astype(BF16)
     squares = jnp.sum(wide * wide, axis=1, keepdims=True)
     column = lanes(wide.shape[0])
     for out in (give, keep):
         out[:, out.shape[1] - LANES :] = jnp.where(column == 0, squares, 0.0)
-    for n, (out, at, tile, index, columns) in enumerate(tiles):
-        if copies:
-            copies[n + 2].wait()
-        out[:, at : at + tile] = jnp.dot(
+    for copy, (out, index, columns, to) in zip(copies[2:], tiles):
+        copy.wait()
+        out[:, to] = jnp.dot(
             scaled, weights[index][:, columns], preferred_element_type=F32
         )
 
 
-def project(place, x, gain, weights, rest):
+def first_project(place, x, gain, weights):
     rows = x.shape[0]
     width = sum(w.shape[1] for w in weights) // 2 + LANES
-    out_shape = [jax.ShapeDtypeStruct((rows, width), F32)] * 2
-    if rest:
-        weights = [resident(weight) for weight in weights]
-        scratch = []
-        out_shape = out_shape + [
+    sources = [in_hbm(array) for array in (*weights, x, gain)]
+    count = 2 + 2 * sum(max(1, w.shape[1] // 2048) for w in weights)
+    return pl.pallas_call(
+        first_project_kernel,
+        out_shape=[jax.ShapeDtypeStruct((rows, width), F32)] * 2,
+        in_specs=[SMEM_SPEC] + [HBM_SPEC] * 5,
+        out_specs=[VMEM_SPEC] * 2,
+        scratch_shapes=[pltpu.VMEM(array.shape, array.dtype) for array in sources]
+        + [pltpu.SemaphoreType.DMA((count,))],
+        compiler_params=LARGE_PARAMS,
+    )(place, *sources)
+
+
+def give_kernel(place, x_ref, gain, sum_ref, mine, other, *refs):
+    weights, (give, scaled_ref, new_x, new_sum) = refs[:3], refs[3:]
+    delta = mine[...].astype(F32) + other[...].astype(F32)
+    new_sum[...] = sum_ref[...] + delta
+    state = (x_ref[...].astype(F32) + delta).astype(BF16)
+    new_x[...] = state
+    wide = state.astype(F32)
+    scaled = (wide * gain[...]).astype(BF16)
+    scaled_ref[...] = scaled
+    squares = jnp.sum(wide * wide, axis=1, keepdims=True)
+    column = lanes(wide.shape[0])
+    give[:, give.shape[1] - LANES :] = jnp.where(column == 0, squares, 0.0)
+    for index, columns, to in column_tiles(place, weights, 1 - place[0]):
+        give[:, to] = jnp.dot(
+            scaled, weights[index][:, columns], preferred_element_type=F32
+        )
+
+
+def give_project(place, x, gain, weights, rest):
+    rows = x.shape[0]
+    width = sum(w.shape[1] for w in weights) // 2 + LANES
+    return pl.pallas_call(
+        give_kernel,
+        out_shape=[
+            jax.ShapeDtypeStruct((rows, width), F32),
+            jax.ShapeDtypeStruct(x.shape, BF16),
             jax.ShapeDtypeStruct(x.shape, BF16),
             jax.ShapeDtypeStruct(x.shape, F32),
-        ]
-    else:
-        weights = [in_hbm(weight) for weight in weights]
-        x, gain = in_hbm(x), in_hbm(gain)
-        count = 2 + 2 * sum(max(1, w.shape[1] // 2048) for w in weights)
-        scratch = [pltpu.VMEM(w.shape, w.dtype) for w in (*weights, x, gain)]
-        scratch.append(pltpu.SemaphoreType.DMA((count,)))
+        ],
+        in_specs=[SMEM_SPEC] + [VMEM_SPEC] * 8,
+        out_specs=[VMEM_SPEC] * 4,
+        compiler_params=PARAMS,
+        cost_estimate=COST,
+    )(place, x, gain, *rest, *[resident(weight) for weight in weights])
+
+
+def keep_kernel(place, scaled_ref, give, *refs):
+    weights, keep = refs[:3], refs[3]
+    scaled = scaled_ref[...]
+    main = keep.shape[1] - LANES
+    keep[:, main:] = give[:, main:]
+    for index, columns, to in column_tiles(place, weights, place[0]):
+        keep[:, to] = jnp.dot(
+            scaled, weights[index][:, columns], preferred_element_type=F32
+        )
+
+
+def keep_project(place, scaled, give, weights):
     return pl.pallas_call(
-        functools.partial(project_kernel, not rest),
-        out_shape=out_shape,
-        in_specs=[SMEM_SPEC]
-        + [VMEM_SPEC if rest else HBM_SPEC] * 5
-        + [VMEM_SPEC] * len(rest),
-        out_specs=[VMEM_SPEC] * len(out_shape),
-        scratch_shapes=scratch,
-        compiler_params=PARAMS if rest else LARGE_PARAMS,
-    )(place, x, gain, *weights, *rest)
+        keep_kernel,
+        out_shape=jax.ShapeDtypeStruct(give.shape, F32),
+        in_specs=[SMEM_SPEC] + [VMEM_SPEC] * 5,
+        out_specs=VMEM_SPEC,
+        compiler_params=PARAMS,
+        cost_estimate=COST,
+    )(place, scaled, give, *[resident(weight) for weight in weights])
 
 
 def pair_sum_kernel(keep, got, total, sent):
@@ -645,24 +691,37 @@
     )(own, stat, *got)
 
 
-def output_kernel(place, mine, other, weight, out):
+def near_output_kernel(place, mine, weight, out):
     half = mine.shape[1]
-    side = place[0]
-    here = pl.ds(pl.multiple_of(side * half, half), half)
-    there = pl.ds(pl.multiple_of((1 - side) * half, half), half)
-    out[...] = jnp.dot(mine[...], weight[here], preferred_element_type=F32) + jnp.dot(
-        other[...], weight[there], preferred_element_type=F32
-    )
-
-
-def output(place, mine, other, weight):
+    rows = pl.ds(pl.multiple_of(place[0] * half, half), half)
+    out[...] = jnp.dot(mine[...], weight[rows], preferred_element_type=F32)
+
+
+def far_output_kernel(place, other, weight, near, out):
+    half = other.shape[1]
+    rows = pl.ds(pl.multiple_of((1 - place[0]) * half, half), half)
+    total = near[...] + jnp.dot(other[...], weight[rows], preferred_element_type=F32)
+    out[...] = total.astype(BF16)
+
+
+def output(place, mine, weight):
+    other = swapped(mine, "side")
+    shape = (mine.shape[0], weight.shape[1])
+    near = pl.pallas_call(
+        near_output_kernel,
+        out_shape=jax.ShapeDtypeStruct(shape, F32),
+        in_specs=[SMEM_SPEC] + [VMEM_SPEC] * 2,
+        out_specs=VMEM_SPEC,
+        compiler_params=PARAMS,
+        cost_estimate=COST,
+    )(place, mine, resident(weight))
     return pl.pallas_call(
-        output_kernel,
-        out_shape=jax.ShapeDtypeStruct((mine.shape[0], weight.shape[1]), F32),
+        far_output_kernel,
+        out_shape=jax.ShapeDtypeStruct(shape, BF16),
         in_specs=[SMEM_SPEC] + [VMEM_SPEC] * 3,
         out_specs=VMEM_SPEC,
         compiler_params=PARAMS,
-    )(place, mine, other, weight)
+    )(place, other, resident(weight), near)
 
 
 def swapped(array, axis):
@@ -702,7 +761,6 @@
     pools = (prefix_keys, prefix_values, suffix_keys, suffix_values)
     weights = (w_query, w_key, w_value)
     far = [swapped(pool, "side") for pool in pools[2:]]
-    bias = live_bias(place, suffix_lengths, page_table, suffix_keys.shape[2])
     half = HD // 2
     freq = 500000.0 ** (-(jnp.arange(half, dtype=F32) * 2.0 / HD))
     position = (
@@ -719,16 +777,20 @@
     rest = ()
     old = []
     for step in range(STEPS):
-        keep, give, *more = project(place, state, gain_row, weights, rest)
-        got_sum = swapped(give, "side")
         if rest:
-            state, update = more
+            give, scaled, state, update = give_project(place, state, gain_row, weights, rest)
+            got_sum = swapped(give, "side")
+            keep = keep_project(place, scaled, give, weights)
+            total, sent = pair_sum(keep, got_sum)
         else:
+            keep, give = first_project(place, state, gain_row, weights)
+            got_sum = swapped(give, "side")
             got_sum, *given = lax.optimization_barrier((got_sum, *far, *pools[:2]))
             far = [swapped(pool, "side") for pool in given[2:]] + given[:2]
-        total, sent = pair_sum(keep, got_sum)
-        if not rest:
-            *own, out_weight = load(place, pools, [w_out], sent)
+            total, sent = pair_sum(keep, got_sum)
+            *own, out_weight, bias = load_caches(
+                place, suffix_lengths, page_table, pools, w_out, sent
+            )
         got = from_others(sent, "seq")
         sent, stat, fresh, *kept = attend(
             features, step, place, total, got, (cosine[step], sine[step], bias), (own, far), old
@@ -736,13 +798,13 @@
         far = kept or far
         got = from_others(sent, "seq")
         if not rest:
-            weights = load(place, (), weights, stat)
+            weights = load(weights, stat)
             got, weights = lax.optimization_barrier((got, weights))
         old.append(fresh)
         mixed = merge(sent, stat, got)
-        part = output(place, mixed, swapped(mixed, "side"), resident(out_weight))
+        part = output(place, mixed, out_weight)
         rest = (update, part, swapped(part, "head"))
-    delta = rest[1] + rest[2]
+    delta = rest[1].astype(F32) + rest[2].astype(F32)
     return ((state.astype(F32) + delta).astype(BF16), update + delta)
 
 

time: 122 us -> 118 us (0.967)
  waiting for transfers between devices: 39.3 us -> 33.7 us
  Pallas kernels: 44.8 us -> 46.9 us
    ppermute x13, waiting for transfers between devices: 16 us -> 8.69 us  [swapped(): return lax.ppermute(array, axis, [(0, 1), (1, 0)])]
    pallas_call x9 -> x13, Pallas kernels: 25.7 us -> 27.9 us  [the longest x1 6.09 us: load_caches(): pl.pallas_call(load_caches_kernel, out_shape=half_shapes(pools) + [pltpu....]
    ppermute x18, waiting for transfers between devices: 23.3 us -> 25 us  [from_others(): lax.ppermute(array, axis, [(i, (i + hop) % size) for i in range(size)])]
  transfers between devices with their start and end apart: 31 -> 31, of which waited for: 20 -> 17; matrix products, arithmetic and copies ran while one was open for 0% -> 0% of each run, Pallas kernels for 14% -> 18%
where the time goes in v4:
time: 118 us
  Pallas kernels  46.9 us (40%)
  starting transfers between devices  35.2 us (30%)
  waiting for transfers between devices  33.7 us (29%)
    ppermute x18, starting transfers between devices, from_others(): lax.ppermute(array, axis, [(i, (i + hop) % size) for i in range(size)])  28.9 us
    ppermute x18, waiting for transfers between devices, from_others(): lax.ppermute(array, axis, [(i, (i + hop) % size) for i in range(size)])  25 us
    pallas_call x3, Pallas kernels, attend(): pl.pallas_call(functools.partial(attend_kernel, features, step, len(got))...  17.8 us
    ppermute x13, waiting for transfers between devices, swapped(): return lax.ppermute(array, axis, [(0, 1), (1, 0)])  8.69 us
    ppermute x13, starting transfers between devices, swapped(): return lax.ppermute(array, axis, [(0, 1), (1, 0)])  6.33 us
    pallas_call x1, Pallas kernels, load_caches(): pl.pallas_call(load_caches_kernel, out_shape=half_shapes(pools) + [pltpu....  6.09 us
    pallas_call x1, Pallas kernels, first_project(): pl.pallas_call(first_project_kernel, out_shape=[jax.ShapeDtypeStruct((row...  5.34 us
    pallas_call x1, Pallas kernels, load(): pl.pallas_call(load_kernel, out_shape=[pltpu.VMEM(w.shape, w.dtype) for w...  3.93 us
  transfers between devices with their start and end apart: 31, of which 17 were waited for; matrix products, arithmetic and copies ran while one was open for 0% of the time, Pallas kernels for 18%

profile of v4, /device:TPU:0, one launch (start us, length us, event | category | flops | bytes accessed | tf_op | source)
XLA Modules:
  0.0 117.7 jit_solution(16238743571753150156)
XLA Ops:
  1.3 5.3 %shard_map.131 = (f32[16,2688]{1,0:T(8,128)S(1)}, f32[16,2688]{1,0:T(8,128)S(1)}) custom-call(s32[4]{0:T(128)S(1)} %pad_add_fusion.place, bf16[1024,4096]{1,0:T(8,128)(2,1)} %refs_0_.3, bf16[1024,512]{1,0:T(8,128)(2,1)} %refs_1_.3, bf16[1024,512]{1,0:T(8,128)(2,1)} %refs_2_.3, bf16[16,1024]{1,0:T(8,128)(2,1)} %x_ref.1, f32[1,1024]{1,0:T(1,128)} %bitcast.17), custom_call_target="tpu_custom_call" | custom-call | tf_op jit(solution)/shard_map/pallas_call | solution.py:357
  9.2 2.9 %collective-permute-start.3 = (bf16[16,2688]{1,0:T(8,128)(2,1)S(1)}, bf16[16,2688]{1,0:T(8,128)(2,1)S(1)}, u32[]{:S(2)}, u32[]{:S(2)}) collective-permute-start(bf16[16,2688]{1,0:T(8,128)(2,1)S(1)} %get-tuple-element.50.after), channel_id=1, source_target_pairs={{0,4},{4,8},{8,12},{12,0},{1,5},{5,9},{9,13},{13,1},{2,6},{6,10},{... | collective-permute-start | bytes 258056 | tf_op jit(solution)/shard_map/ppermute | solution.py:734
  12.1 2.6 %collective-permute-start.4 = (bf16[16,2688]{1,0:T(8,128)(2,1)S(1)}, bf16[16,2688]{1,0:T(8,128)(2,1)S(1)}, u32[]{:S(2)}, u32[]{:S(2)}) collective-permute-start(bf16[16,2688]{1,0:T(8,128)(2,1)S(1)} %get-tuple-element.50.after), channel_id=1, source_target_pairs={{0,8},{4,12},{8,0},{12,4},{1,9},{5,13},{9,1},{13,5},{2,10},{6,14},... | collective-permute-start | bytes 258056 | tf_op jit(solution)/shard_map/ppermute | solution.py:734
  14.7 1.3 %collective-permute-start.5 = (bf16[16,2688]{1,0:T(8,128)(2,1)S(1)}, bf16[16,2688]{1,0:T(8,128)(2,1)S(1)}, u32[]{:S(2)}, u32[]{:S(2)}) collective-permute-start(bf16[16,2688]{1,0:T(8,128)(2,1)S(1)} %get-tuple-element.50.after), channel_id=1, source_target_pairs={{0,12},{4,0},{8,4},{12,8},{1,13},{5,1},{9,5},{13,9},{2,14},{6,2},{... | collective-permute-start | bytes 258056 | tf_op jit(solution)/shard_map/ppermute | solution.py:734
  16.1 6.1 %shard_map.133 = (bf16[2,2,4096,128]{3,2,1,0:T(8,128)(2,1)S(1)}, bf16[2,16,2,128,128]{4,3,2,1,0:T(8,128)(2,1)S(1)}, bf16[4096,1024]{1,0:T(8,128)(2,1)S(1)}, f32[2,16,2048]{2,1,0:T(8,128)S(1)}) custom-call(s32[4]{0:T(128)S(1)} %pad_add_fusion.place, s32[16]{0:T(128)S(1)} %copy-done.2, s32[16,8]{1,0:T(8,128)S(1)} %copy.14.table, bf16[1,4,4096,128]{3,2,1,0:T(8,128)(2,1)} %pk.1, ...), custom_call_target="tpu_custom_call" | custom-call | bytes 33554432 | tf_op jit(solution)/shard_map/pallas_call | solution.py:281
  22.3 6.4 %shard_map.134 = (bf16[16,2176]{1,0:T(8,128)(2,1)S(1)}, f32[16,128]{1,0:T(8,128)S(1)}, bf16[16,512]{1,0:T(8,128)(2,1)S(1)}, bf16[2,2,4096,128]{3,2,1,0:T(8,128)(2,1)S(1)}, bf16[2,16,2,128,128]{4,3,2,1,0:T(8,128)(2,1)S(1)}) custom-call(s32[4]{0:T(128)S(1)} %pad_add_fusion.place, f32[16,2688]{1,0:T(8,128)S(1)} %get-tuple-element.49.refs_0_, ...), custom_call_target="tpu_custom_call" | custom-call | tf_op jit(solution)/shard_map/pallas_call | solution.py:646
  28.7 4.5 %collective-permute-start.10 = (bf16[16,2176]{1,0:T(8,128)(2,1)S(1)}, bf16[16,2176]{1,0:T(8,128)(2,1)S(1)}, u32[]{:S(2)}, u32[]{:S(2)}) collective-permute-start(bf16[16,2176]{1,0:T(8,128)(2,1)S(1)} %get-tuple-element.58.own), channel_id=1, source_target_pairs={{0,12},{4,0},{8,4},{12,8},{1,13},{5,1},{9,5},{13,9},{2,14},{6,2},{... | collective-permute-start | bytes 208904 | tf_op jit(solution)/shard_map/ppermute | solution.py:734
  34.2 3.9 %shard_map.135 = (bf16[1024,4096]{1,0:T(8,128)(2,1)S(1)}, bf16[1024,512]{1,0:T(8,128)(2,1)S(1)}, bf16[1024,512]{1,0:T(8,128)(2,1)S(1)}) custom-call(bf16[1024,4096]{1,0:T(8,128)(2,1)} %refs_0_.3, bf16[1024,512]{1,0:T(8,128)(2,1)} %refs_1_.3, bf16[1024,512]{1,0:T(8,128)(2,1)} %refs_2_.3, f32[16,128]{1,0:T(8,128)S(1)} %get-tuple-element.59.refs_3_.stat), custom_call_target="tpu_custom_call" | custom-call | bytes 33554432 | tf_op jit(solution)/shard_map/pallas_call | solution.py:303
  38.2 1.6 %collective-permute-done.8.refs_0_ = bf16[16,2176]{1,0:T(8,128)(2,1)S(1)} collective-permute-done((bf16[16,2176]{1,0:T(8,128)(2,1)S(1)}, bf16[16,2176]{1,0:T(8,128)(2,1)S(1)}, u32[]{:S(2)}, u32[]{:S(2)}) %collective-permute-start.8) | collective-permute-done | bytes 69664 | tf_op jit(solution)/shard_map/ppermute | solution.py:734
  39.8 1.4 %collective-permute-done.9.refs_1_ = bf16[16,2176]{1,0:T(8,128)(2,1)S(1)} collective-permute-done((bf16[16,2176]{1,0:T(8,128)(2,1)S(1)}, bf16[16,2176]{1,0:T(8,128)(2,1)S(1)}, u32[]{:S(2)}, u32[]{:S(2)}) %collective-permute-start.9) | collective-permute-done | bytes 69664 | tf_op jit(solution)/shard_map/ppermute | solution.py:734
  44.0 1.5 %collective-permute-start.12 = (bf16[16,1024]{1,0:T(8,128)(2,1)S(1)}, bf16[16,1024]{1,0:T(8,128)(2,1)S(1)}, u32[]{:S(2)}, u32[]{:S(2)}) collective-permute-start(bf16[16,1024]{1,0:T(8,128)(2,1)S(1)} %shard_map.138.mine), channel_id=1, source_target_pairs={{0,2},{2,0},{1,3},{3,1},{4,6},{6,4},{5,7},{7,5},{8,10},{10,8},{9,1... | collective-permute-start | bytes 98312 | tf_op jit(solution)/shard_map/ppermute | solution.py:728
  45.5 2.4 %collective-permute-done.12.other = bf16[16,1024]{1,0:T(8,128)(2,1)S(1)} collective-permute-done((bf16[16,1024]{1,0:T(8,128)(2,1)S(1)}, bf16[16,1024]{1,0:T(8,128)(2,1)S(1)}, u32[]{:S(2)}, u32[]{:S(2)}) %collective-permute-start.12) | collective-permute-done | bytes 32800 | tf_op jit(solution)/shard_map/ppermute | solution.py:728
  51.2 2.0 %collective-permute-start.15 = (bf16[16,2688]{1,0:T(8,128)(2,1)S(1)}, bf16[16,2688]{1,0:T(8,128)(2,1)S(1)}, u32[]{:S(2)}, u32[]{:S(2)}) collective-permute-start(bf16[16,2688]{1,0:T(8,128)(2,1)S(1)} %get-tuple-element.75), channel_id=1, source_target_pairs={{0,8},{4,12},{8,0},{12,4},{1,9},{5,13},{9,1},{13,5},{2,10},{6,14},... | collective-permute-start | bytes 258056 | tf_op jit(solution)/shard_map/ppermute | solution.py:734
  53.2 1.5 %collective-permute-start.16 = (bf16[16,2688]{1,0:T(8,128)(2,1)S(1)}, bf16[16,2688]{1,0:T(8,128)(2,1)S(1)}, u32[]{:S(2)}, u32[]{:S(2)}) collective-permute-start(bf16[16,2688]{1,0:T(8,128)(2,1)S(1)} %get-tuple-element.75), channel_id=1, source_target_pairs={{0,12},{4,0},{8,4},{12,8},{1,13},{5,1},{9,5},{13,9},{2,14},{6,2},{... | collective-permute-start | bytes 258056 | tf_op jit(solution)/shard_map/ppermute | solution.py:734
  54.7 3.4 %collective-permute-done.14.refs_1_ = bf16[16,2688]{1,0:T(8,128)(2,1)S(1)} collective-permute-done((bf16[16,2688]{1,0:T(8,128)(2,1)S(1)}, bf16[16,2688]{1,0:T(8,128)(2,1)S(1)}, u32[]{:S(2)}, u32[]{:S(2)}) %collective-permute-start.14) | collective-permute-done | bytes 86048 | tf_op jit(solution)/shard_map/ppermute | solution.py:734
  58.1 3.1 %collective-permute-done.15.refs_2_ = bf16[16,2688]{1,0:T(8,128)(2,1)S(1)} collective-permute-done((bf16[16,2688]{1,0:T(8,128)(2,1)S(1)}, bf16[16,2688]{1,0:T(8,128)(2,1)S(1)}, u32[]{:S(2)}, u32[]{:S(2)}) %collective-permute-start.15) | collective-permute-done | bytes 86048 | tf_op jit(solution)/shard_map/ppermute | solution.py:734
  61.2 5.5 %shard_map.142 = (bf16[16,2176]{1,0:T(8,128)(2,1)S(1)}, f32[16,128]{1,0:T(8,128)S(1)}, bf16[16,512]{1,0:T(8,128)(2,1)S(1)}) custom-call(s32[4]{0:T(128)S(1)} %pad_add_fusion.place, f32[16,2688]{1,0:T(8,128)S(1)} %get-tuple-element.74.refs_0_, bf16[16,2688]{1,0:T(8,128)(2,1)S(1)} %collective-permute-done.14.refs_1_, ...), custom_call_target="tpu_custom_call" | custom-call | tf_op jit(solution)/shard_map/pallas_call | solution.py:646
  66.6 1.7 %collective-permute-start.17 = (bf16[16,2176]{1,0:T(8,128)(2,1)S(1)}, bf16[16,2176]{1,0:T(8,128)(2,1)S(1)}, u32[]{:S(2)}, u32[]{:S(2)}) collective-permute-start(bf16[16,2176]{1,0:T(8,128)(2,1)S(1)} %get-tuple-element.79.own), channel_id=1, source_target_pairs={{0,4},{4,8},{8,12},{12,0},{1,5},{5,9},{9,13},{13,1},{2,6},{6,10},{... | collective-permute-start | bytes 208904 | tf_op jit(solution)/shard_map/ppermute | solution.py:734
  70.8 2.8 %collective-permute-done.17.refs_0_ = bf16[16,2176]{1,0:T(8,128)(2,1)S(1)} collective-permute-done((bf16[16,2176]{1,0:T(8,128)(2,1)S(1)}, bf16[16,2176]{1,0:T(8,128)(2,1)S(1)}, u32[]{:S(2)}, u32[]{:S(2)}) %collective-permute-start.17) | collective-permute-done | bytes 69664 | tf_op jit(solution)/shard_map/ppermute | solution.py:734
  73.5 1.6 %collective-permute-done.18.refs_1_ = bf16[16,2176]{1,0:T(8,128)(2,1)S(1)} collective-permute-done((bf16[16,2176]{1,0:T(8,128)(2,1)S(1)}, bf16[16,2176]{1,0:T(8,128)(2,1)S(1)}, u32[]{:S(2)}, u32[]{:S(2)}) %collective-permute-start.18) | collective-permute-done | bytes 69664 | tf_op jit(solution)/shard_map/ppermute | solution.py:734
  78.0 1.5 %collective-permute-start.21 = (bf16[16,1024]{1,0:T(8,128)(2,1)S(1)}, bf16[16,1024]{1,0:T(8,128)(2,1)S(1)}, u32[]{:S(2)}, u32[]{:S(2)}) collective-permute-start(bf16[16,1024]{1,0:T(8,128)(2,1)S(1)} %shard_map.145.mine), channel_id=1, source_target_pairs={{0,2},{2,0},{1,3},{3,1},{4,6},{6,4},{5,7},{7,5},{8,10},{10,8},{9,1... | collective-permute-start | bytes 98312 | tf_op jit(solution)/shard_map/ppermute | solution.py:728
  79.5 2.4 %collective-permute-done.21.other = bf16[16,1024]{1,0:T(8,128)(2,1)S(1)} collective-permute-done((bf16[16,1024]{1,0:T(8,128)(2,1)S(1)}, bf16[16,1024]{1,0:T(8,128)(2,1)S(1)}, u32[]{:S(2)}, u32[]{:S(2)}) %collective-permute-start.21) | collective-permute-done | bytes 32800 | tf_op jit(solution)/shard_map/ppermute | solution.py:728
  86.1 2.1 %collective-permute-start.24 = (bf16[16,2688]{1,0:T(8,128)(2,1)S(1)}, bf16[16,2688]{1,0:T(8,128)(2,1)S(1)}, u32[]{:S(2)}, u32[]{:S(2)}) collective-permute-start(bf16[16,2688]{1,0:T(8,128)(2,1)S(1)} %get-tuple-element.85), channel_id=1, source_target_pairs={{0,8},{4,12},{8,0},{12,4},{1,9},{5,13},{9,1},{13,5},{2,10},{6,14},... | collective-permute-start | bytes 258056 | tf_op jit(solution)/shard_map/ppermute | solution.py:734
  88.6 3.4 %collective-permute-done.23.refs_1_ = bf16[16,2688]{1,0:T(8,128)(2,1)S(1)} collective-permute-done((bf16[16,2688]{1,0:T(8,128)(2,1)S(1)}, bf16[16,2688]{1,0:T(8,128)(2,1)S(1)}, u32[]{:S(2)}, u32[]{:S(2)}) %collective-permute-start.23) | collective-permute-done | bytes 86048 | tf_op jit(solution)/shard_map/ppermute | solution.py:734
  92.0 3.2 %collective-permute-done.24.refs_2_ = bf16[16,2688]{1,0:T(8,128)(2,1)S(1)} collective-permute-done((bf16[16,2688]{1,0:T(8,128)(2,1)S(1)}, bf16[16,2688]{1,0:T(8,128)(2,1)S(1)}, u32[]{:S(2)}, u32[]{:S(2)}) %collective-permute-start.24) | collective-permute-done | bytes 86048 | tf_op jit(solution)/shard_map/ppermute | solution.py:734
  95.2 6.0 %shard_map.149 = (bf16[16,2176]{1,0:T(8,128)(2,1)S(1)}, f32[16,128]{1,0:T(8,128)S(1)}, bf16[16,512]{1,0:T(8,128)(2,1)}) custom-call(s32[4]{0:T(128)S(1)} %pad_add_fusion.place, f32[16,2688]{1,0:T(8,128)S(1)} %get-tuple-element.84.refs_0_, bf16[16,2688]{1,0:T(8,128)(2,1)S(1)} %collective-permute-done.23.refs_1_, ...), custom_call_target="tpu_custom_call" | custom-call | tf_op jit(solution)/shard_map/pallas_call | solution.py:646
  101.2 2.3 %collective-permute-start.26 = (bf16[16,2176]{1,0:T(8,128)(2,1)S(1)}, bf16[16,2176]{1,0:T(8,128)(2,1)S(1)}, u32[]{:S(2)}, u32[]{:S(2)}) collective-permute-start(bf16[16,2176]{1,0:T(8,128)(2,1)S(1)} %get-tuple-element.87.own), channel_id=1, source_target_pairs={{0,4},{4,8},{8,12},{12,0},{1,5},{5,9},{9,13},{13,1},{2,6},{6,10},{... | collective-permute-start | bytes 208904 | tf_op jit(solution)/shard_map/ppermute | solution.py:734
  104.3 1.6 %collective-permute-start.28 = (bf16[16,2176]{1,0:T(8,128)(2,1)S(1)}, bf16[16,2176]{1,0:T(8,128)(2,1)S(1)}, u32[]{:S(2)}, u32[]{:S(2)}) collective-permute-start(bf16[16,2176]{1,0:T(8,128)(2,1)S(1)} %get-tuple-element.87.own), channel_id=1, source_target_pairs={{0,12},{4,0},{8,4},{12,8},{1,13},{5,1},{9,5},{13,9},{2,14},{6,2},{... | collective-permute-start | bytes 208904 | tf_op jit(solution)/shard_map/ppermute | solution.py:734
  105.9 2.2 %collective-permute-done.26.refs_0_ = bf16[16,2176]{1,0:T(8,128)(2,1)S(1)} collective-permute-done((bf16[16,2176]{1,0:T(8,128)(2,1)S(1)}, bf16[16,2176]{1,0:T(8,128)(2,1)S(1)}, u32[]{:S(2)}, u32[]{:S(2)}) %collective-permute-start.26) | collective-permute-done | bytes 69664 | tf_op jit(solution)/shard_map/ppermute | solution.py:734
  108.1 2.2 %collective-permute-done.27.refs_1_ = bf16[16,2176]{1,0:T(8,128)(2,1)S(1)} collective-permute-done((bf16[16,2176]{1,0:T(8,128)(2,1)S(1)}, bf16[16,2176]{1,0:T(8,128)(2,1)S(1)}, u32[]{:S(2)}, u32[]{:S(2)}) %collective-permute-start.27) | collective-permute-done | bytes 69664 | tf_op jit(solution)/shard_map/ppermute | solution.py:734
  113.2 1.5 %collective-permute-start.30 = (bf16[16,1024]{1,0:T(8,128)(2,1)S(1)}, bf16[16,1024]{1,0:T(8,128)(2,1)S(1)}, u32[]{:S(2)}, u32[]{:S(2)}) collective-permute-start(bf16[16,1024]{1,0:T(8,128)(2,1)S(1)} %shard_map.152), channel_id=1, source_target_pairs={{0,2},{2,0},{1,3},{3,1},{4,6},{6,4},{5,7},{7,5},{8,10},{10,8},{9,1... | collective-permute-start | bytes 98312 | tf_op jit(solution)/shard_map/ppermute | solution.py:728
  114.7 2.4 %collective-permute-done.30 = bf16[16,1024]{1,0:T(8,128)(2,1)S(1)} collective-permute-done((bf16[16,1024]{1,0:T(8,128)(2,1)S(1)}, bf16[16,1024]{1,0:T(8,128)(2,1)S(1)}, u32[]{:S(2)}, u32[]{:S(2)}) %collective-permute-start.30) | collective-permute-done | bytes 32800 | tf_op jit(solution)/shard_map/ppermute | solution.py:728
  (71 shorter events, 24.4 us)
Async XLA Ops:
  0.6 7.6 %collective-permute-start.1 = (bf16[16,4,128,128]{3,2,1,0:T(8,128)(2,1)}, bf16[16,4,128,128]{3,2,1,0:T(8,128)(2,1)S(1)}, u32[]{:S(2)}, u32[]{:S(2)}) collective-permute-start(bf16[16,4,128,128]{3,2,1,0:T(8,128)(2,1)} %sk.1), channel_id=1, source_target_pairs={{0,1},{1,0},{2,3},{3,2},{4,5},{5,4},{6,7},{7,6},{8,9},{9,8},{10,11... | collective-permute-start | bytes 6291464 | tf_op jit(solution)/shard_map/ppermute | solution.py:728
  1.1 7.1 %collective-permute-start.2 = (bf16[16,4,128,128]{3,2,1,0:T(8,128)(2,1)}, bf16[16,4,128,128]{3,2,1,0:T(8,128)(2,1)}, u32[]{:S(2)}, u32[]{:S(2)}) collective-permute-start(bf16[16,4,128,128]{3,2,1,0:T(8,128)(2,1)} %sv.1), channel_id=1, source_target_pairs={{0,1},{1,0},{2,3},{3,2},{4,5},{5,4},{6,7},{7,6},{8,9},{9,8},{10,11... | collective-permute-start | bytes 6291464 | tf_op jit(solution)/shard_map/ppermute | solution.py:728
  6.7 1.5 %collective-permute-start = (f32[16,2688]{1,0:T(8,128)S(1)}, f32[16,2688]{1,0:T(8,128)S(1)}, u32[]{:S(2)}, u32[]{:S(2)}) collective-permute-start(f32[16,2688]{1,0:T(8,128)S(1)} %get-tuple-element.47), channel_id=1, source_target_pairs={{0,1},{1,0},{2,3},{3,2},{4,5},{5,4},{6,7},{7,6},{8,9},{9,8},{10,11... | collective-permute-start | bytes 516104 | tf_op jit(solution)/shard_map/ppermute | solution.py:728
  8.2 14.0 %copy-start.3 = (bf16[16,4,128,128]{3,2,1,0:T(8,128)(2,1)}, bf16[16,4,128,128]{3,2,1,0:T(8,128)(2,1)S(1)}, u32[]{:S(2)}) copy-start(bf16[16,4,128,128]{3,2,1,0:T(8,128)(2,1)S(1)} %collective-permute-done.1.refs_11_) | copy-start | bytes 6291460
  8.3 14.0 %collective-permute-start.6 = (bf16[1,4,4096,128]{3,2,1,0:T(8,128)(2,1)}, bf16[1,4,4096,128]{3,2,1,0:T(8,128)(2,1)}, u32[]{:S(2)}, u32[]{:S(2)}) collective-permute-start(bf16[1,4,4096,128]{3,2,1,0:T(8,128)(2,1)} %pk.1), channel_id=1, source_target_pairs={{0,1},{1,0},{2,3},{3,2},{4,5},{5,4},{6,7},{7,6},{8,9},{9,8},{10,11... | collective-permute-start | bytes 12582920 | tf_op jit(solution)/shard_map/ppermute | solution.py:728
  8.6 13.6 %collective-permute-start.7 = (bf16[1,4,4096,128]{3,2,1,0:T(8,128)(2,1)}, bf16[1,4,4096,128]{3,2,1,0:T(8,128)(2,1)}, u32[]{:S(2)}, u32[]{:S(2)}) collective-permute-start(bf16[1,4,4096,128]{3,2,1,0:T(8,128)(2,1)} %pv.1), channel_id=1, source_target_pairs={{0,1},{1,0},{2,3},{3,2},{4,5},{5,4},{6,7},{7,6},{8,9},{9,8},{10,11... | collective-permute-start | bytes 12582920 | tf_op jit(solution)/shard_map/ppermute | solution.py:728
  9.2 13.1 %collective-permute-start.3 = (bf16[16,2688]{1,0:T(8,128)(2,1)S(1)}, bf16[16,2688]{1,0:T(8,128)(2,1)S(1)}, u32[]{:S(2)}, u32[]{:S(2)}) collective-permute-start(bf16[16,2688]{1,0:T(8,128)(2,1)S(1)} %get-tuple-element.50.after), channel_id=1, source_target_pairs={{0,4},{4,8},{8,12},{12,0},{1,5},{5,9},{9,13},{13,1},{2,6},{6,10},{... | collective-permute-start | bytes 258056 | tf_op jit(solution)/shard_map/ppermute | solution.py:734
  12.1 10.1 %collective-permute-start.4 = (bf16[16,2688]{1,0:T(8,128)(2,1)S(1)}, bf16[16,2688]{1,0:T(8,128)(2,1)S(1)}, u32[]{:S(2)}, u32[]{:S(2)}) collective-permute-start(bf16[16,2688]{1,0:T(8,128)(2,1)S(1)} %get-tuple-element.50.after), channel_id=1, source_target_pairs={{0,8},{4,12},{8,0},{12,4},{1,9},{5,13},{9,1},{13,5},{2,10},{6,14},... | collective-permute-start | bytes 258056 | tf_op jit(solution)/shard_map/ppermute | solution.py:734
  14.7 7.6 %collective-permute-start.5 = (bf16[16,2688]{1,0:T(8,128)(2,1)S(1)}, bf16[16,2688]{1,0:T(8,128)(2,1)S(1)}, u32[]{:S(2)}, u32[]{:S(2)}) collective-permute-start(bf16[16,2688]{1,0:T(8,128)(2,1)S(1)} %get-tuple-element.50.after), channel_id=1, source_target_pairs={{0,12},{4,0},{8,4},{12,8},{1,13},{5,1},{9,5},{13,9},{2,14},{6,2},{... | collective-permute-start | bytes 258056 | tf_op jit(solution)/shard_map/ppermute | solution.py:734
  28.7 9.5 %collective-permute-start.10 = (bf16[16,2176]{1,0:T(8,128)(2,1)S(1)}, bf16[16,2176]{1,0:T(8,128)(2,1)S(1)}, u32[]{:S(2)}, u32[]{:S(2)}) collective-permute-start(bf16[16,2176]{1,0:T(8,128)(2,1)S(1)} %get-tuple-element.58.own), channel_id=1, source_target_pairs={{0,12},{4,0},{8,4},{12,8},{1,13},{5,1},{9,5},{13,9},{2,14},{6,2},{... | collective-permute-start | bytes 208904 | tf_op jit(solution)/shard_map/ppermute | solution.py:734
  33.2 6.6 %collective-permute-start.8 = (bf16[16,2176]{1,0:T(8,128)(2,1)S(1)}, bf16[16,2176]{1,0:T(8,128)(2,1)S(1)}, u32[]{:S(2)}, u32[]{:S(2)}) collective-permute-start(bf16[16,2176]{1,0:T(8,128)(2,1)S(1)} %get-tuple-element.58.own), channel_id=1, source_target_pairs={{0,4},{4,8},{8,12},{12,0},{1,5},{5,9},{9,13},{13,1},{2,6},{6,10},{... | collective-permute-start | bytes 208904 | tf_op jit(solution)/shard_map/ppermute | solution.py:734
  33.2 8.0 %collective-permute-start.9 = (bf16[16,2176]{1,0:T(8,128)(2,1)S(1)}, bf16[16,2176]{1,0:T(8,128)(2,1)S(1)}, u32[]{:S(2)}, u32[]{:S(2)}) collective-permute-start(bf16[16,2176]{1,0:T(8,128)(2,1)S(1)} %get-tuple-element.58.own), channel_id=1, source_target_pairs={{0,8},{4,12},{8,0},{12,4},{1,9},{5,13},{9,1},{13,5},{2,10},{6,14},... | collective-permute-start | bytes 208904 | tf_op jit(solution)/shard_map/ppermute | solution.py:734
  41.5 1.3 %collective-permute-start.11 = (bf16[16,2048]{1,0:T(8,128)(2,1)S(1)}, bf16[16,2048]{1,0:T(8,128)(2,1)S(1)}, u32[]{:S(2)}, u32[]{:S(2)}) collective-permute-start(bf16[16,2048]{1,0:T(8,128)(2,1)S(1)} %shard_map.136.mine), channel_id=1, source_target_pairs={{0,1},{1,0},{2,3},{3,2},{4,5},{5,4},{6,7},{7,6},{8,9},{9,8},{10,11... | collective-permute-start | bytes 196616 | tf_op jit(solution)/shard_map/ppermute | solution.py:728
  44.0 3.9 %collective-permute-start.12 = (bf16[16,1024]{1,0:T(8,128)(2,1)S(1)}, bf16[16,1024]{1,0:T(8,128)(2,1)S(1)}, u32[]{:S(2)}, u32[]{:S(2)}) collective-permute-start(bf16[16,1024]{1,0:T(8,128)(2,1)S(1)} %shard_map.138.mine), channel_id=1, source_target_pairs={{0,2},{2,0},{1,3},{3,1},{4,6},{6,4},{5,7},{7,5},{8,10},{10,8},{9,1... | collective-permute-start | bytes 98312 | tf_op jit(solution)/shard_map/ppermute | solution.py:728
  49.3 1.4 %collective-permute-start.13 = (f32[16,2688]{1,0:T(8,128)S(1)}, f32[16,2688]{1,0:T(8,128)S(1)}, u32[]{:S(2)}, u32[]{:S(2)}) collective-permute-start(f32[16,2688]{1,0:T(8,128)S(1)} %get-tuple-element.73.give), channel_id=1, source_target_pairs={{0,1},{1,0},{2,3},{3,2},{4,5},{5,4},{6,7},{7,6},{8,9},{9,8},{10,11... | collective-permute-start | bytes 516104 | tf_op jit(solution)/shard_map/ppermute | solution.py:728
  50.8 7.2 %collective-permute-start.14 = (bf16[16,2688]{1,0:T(8,128)(2,1)S(1)}, bf16[16,2688]{1,0:T(8,128)(2,1)S(1)}, u32[]{:S(2)}, u32[]{:S(2)}) collective-permute-start(bf16[16,2688]{1,0:T(8,128)(2,1)S(1)} %get-tuple-element.75), channel_id=1, source_target_pairs={{0,4},{4,8},{8,12},{12,0},{1,5},{5,9},{9,13},{13,1},{2,6},{6,10},{... | collective-permute-start | bytes 258056 | tf_op jit(solution)/shard_map/ppermute | solution.py:734
  51.2 10.0 %collective-permute-start.15 = (bf16[16,2688]{1,0:T(8,128)(2,1)S(1)}, bf16[16,2688]{1,0:T(8,128)(2,1)S(1)}, u32[]{:S(2)}, u32[]{:S(2)}) collective-permute-start(bf16[16,2688]{1,0:T(8,128)(2,1)S(1)} %get-tuple-element.75), channel_id=1, source_target_pairs={{0,8},{4,12},{8,0},{12,4},{1,9},{5,13},{9,1},{13,5},{2,10},{6,14},... | collective-permute-start | bytes 258056 | tf_op jit(solution)/shard_map/ppermute | solution.py:734
  53.2 8.0 %collective-permute-start.16 = (bf16[16,2688]{1,0:T(8,128)(2,1)S(1)}, bf16[16,2688]{1,0:T(8,128)(2,1)S(1)}, u32[]{:S(2)}, u32[]{:S(2)}) collective-permute-start(bf16[16,2688]{1,0:T(8,128)(2,1)S(1)} %get-tuple-element.75), channel_id=1, source_target_pairs={{0,12},{4,0},{8,4},{12,8},{1,13},{5,1},{9,5},{13,9},{2,14},{6,2},{... | collective-permute-start | bytes 258056 | tf_op jit(solution)/shard_map/ppermute | solution.py:734
  66.6 6.9 %collective-permute-start.17 = (bf16[16,2176]{1,0:T(8,128)(2,1)S(1)}, bf16[16,2176]{1,0:T(8,128)(2,1)S(1)}, u32[]{:S(2)}, u32[]{:S(2)}) collective-permute-start(bf16[16,2176]{1,0:T(8,128)(2,1)S(1)} %get-tuple-element.79.own), channel_id=1, source_target_pairs={{0,4},{4,8},{8,12},{12,0},{1,5},{5,9},{9,13},{13,1},{2,6},{6,10},{... | collective-permute-start | bytes 208904 | tf_op jit(solution)/shard_map/ppermute | solution.py:734
  68.3 6.8 %collective-permute-start.18 = (bf16[16,2176]{1,0:T(8,128)(2,1)S(1)}, bf16[16,2176]{1,0:T(8,128)(2,1)S(1)}, u32[]{:S(2)}, u32[]{:S(2)}) collective-permute-start(bf16[16,2176]{1,0:T(8,128)(2,1)S(1)} %get-tuple-element.79.own), channel_id=1, source_target_pairs={{0,8},{4,12},{8,0},{12,4},{1,9},{5,13},{9,1},{13,5},{2,10},{6,14},... | collective-permute-start | bytes 208904 | tf_op jit(solution)/shard_map/ppermute | solution.py:734
  69.5 5.6 %collective-permute-start.19 = (bf16[16,2176]{1,0:T(8,128)(2,1)S(1)}, bf16[16,2176]{1,0:T(8,128)(2,1)S(1)}, u32[]{:S(2)}, u32[]{:S(2)}) collective-permute-start(bf16[16,2176]{1,0:T(8,128)(2,1)S(1)} %get-tuple-element.79.own), channel_id=1, source_target_pairs={{0,12},{4,0},{8,4},{12,8},{1,13},{5,1},{9,5},{13,9},{2,14},{6,2},{... | collective-permute-start | bytes 208904 | tf_op jit(solution)/shard_map/ppermute | solution.py:734
  75.5 1.3 %collective-permute-start.20 = (bf16[16,2048]{1,0:T(8,128)(2,1)S(1)}, bf16[16,2048]{1,0:T(8,128)(2,1)S(1)}, u32[]{:S(2)}, u32[]{:S(2)}) collective-permute-start(bf16[16,2048]{1,0:T(8,128)(2,1)S(1)} %shard_map.143.mine), channel_id=1, source_target_pairs={{0,1},{1,0},{2,3},{3,2},{4,5},{5,4},{6,7},{7,6},{8,9},{9,8},{10,11... | collective-permute-start | bytes 196616 | tf_op jit(solution)/shard_map/ppermute | solution.py:728
  78.0 3.9 %collective-permute-start.21 = (bf16[16,1024]{1,0:T(8,128)(2,1)S(1)}, bf16[16,1024]{1,0:T(8,128)(2,1)S(1)}, u32[]{:S(2)}, u32[]{:S(2)}) collective-permute-start(bf16[16,1024]{1,0:T(8,128)(2,1)S(1)} %shard_map.145.mine), channel_id=1, source_target_pairs={{0,2},{2,0},{1,3},{3,1},{4,6},{6,4},{5,7},{7,5},{8,10},{10,8},{9,1... | collective-permute-start | bytes 98312 | tf_op jit(solution)/shard_map/ppermute | solution.py:728
  83.3 1.4 %collective-permute-start.22 = (f32[16,2688]{1,0:T(8,128)S(1)}, f32[16,2688]{1,0:T(8,128)S(1)}, u32[]{:S(2)}, u32[]{:S(2)}) collective-permute-start(f32[16,2688]{1,0:T(8,128)S(1)} %get-tuple-element.83.give), channel_id=1, source_target_pairs={{0,1},{1,0},{2,3},{3,2},{4,5},{5,4},{6,7},{7,6},{8,9},{9,8},{10,11... | collective-permute-start | bytes 516104 | tf_op jit(solution)/shard_map/ppermute | solution.py:728
  84.8 7.2 %collective-permute-start.23 = (bf16[16,2688]{1,0:T(8,128)(2,1)S(1)}, bf16[16,2688]{1,0:T(8,128)(2,1)S(1)}, u32[]{:S(2)}, u32[]{:S(2)}) collective-permute-start(bf16[16,2688]{1,0:T(8,128)(2,1)S(1)} %get-tuple-element.85), channel_id=1, source_target_pairs={{0,4},{4,8},{8,12},{12,0},{1,5},{5,9},{9,13},{13,1},{2,6},{6,10},{... | collective-permute-start | bytes 258056 | tf_op jit(solution)/shard_map/ppermute | solution.py:734
  86.1 9.1 %collective-permute-start.24 = (bf16[16,2688]{1,0:T(8,128)(2,1)S(1)}, bf16[16,2688]{1,0:T(8,128)(2,1)S(1)}, u32[]{:S(2)}, u32[]{:S(2)}) collective-permute-start(bf16[16,2688]{1,0:T(8,128)(2,1)S(1)} %get-tuple-element.85), channel_id=1, source_target_pairs={{0,8},{4,12},{8,0},{12,4},{1,9},{5,13},{9,1},{13,5},{2,10},{6,14},... | collective-permute-start | bytes 258056 | tf_op jit(solution)/shard_map/ppermute | solution.py:734
  88.2 7.0 %collective-permute-start.25 = (bf16[16,2688]{1,0:T(8,128)(2,1)S(1)}, bf16[16,2688]{1,0:T(8,128)(2,1)S(1)}, u32[]{:S(2)}, u32[]{:S(2)}) collective-permute-start(bf16[16,2688]{1,0:T(8,128)(2,1)S(1)} %get-tuple-element.85), channel_id=1, source_target_pairs={{0,12},{4,0},{8,4},{12,8},{1,13},{5,1},{9,5},{13,9},{2,14},{6,2},{... | collective-permute-start | bytes 258056 | tf_op jit(solution)/shard_map/ppermute | solution.py:734
  101.2 6.9 %collective-permute-start.26 = (bf16[16,2176]{1,0:T(8,128)(2,1)S(1)}, bf16[16,2176]{1,0:T(8,128)(2,1)S(1)}, u32[]{:S(2)}, u32[]{:S(2)}) collective-permute-start(bf16[16,2176]{1,0:T(8,128)(2,1)S(1)} %get-tuple-element.87.own), channel_id=1, source_target_pairs={{0,4},{4,8},{8,12},{12,0},{1,5},{5,9},{9,13},{13,1},{2,6},{6,10},{... | collective-permute-start | bytes 208904 | tf_op jit(solution)/shard_map/ppermute | solution.py:734
  103.5 6.8 %collective-permute-start.27 = (bf16[16,2176]{1,0:T(8,128)(2,1)S(1)}, bf16[16,2176]{1,0:T(8,128)(2,1)S(1)}, u32[]{:S(2)}, u32[]{:S(2)}) collective-permute-start(bf16[16,2176]{1,0:T(8,128)(2,1)S(1)} %get-tuple-element.87.own), channel_id=1, source_target_pairs={{0,8},{4,12},{8,0},{12,4},{1,9},{5,13},{9,1},{13,5},{2,10},{6,14},... | collective-permute-start | bytes 208904 | tf_op jit(solution)/shard_map/ppermute | solution.py:734
  104.3 6.0 %collective-permute-start.28 = (bf16[16,2176]{1,0:T(8,128)(2,1)S(1)}, bf16[16,2176]{1,0:T(8,128)(2,1)S(1)}, u32[]{:S(2)}, u32[]{:S(2)}) collective-permute-start(bf16[16,2176]{1,0:T(8,128)(2,1)S(1)} %get-tuple-element.87.own), channel_id=1, source_target_pairs={{0,12},{4,0},{8,4},{12,8},{1,13},{5,1},{9,5},{13,9},{2,14},{6,2},{... | collective-permute-start | bytes 208904 | tf_op jit(solution)/shard_map/ppermute | solution.py:734
  110.6 1.3 %collective-permute-start.29 = (bf16[16,2048]{1,0:T(8,128)(2,1)S(1)}, bf16[16,2048]{1,0:T(8,128)(2,1)S(1)}, u32[]{:S(2)}, u32[]{:S(2)}) collective-permute-start(bf16[16,2048]{1,0:T(8,128)(2,1)S(1)} %shard_map.150.mine), channel_id=1, source_target_pairs={{0,1},{1,0},{2,3},{3,2},{4,5},{5,4},{6,7},{7,6},{8,9},{9,8},{10,11... | collective-permute-start | bytes 196616 | tf_op jit(solution)/shard_map/ppermute | solution.py:728
  113.2 3.9 %collective-permute-start.30 = (bf16[16,1024]{1,0:T(8,128)(2,1)S(1)}, bf16[16,1024]{1,0:T(8,128)(2,1)S(1)}, u32[]{:S(2)}, u32[]{:S(2)}) collective-permute-start(bf16[16,1024]{1,0:T(8,128)(2,1)S(1)} %shard_map.152), channel_id=1, source_target_pairs={{0,2},{2,0},{1,3},{3,1},{4,6},{6,4},{5,7},{7,5},{8,10},{10,8},{9,1... | collective-permute-start | bytes 98312 | tf_op jit(solution)/shard_map/ppermute | solution.py:728
  (4 other events, 25.4 us)

commit v5 on v4

--- a/solution.py
+++ b/solution.py
@@ -202,6 +202,12 @@
     return pltpu.with_memory_space_constraint(array, pltpu.HBM)
 
 
+def whereabouts():
+    seq, side = lax.axis_index("seq"), lax.axis_index("side")
+    base = seq * (2 * SAMP_DEV)
+    return side, base, base + (1 - side) * SAMP_DEV, base + side * SAMP_DEV, seq
+
+
 def lanes(rows):
     return lax.broadcasted_iota(jnp.int32, (rows, LANES), 1)
 
@@ -265,8 +271,9 @@
 
 
 def load_caches_kernel(
-    place, lengths, table, pk, pv, sk, sv, w_out, after, prefix, suffix, kept_out, bias, sems
+    lengths, table, pk, pv, sk, sv, w_out, after, prefix, suffix, kept_out, bias, sems
 ):
+    place = whereabouts()
     pairs = halves(place, (pk, pv, sk, sv), prefix, suffix) + [(w_out, kept_out)]
     copies = copied(pairs, sems)
     live_bias(place, lengths, table, bias)
@@ -274,7 +281,7 @@
         copy.wait()
 
 
-def load_caches(place, lengths, table, pools, w_out, after):
+def load_caches(lengths, table, pools, w_out, after):
     page = pools[2].shape[2]
     tokens = SAMP_DEV * table.shape[1] * page
     sources = [in_hbm(array) for array in (*pools, w_out)]
@@ -285,12 +292,12 @@
             pltpu.VMEM(w_out.shape, w_out.dtype),
             jax.ShapeDtypeStruct((2, SAMP_DEV * GROUP, tokens), F32),
         ],
-        in_specs=[SMEM_SPEC] * 3 + [HBM_SPEC] * 5 + [VMEM_SPEC],
+        in_specs=[SMEM_SPEC] * 2 + [HBM_SPEC] * 5 + [VMEM_SPEC],
         out_specs=[VMEM_SPEC] * 4,
         scratch_shapes=[pltpu.SemaphoreType.DMA((5,))],
         compiler_params=PARAMS,
         cost_estimate=pl.CostEstimate(flops=0, bytes_accessed=1 << 25, transcendentals=0),
-    )(place, lengths, table, *sources, after)
+    )(lengths, table, *sources, after)
 
 
 def load_kernel(*refs):
@@ -323,16 +330,34 @@
     return tiles
 
 
-def first_project_kernel(place, *refs):
+def project_half(scaled, weights, tiles, out, arrive=lambda: None):
+    vectors, width = [], 0
+    for index, columns, to in tiles:
+        arrive()
+        part = jnp.dot(scaled, weights[index][:, columns], preferred_element_type=F32)
+        if index == 0:
+            out[:, to] = part
+            width = to.stop
+        else:
+            vectors += [part[:, at : at + HD] for at in range(0, part.shape[1], HD)]
+    span = 2 * SAMP_DEV
+    for chip in range(scaled.shape[0] // span):
+        part = slice(chip * span, (chip + 1) * span)
+        out[:, width + chip * HD : width + (chip + 1) * HD] = jnp.concatenate(
+            [vector[part] for vector in vectors], axis=0
+        )
+
+
+def first_project_kernel(*refs):
+    place = whereabouts()
     sources, (keep, give, *buffers, sems) = refs[:5], refs[5:]
     weights, (x_ref, gain) = buffers[:3], buffers[3:]
     outs = ((give, 1 - place[0]), (keep, place[0]))
-    tiles = [
-        (out, *tile) for out, who in outs for tile in column_tiles(place, weights, who)
-    ]
+    halves_of = [(out, column_tiles(place, weights, who)) for out, who in outs]
     pairs = list(zip(sources[3:], buffers[3:]))
-    for _, index, columns, _ in tiles:
-        pairs.append((sources[index].at[:, columns], weights[index].at[:, columns]))
+    for _, tiles in halves_of:
+        for index, columns, _ in tiles:
+            pairs.append((sources[index].at[:, columns], weights[index].at[:, columns]))
     copies = copied(pairs, sems)
     copies[0].wait()
     copies[1].wait()
@@ -342,14 +367,12 @@
     column = lanes(wide.shape[0])
     for out in (give, keep):
         out[:, out.shape[1] - LANES :] = jnp.where(column == 0, squares, 0.0)
-    for copy, (out, index, columns, to) in zip(copies[2:], tiles):
-        copy.wait()
-        out[:, to] = jnp.dot(
-            scaled, weights[index][:, columns], preferred_element_type=F32
-        )
-
-
-def first_project(place, x, gain, weights):
+    waiting = iter(copies[2:])
+    for out, tiles in halves_of:
+        project_half(scaled, weights, tiles, out, lambda: next(waiting).wait())
+
+
+def first_project(x, gain, weights):
     rows = x.shape[0]
     width = sum(w.shape[1] for w in weights) // 2 + LANES
     sources = [in_hbm(array) for array in (*weights, x, gain)]
@@ -357,15 +380,16 @@
     return pl.pallas_call(
         first_project_kernel,
         out_shape=[jax.ShapeDtypeStruct((rows, width), F32)] * 2,
-        in_specs=[SMEM_SPEC] + [HBM_SPEC] * 5,
+        in_specs=[HBM_SPEC] * 5,
         out_specs=[VMEM_SPEC] * 2,
         scratch_shapes=[pltpu.VMEM(array.shape, array.dtype) for array in sources]
         + [pltpu.SemaphoreType.DMA((count,))],
         compiler_params=LARGE_PARAMS,
-    )(place, *sources)
-
-
-def give_kernel(place, x_ref, gain, sum_ref, mine, other, *refs):
+    )(*sources)
+
+
+def give_kernel(x_ref, gain, sum_ref, mine, other, *refs):
+    place = whereabouts()
     weights, (give, scaled_ref, new_x, new_sum) = refs[:3], refs[3:]
     delta = mine[...].astype(F32) + other[...].astype(F32)
     new_sum[...] = sum_ref[...] + delta
@@ -377,13 +401,10 @@
     squares = jnp.sum(wide * wide, axis=1, keepdims=True)
     column = lanes(wide.shape[0])
     give[:, give.shape[1] - LANES :] = jnp.where(column == 0, squares, 0.0)
-    for index, columns, to in column_tiles(place, weights, 1 - place[0]):
-        give[:, to] = jnp.dot(
-            scaled, weights[index][:, columns], preferred_element_type=F32
-        )
-
-
-def give_project(place, x, gain, weights, rest):
+    project_half(scaled, weights, column_tiles(place, weights, 1 - place[0]), give)
+
+
+def give_project(x, gain, weights, rest):
     rows = x.shape[0]
     width = sum(w.shape[1] for w in weights) // 2 + LANES
     return pl.pallas_call(
@@ -394,56 +415,62 @@
             jax.ShapeDtypeStruct(x.shape, BF16),
             jax.ShapeDtypeStruct(x.shape, F32),
         ],
-        in_specs=[SMEM_SPEC] + [VMEM_SPEC] * 8,
+        in_specs=[VMEM_SPEC] * 8,
         out_specs=[VMEM_SPEC] * 4,
         compiler_params=PARAMS,
         cost_estimate=COST,
-    )(place, x, gain, *rest, *[resident(weight) for weight in weights])
-
-
-def keep_kernel(place, scaled_ref, give, *refs):
+    )(x, gain, *rest, *[resident(weight) for weight in weights])
+
+
+def keep_kernel(scaled_ref, give, *refs):
+    place = whereabouts()
     weights, keep = refs[:3], refs[3]
     scaled = scaled_ref[...]
     main = keep.shape[1] - LANES
     keep[:, main:] = give[:, main:]
-    for index, columns, to in column_tiles(place, weights, place[0]):
-        keep[:, to] = jnp.dot(
-            scaled, weights[index][:, columns], preferred_element_type=F32
-        )
-
-
-def keep_project(place, scaled, give, weights):
+    project_half(scaled, weights, column_tiles(place, weights, place[0]), keep)
+
+
+def keep_project(scaled, give, weights):
     return pl.pallas_call(
         keep_kernel,
         out_shape=jax.ShapeDtypeStruct(give.shape, F32),
-        in_specs=[SMEM_SPEC] + [VMEM_SPEC] * 5,
+        in_specs=[VMEM_SPEC] * 5,
         out_specs=VMEM_SPEC,
         compiler_params=PARAMS,
         cost_estimate=COST,
-    )(place, scaled, give, *[resident(weight) for weight in weights])
-
-
-def pair_sum_kernel(keep, got, total, sent):
+    )(scaled, give, *[resident(weight) for weight in weights])
+
+
+def pair_sum_kernel(query_width, keep, got, total, *sent):
+    place = whereabouts()
     both = keep[...] + got[...]
     total[...] = both
+    rows = both.shape[0]
     main = both.shape[1] - LANES
-    sent[:, :main] = both[:, :main].astype(BF16)
-    column = lanes(both.shape[0])
+    chips = (main - query_width) // HD
+    column = lanes(rows)
     high, middle, low = pieces(both[:, main : main + 1])
-    sent[:, main:] = jnp.where(
+    stats = jnp.where(
         column == 0, high, jnp.where(column == 1, middle, jnp.where(column == 2, low, 0.0))
     ).astype(BF16)
-
-
-def pair_sum(keep, got):
+    query = both[:, :query_width].astype(BF16)
+    for hop, out in enumerate(sent, 1):
+        chip = lax.rem(place[4] + hop, chips)
+        block = pl.ds(pl.multiple_of(query_width + chip * HD, HD), HD)
+        out[:, :query_width] = query
+        out[:, query_width : query_width + HD] = total[:, block].astype(BF16)
+        out[:, query_width + HD :] = stats
+
+
+def pair_sum(keep, got, query_width, hops):
+    rows = keep.shape[0]
+    sent = jax.ShapeDtypeStruct((rows, query_width + HD + LANES), BF16)
     return pl.pallas_call(
-        pair_sum_kernel,
-        out_shape=[
-            jax.ShapeDtypeStruct(keep.shape, F32),
-            jax.ShapeDtypeStruct(keep.shape, BF16),
-        ],
+        functools.partial(pair_sum_kernel, query_width),
+        out_shape=[jax.ShapeDtypeStruct(keep.shape, F32)] + [sent] * hops,
         in_specs=[VMEM_SPEC] * 2,
-        out_specs=[VMEM_SPEC] * 2,
+        out_specs=[VMEM_SPEC] * (1 + hops),
         compiler_params=PARAMS,
     )(keep, got)
 
@@ -464,21 +491,25 @@
     )
 
 
-def weigh(scores, top, values, scale):
-    total, acc = None, None
-    for score, value in zip(scores, values):
-        expo = jnp.exp2((score - top) * scale)
-        part = lane_fold(jnp.add, expo)
-        term = jnp.dot(expo.astype(BF16), value, preferred_element_type=F32)
-        total = part if total is None else total + part
-        acc = term if acc is None else acc + term
-    return jnp.sum(total, axis=1, keepdims=True), acc
-
-
-def attend_kernel(features, step, others, place, *refs):
+def weigh(scores, top, values):
+    terms = [
+        jnp.dot(
+            jnp.exp2(score - top).astype(BF16),
+            jnp.concatenate([value, jnp.ones_like(value)], axis=1),
+            preferred_element_type=F32,
+        )
+        for score, value in zip(scores, values)
+    ]
+    both = functools.reduce(jnp.add, terms)
+    return both[:, HD : HD + 1], both[:, :HD]
+
+
+def attend_kernel(features, step, others, *refs):
+    place = whereabouts()
     total_ref = refs[0]
     got = refs[1 : 1 + others]
-    cos_ref, sin_ref, bias_ref = refs[1 + others : 4 + others]
+    cos_ref, sin_ref, new_cos, new_sin, bias_ref = refs[1 + others : 6 + others]
+    refs = refs[2:]
     own_prefix, own_suffix, *far = refs[4 + others : (10 if step == 0 else 8) + others]
     refs = refs[(10 if step == 0 else 8) + others :]
     old, (sent, stat, fresh) = refs[:step], refs[step : 3 + step]
@@ -499,23 +530,19 @@
 
     stats = total_ref[:, width : width + 1]
     for ref in got:
-        stats = stats + jnp.sum(ref[:, width:].astype(F32), axis=1, keepdims=True)
+        stats = stats + jnp.sum(ref[:, query_width + HD :].astype(F32), axis=1, keepdims=True)
     inverse = lax.rsqrt(stats / features + 1e-05)
     cosine = cos_ref[...]
     sine = sin_ref[...]
 
-    def block(at):
+    def query_block(at):
         value = total_ref[:, at : at + HD]
         for ref in got:
             value = value + ref[:, at : at + HD].astype(F32)
-        return value * inverse
-
-    def turned(at):
-        value = block(at)
+        value = value * (inverse * scale)
         return (value * cosine + pltpu.roll(value, HD // 2, 1) * sine).astype(BF16)
 
     sample = lax.broadcasted_iota(jnp.int32, (rows, 1), 0)
-    owned = (sample >= base) & (sample < base + 2 * SAMP_DEV)
     few_rows = SAMP_DEV * GROUP
     pick_row = lax.broadcasted_iota(jnp.int32, (few_rows, GROUP * rows), 0)
     pick_column = lax.broadcasted_iota(jnp.int32, (few_rows, GROUP * rows), 1)
@@ -524,34 +551,42 @@
     column = lanes(rows)
 
     queries = [
-        [turned((head * GROUP + g) * HD) for g in range(GROUP)] for head in range(heads)
+        [query_block((head * GROUP + g) * HD) for g in range(GROUP)] for head in range(heads)
     ]
     packed = [jnp.concatenate(query, axis=0) for query in queries]
-    keys, values = [], []
-    for head in range(heads):
-        new_key = turned(query_width + head * HD)
-        new_value = block(query_width + (heads + head) * HD).astype(BF16)
-        key_part = slice(head * HD, (head + 1) * HD)
-        value_part = slice((heads + head) * HD, (heads + head + 1) * HD)
-        fresh[:, key_part] = new_key
-        fresh[:, value_part] = new_value
-        keys.append([ref[:, key_part].astype(F32) for ref in old] + [new_key.astype(F32)])
-        values.append([ref[:, value_part].astype(F32) for ref in old] + [new_value.astype(F32)])
+    span = 2 * SAMP_DEV
+    mine = pl.ds(pl.multiple_of(query_width + place[4] * HD, HD), HD)
+    new = total_ref[:, mine]
+    for ref in got:
+        new = new + ref[:, query_width : query_width + HD].astype(F32)
+    vector_row = lax.broadcasted_iota(jnp.int32, (rows, 1), 0) % span
+    new_inverse = jnp.zeros((rows, 1), F32)
+    for i in range(span):
+        one = jnp.sum(jnp.where(sample == base + i, inverse, 0.0), axis=0, keepdims=True)
+        new_inverse = jnp.where(vector_row == i, one, new_inverse)
+    new = new * new_inverse
+    new = new * new_cos[...] + pltpu.roll(new, HD // 2, 1) * new_sin[...]
+    half = rows // 2
+    fresh[:rows] = new.astype(BF16)
+    fresh[rows:] = jnp.concatenate([new[half:], new[:half]], axis=0).astype(BF16)
+    padding = jnp.zeros((LANES - (step + 1) * rows, HD), BF16)
+    new_keys = jnp.concatenate([ref[:rows] for ref in (*old, fresh)] + [padding], axis=0)
+    new_values = jnp.concatenate([ref[rows:] for ref in (*old, fresh)] + [padding], axis=0)
+    line = lax.broadcasted_iota(jnp.int32, (GROUP * rows, LANES), 0) % rows - base
+    token = lax.broadcasted_iota(jnp.int32, (GROUP * rows, LANES), 1)
+    new_scores = [
+        jnp.where(
+            (token < (step + 1) * rows) & (token % rows == line + head * span)
+            & (line >= 0) & (line < span),
+            against(packed[head], new_keys),
+            -jnp.inf,
+        )
+        for head in range(heads)
+    ]
     few = [
         [jnp.dot(pick, packed[head], preferred_element_type=F32).astype(BF16) for pick in picks]
         for head in range(heads)
     ]
-    fresh_scores = [
-        [
-            [
-                jnp.sum(query.astype(F32) * key, axis=1, keepdims=True)
-                for key in keys[head]
-            ]
-            for query in queries[head]
-        ]
-        for head in range(heads)
-    ]
-
     slots, page = own_suffix.shape[1], own_suffix.shape[3]
     length = own_prefix.shape[2]
     chunk = min(2048, length)
@@ -574,24 +609,26 @@
                         packed[head], prefix[src][0, head, at : at + chunk]
                     )
     near_tops = [[row_max([score]) for score in scores] for scores in near_scores]
+    for head in range(heads):
+        far_scores[head].append(new_scores[head])
     far_tops = [row_max(scores) for scores in far_scores]
     for copy in waits[2:]:
         copy.wait()
     near = [
         [
-            weigh([near_scores[head][src]], near_tops[head][src], [pool(1, src, head)], scale)
+            weigh([near_scores[head][src]], near_tops[head][src], [pool(1, src, head)])
             for src in range(2)
         ]
         for head in range(heads)
     ]
 
-    stat_value = jnp.zeros((rows, LANES), F32)
+    tops = jnp.zeros((rows, LANES), F32)
+    totals = jnp.zeros((rows, LANES), F32)
     for head in range(heads):
         far_total, far_acc = weigh(
             far_scores[head],
             far_tops[head],
-            [prefix[src][1, head, at : at + chunk] for src, at in pieces_of],
-            scale,
+            [prefix[src][1, head, at : at + chunk] for src, at in pieces_of] + [new_values],
         )
         for g in range(GROUP):
             part = slice(g * rows, (g + 1) * rows)
@@ -607,29 +644,25 @@
                     total = jnp.where(here, near[head][src][0][line], total)
                     acc = jnp.where(here, near[head][src][1][line], acc)
             top = jnp.maximum(far_top, near_top)
-            scores = fresh_scores[head][g]
-            for score in scores:
-                top = jnp.where(owned, jnp.maximum(top, score), top)
-            far_weight = jnp.exp2((far_top - top) * scale)
-            near_weight = jnp.exp2((near_top - top) * scale)
+            far_weight = jnp.exp2(far_top - top)
+            near_weight = jnp.exp2(near_top - top)
             total = total * near_weight + far_total[part] * far_weight
             acc = acc * near_weight + far_acc[part] * far_weight
-            for score, value in zip(scores, values[head]):
-                expo = jnp.where(owned, jnp.exp2(jnp.where(owned, score - top, 0.0) * scale), 0.0)
-                total = total + expo
-                acc = acc + expo.astype(BF16).astype(F32) * value
             index = head * GROUP + g
-            sent[:, index * HD : (index + 1) * HD] = (acc / total).astype(BF16)
-            level = top * scale + jnp.log2(total)
-            stat_value = jnp.where(column == index, level, stat_value)
-    high, middle, low = pieces(stat_value)
+            sent[:, index * HD : (index + 1) * HD] = acc.astype(BF16)
+            tops = jnp.where(column == index, top, tops)
+            totals = jnp.where(column == index, total, totals)
     many = heads * GROUP
-    stat[...] = stat_value
-    shifted = high + pltpu.roll(middle, many, 1) + pltpu.roll(low, 2 * many, 1)
-    sent[:, many * HD :] = shifted.astype(BF16)
-
-
-def attend(features, step, place, total, got, tables, caches, old):
+    stat[:, :LANES] = tops
+    stat[:, LANES:] = totals
+    parts = [*pieces(tops), *pieces(totals)]
+    packed_stats = parts[0]
+    for n, part in enumerate(parts[1:], 1):
+        packed_stats = packed_stats + pltpu.roll(part, n * many, 1)
+    sent[:, many * HD :] = packed_stats.astype(BF16)
+
+
+def attend(features, step, total, got, tables, caches, old):
     rows = total.shape[0]
     own, far = caches
     heads = own[0].shape[1]
@@ -643,35 +676,40 @@
         specs = [VMEM_SPEC] * 4
         out_shape, scratch = [], []
     small = [total, *got, *tables]
+    last = step == STEPS - 1
+    if last:
+        scratch = [pltpu.VMEM((2 * rows, HD), BF16)]
+    else:
+        out_shape = [jax.ShapeDtypeStruct((2 * rows, HD), BF16)] + out_shape
     return pl.pallas_call(
         functools.partial(attend_kernel, features, step, len(got)),
         out_shape=[
             jax.ShapeDtypeStruct((rows, heads * GROUP * HD + LANES), BF16),
-            jax.ShapeDtypeStruct((rows, LANES), F32),
-            jax.ShapeDtypeStruct((rows, 2 * heads * HD), BF16),
+            jax.ShapeDtypeStruct((rows, 2 * LANES), F32),
             *out_shape,
         ],
-        in_specs=[SMEM_SPEC] + [VMEM_SPEC] * len(small) + specs + [VMEM_SPEC] * len(old),
-        out_specs=[VMEM_SPEC] * (3 + len(out_shape)),
+        in_specs=[VMEM_SPEC] * len(small) + specs + [VMEM_SPEC] * len(old),
+        out_specs=[VMEM_SPEC] * (2 + len(out_shape)),
         scratch_shapes=scratch,
         compiler_params=LARGE_PARAMS,
-    )(place, *small, *inputs, *old)
+    )(*small, *inputs, *old)
 
 
 def merge_kernel(own, stat, *refs):
     got, out = refs[:-1], refs[-1]
     many = out.shape[1] // HD
-    levels = [stat[...]]
+    tops, totals = [stat[:, :LANES]], [stat[:, LANES:]]
     for ref in got:
         packed = ref[:, many * HD :].astype(F32)
-        levels.append(
-            packed
-            + pltpu.roll(packed, LANES - many, 1)
-            + pltpu.roll(packed, LANES - 2 * many, 1)
-        )
-    top = functools.reduce(jnp.maximum, levels)
-    weights = [jnp.exp2(level - top) for level in levels]
-    share = 1.0 / functools.reduce(jnp.add, weights)
+        turns = [packed] + [pltpu.roll(packed, LANES - n * many, 1) for n in range(1, 6)]
+        tops.append(turns[0] + turns[1] + turns[2])
+        totals.append(turns[3] + turns[4] + turns[5])
+    used = lanes(own.shape[0]) < many
+    tops = [jnp.where(used, top, 0.0) for top in tops]
+    top = functools.reduce(jnp.maximum, tops)
+    weights = [jnp.exp2(each - top) for each in tops]
+    total = functools.reduce(jnp.add, [w * t for w, t in zip(weights, totals)])
+    share = 1.0 / jnp.where(used, total, 1.0)
     weights = [weight * share for weight in weights]
     for index in range(many):
         part = slice(index * HD, (index + 1) * HD)
@@ -691,49 +729,73 @@
     )(own, stat, *got)
 
 
-def near_output_kernel(place, mine, weight, out):
+def near_output_kernel(mine, weight, out):
+    place = whereabouts()
     half = mine.shape[1]
     rows = pl.ds(pl.multiple_of(place[0] * half, half), half)
     out[...] = jnp.dot(mine[...], weight[rows], preferred_element_type=F32)
 
 
-def far_output_kernel(place, other, weight, near, out):
+def far_output_kernel(other, weight, near, out):
+    place = whereabouts()
     half = other.shape[1]
     rows = pl.ds(pl.multiple_of((1 - place[0]) * half, half), half)
     total = near[...] + jnp.dot(other[...], weight[rows], preferred_element_type=F32)
     out[...] = total.astype(BF16)
 
 
-def output(place, mine, weight):
+def output(mine, weight):
     other = swapped(mine, "side")
     shape = (mine.shape[0], weight.shape[1])
     near = pl.pallas_call(
         near_output_kernel,
         out_shape=jax.ShapeDtypeStruct(shape, F32),
-        in_specs=[SMEM_SPEC] + [VMEM_SPEC] * 2,
+        in_specs=[VMEM_SPEC] * 2,
         out_specs=VMEM_SPEC,
         compiler_params=PARAMS,
         cost_estimate=COST,
-    )(place, mine, resident(weight))
+    )(mine, resident(weight))
     return pl.pallas_call(
         far_output_kernel,
         out_shape=jax.ShapeDtypeStruct(shape, BF16),
-        in_specs=[SMEM_SPEC] + [VMEM_SPEC] * 3,
+        in_specs=[VMEM_SPEC] * 3,
         out_specs=VMEM_SPEC,
         compiler_params=PARAMS,
-    )(place, other, resident(weight), near)
+    )(other, resident(weight), near)
 
 
 def swapped(array, axis):
     return lax.ppermute(array, axis, [(0, 1), (1, 0)])
 
 
-def from_others(array, axis):
+def from_others(arrays, axis):
     size = lax.axis_size(axis)
     return [
         lax.ppermute(array, axis, [(i, (i + hop) % size) for i in range(size)])
-        for hop in range(1, size)
+        for hop, array in enumerate(arrays, 1)
     ]
+
+
+def rotations(lengths, base):
+    half = HD // 2
+    freq = 500000.0 ** (-(jnp.arange(half, dtype=F32) * 2.0 / HD))
+    position = (
+        PREFIX + lengths[None, :] + jnp.arange(STEPS, dtype=jnp.int32)[:, None]
+    ).astype(F32)
+    angle = position[..., None] * freq
+    cosine, sine = jnp.cos(angle), jnp.sin(angle)
+    cosine = jnp.concatenate([cosine, cosine], axis=-1)
+    sine = jnp.concatenate([-sine, sine], axis=-1)
+    span = 2 * SAMP_DEV
+    vectors = lengths.shape[0] // span
+    new_cosine = lax.dynamic_slice_in_dim(cosine, base, span, 1)
+    new_sine = lax.dynamic_slice_in_dim(sine, base, span, 1)
+    turns = vectors // 2
+    new_cosine = jnp.concatenate(
+        [new_cosine] * turns + [jnp.ones_like(new_cosine)] * turns, axis=1
+    )
+    new_sine = jnp.concatenate([new_sine] * turns + [jnp.zeros_like(new_sine)] * turns, axis=1)
+    return cosine, sine, new_cosine, new_sine
 
 
 def local_split(
@@ -750,27 +812,14 @@
     suffix_lengths,
     page_table,
 ):
-    samples, width = hidden.shape
-    features = width * lax.axis_size(("seq", "side"))
-    seq = lax.axis_index("seq")
-    side = lax.axis_index("side")
-    base = seq * (2 * SAMP_DEV)
-    first_own = base + (1 - side) * SAMP_DEV
-    first_got = base + side * SAMP_DEV
-    place = jnp.stack([side, base, first_own, first_got]).astype(jnp.int32)
+    features = hidden.shape[1] * lax.axis_size(("seq", "side"))
+    base = lax.axis_index("seq") * (2 * SAMP_DEV)
     pools = (prefix_keys, prefix_values, suffix_keys, suffix_values)
     weights = (w_query, w_key, w_value)
     far = [swapped(pool, "side") for pool in pools[2:]]
-    half = HD // 2
-    freq = 500000.0 ** (-(jnp.arange(half, dtype=F32) * 2.0 / HD))
-    position = (
-        PREFIX + suffix_lengths[None, :] + jnp.arange(STEPS, dtype=jnp.int32)[:, None]
-    ).astype(F32)
-    angle = position[..., None] * freq
-    cosine, sine = jnp.cos(angle), jnp.sin(angle)
-    cosine = jnp.concatenate([cosine, cosine], axis=-1)
-    sine = jnp.concatenate([-sine, sine], axis=-1)
     gain_row = gain[None, :]
+    query_width = w_query.shape[1] // 2
+    hops = lax.axis_size("seq") - 1
 
     state = hidden
     update = jnp.zeros(hidden.shape, F32)
@@ -778,31 +827,34 @@
     old = []
     for step in range(STEPS):
         if rest:
-            give, scaled, state, update = give_project(place, state, gain_row, weights, rest)
+            give, scaled, state, update = give_project(state, gain_row, weights, rest)
             got_sum = swapped(give, "side")
-            keep = keep_project(place, scaled, give, weights)
-            total, sent = pair_sum(keep, got_sum)
+            keep = keep_project(scaled, give, weights)
+            total, *sent = pair_sum(keep, got_sum, query_width, hops)
         else:
-            keep, give = first_project(place, state, gain_row, weights)
+            keep, give = first_project(state, gain_row, weights)
             got_sum = swapped(give, "side")
             got_sum, *given = lax.optimization_barrier((got_sum, *far, *pools[:2]))
             far = [swapped(pool, "side") for pool in given[2:]] + given[:2]
-            total, sent = pair_sum(keep, got_sum)
-            *own, out_weight, bias = load_caches(
-                place, suffix_lengths, page_table, pools, w_out, sent
+            total, *sent = pair_sum(keep, got_sum, query_width, hops)
+            *sent, lengths, table = lax.optimization_barrier(
+                (*sent, suffix_lengths, page_table)
             )
+            turning = rotations(lengths, base)
+            *own, out_weight, bias = load_caches(lengths, table, pools, w_out, sent[0])
         got = from_others(sent, "seq")
-        sent, stat, fresh, *kept = attend(
-            features, step, place, total, got, (cosine[step], sine[step], bias), (own, far), old
-        )
-        far = kept or far
-        got = from_others(sent, "seq")
+        tables = (*[each[step] for each in turning], bias)
+        sent, stat, *kept = attend(
+            features, step, total, got, tables, (own, far), old
+        )
+        far = kept[1:] or far
+        got = from_others([sent] * hops, "seq")
         if not rest:
             weights = load(weights, stat)
             got, weights = lax.optimization_barrier((got, weights))
-        old.append(fresh)
+        old += kept[:1]
         mixed = merge(sent, stat, got)
-        part = output(place, mixed, out_weight)
+        part = output(mixed, out_weight)
         rest = (update, part, swapped(part, "head"))
     delta = rest[1].astype(F32) + rest[2].astype(F32)
     return ((state.astype(F32) + delta).astype(BF16), update + delta)
@@ -815,7 +867,9 @@
         and mesh.shape["side"] == 2
         and heads % 2 == 0
         and args[6].shape[0] == mesh.shape["groups"]
-        and heads // 2 * GROUP * 3 <= LANES
+        and heads // 2 * GROUP * 6 <= LANES
+        and mesh.shape["seq"] == heads
+        and args[0].shape[0] // mesh.shape["groups"] * STEPS <= LANES
     )
 
 

time: 118 us -> 109 us (0.924)
  Pallas kernels: 46.9 us -> 37.5 us
    pallas_call x3, Pallas kernels: 17.8 us -> 14.3 us  [attend(): pl.pallas_call(functools.partial(attend_kernel, features, step, len(got))...]
    ppermute x13, waiting for transfers between devices: 8.69 us -> 12 us  [swapped(): return lax.ppermute(array, axis, [(0, 1), (1, 0)])]
    ppermute x18, waiting for transfers between devices: 25 us -> 22.8 us  [from_others(): lax.ppermute(array, axis, [(i, (i + hop) % size) for i in range(size)])]
    pallas_call x3, Pallas kernels: 3.57 us -> 1.95 us  [output(): pl.pallas_call(far_output_kernel, out_shape=jax.ShapeDtypeStruct(shape, B...]
    pallas_call x3, Pallas kernels: 3.57 us -> 1.96 us  [output(): pl.pallas_call(near_output_kernel, out_shape=jax.ShapeDtypeStruct(shape,...]
  transfers between devices with their start and end apart: 31 -> 31, of which waited for: 17 -> 20; matrix products, arithmetic and copies ran while one was open for 0% -> 1% of each run, Pallas kernels for 18% -> 17%
where the time goes in v5:
time: 109 us
  Pallas kernels  37.5 us (34%)
  waiting for transfers between devices  34.8 us (32%)
  starting transfers between devices  34.4 us (32%)
  other arithmetic  1.16 us (1%)
    ppermute x18, starting transfers between devices, from_others(): lax.ppermute(array, axis, [(i, (i + hop) % size) for i in range(size)])  28.1 us
    ppermute x18, waiting for transfers between devices, from_others(): lax.ppermute(array, axis, [(i, (i + hop) % size) for i in range(size)])  22.8 us
    pallas_call x3, Pallas kernels, attend(): pl.pallas_call(functools.partial(attend_kernel, features, step, len(got))...  14.3 us
    ppermute x13, waiting for transfers between devices, swapped(): return lax.ppermute(array, axis, [(0, 1), (1, 0)])  12 us
    ppermute x13, starting transfers between devices, swapped(): return lax.ppermute(array, axis, [(0, 1), (1, 0)])  6.34 us
    pallas_call x1, Pallas kernels, load_caches(): pl.pallas_call(load_caches_kernel, out_shape=half_shapes(pools) + [pltpu....  6.07 us
    pallas_call x1, Pallas kernels, first_project(): pl.pallas_call(first_project_kernel, out_shape=[jax.ShapeDtypeStruct((row...  4.83 us
    pallas_call x1, Pallas kernels, load(): pl.pallas_call(load_kernel, out_shape=[pltpu.VMEM(w.shape, w.dtype) for w...  3.93 us
  transfers between devices with their start and end apart: 31, of which 20 were waited for; matrix products, arithmetic and copies ran while one was open for 1% of the time, Pallas kernels for 17%

profile of v5, /device:TPU:0, one launch (start us, length us, event | category | flops | bytes accessed | tf_op | source)
XLA Modules:
  0.0 108.9 jit_solution(7232887210509572181)
XLA Ops:
  1.2 4.8 %shard_map.131 = (f32[16,2688]{1,0:T(8,128)S(1)}, f32[16,2688]{1,0:T(8,128)S(1)}) custom-call(bf16[1024,4096]{1,0:T(8,128)(2,1)} %refs_0_.3, bf16[1024,512]{1,0:T(8,128)(2,1)} %refs_1_.3, bf16[1024,512]{1,0:T(8,128)(2,1)} %refs_2_.3, bf16[16,1024]{1,0:T(8,128)(2,1)} %x_ref.1, f32[1,1024]{1,0:T(1,128)} %bitcast.25), custom_call_target="tpu_custom_call" | custom-call | tf_op jit(solution)/shard_map/pallas_call | solution.py:380
  6.6 1.6 %collective-permute-done.got = f32[16,2688]{1,0:T(8,128)S(1)} collective-permute-done((f32[16,2688]{1,0:T(8,128)S(1)}, f32[16,2688]{1,0:T(8,128)S(1)}, u32[]{:S(2)}, u32[]{:S(2)}) %collective-permute-start) | collective-permute-done | bytes 172064 | tf_op jit(solution)/shard_map/ppermute | solution.py:768
  9.1 2.9 %collective-permute-start.3 = (bf16[16,2304]{1,0:T(8,128)(2,1)S(1)}, bf16[16,2304]{1,0:T(8,128)(2,1)S(1)}, u32[]{:S(2)}, u32[]{:S(2)}) collective-permute-start(bf16[16,2304]{1,0:T(8,128)(2,1)S(1)} %get-tuple-element.64.after), channel_id=1, source_target_pairs={{0,4},{4,8},{8,12},{12,0},{1,5},{5,9},{9,13},{13,1},{2,6},{6,10},{... | collective-permute-start | bytes 221192 | tf_op jit(solution)/shard_map/ppermute | solution.py:774
  12.1 2.6 %collective-permute-start.4 = (bf16[16,2304]{1,0:T(8,128)(2,1)S(1)}, bf16[16,2304]{1,0:T(8,128)(2,1)S(1)}, u32[]{:S(2)}, u32[]{:S(2)}) collective-permute-start(bf16[16,2304]{1,0:T(8,128)(2,1)S(1)} %get-tuple-element.65), channel_id=1, source_target_pairs={{0,8},{4,12},{8,0},{12,4},{1,9},{5,13},{9,1},{13,5},{2,10},{6,14},... | collective-permute-start | bytes 221192 | tf_op jit(solution)/shard_map/ppermute | solution.py:774
  16.0 6.1 %shard_map.133 = (bf16[2,2,4096,128]{3,2,1,0:T(8,128)(2,1)S(1)}, bf16[2,16,2,128,128]{4,3,2,1,0:T(8,128)(2,1)S(1)}, bf16[4096,1024]{1,0:T(8,128)(2,1)S(1)}, f32[2,16,2048]{2,1,0:T(8,128)S(1)}) custom-call(s32[16]{0:T(128)S(1)} %copy-done.2, s32[16,8]{1,0:T(8,128)S(1)} %copy.14.table, bf16[1,4,4096,128]{3,2,1,0:T(8,128)(2,1)} %pk.1, ...), custom_call_target="tpu_custom_call" | custom-call | bytes 33554432 | tf_op jit(solution)/shard_map/pallas_call | solution.py:288
  22.7 5.5 %shard_map.134 = (bf16[16,2176]{1,0:T(8,128)(2,1)S(1)}, f32[16,256]{1,0:T(8,128)S(1)}, bf16[32,128]{1,0:T(8,128)(2,1)S(1)}, bf16[2,2,4096,128]{3,2,1,0:T(8,128)(2,1)S(1)}, bf16[2,16,2,128,128]{4,3,2,1,0:T(8,128)(2,1)S(1)}) custom-call(f32[16,2688]{1,0:T(8,128)S(1)} %get-tuple-element.60.refs_0_, bf16[16,2304]{1,0:T(8,128)(2,1)S(1)} %collective-permute-done.3.refs_1_, ...), custom_call_target="tpu_custom_call" | custom-call | tf_op jit(solution)/shard_map/pallas_call | solution.py:684
  28.2 4.1 %collective-permute-start.10 = (bf16[16,2176]{1,0:T(8,128)(2,1)S(1)}, bf16[16,2176]{1,0:T(8,128)(2,1)S(1)}, u32[]{:S(2)}, u32[]{:S(2)}) collective-permute-start(bf16[16,2176]{1,0:T(8,128)(2,1)S(1)} %get-tuple-element.76.own), channel_id=1, source_target_pairs={{0,12},{4,0},{8,4},{12,8},{1,13},{5,1},{9,5},{13,9},{2,14},{6,2},{... | collective-permute-start | bytes 208904 | tf_op jit(solution)/shard_map/ppermute | solution.py:774
  33.3 3.9 %shard_map.135 = (bf16[1024,4096]{1,0:T(8,128)(2,1)S(1)}, bf16[1024,512]{1,0:T(8,128)(2,1)S(1)}, bf16[1024,512]{1,0:T(8,128)(2,1)S(1)}) custom-call(bf16[1024,4096]{1,0:T(8,128)(2,1)} %refs_0_.3, bf16[1024,512]{1,0:T(8,128)(2,1)} %refs_1_.3, bf16[1024,512]{1,0:T(8,128)(2,1)} %refs_2_.3, f32[16,256]{1,0:T(8,128)S(1)} %get-tuple-element.77.refs_3_.stat), custom_call_target="tpu_custom_call" | custom-call | bytes 33554432 | tf_op jit(solution)/shard_map/pallas_call | solution.py:310
  37.3 1.6 %collective-permute-done.8.refs_0_ = bf16[16,2176]{1,0:T(8,128)(2,1)S(1)} collective-permute-done((bf16[16,2176]{1,0:T(8,128)(2,1)S(1)}, bf16[16,2176]{1,0:T(8,128)(2,1)S(1)}, u32[]{:S(2)}, u32[]{:S(2)}) %collective-permute-start.8) | collective-permute-done | bytes 69664 | tf_op jit(solution)/shard_map/ppermute | solution.py:774
  38.9 1.4 %collective-permute-done.9.refs_1_ = bf16[16,2176]{1,0:T(8,128)(2,1)S(1)} collective-permute-done((bf16[16,2176]{1,0:T(8,128)(2,1)S(1)}, bf16[16,2176]{1,0:T(8,128)(2,1)S(1)}, u32[]{:S(2)}, u32[]{:S(2)}) %collective-permute-start.9) | collective-permute-done | bytes 69664 | tf_op jit(solution)/shard_map/ppermute | solution.py:774
  42.6 1.5 %collective-permute-start.12 = (bf16[16,1024]{1,0:T(8,128)(2,1)S(1)}, bf16[16,1024]{1,0:T(8,128)(2,1)S(1)}, u32[]{:S(2)}, u32[]{:S(2)}) collective-permute-start(bf16[16,1024]{1,0:T(8,128)(2,1)S(1)} %shard_map.138.mine), channel_id=1, source_target_pairs={{0,2},{2,0},{1,3},{3,1},{4,6},{6,4},{5,7},{7,5},{8,10},{10,8},{9,1... | collective-permute-start | bytes 98312 | tf_op jit(solution)/shard_map/ppermute | solution.py:768
  44.1 2.4 %collective-permute-done.12.other = bf16[16,1024]{1,0:T(8,128)(2,1)S(1)} collective-permute-done((bf16[16,1024]{1,0:T(8,128)(2,1)S(1)}, bf16[16,1024]{1,0:T(8,128)(2,1)S(1)}, u32[]{:S(2)}, u32[]{:S(2)}) %collective-permute-start.12) | collective-permute-done | bytes 32800 | tf_op jit(solution)/shard_map/ppermute | solution.py:768
  49.2 2.0 %collective-permute-start.15 = (bf16[16,2304]{1,0:T(8,128)(2,1)S(1)}, bf16[16,2304]{1,0:T(8,128)(2,1)S(1)}, u32[]{:S(2)}, u32[]{:S(2)}) collective-permute-start(bf16[16,2304]{1,0:T(8,128)(2,1)S(1)} %get-tuple-element.94), channel_id=1, source_target_pairs={{0,8},{4,12},{8,0},{12,4},{1,9},{5,13},{9,1},{13,5},{2,10},{6,14},... | collective-permute-start | bytes 221192 | tf_op jit(solution)/shard_map/ppermute | solution.py:774
  51.2 1.5 %collective-permute-start.16 = (bf16[16,2304]{1,0:T(8,128)(2,1)S(1)}, bf16[16,2304]{1,0:T(8,128)(2,1)S(1)}, u32[]{:S(2)}, u32[]{:S(2)}) collective-permute-start(bf16[16,2304]{1,0:T(8,128)(2,1)S(1)} %get-tuple-element.95), channel_id=1, source_target_pairs={{0,12},{4,0},{8,4},{12,8},{1,13},{5,1},{9,5},{13,9},{2,14},{6,2},{... | collective-permute-start | bytes 221192 | tf_op jit(solution)/shard_map/ppermute | solution.py:774
  52.7 3.2 %collective-permute-done.14.refs_1_ = bf16[16,2304]{1,0:T(8,128)(2,1)S(1)} collective-permute-done((bf16[16,2304]{1,0:T(8,128)(2,1)S(1)}, bf16[16,2304]{1,0:T(8,128)(2,1)S(1)}, u32[]{:S(2)}, u32[]{:S(2)}) %collective-permute-start.14) | collective-permute-done | bytes 73760 | tf_op jit(solution)/shard_map/ppermute | solution.py:774
  55.9 2.2 %collective-permute-done.15.refs_2_ = bf16[16,2304]{1,0:T(8,128)(2,1)S(1)} collective-permute-done((bf16[16,2304]{1,0:T(8,128)(2,1)S(1)}, bf16[16,2304]{1,0:T(8,128)(2,1)S(1)}, u32[]{:S(2)}, u32[]{:S(2)}) %collective-permute-start.15) | collective-permute-done | bytes 73760 | tf_op jit(solution)/shard_map/ppermute | solution.py:774
  58.0 4.4 %shard_map.142 = (bf16[16,2176]{1,0:T(8,128)(2,1)S(1)}, f32[16,256]{1,0:T(8,128)S(1)}, bf16[32,128]{1,0:T(8,128)(2,1)S(1)}) custom-call(f32[16,2688]{1,0:T(8,128)S(1)} %get-tuple-element.92.refs_0_, bf16[16,2304]{1,0:T(8,128)(2,1)S(1)} %collective-permute-done.14.refs_1_, bf16[16,2304]{1,0:T(8,128)(2,1)S(1)} %collective-permute-done.15.refs_2_, ...), custom_call_target="tpu_custom_call" | custom-call | tf_op jit(solution)/shard_map/pallas_call | solution.py:684
  62.4 1.5 %collective-permute-start.17 = (bf16[16,2176]{1,0:T(8,128)(2,1)S(1)}, bf16[16,2176]{1,0:T(8,128)(2,1)S(1)}, u32[]{:S(2)}, u32[]{:S(2)}) collective-permute-start(bf16[16,2176]{1,0:T(8,128)(2,1)S(1)} %get-tuple-element.99.own), channel_id=1, source_target_pairs={{0,4},{4,8},{8,12},{12,0},{1,5},{5,9},{9,13},{13,1},{2,6},{6,10},{... | collective-permute-start | bytes 208904 | tf_op jit(solution)/shard_map/ppermute | solution.py:774
  66.3 3.0 %collective-permute-done.17.refs_0_ = bf16[16,2176]{1,0:T(8,128)(2,1)S(1)} collective-permute-done((bf16[16,2176]{1,0:T(8,128)(2,1)S(1)}, bf16[16,2176]{1,0:T(8,128)(2,1)S(1)}, u32[]{:S(2)}, u32[]{:S(2)}) %collective-permute-start.17) | collective-permute-done | bytes 69664 | tf_op jit(solution)/shard_map/ppermute | solution.py:774
  69.3 1.5 %collective-permute-done.18.refs_1_ = bf16[16,2176]{1,0:T(8,128)(2,1)S(1)} collective-permute-done((bf16[16,2176]{1,0:T(8,128)(2,1)S(1)}, bf16[16,2176]{1,0:T(8,128)(2,1)S(1)}, u32[]{:S(2)}, u32[]{:S(2)}) %collective-permute-start.18) | collective-permute-done | bytes 69664 | tf_op jit(solution)/shard_map/ppermute | solution.py:774
  73.1 1.5 %collective-permute-start.21 = (bf16[16,1024]{1,0:T(8,128)(2,1)S(1)}, bf16[16,1024]{1,0:T(8,128)(2,1)S(1)}, u32[]{:S(2)}, u32[]{:S(2)}) collective-permute-start(bf16[16,1024]{1,0:T(8,128)(2,1)S(1)} %shard_map.145.mine), channel_id=1, source_target_pairs={{0,2},{2,0},{1,3},{3,1},{4,6},{6,4},{5,7},{7,5},{8,10},{10,8},{9,1... | collective-permute-start | bytes 98312 | tf_op jit(solution)/shard_map/ppermute | solution.py:768
  74.6 2.4 %collective-permute-done.21.other = bf16[16,1024]{1,0:T(8,128)(2,1)S(1)} collective-permute-done((bf16[16,1024]{1,0:T(8,128)(2,1)S(1)}, bf16[16,1024]{1,0:T(8,128)(2,1)S(1)}, u32[]{:S(2)}, u32[]{:S(2)}) %collective-permute-start.21) | collective-permute-done | bytes 32800 | tf_op jit(solution)/shard_map/ppermute | solution.py:768
  80.7 2.0 %collective-permute-start.24 = (bf16[16,2304]{1,0:T(8,128)(2,1)S(1)}, bf16[16,2304]{1,0:T(8,128)(2,1)S(1)}, u32[]{:S(2)}, u32[]{:S(2)}) collective-permute-start(bf16[16,2304]{1,0:T(8,128)(2,1)S(1)} %get-tuple-element.106), channel_id=1, source_target_pairs={{0,8},{4,12},{8,0},{12,4},{1,9},{5,13},{9,1},{13,5},{2,10},{6,14},... | collective-permute-start | bytes 221192 | tf_op jit(solution)/shard_map/ppermute | solution.py:774
  83.2 3.2 %collective-permute-done.23.refs_1_ = bf16[16,2304]{1,0:T(8,128)(2,1)S(1)} collective-permute-done((bf16[16,2304]{1,0:T(8,128)(2,1)S(1)}, bf16[16,2304]{1,0:T(8,128)(2,1)S(1)}, u32[]{:S(2)}, u32[]{:S(2)}) %collective-permute-start.23) | collective-permute-done | bytes 73760 | tf_op jit(solution)/shard_map/ppermute | solution.py:774
  86.4 2.4 %collective-permute-done.24.refs_2_ = bf16[16,2304]{1,0:T(8,128)(2,1)S(1)} collective-permute-done((bf16[16,2304]{1,0:T(8,128)(2,1)S(1)}, bf16[16,2304]{1,0:T(8,128)(2,1)S(1)}, u32[]{:S(2)}, u32[]{:S(2)}) %collective-permute-start.24) | collective-permute-done | bytes 73760 | tf_op jit(solution)/shard_map/ppermute | solution.py:774
  88.7 4.4 %shard_map.149 = (bf16[16,2176]{1,0:T(8,128)(2,1)S(1)}, f32[16,256]{1,0:T(8,128)S(1)}) custom-call(f32[16,2688]{1,0:T(8,128)S(1)} %get-tuple-element.104.refs_0_, bf16[16,2304]{1,0:T(8,128)(2,1)S(1)} %collective-permute-done.23.refs_1_, bf16[16,2304]{1,0:T(8,128)(2,1)S(1)} %collective-permute-done.24.refs_2_, ...), custom_call_target="tpu_custom_call" | custom-call | tf_op jit(solution)/shard_map/pallas_call | solution.py:684
  93.1 2.1 %collective-permute-start.26 = (bf16[16,2176]{1,0:T(8,128)(2,1)S(1)}, bf16[16,2176]{1,0:T(8,128)(2,1)S(1)}, u32[]{:S(2)}, u32[]{:S(2)}) collective-permute-start(bf16[16,2176]{1,0:T(8,128)(2,1)S(1)} %get-tuple-element.109.own), channel_id=1, source_target_pairs={{0,4},{4,8},{8,12},{12,0},{1,5},{5,9},{9,13},{13,1},{2,6},{6,10},{... | collective-permute-start | bytes 208904 | tf_op jit(solution)/shard_map/ppermute | solution.py:774
  96.2 1.4 %collective-permute-start.28 = (bf16[16,2176]{1,0:T(8,128)(2,1)S(1)}, bf16[16,2176]{1,0:T(8,128)(2,1)S(1)}, u32[]{:S(2)}, u32[]{:S(2)}) collective-permute-start(bf16[16,2176]{1,0:T(8,128)(2,1)S(1)} %get-tuple-element.109.own), channel_id=1, source_target_pairs={{0,12},{4,0},{8,4},{12,8},{1,13},{5,1},{9,5},{13,9},{2,14},{6,2},{... | collective-permute-start | bytes 208904 | tf_op jit(solution)/shard_map/ppermute | solution.py:774
  97.6 2.2 %collective-permute-done.26.refs_0_ = bf16[16,2176]{1,0:T(8,128)(2,1)S(1)} collective-permute-done((bf16[16,2176]{1,0:T(8,128)(2,1)S(1)}, bf16[16,2176]{1,0:T(8,128)(2,1)S(1)}, u32[]{:S(2)}, u32[]{:S(2)}) %collective-permute-start.26) | collective-permute-done | bytes 69664 | tf_op jit(solution)/shard_map/ppermute | solution.py:774
  99.8 2.2 %collective-permute-done.27.refs_1_ = bf16[16,2176]{1,0:T(8,128)(2,1)S(1)} collective-permute-done((bf16[16,2176]{1,0:T(8,128)(2,1)S(1)}, bf16[16,2176]{1,0:T(8,128)(2,1)S(1)}, u32[]{:S(2)}, u32[]{:S(2)}) %collective-permute-start.27) | collective-permute-done | bytes 69664 | tf_op jit(solution)/shard_map/ppermute | solution.py:774
  104.3 1.5 %collective-permute-start.30 = (bf16[16,1024]{1,0:T(8,128)(2,1)S(1)}, bf16[16,1024]{1,0:T(8,128)(2,1)S(1)}, u32[]{:S(2)}, u32[]{:S(2)}) collective-permute-start(bf16[16,1024]{1,0:T(8,128)(2,1)S(1)} %shard_map.152), channel_id=1, source_target_pairs={{0,2},{2,0},{1,3},{3,1},{4,6},{6,4},{5,7},{7,5},{8,10},{10,8},{9,1... | collective-permute-start | bytes 98312 | tf_op jit(solution)/shard_map/ppermute | solution.py:768
  105.8 2.4 %collective-permute-done.30 = bf16[16,1024]{1,0:T(8,128)(2,1)S(1)} collective-permute-done((bf16[16,1024]{1,0:T(8,128)(2,1)S(1)}, bf16[16,1024]{1,0:T(8,128)(2,1)S(1)}, u32[]{:S(2)}, u32[]{:S(2)}) %collective-permute-start.30) | collective-permute-done | bytes 32800 | tf_op jit(solution)/shard_map/ppermute | solution.py:768
  (79 shorter events, 22.8 us)
Async XLA Ops:
  0.6 7.6 %collective-permute-start.1 = (bf16[16,4,128,128]{3,2,1,0:T(8,128)(2,1)}, bf16[16,4,128,128]{3,2,1,0:T(8,128)(2,1)S(1)}, u32[]{:S(2)}, u32[]{:S(2)}) collective-permute-start(bf16[16,4,128,128]{3,2,1,0:T(8,128)(2,1)} %sk.1), channel_id=1, source_target_pairs={{0,1},{1,0},{2,3},{3,2},{4,5},{5,4},{6,7},{7,6},{8,9},{9,8},{10,11... | collective-permute-start | bytes 6291464 | tf_op jit(solution)/shard_map/ppermute | solution.py:768
  1.1 7.1 %collective-permute-start.2 = (bf16[16,4,128,128]{3,2,1,0:T(8,128)(2,1)}, bf16[16,4,128,128]{3,2,1,0:T(8,128)(2,1)}, u32[]{:S(2)}, u32[]{:S(2)}) collective-permute-start(bf16[16,4,128,128]{3,2,1,0:T(8,128)(2,1)} %sv.1), channel_id=1, source_target_pairs={{0,1},{1,0},{2,3},{3,2},{4,5},{5,4},{6,7},{7,6},{8,9},{9,8},{10,11... | collective-permute-start | bytes 6291464 | tf_op jit(solution)/shard_map/ppermute | solution.py:768
  1.2 14.8 %copy-start.2 = (s32[16]{0:T(128)S(1)}, s32[16]{0:T(128)}, u32[]{:S(2)}) copy-start(s32[16]{0:T(128)} %lengths) | copy-start | bytes 196
  6.1 2.1 %collective-permute-start = (f32[16,2688]{1,0:T(8,128)S(1)}, f32[16,2688]{1,0:T(8,128)S(1)}, u32[]{:S(2)}, u32[]{:S(2)}) collective-permute-start(f32[16,2688]{1,0:T(8,128)S(1)} %get-tuple-element.58), channel_id=1, source_target_pairs={{0,1},{1,0},{2,3},{3,2},{4,5},{5,4},{6,7},{7,6},{8,9},{9,8},{10,11... | collective-permute-start | bytes 516104 | tf_op jit(solution)/shard_map/ppermute | solution.py:768
  8.3 14.4 %collective-permute-start.6 = (bf16[1,4,4096,128]{3,2,1,0:T(8,128)(2,1)}, bf16[1,4,4096,128]{3,2,1,0:T(8,128)(2,1)}, u32[]{:S(2)}, u32[]{:S(2)}) collective-permute-start(bf16[1,4,4096,128]{3,2,1,0:T(8,128)(2,1)} %pk.1), channel_id=1, source_target_pairs={{0,1},{1,0},{2,3},{3,2},{4,5},{5,4},{6,7},{7,6},{8,9},{9,8},{10,11... | collective-permute-start | bytes 12582920 | tf_op jit(solution)/shard_map/ppermute | solution.py:768
  8.7 14.0 %collective-permute-start.7 = (bf16[1,4,4096,128]{3,2,1,0:T(8,128)(2,1)}, bf16[1,4,4096,128]{3,2,1,0:T(8,128)(2,1)}, u32[]{:S(2)}, u32[]{:S(2)}) collective-permute-start(bf16[1,4,4096,128]{3,2,1,0:T(8,128)(2,1)} %pv.1), channel_id=1, source_target_pairs={{0,1},{1,0},{2,3},{3,2},{4,5},{5,4},{6,7},{7,6},{8,9},{9,8},{10,11... | collective-permute-start | bytes 12582920 | tf_op jit(solution)/shard_map/ppermute | solution.py:768
  9.1 13.5 %collective-permute-start.3 = (bf16[16,2304]{1,0:T(8,128)(2,1)S(1)}, bf16[16,2304]{1,0:T(8,128)(2,1)S(1)}, u32[]{:S(2)}, u32[]{:S(2)}) collective-permute-start(bf16[16,2304]{1,0:T(8,128)(2,1)S(1)} %get-tuple-element.64.after), channel_id=1, source_target_pairs={{0,4},{4,8},{8,12},{12,0},{1,5},{5,9},{9,13},{13,1},{2,6},{6,10},{... | collective-permute-start | bytes 221192 | tf_op jit(solution)/shard_map/ppermute | solution.py:774
  12.1 10.6 %collective-permute-start.4 = (bf16[16,2304]{1,0:T(8,128)(2,1)S(1)}, bf16[16,2304]{1,0:T(8,128)(2,1)S(1)}, u32[]{:S(2)}, u32[]{:S(2)}) collective-permute-start(bf16[16,2304]{1,0:T(8,128)(2,1)S(1)} %get-tuple-element.65), channel_id=1, source_target_pairs={{0,8},{4,12},{8,0},{12,4},{1,9},{5,13},{9,1},{13,5},{2,10},{6,14},... | collective-permute-start | bytes 221192 | tf_op jit(solution)/shard_map/ppermute | solution.py:774
  14.7 8.0 %collective-permute-start.5 = (bf16[16,2304]{1,0:T(8,128)(2,1)S(1)}, bf16[16,2304]{1,0:T(8,128)(2,1)S(1)}, u32[]{:S(2)}, u32[]{:S(2)}) collective-permute-start(bf16[16,2304]{1,0:T(8,128)(2,1)S(1)} %get-tuple-element.66), channel_id=1, source_target_pairs={{0,12},{4,0},{8,4},{12,8},{1,13},{5,1},{9,5},{13,9},{2,14},{6,2},{... | collective-permute-start | bytes 221192 | tf_op jit(solution)/shard_map/ppermute | solution.py:774
  28.2 9.1 %collective-permute-start.10 = (bf16[16,2176]{1,0:T(8,128)(2,1)S(1)}, bf16[16,2176]{1,0:T(8,128)(2,1)S(1)}, u32[]{:S(2)}, u32[]{:S(2)}) collective-permute-start(bf16[16,2176]{1,0:T(8,128)(2,1)S(1)} %get-tuple-element.76.own), channel_id=1, source_target_pairs={{0,12},{4,0},{8,4},{12,8},{1,13},{5,1},{9,5},{13,9},{2,14},{6,2},{... | collective-permute-start | bytes 208904 | tf_op jit(solution)/shard_map/ppermute | solution.py:774
  32.3 6.6 %collective-permute-start.8 = (bf16[16,2176]{1,0:T(8,128)(2,1)S(1)}, bf16[16,2176]{1,0:T(8,128)(2,1)S(1)}, u32[]{:S(2)}, u32[]{:S(2)}) collective-permute-start(bf16[16,2176]{1,0:T(8,128)(2,1)S(1)} %get-tuple-element.76.own), channel_id=1, source_target_pairs={{0,4},{4,8},{8,12},{12,0},{1,5},{5,9},{9,13},{13,1},{2,6},{6,10},{... | collective-permute-start | bytes 208904 | tf_op jit(solution)/shard_map/ppermute | solution.py:774
  32.3 8.0 %collective-permute-start.9 = (bf16[16,2176]{1,0:T(8,128)(2,1)S(1)}, bf16[16,2176]{1,0:T(8,128)(2,1)S(1)}, u32[]{:S(2)}, u32[]{:S(2)}) collective-permute-start(bf16[16,2176]{1,0:T(8,128)(2,1)S(1)} %get-tuple-element.76.own), channel_id=1, source_target_pairs={{0,8},{4,12},{8,0},{12,4},{1,9},{5,13},{9,1},{13,5},{2,10},{6,14},... | collective-permute-start | bytes 208904 | tf_op jit(solution)/shard_map/ppermute | solution.py:774
  40.6 1.3 %collective-permute-start.11 = (bf16[16,2048]{1,0:T(8,128)(2,1)S(1)}, bf16[16,2048]{1,0:T(8,128)(2,1)S(1)}, u32[]{:S(2)}, u32[]{:S(2)}) collective-permute-start(bf16[16,2048]{1,0:T(8,128)(2,1)S(1)} %shard_map.136.mine), channel_id=1, source_target_pairs={{0,1},{1,0},{2,3},{3,2},{4,5},{5,4},{6,7},{7,6},{8,9},{9,8},{10,11... | collective-permute-start | bytes 196616 | tf_op jit(solution)/shard_map/ppermute | solution.py:768
  42.6 3.9 %collective-permute-start.12 = (bf16[16,1024]{1,0:T(8,128)(2,1)S(1)}, bf16[16,1024]{1,0:T(8,128)(2,1)S(1)}, u32[]{:S(2)}, u32[]{:S(2)}) collective-permute-start(bf16[16,1024]{1,0:T(8,128)(2,1)S(1)} %shard_map.138.mine), channel_id=1, source_target_pairs={{0,2},{2,0},{1,3},{3,1},{4,6},{6,4},{5,7},{7,5},{8,10},{10,8},{9,1... | collective-permute-start | bytes 98312 | tf_op jit(solution)/shard_map/ppermute | solution.py:768
  47.3 1.4 %collective-permute-start.13 = (f32[16,2688]{1,0:T(8,128)S(1)}, f32[16,2688]{1,0:T(8,128)S(1)}, u32[]{:S(2)}, u32[]{:S(2)}) collective-permute-start(f32[16,2688]{1,0:T(8,128)S(1)} %get-tuple-element.91.give), channel_id=1, source_target_pairs={{0,1},{1,0},{2,3},{3,2},{4,5},{5,4},{6,7},{7,6},{8,9},{9,8},{10,11... | collective-permute-start | bytes 516104 | tf_op jit(solution)/shard_map/ppermute | solution.py:768
  48.8 7.0 %collective-permute-start.14 = (bf16[16,2304]{1,0:T(8,128)(2,1)S(1)}, bf16[16,2304]{1,0:T(8,128)(2,1)S(1)}, u32[]{:S(2)}, u32[]{:S(2)}) collective-permute-start(bf16[16,2304]{1,0:T(8,128)(2,1)S(1)} %get-tuple-element.93), channel_id=1, source_target_pairs={{0,4},{4,8},{8,12},{12,0},{1,5},{5,9},{9,13},{13,1},{2,6},{6,10},{... | collective-permute-start | bytes 221192 | tf_op jit(solution)/shard_map/ppermute | solution.py:774
  49.2 8.8 %collective-permute-start.15 = (bf16[16,2304]{1,0:T(8,128)(2,1)S(1)}, bf16[16,2304]{1,0:T(8,128)(2,1)S(1)}, u32[]{:S(2)}, u32[]{:S(2)}) collective-permute-start(bf16[16,2304]{1,0:T(8,128)(2,1)S(1)} %get-tuple-element.94), channel_id=1, source_target_pairs={{0,8},{4,12},{8,0},{12,4},{1,9},{5,13},{9,1},{13,5},{2,10},{6,14},... | collective-permute-start | bytes 221192 | tf_op jit(solution)/shard_map/ppermute | solution.py:774
  51.2 6.8 %collective-permute-start.16 = (bf16[16,2304]{1,0:T(8,128)(2,1)S(1)}, bf16[16,2304]{1,0:T(8,128)(2,1)S(1)}, u32[]{:S(2)}, u32[]{:S(2)}) collective-permute-start(bf16[16,2304]{1,0:T(8,128)(2,1)S(1)} %get-tuple-element.95), channel_id=1, source_target_pairs={{0,12},{4,0},{8,4},{12,8},{1,13},{5,1},{9,5},{13,9},{2,14},{6,2},{... | collective-permute-start | bytes 221192 | tf_op jit(solution)/shard_map/ppermute | solution.py:774
  62.4 6.9 %collective-permute-start.17 = (bf16[16,2176]{1,0:T(8,128)(2,1)S(1)}, bf16[16,2176]{1,0:T(8,128)(2,1)S(1)}, u32[]{:S(2)}, u32[]{:S(2)}) collective-permute-start(bf16[16,2176]{1,0:T(8,128)(2,1)S(1)} %get-tuple-element.99.own), channel_id=1, source_target_pairs={{0,4},{4,8},{8,12},{12,0},{1,5},{5,9},{9,13},{13,1},{2,6},{6,10},{... | collective-permute-start | bytes 208904 | tf_op jit(solution)/shard_map/ppermute | solution.py:774
  63.9 6.9 %collective-permute-start.18 = (bf16[16,2176]{1,0:T(8,128)(2,1)S(1)}, bf16[16,2176]{1,0:T(8,128)(2,1)S(1)}, u32[]{:S(2)}, u32[]{:S(2)}) collective-permute-start(bf16[16,2176]{1,0:T(8,128)(2,1)S(1)} %get-tuple-element.99.own), channel_id=1, source_target_pairs={{0,8},{4,12},{8,0},{12,4},{1,9},{5,13},{9,1},{13,5},{2,10},{6,14},... | collective-permute-start | bytes 208904 | tf_op jit(solution)/shard_map/ppermute | solution.py:774
  65.2 5.6 %collective-permute-start.19 = (bf16[16,2176]{1,0:T(8,128)(2,1)S(1)}, bf16[16,2176]{1,0:T(8,128)(2,1)S(1)}, u32[]{:S(2)}, u32[]{:S(2)}) collective-permute-start(bf16[16,2176]{1,0:T(8,128)(2,1)S(1)} %get-tuple-element.99.own), channel_id=1, source_target_pairs={{0,12},{4,0},{8,4},{12,8},{1,13},{5,1},{9,5},{13,9},{2,14},{6,2},{... | collective-permute-start | bytes 208904 | tf_op jit(solution)/shard_map/ppermute | solution.py:774
  71.1 1.3 %collective-permute-start.20 = (bf16[16,2048]{1,0:T(8,128)(2,1)S(1)}, bf16[16,2048]{1,0:T(8,128)(2,1)S(1)}, u32[]{:S(2)}, u32[]{:S(2)}) collective-permute-start(bf16[16,2048]{1,0:T(8,128)(2,1)S(1)} %shard_map.143.mine), channel_id=1, source_target_pairs={{0,1},{1,0},{2,3},{3,2},{4,5},{5,4},{6,7},{7,6},{8,9},{9,8},{10,11... | collective-permute-start | bytes 196616 | tf_op jit(solution)/shard_map/ppermute | solution.py:768
  73.1 3.9 %collective-permute-start.21 = (bf16[16,1024]{1,0:T(8,128)(2,1)S(1)}, bf16[16,1024]{1,0:T(8,128)(2,1)S(1)}, u32[]{:S(2)}, u32[]{:S(2)}) collective-permute-start(bf16[16,1024]{1,0:T(8,128)(2,1)S(1)} %shard_map.145.mine), channel_id=1, source_target_pairs={{0,2},{2,0},{1,3},{3,1},{4,6},{6,4},{5,7},{7,5},{8,10},{10,8},{9,1... | collective-permute-start | bytes 98312 | tf_op jit(solution)/shard_map/ppermute | solution.py:768
  77.8 1.4 %collective-permute-start.22 = (f32[16,2688]{1,0:T(8,128)S(1)}, f32[16,2688]{1,0:T(8,128)S(1)}, u32[]{:S(2)}, u32[]{:S(2)}) collective-permute-start(f32[16,2688]{1,0:T(8,128)S(1)} %get-tuple-element.103.give), channel_id=1, source_target_pairs={{0,1},{1,0},{2,3},{3,2},{4,5},{5,4},{6,7},{7,6},{8,9},{9,8},{10,11... | collective-permute-start | bytes 516104 | tf_op jit(solution)/shard_map/ppermute | solution.py:768
  79.3 7.0 %collective-permute-start.23 = (bf16[16,2304]{1,0:T(8,128)(2,1)S(1)}, bf16[16,2304]{1,0:T(8,128)(2,1)S(1)}, u32[]{:S(2)}, u32[]{:S(2)}) collective-permute-start(bf16[16,2304]{1,0:T(8,128)(2,1)S(1)} %get-tuple-element.105), channel_id=1, source_target_pairs={{0,4},{4,8},{8,12},{12,0},{1,5},{5,9},{9,13},{13,1},{2,6},{6,10},{... | collective-permute-start | bytes 221192 | tf_op jit(solution)/shard_map/ppermute | solution.py:774
  80.7 8.1 %collective-permute-start.24 = (bf16[16,2304]{1,0:T(8,128)(2,1)S(1)}, bf16[16,2304]{1,0:T(8,128)(2,1)S(1)}, u32[]{:S(2)}, u32[]{:S(2)}) collective-permute-start(bf16[16,2304]{1,0:T(8,128)(2,1)S(1)} %get-tuple-element.106), channel_id=1, source_target_pairs={{0,8},{4,12},{8,0},{12,4},{1,9},{5,13},{9,1},{13,5},{2,10},{6,14},... | collective-permute-start | bytes 221192 | tf_op jit(solution)/shard_map/ppermute | solution.py:774
  82.7 6.0 %collective-permute-start.25 = (bf16[16,2304]{1,0:T(8,128)(2,1)S(1)}, bf16[16,2304]{1,0:T(8,128)(2,1)S(1)}, u32[]{:S(2)}, u32[]{:S(2)}) collective-permute-start(bf16[16,2304]{1,0:T(8,128)(2,1)S(1)} %get-tuple-element.107), channel_id=1, source_target_pairs={{0,12},{4,0},{8,4},{12,8},{1,13},{5,1},{9,5},{13,9},{2,14},{6,2},{... | collective-permute-start | bytes 221192 | tf_op jit(solution)/shard_map/ppermute | solution.py:774
  93.1 6.7 %collective-permute-start.26 = (bf16[16,2176]{1,0:T(8,128)(2,1)S(1)}, bf16[16,2176]{1,0:T(8,128)(2,1)S(1)}, u32[]{:S(2)}, u32[]{:S(2)}) collective-permute-start(bf16[16,2176]{1,0:T(8,128)(2,1)S(1)} %get-tuple-element.109.own), channel_id=1, source_target_pairs={{0,4},{4,8},{8,12},{12,0},{1,5},{5,9},{9,13},{13,1},{2,6},{6,10},{... | collective-permute-start | bytes 208904 | tf_op jit(solution)/shard_map/ppermute | solution.py:774
  95.2 6.8 %collective-permute-start.27 = (bf16[16,2176]{1,0:T(8,128)(2,1)S(1)}, bf16[16,2176]{1,0:T(8,128)(2,1)S(1)}, u32[]{:S(2)}, u32[]{:S(2)}) collective-permute-start(bf16[16,2176]{1,0:T(8,128)(2,1)S(1)} %get-tuple-element.109.own), channel_id=1, source_target_pairs={{0,8},{4,12},{8,0},{12,4},{1,9},{5,13},{9,1},{13,5},{2,10},{6,14},... | collective-permute-start | bytes 208904 | tf_op jit(solution)/shard_map/ppermute | solution.py:774
  96.2 5.8 %collective-permute-start.28 = (bf16[16,2176]{1,0:T(8,128)(2,1)S(1)}, bf16[16,2176]{1,0:T(8,128)(2,1)S(1)}, u32[]{:S(2)}, u32[]{:S(2)}) collective-permute-start(bf16[16,2176]{1,0:T(8,128)(2,1)S(1)} %get-tuple-element.109.own), channel_id=1, source_target_pairs={{0,12},{4,0},{8,4},{12,8},{1,13},{5,1},{9,5},{13,9},{2,14},{6,2},{... | collective-permute-start | bytes 208904 | tf_op jit(solution)/shard_map/ppermute | solution.py:774
  102.4 1.3 %collective-permute-start.29 = (bf16[16,2048]{1,0:T(8,128)(2,1)S(1)}, bf16[16,2048]{1,0:T(8,128)(2,1)S(1)}, u32[]{:S(2)}, u32[]{:S(2)}) collective-permute-start(bf16[16,2048]{1,0:T(8,128)(2,1)S(1)} %shard_map.150.mine), channel_id=1, source_target_pairs={{0,1},{1,0},{2,3},{3,2},{4,5},{5,4},{6,7},{7,6},{8,9},{9,8},{10,11... | collective-permute-start | bytes 196616 | tf_op jit(solution)/shard_map/ppermute | solution.py:768
  104.3 3.9 %collective-permute-start.30 = (bf16[16,1024]{1,0:T(8,128)(2,1)S(1)}, bf16[16,1024]{1,0:T(8,128)(2,1)S(1)}, u32[]{:S(2)}, u32[]{:S(2)}) collective-permute-start(bf16[16,1024]{1,0:T(8,128)(2,1)S(1)} %shard_map.152), channel_id=1, source_target_pairs={{0,2},{2,0},{1,3},{3,1},{4,6},{6,4},{5,7},{7,5},{8,10},{10,8},{9,1... | collective-permute-start | bytes 98312 | tf_op jit(solution)/shard_map/ppermute | solution.py:768
  (4 other events, 32.1 us)

commit v6 on v5

--- a/solution.py
+++ b/solution.py
@@ -243,7 +243,7 @@
         (sk.at[:, part], suffix.at[0]),
         (pk.at[0, part], prefix.at[0]),
         (sv.at[:, part], suffix.at[1]),
-        (pv.at[0, part], prefix.at[1]),
+        (pv.at[0] if pv.shape[1] == heads else pv.at[0, part], prefix.at[1]),
     ]
 
 
@@ -253,6 +253,37 @@
         pltpu.VMEM((2, pk.shape[1] // 2) + pk.shape[2:], pk.dtype),
         pltpu.VMEM((2, sk.shape[0], sk.shape[1] // 2) + sk.shape[2:], sk.dtype),
     ]
+
+
+def cut_kernel(pool, after, out, held, sems):
+    place = whereabouts()
+    heads, length = out.shape[1:3]
+    parts = [(h, pl.ds(at, length // 2)) for h in range(heads) for at in (0, length // 2)]
+    source = pool.at[0, pl.ds((1 - place[0]) * heads, heads)]
+    reads = copied([(source.at[part], held.at[part]) for part in parts], sems.at[0])
+    writes = []
+    for n, (read, part) in enumerate(zip(reads, parts)):
+        read.wait()
+        writes.append(pltpu.make_async_copy(held.at[part], out.at[0].at[part], sems.at[1, n]))
+        writes[-1].start()
+    for write in writes:
+        write.wait()
+
+
+def cut(pool, after):
+    shape = (pool.shape[0], pool.shape[1] // 2) + pool.shape[2:]
+    return pl.pallas_call(
+        cut_kernel,
+        out_shape=jax.ShapeDtypeStruct(shape, pool.dtype),
+        in_specs=[HBM_SPEC, VMEM_SPEC],
+        out_specs=HBM_SPEC,
+        scratch_shapes=[
+            pltpu.VMEM(shape[1:], pool.dtype),
+            pltpu.SemaphoreType.DMA((2, 2 * shape[1])),
+        ],
+        compiler_params=PARAMS,
+        cost_estimate=pl.CostEstimate(flops=0, bytes_accessed=1 << 23, transcendentals=0),
+    )(in_hbm(pool), after)
 
 
 def live_bias(place, lengths, table, bias):
@@ -834,14 +865,17 @@
         else:
             keep, give = first_project(state, gain_row, weights)
             got_sum = swapped(give, "side")
-            got_sum, *given = lax.optimization_barrier((got_sum, *far, *pools[:2]))
-            far = [swapped(pool, "side") for pool in given[2:]] + given[:2]
+            got_sum, *far, keys, values = lax.optimization_barrier((got_sum, *far, *pools[:2]))
+            far = [swapped(keys, "side"), *far]
             total, *sent = pair_sum(keep, got_sum, query_width, hops)
-            *sent, lengths, table = lax.optimization_barrier(
-                (*sent, suffix_lengths, page_table)
+            *sent, lengths, table, values = lax.optimization_barrier(
+                (*sent, suffix_lengths, page_table, values)
             )
+            values = cut(values, sent[0])
+            after, values = lax.optimization_barrier((sent[0], values))
+            far.insert(1, swapped(values, "side"))
             turning = rotations(lengths, base)
-            *own, out_weight, bias = load_caches(lengths, table, pools, w_out, sent[0])
+            *own, out_weight, bias = load_caches(lengths, table, pools, w_out, after)
         got = from_others(sent, "seq")
         tables = (*[each[step] for each in turning], bias)
         sent, stat, *kept = attend(

time: 109 us -> 110 us (level)
  starting transfers between devices: 34.4 us -> 29.6 us
  waiting for transfers between devices: 34.8 us -> 37.6 us
  Pallas kernels: 37.5 us -> 40.1 us
    ppermute x18, starting transfers between devices: 28.1 us -> 22.9 us  [from_others(): lax.ppermute(array, axis, [(i, (i + hop) % size) for i in range(size)])]
    ppermute x18, waiting for transfers between devices: 22.8 us -> 25.7 us  [from_others(): lax.ppermute(array, axis, [(i, (i + hop) % size) for i in range(size)])]
    pallas_call x0 -> x1, Pallas kernels: none -> 2.57 us  [cut(): pl.pallas_call(cut_kernel, out_shape=jax.ShapeDtypeStruct(shape, pool.dty...]
  transfers between devices with their start and end apart: 31 -> 31, of which waited for: 20 -> 18; matrix products, arithmetic and copies ran while one was open for 1% -> 1% of each run, Pallas kernels for 17% -> 19%
where the time goes in v6:
time: 110 us
  Pallas kernels  40.1 us (36%)
  waiting for transfers between devices  37.6 us (34%)
  starting transfers between devices  29.6 us (27%)
  other arithmetic  1.16 us (1%)
    ppermute x18, waiting for transfers between devices, from_others(): lax.ppermute(array, axis, [(i, (i + hop) % size) for i in range(size)])  25.7 us
    ppermute x18, starting transfers between devices, from_others(): lax.ppermute(array, axis, [(i, (i + hop) % size) for i in range(size)])  22.9 us
    pallas_call x3, Pallas kernels, attend(): pl.pallas_call(functools.partial(attend_kernel, features, step, len(got))...  14.3 us
    ppermute x13, waiting for transfers between devices, swapped(): return lax.ppermute(array, axis, [(0, 1), (1, 0)])  11.9 us
    ppermute x13, starting transfers between devices, swapped(): return lax.ppermute(array, axis, [(0, 1), (1, 0)])  6.73 us
    pallas_call x1, Pallas kernels, load_caches(): pl.pallas_call(load_caches_kernel, out_shape=half_shapes(pools) + [pltpu....  6.07 us
    pallas_call x1, Pallas kernels, first_project(): pl.pallas_call(first_project_kernel, out_shape=[jax.ShapeDtypeStruct((row...  4.8 us
    pallas_call x1, Pallas kernels, load(): pl.pallas_call(load_kernel, out_shape=[pltpu.VMEM(w.shape, w.dtype) for w...  3.93 us
  transfers between devices with their start and end apart: 31, of which 18 were waited for; matrix products, arithmetic and copies ran while one was open for 1% of the time, Pallas kernels for 19%

profile of v6, /device:TPU:0, one launch (start us, length us, event | category | flops | bytes accessed | tf_op | source)
XLA Modules:
  0.0 109.5 jit_solution(12208053695861508303)
XLA Ops:
  1.2 4.8 %shard_map.131 = (f32[16,2688]{1,0:T(8,128)S(1)}, f32[16,2688]{1,0:T(8,128)S(1)}) custom-call(bf16[1024,4096]{1,0:T(8,128)(2,1)} %refs_0_.3, bf16[1024,512]{1,0:T(8,128)(2,1)} %refs_1_.3, bf16[1024,512]{1,0:T(8,128)(2,1)} %refs_2_.3, bf16[16,1024]{1,0:T(8,128)(2,1)} %x_ref.1, f32[1,1024]{1,0:T(1,128)} %bitcast.25), custom_call_target="tpu_custom_call" | custom-call | tf_op jit(solution)/shard_map/pallas_call | solution.py:411
  6.6 1.6 %collective-permute-done.got = f32[16,2688]{1,0:T(8,128)S(1)} collective-permute-done((f32[16,2688]{1,0:T(8,128)S(1)}, f32[16,2688]{1,0:T(8,128)S(1)}, u32[]{:S(2)}, u32[]{:S(2)}) %collective-permute-start) | collective-permute-done | bytes 172064 | tf_op jit(solution)/shard_map/ppermute | solution.py:799
  8.7 2.6 %shard_map.133 = bf16[1,2,4096,128]{3,2,1,0:T(8,128)(2,1)S(1)} custom-call(bf16[1,4,4096,128]{3,2,1,0:T(8,128)(2,1)} %pv.1, bf16[16,2304]{1,0:T(8,128)(2,1)S(1)} %get-tuple-element.74.after), custom_call_target="tpu_custom_call" | custom-call | bytes 8388608 | tf_op jit(solution)/shard_map/pallas_call | solution.py:275
  11.9 2.7 %collective-permute-start.3 = (bf16[16,2304]{1,0:T(8,128)(2,1)S(1)}, bf16[16,2304]{1,0:T(8,128)(2,1)S(1)}, u32[]{:S(2)}, u32[]{:S(2)}) collective-permute-start(bf16[16,2304]{1,0:T(8,128)(2,1)S(1)} %get-tuple-element.74.after), channel_id=1, source_target_pairs={{0,4},{4,8},{8,12},{12,0},{1,5},{5,9},{9,13},{13,1},{2,6},{6,10},{... | collective-permute-start | bytes 221192 | tf_op jit(solution)/shard_map/ppermute | solution.py:805
  14.7 2.6 %collective-permute-start.4 = (bf16[16,2304]{1,0:T(8,128)(2,1)S(1)}, bf16[16,2304]{1,0:T(8,128)(2,1)S(1)}, u32[]{:S(2)}, u32[]{:S(2)}) collective-permute-start(bf16[16,2304]{1,0:T(8,128)(2,1)S(1)} %get-tuple-element.69), channel_id=1, source_target_pairs={{0,8},{4,12},{8,0},{12,4},{1,9},{5,13},{9,1},{13,5},{2,10},{6,14},... | collective-permute-start | bytes 221192 | tf_op jit(solution)/shard_map/ppermute | solution.py:805
  18.6 6.1 %shard_map.134 = (bf16[2,2,4096,128]{3,2,1,0:T(8,128)(2,1)S(1)}, bf16[2,16,2,128,128]{4,3,2,1,0:T(8,128)(2,1)S(1)}, bf16[4096,1024]{1,0:T(8,128)(2,1)S(1)}, f32[2,16,2048]{2,1,0:T(8,128)S(1)}) custom-call(s32[16]{0:T(128)S(1)} %copy-done.2, s32[16,8]{1,0:T(8,128)S(1)} %copy.14.table, bf16[1,4,4096,128]{3,2,1,0:T(8,128)(2,1)} %pk.1, ...), custom_call_target="tpu_custom_call" | custom-call | bytes 33554432 | tf_op jit(solution)/shard_map/pallas_call | solution.py:319
  25.3 5.5 %shard_map.135 = (bf16[16,2176]{1,0:T(8,128)(2,1)S(1)}, f32[16,256]{1,0:T(8,128)S(1)}, bf16[32,128]{1,0:T(8,128)(2,1)S(1)}, bf16[2,2,4096,128]{3,2,1,0:T(8,128)(2,1)S(1)}, bf16[2,16,2,128,128]{4,3,2,1,0:T(8,128)(2,1)S(1)}) custom-call(f32[16,2688]{1,0:T(8,128)S(1)} %get-tuple-element.63.refs_0_, bf16[16,2304]{1,0:T(8,128)(2,1)S(1)} %collective-permute-done.3.refs_1_, ...), custom_call_target="tpu_custom_call" | custom-call | tf_op jit(solution)/shard_map/pallas_call | solution.py:715
  31.5 1.5 %collective-permute-start.9 = (bf16[16,2176]{1,0:T(8,128)(2,1)S(1)}, bf16[16,2176]{1,0:T(8,128)(2,1)S(1)}, u32[]{:S(2)}, u32[]{:S(2)}) collective-permute-start(bf16[16,2176]{1,0:T(8,128)(2,1)S(1)} %get-tuple-element.82.own), channel_id=1, source_target_pairs={{0,8},{4,12},{8,0},{12,4},{1,9},{5,13},{9,1},{13,5},{2,10},{6,14},... | collective-permute-start | bytes 208904 | tf_op jit(solution)/shard_map/ppermute | solution.py:805
  33.0 3.9 %shard_map.136 = (bf16[1024,4096]{1,0:T(8,128)(2,1)S(1)}, bf16[1024,512]{1,0:T(8,128)(2,1)S(1)}, bf16[1024,512]{1,0:T(8,128)(2,1)S(1)}) custom-call(bf16[1024,4096]{1,0:T(8,128)(2,1)} %refs_0_.3, bf16[1024,512]{1,0:T(8,128)(2,1)} %refs_1_.3, bf16[1024,512]{1,0:T(8,128)(2,1)} %refs_2_.3, f32[16,256]{1,0:T(8,128)S(1)} %get-tuple-element.83.refs_3_.stat), custom_call_target="tpu_custom_call" | custom-call | bytes 33554432 | tf_op jit(solution)/shard_map/pallas_call | solution.py:341
  37.0 2.6 %collective-permute-done.9.refs_1_ = bf16[16,2176]{1,0:T(8,128)(2,1)S(1)} collective-permute-done((bf16[16,2176]{1,0:T(8,128)(2,1)S(1)}, bf16[16,2176]{1,0:T(8,128)(2,1)S(1)}, u32[]{:S(2)}, u32[]{:S(2)}) %collective-permute-start.9) | collective-permute-done | bytes 69664 | tf_op jit(solution)/shard_map/ppermute | solution.py:805
  41.9 1.5 %collective-permute-start.12 = (bf16[16,1024]{1,0:T(8,128)(2,1)S(1)}, bf16[16,1024]{1,0:T(8,128)(2,1)S(1)}, u32[]{:S(2)}, u32[]{:S(2)}) collective-permute-start(bf16[16,1024]{1,0:T(8,128)(2,1)S(1)} %shard_map.139.mine), channel_id=1, source_target_pairs={{0,2},{2,0},{1,3},{3,1},{4,6},{6,4},{5,7},{7,5},{8,10},{10,8},{9,1... | collective-permute-start | bytes 98312 | tf_op jit(solution)/shard_map/ppermute | solution.py:799
  43.4 2.4 %collective-permute-done.12.other = bf16[16,1024]{1,0:T(8,128)(2,1)S(1)} collective-permute-done((bf16[16,1024]{1,0:T(8,128)(2,1)S(1)}, bf16[16,1024]{1,0:T(8,128)(2,1)S(1)}, u32[]{:S(2)}, u32[]{:S(2)}) %collective-permute-start.12) | collective-permute-done | bytes 32800 | tf_op jit(solution)/shard_map/ppermute | solution.py:799
  48.1 1.8 %collective-permute-start.15 = (bf16[16,2304]{1,0:T(8,128)(2,1)S(1)}, bf16[16,2304]{1,0:T(8,128)(2,1)S(1)}, u32[]{:S(2)}, u32[]{:S(2)}) collective-permute-start(bf16[16,2304]{1,0:T(8,128)(2,1)S(1)} %get-tuple-element.100), channel_id=1, source_target_pairs={{0,8},{4,12},{8,0},{12,4},{1,9},{5,13},{9,1},{13,5},{2,10},{6,14},... | collective-permute-start | bytes 221192 | tf_op jit(solution)/shard_map/ppermute | solution.py:805
  49.9 2.1 %collective-permute-start.16 = (bf16[16,2304]{1,0:T(8,128)(2,1)S(1)}, bf16[16,2304]{1,0:T(8,128)(2,1)S(1)}, u32[]{:S(2)}, u32[]{:S(2)}) collective-permute-start(bf16[16,2304]{1,0:T(8,128)(2,1)S(1)} %get-tuple-element.101), channel_id=1, source_target_pairs={{0,12},{4,0},{8,4},{12,8},{1,13},{5,1},{9,5},{13,9},{2,14},{6,2},{... | collective-permute-start | bytes 221192 | tf_op jit(solution)/shard_map/ppermute | solution.py:805
  52.1 3.1 %collective-permute-done.14.refs_1_ = bf16[16,2304]{1,0:T(8,128)(2,1)S(1)} collective-permute-done((bf16[16,2304]{1,0:T(8,128)(2,1)S(1)}, bf16[16,2304]{1,0:T(8,128)(2,1)S(1)}, u32[]{:S(2)}, u32[]{:S(2)}) %collective-permute-start.14) | collective-permute-done | bytes 73760 | tf_op jit(solution)/shard_map/ppermute | solution.py:805
  55.1 2.2 %collective-permute-done.15.refs_2_ = bf16[16,2304]{1,0:T(8,128)(2,1)S(1)} collective-permute-done((bf16[16,2304]{1,0:T(8,128)(2,1)S(1)}, bf16[16,2304]{1,0:T(8,128)(2,1)S(1)}, u32[]{:S(2)}, u32[]{:S(2)}) %collective-permute-start.15) | collective-permute-done | bytes 73760 | tf_op jit(solution)/shard_map/ppermute | solution.py:805
  57.3 4.4 %shard_map.143 = (bf16[16,2176]{1,0:T(8,128)(2,1)S(1)}, f32[16,256]{1,0:T(8,128)S(1)}, bf16[32,128]{1,0:T(8,128)(2,1)S(1)}) custom-call(f32[16,2688]{1,0:T(8,128)S(1)} %get-tuple-element.98.refs_0_, bf16[16,2304]{1,0:T(8,128)(2,1)S(1)} %collective-permute-done.14.refs_1_, bf16[16,2304]{1,0:T(8,128)(2,1)S(1)} %collective-permute-done.15.refs_2_, ...), custom_call_target="tpu_custom_call" | custom-call | tf_op jit(solution)/shard_map/pallas_call | solution.py:715
  61.7 2.0 %collective-permute-start.19 = (bf16[16,2176]{1,0:T(8,128)(2,1)S(1)}, bf16[16,2176]{1,0:T(8,128)(2,1)S(1)}, u32[]{:S(2)}, u32[]{:S(2)}) collective-permute-start(bf16[16,2176]{1,0:T(8,128)(2,1)S(1)} %get-tuple-element.105.own), channel_id=1, source_target_pairs={{0,12},{4,0},{8,4},{12,8},{1,13},{5,1},{9,5},{13,9},{2,14},{6,2},{... | collective-permute-start | bytes 208904 | tf_op jit(solution)/shard_map/ppermute | solution.py:805
  64.6 1.6 %collective-permute-done.19.refs_2_ = bf16[16,2176]{1,0:T(8,128)(2,1)S(1)} collective-permute-done((bf16[16,2176]{1,0:T(8,128)(2,1)S(1)}, bf16[16,2176]{1,0:T(8,128)(2,1)S(1)}, u32[]{:S(2)}, u32[]{:S(2)}) %collective-permute-start.19) | collective-permute-done | bytes 69664 | tf_op jit(solution)/shard_map/ppermute | solution.py:805
  66.3 4.8 %collective-permute-done.18.refs_1_ = bf16[16,2176]{1,0:T(8,128)(2,1)S(1)} collective-permute-done((bf16[16,2176]{1,0:T(8,128)(2,1)S(1)}, bf16[16,2176]{1,0:T(8,128)(2,1)S(1)}, u32[]{:S(2)}, u32[]{:S(2)}) %collective-permute-start.18) | collective-permute-done | bytes 69664 | tf_op jit(solution)/shard_map/ppermute | solution.py:805
  73.4 1.5 %collective-permute-start.21 = (bf16[16,1024]{1,0:T(8,128)(2,1)S(1)}, bf16[16,1024]{1,0:T(8,128)(2,1)S(1)}, u32[]{:S(2)}, u32[]{:S(2)}) collective-permute-start(bf16[16,1024]{1,0:T(8,128)(2,1)S(1)} %shard_map.146.mine), channel_id=1, source_target_pairs={{0,2},{2,0},{1,3},{3,1},{4,6},{6,4},{5,7},{7,5},{8,10},{10,8},{9,1... | collective-permute-start | bytes 98312 | tf_op jit(solution)/shard_map/ppermute | solution.py:799
  74.9 2.4 %collective-permute-done.21.other = bf16[16,1024]{1,0:T(8,128)(2,1)S(1)} collective-permute-done((bf16[16,1024]{1,0:T(8,128)(2,1)S(1)}, bf16[16,1024]{1,0:T(8,128)(2,1)S(1)}, u32[]{:S(2)}, u32[]{:S(2)}) %collective-permute-start.21) | collective-permute-done | bytes 32800 | tf_op jit(solution)/shard_map/ppermute | solution.py:799
  79.7 1.9 %collective-permute-start.24 = (bf16[16,2304]{1,0:T(8,128)(2,1)S(1)}, bf16[16,2304]{1,0:T(8,128)(2,1)S(1)}, u32[]{:S(2)}, u32[]{:S(2)}) collective-permute-start(bf16[16,2304]{1,0:T(8,128)(2,1)S(1)} %get-tuple-element.112), channel_id=1, source_target_pairs={{0,8},{4,12},{8,0},{12,4},{1,9},{5,13},{9,1},{13,5},{2,10},{6,14},... | collective-permute-start | bytes 221192 | tf_op jit(solution)/shard_map/ppermute | solution.py:805
  81.6 2.3 %collective-permute-start.25 = (bf16[16,2304]{1,0:T(8,128)(2,1)S(1)}, bf16[16,2304]{1,0:T(8,128)(2,1)S(1)}, u32[]{:S(2)}, u32[]{:S(2)}) collective-permute-start(bf16[16,2304]{1,0:T(8,128)(2,1)S(1)} %get-tuple-element.113), channel_id=1, source_target_pairs={{0,12},{4,0},{8,4},{12,8},{1,13},{5,1},{9,5},{13,9},{2,14},{6,2},{... | collective-permute-start | bytes 221192 | tf_op jit(solution)/shard_map/ppermute | solution.py:805
  83.9 2.8 %collective-permute-done.23.refs_1_ = bf16[16,2304]{1,0:T(8,128)(2,1)S(1)} collective-permute-done((bf16[16,2304]{1,0:T(8,128)(2,1)S(1)}, bf16[16,2304]{1,0:T(8,128)(2,1)S(1)}, u32[]{:S(2)}, u32[]{:S(2)}) %collective-permute-start.23) | collective-permute-done | bytes 73760 | tf_op jit(solution)/shard_map/ppermute | solution.py:805
  86.7 2.2 %collective-permute-done.24.refs_2_ = bf16[16,2304]{1,0:T(8,128)(2,1)S(1)} collective-permute-done((bf16[16,2304]{1,0:T(8,128)(2,1)S(1)}, bf16[16,2304]{1,0:T(8,128)(2,1)S(1)}, u32[]{:S(2)}, u32[]{:S(2)}) %collective-permute-start.24) | collective-permute-done | bytes 73760 | tf_op jit(solution)/shard_map/ppermute | solution.py:805
  88.8 4.4 %shard_map.150 = (bf16[16,2176]{1,0:T(8,128)(2,1)S(1)}, f32[16,256]{1,0:T(8,128)S(1)}) custom-call(f32[16,2688]{1,0:T(8,128)S(1)} %get-tuple-element.110.refs_0_, bf16[16,2304]{1,0:T(8,128)(2,1)S(1)} %collective-permute-done.23.refs_1_, bf16[16,2304]{1,0:T(8,128)(2,1)S(1)} %collective-permute-done.24.refs_2_, ...), custom_call_target="tpu_custom_call" | custom-call | tf_op jit(solution)/shard_map/pallas_call | solution.py:715
  93.2 2.1 %collective-permute-start.28 = (bf16[16,2176]{1,0:T(8,128)(2,1)S(1)}, bf16[16,2176]{1,0:T(8,128)(2,1)S(1)}, u32[]{:S(2)}, u32[]{:S(2)}) collective-permute-start(bf16[16,2176]{1,0:T(8,128)(2,1)S(1)} %get-tuple-element.115.own), channel_id=1, source_target_pairs={{0,12},{4,0},{8,4},{12,8},{1,13},{5,1},{9,5},{13,9},{2,14},{6,2},{... | collective-permute-start | bytes 208904 | tf_op jit(solution)/shard_map/ppermute | solution.py:805
  96.2 1.8 %collective-permute-done.28.refs_2_ = bf16[16,2176]{1,0:T(8,128)(2,1)S(1)} collective-permute-done((bf16[16,2176]{1,0:T(8,128)(2,1)S(1)}, bf16[16,2176]{1,0:T(8,128)(2,1)S(1)}, u32[]{:S(2)}, u32[]{:S(2)}) %collective-permute-start.28) | collective-permute-done | bytes 69664 | tf_op jit(solution)/shard_map/ppermute | solution.py:805
  98.0 4.7 %collective-permute-done.27.refs_1_ = bf16[16,2176]{1,0:T(8,128)(2,1)S(1)} collective-permute-done((bf16[16,2176]{1,0:T(8,128)(2,1)S(1)}, bf16[16,2176]{1,0:T(8,128)(2,1)S(1)}, u32[]{:S(2)}, u32[]{:S(2)}) %collective-permute-start.27) | collective-permute-done | bytes 69664 | tf_op jit(solution)/shard_map/ppermute | solution.py:805
  105.0 1.5 %collective-permute-start.30 = (bf16[16,1024]{1,0:T(8,128)(2,1)S(1)}, bf16[16,1024]{1,0:T(8,128)(2,1)S(1)}, u32[]{:S(2)}, u32[]{:S(2)}) collective-permute-start(bf16[16,1024]{1,0:T(8,128)(2,1)S(1)} %shard_map.153), channel_id=1, source_target_pairs={{0,2},{2,0},{1,3},{3,1},{4,6},{6,4},{5,7},{7,5},{8,10},{10,8},{9,1... | collective-permute-start | bytes 98312 | tf_op jit(solution)/shard_map/ppermute | solution.py:799
  106.5 2.4 %collective-permute-done.30 = bf16[16,1024]{1,0:T(8,128)(2,1)S(1)} collective-permute-done((bf16[16,1024]{1,0:T(8,128)(2,1)S(1)}, bf16[16,1024]{1,0:T(8,128)(2,1)S(1)}, u32[]{:S(2)}, u32[]{:S(2)}) %collective-permute-start.30) | collective-permute-done | bytes 32800 | tf_op jit(solution)/shard_map/ppermute | solution.py:799
  (82 shorter events, 18.9 us)
Async XLA Ops:
  0.6 7.6 %collective-permute-start.1 = (bf16[16,4,128,128]{3,2,1,0:T(8,128)(2,1)}, bf16[16,4,128,128]{3,2,1,0:T(8,128)(2,1)S(1)}, u32[]{:S(2)}, u32[]{:S(2)}) collective-permute-start(bf16[16,4,128,128]{3,2,1,0:T(8,128)(2,1)} %sk.1), channel_id=1, source_target_pairs={{0,1},{1,0},{2,3},{3,2},{4,5},{5,4},{6,7},{7,6},{8,9},{9,8},{10,11... | collective-permute-start | bytes 6291464 | tf_op jit(solution)/shard_map/ppermute | solution.py:799
  1.1 7.0 %collective-permute-start.2 = (bf16[16,4,128,128]{3,2,1,0:T(8,128)(2,1)}, bf16[16,4,128,128]{3,2,1,0:T(8,128)(2,1)S(1)}, u32[]{:S(2)}, u32[]{:S(2)}) collective-permute-start(bf16[16,4,128,128]{3,2,1,0:T(8,128)(2,1)} %sv.1), channel_id=1, source_target_pairs={{0,1},{1,0},{2,3},{3,2},{4,5},{5,4},{6,7},{7,6},{8,9},{9,8},{10,11... | collective-permute-start | bytes 6291464 | tf_op jit(solution)/shard_map/ppermute | solution.py:799
  6.0 12.6 %copy-start.2 = (s32[16]{0:T(128)S(1)}, s32[16]{0:T(128)}, u32[]{:S(2)}) copy-start(s32[16]{0:T(128)} %lengths) | copy-start | bytes 196
  6.1 2.1 %collective-permute-start = (f32[16,2688]{1,0:T(8,128)S(1)}, f32[16,2688]{1,0:T(8,128)S(1)}, u32[]{:S(2)}, u32[]{:S(2)}) collective-permute-start(f32[16,2688]{1,0:T(8,128)S(1)} %get-tuple-element.61), channel_id=1, source_target_pairs={{0,1},{1,0},{2,3},{3,2},{4,5},{5,4},{6,7},{7,6},{8,9},{9,8},{10,11... | collective-permute-start | bytes 516104 | tf_op jit(solution)/shard_map/ppermute | solution.py:799
  8.2 17.1 %collective-permute-start.6 = (bf16[1,4,4096,128]{3,2,1,0:T(8,128)(2,1)}, bf16[1,4,4096,128]{3,2,1,0:T(8,128)(2,1)}, u32[]{:S(2)}, u32[]{:S(2)}) collective-permute-start(bf16[1,4,4096,128]{3,2,1,0:T(8,128)(2,1)} %pk.1), channel_id=1, source_target_pairs={{0,1},{1,0},{2,3},{3,2},{4,5},{5,4},{6,7},{7,6},{8,9},{9,8},{10,11... | collective-permute-start | bytes 12582920 | tf_op jit(solution)/shard_map/ppermute | solution.py:799
  11.3 14.0 %collective-permute-start.7 = (bf16[1,2,4096,128]{3,2,1,0:T(8,128)(2,1)S(1)}, bf16[1,2,4096,128]{3,2,1,0:T(8,128)(2,1)}, u32[]{:S(2)}, u32[]{:S(2)}) collective-permute-start(bf16[1,2,4096,128]{3,2,1,0:T(8,128)(2,1)S(1)} %shard_map.133), channel_id=1, source_target_pairs={{0,1},{1,0},{2,3},{3,2},{4,5},{5,4},{6,7},{7,6},{8,9},{9,8},{10,11... | collective-permute-start | bytes 6291464 | tf_op jit(solution)/shard_map/ppermute | solution.py:799
  11.9 13.3 %collective-permute-start.3 = (bf16[16,2304]{1,0:T(8,128)(2,1)S(1)}, bf16[16,2304]{1,0:T(8,128)(2,1)S(1)}, u32[]{:S(2)}, u32[]{:S(2)}) collective-permute-start(bf16[16,2304]{1,0:T(8,128)(2,1)S(1)} %get-tuple-element.74.after), channel_id=1, source_target_pairs={{0,4},{4,8},{8,12},{12,0},{1,5},{5,9},{9,13},{13,1},{2,6},{6,10},{... | collective-permute-start | bytes 221192 | tf_op jit(solution)/shard_map/ppermute | solution.py:805
  14.7 10.5 %collective-permute-start.4 = (bf16[16,2304]{1,0:T(8,128)(2,1)S(1)}, bf16[16,2304]{1,0:T(8,128)(2,1)S(1)}, u32[]{:S(2)}, u32[]{:S(2)}) collective-permute-start(bf16[16,2304]{1,0:T(8,128)(2,1)S(1)} %get-tuple-element.69), channel_id=1, source_target_pairs={{0,8},{4,12},{8,0},{12,4},{1,9},{5,13},{9,1},{13,5},{2,10},{6,14},... | collective-permute-start | bytes 221192 | tf_op jit(solution)/shard_map/ppermute | solution.py:805
  17.3 8.0 %collective-permute-start.5 = (bf16[16,2304]{1,0:T(8,128)(2,1)S(1)}, bf16[16,2304]{1,0:T(8,128)(2,1)S(1)}, u32[]{:S(2)}, u32[]{:S(2)}) collective-permute-start(bf16[16,2304]{1,0:T(8,128)(2,1)S(1)} %get-tuple-element.70), channel_id=1, source_target_pairs={{0,12},{4,0},{8,4},{12,8},{1,13},{5,1},{9,5},{13,9},{2,14},{6,2},{... | collective-permute-start | bytes 221192 | tf_op jit(solution)/shard_map/ppermute | solution.py:805
  30.8 6.2 %collective-permute-start.10 = (bf16[16,2176]{1,0:T(8,128)(2,1)S(1)}, bf16[16,2176]{1,0:T(8,128)(2,1)S(1)}, u32[]{:S(2)}, u32[]{:S(2)}) collective-permute-start(bf16[16,2176]{1,0:T(8,128)(2,1)S(1)} %get-tuple-element.82.own), channel_id=1, source_target_pairs={{0,12},{4,0},{8,4},{12,8},{1,13},{5,1},{9,5},{13,9},{2,14},{6,2},{... | collective-permute-start | bytes 208904 | tf_op jit(solution)/shard_map/ppermute | solution.py:805
  31.5 8.1 %collective-permute-start.9 = (bf16[16,2176]{1,0:T(8,128)(2,1)S(1)}, bf16[16,2176]{1,0:T(8,128)(2,1)S(1)}, u32[]{:S(2)}, u32[]{:S(2)}) collective-permute-start(bf16[16,2176]{1,0:T(8,128)(2,1)S(1)} %get-tuple-element.82.own), channel_id=1, source_target_pairs={{0,8},{4,12},{8,0},{12,4},{1,9},{5,13},{9,1},{13,5},{2,10},{6,14},... | collective-permute-start | bytes 208904 | tf_op jit(solution)/shard_map/ppermute | solution.py:805
  33.0 6.5 %collective-permute-start.8 = (bf16[16,2176]{1,0:T(8,128)(2,1)S(1)}, bf16[16,2176]{1,0:T(8,128)(2,1)S(1)}, u32[]{:S(2)}, u32[]{:S(2)}) collective-permute-start(bf16[16,2176]{1,0:T(8,128)(2,1)S(1)} %get-tuple-element.82.own), channel_id=1, source_target_pairs={{0,4},{4,8},{8,12},{12,0},{1,5},{5,9},{9,13},{13,1},{2,6},{6,10},{... | collective-permute-start | bytes 208904 | tf_op jit(solution)/shard_map/ppermute | solution.py:805
  39.9 1.3 %collective-permute-start.11 = (bf16[16,2048]{1,0:T(8,128)(2,1)S(1)}, bf16[16,2048]{1,0:T(8,128)(2,1)S(1)}, u32[]{:S(2)}, u32[]{:S(2)}) collective-permute-start(bf16[16,2048]{1,0:T(8,128)(2,1)S(1)} %shard_map.137.mine), channel_id=1, source_target_pairs={{0,1},{1,0},{2,3},{3,2},{4,5},{5,4},{6,7},{7,6},{8,9},{9,8},{10,11... | collective-permute-start | bytes 196616 | tf_op jit(solution)/shard_map/ppermute | solution.py:799
  41.9 3.9 %collective-permute-start.12 = (bf16[16,1024]{1,0:T(8,128)(2,1)S(1)}, bf16[16,1024]{1,0:T(8,128)(2,1)S(1)}, u32[]{:S(2)}, u32[]{:S(2)}) collective-permute-start(bf16[16,1024]{1,0:T(8,128)(2,1)S(1)} %shard_map.139.mine), channel_id=1, source_target_pairs={{0,2},{2,0},{1,3},{3,1},{4,6},{6,4},{5,7},{7,5},{8,10},{10,8},{9,1... | collective-permute-start | bytes 98312 | tf_op jit(solution)/shard_map/ppermute | solution.py:799
  46.6 1.4 %collective-permute-start.13 = (f32[16,2688]{1,0:T(8,128)S(1)}, f32[16,2688]{1,0:T(8,128)S(1)}, u32[]{:S(2)}, u32[]{:S(2)}) collective-permute-start(f32[16,2688]{1,0:T(8,128)S(1)} %get-tuple-element.97.give), channel_id=1, source_target_pairs={{0,1},{1,0},{2,3},{3,2},{4,5},{5,4},{6,7},{7,6},{8,9},{9,8},{10,11... | collective-permute-start | bytes 516104 | tf_op jit(solution)/shard_map/ppermute | solution.py:799
  48.1 7.0 %collective-permute-start.14 = (bf16[16,2304]{1,0:T(8,128)(2,1)S(1)}, bf16[16,2304]{1,0:T(8,128)(2,1)S(1)}, u32[]{:S(2)}, u32[]{:S(2)}) collective-permute-start(bf16[16,2304]{1,0:T(8,128)(2,1)S(1)} %get-tuple-element.99), channel_id=1, source_target_pairs={{0,4},{4,8},{8,12},{12,0},{1,5},{5,9},{9,13},{13,1},{2,6},{6,10},{... | collective-permute-start | bytes 221192 | tf_op jit(solution)/shard_map/ppermute | solution.py:805
  48.1 9.2 %collective-permute-start.15 = (bf16[16,2304]{1,0:T(8,128)(2,1)S(1)}, bf16[16,2304]{1,0:T(8,128)(2,1)S(1)}, u32[]{:S(2)}, u32[]{:S(2)}) collective-permute-start(bf16[16,2304]{1,0:T(8,128)(2,1)S(1)} %get-tuple-element.100), channel_id=1, source_target_pairs={{0,8},{4,12},{8,0},{12,4},{1,9},{5,13},{9,1},{13,5},{2,10},{6,14},... | collective-permute-start | bytes 221192 | tf_op jit(solution)/shard_map/ppermute | solution.py:805
  49.9 7.4 %collective-permute-start.16 = (bf16[16,2304]{1,0:T(8,128)(2,1)S(1)}, bf16[16,2304]{1,0:T(8,128)(2,1)S(1)}, u32[]{:S(2)}, u32[]{:S(2)}) collective-permute-start(bf16[16,2304]{1,0:T(8,128)(2,1)S(1)} %get-tuple-element.101), channel_id=1, source_target_pairs={{0,12},{4,0},{8,4},{12,8},{1,13},{5,1},{9,5},{13,9},{2,14},{6,2},{... | collective-permute-start | bytes 221192 | tf_op jit(solution)/shard_map/ppermute | solution.py:805
  61.7 4.6 %collective-permute-start.19 = (bf16[16,2176]{1,0:T(8,128)(2,1)S(1)}, bf16[16,2176]{1,0:T(8,128)(2,1)S(1)}, u32[]{:S(2)}, u32[]{:S(2)}) collective-permute-start(bf16[16,2176]{1,0:T(8,128)(2,1)S(1)} %get-tuple-element.105.own), channel_id=1, source_target_pairs={{0,12},{4,0},{8,4},{12,8},{1,13},{5,1},{9,5},{13,9},{2,14},{6,2},{... | collective-permute-start | bytes 208904 | tf_op jit(solution)/shard_map/ppermute | solution.py:805
  63.7 7.4 %collective-permute-start.18 = (bf16[16,2176]{1,0:T(8,128)(2,1)S(1)}, bf16[16,2176]{1,0:T(8,128)(2,1)S(1)}, u32[]{:S(2)}, u32[]{:S(2)}) collective-permute-start(bf16[16,2176]{1,0:T(8,128)(2,1)S(1)} %get-tuple-element.105.own), channel_id=1, source_target_pairs={{0,8},{4,12},{8,0},{12,4},{1,9},{5,13},{9,1},{13,5},{2,10},{6,14},... | collective-permute-start | bytes 208904 | tf_op jit(solution)/shard_map/ppermute | solution.py:805
  64.6 6.5 %collective-permute-start.17 = (bf16[16,2176]{1,0:T(8,128)(2,1)S(1)}, bf16[16,2176]{1,0:T(8,128)(2,1)S(1)}, u32[]{:S(2)}, u32[]{:S(2)}) collective-permute-start(bf16[16,2176]{1,0:T(8,128)(2,1)S(1)} %get-tuple-element.105.own), channel_id=1, source_target_pairs={{0,4},{4,8},{8,12},{12,0},{1,5},{5,9},{9,13},{13,1},{2,6},{6,10},{... | collective-permute-start | bytes 208904 | tf_op jit(solution)/shard_map/ppermute | solution.py:805
  71.4 1.3 %collective-permute-start.20 = (bf16[16,2048]{1,0:T(8,128)(2,1)S(1)}, bf16[16,2048]{1,0:T(8,128)(2,1)S(1)}, u32[]{:S(2)}, u32[]{:S(2)}) collective-permute-start(bf16[16,2048]{1,0:T(8,128)(2,1)S(1)} %shard_map.144.mine), channel_id=1, source_target_pairs={{0,1},{1,0},{2,3},{3,2},{4,5},{5,4},{6,7},{7,6},{8,9},{9,8},{10,11... | collective-permute-start | bytes 196616 | tf_op jit(solution)/shard_map/ppermute | solution.py:799
  73.4 3.9 %collective-permute-start.21 = (bf16[16,1024]{1,0:T(8,128)(2,1)S(1)}, bf16[16,1024]{1,0:T(8,128)(2,1)S(1)}, u32[]{:S(2)}, u32[]{:S(2)}) collective-permute-start(bf16[16,1024]{1,0:T(8,128)(2,1)S(1)} %shard_map.146.mine), channel_id=1, source_target_pairs={{0,2},{2,0},{1,3},{3,1},{4,6},{6,4},{5,7},{7,5},{8,10},{10,8},{9,1... | collective-permute-start | bytes 98312 | tf_op jit(solution)/shard_map/ppermute | solution.py:799
  78.1 1.4 %collective-permute-start.22 = (f32[16,2688]{1,0:T(8,128)S(1)}, f32[16,2688]{1,0:T(8,128)S(1)}, u32[]{:S(2)}, u32[]{:S(2)}) collective-permute-start(f32[16,2688]{1,0:T(8,128)S(1)} %get-tuple-element.109.give), channel_id=1, source_target_pairs={{0,1},{1,0},{2,3},{3,2},{4,5},{5,4},{6,7},{7,6},{8,9},{9,8},{10,11... | collective-permute-start | bytes 516104 | tf_op jit(solution)/shard_map/ppermute | solution.py:799
  79.6 7.0 %collective-permute-start.23 = (bf16[16,2304]{1,0:T(8,128)(2,1)S(1)}, bf16[16,2304]{1,0:T(8,128)(2,1)S(1)}, u32[]{:S(2)}, u32[]{:S(2)}) collective-permute-start(bf16[16,2304]{1,0:T(8,128)(2,1)S(1)} %get-tuple-element.111), channel_id=1, source_target_pairs={{0,4},{4,8},{8,12},{12,0},{1,5},{5,9},{9,13},{13,1},{2,6},{6,10},{... | collective-permute-start | bytes 221192 | tf_op jit(solution)/shard_map/ppermute | solution.py:805
  79.7 9.2 %collective-permute-start.24 = (bf16[16,2304]{1,0:T(8,128)(2,1)S(1)}, bf16[16,2304]{1,0:T(8,128)(2,1)S(1)}, u32[]{:S(2)}, u32[]{:S(2)}) collective-permute-start(bf16[16,2304]{1,0:T(8,128)(2,1)S(1)} %get-tuple-element.112), channel_id=1, source_target_pairs={{0,8},{4,12},{8,0},{12,4},{1,9},{5,13},{9,1},{13,5},{2,10},{6,14},... | collective-permute-start | bytes 221192 | tf_op jit(solution)/shard_map/ppermute | solution.py:805
  81.6 7.2 %collective-permute-start.25 = (bf16[16,2304]{1,0:T(8,128)(2,1)S(1)}, bf16[16,2304]{1,0:T(8,128)(2,1)S(1)}, u32[]{:S(2)}, u32[]{:S(2)}) collective-permute-start(bf16[16,2304]{1,0:T(8,128)(2,1)S(1)} %get-tuple-element.113), channel_id=1, source_target_pairs={{0,12},{4,0},{8,4},{12,8},{1,13},{5,1},{9,5},{13,9},{2,14},{6,2},{... | collective-permute-start | bytes 221192 | tf_op jit(solution)/shard_map/ppermute | solution.py:805
  93.2 4.7 %collective-permute-start.28 = (bf16[16,2176]{1,0:T(8,128)(2,1)S(1)}, bf16[16,2176]{1,0:T(8,128)(2,1)S(1)}, u32[]{:S(2)}, u32[]{:S(2)}) collective-permute-start(bf16[16,2176]{1,0:T(8,128)(2,1)S(1)} %get-tuple-element.115.own), channel_id=1, source_target_pairs={{0,12},{4,0},{8,4},{12,8},{1,13},{5,1},{9,5},{13,9},{2,14},{6,2},{... | collective-permute-start | bytes 208904 | tf_op jit(solution)/shard_map/ppermute | solution.py:805
  95.4 7.3 %collective-permute-start.27 = (bf16[16,2176]{1,0:T(8,128)(2,1)S(1)}, bf16[16,2176]{1,0:T(8,128)(2,1)S(1)}, u32[]{:S(2)}, u32[]{:S(2)}) collective-permute-start(bf16[16,2176]{1,0:T(8,128)(2,1)S(1)} %get-tuple-element.115.own), channel_id=1, source_target_pairs={{0,8},{4,12},{8,0},{12,4},{1,9},{5,13},{9,1},{13,5},{2,10},{6,14},... | collective-permute-start | bytes 208904 | tf_op jit(solution)/shard_map/ppermute | solution.py:805
  96.2 6.5 %collective-permute-start.26 = (bf16[16,2176]{1,0:T(8,128)(2,1)S(1)}, bf16[16,2176]{1,0:T(8,128)(2,1)S(1)}, u32[]{:S(2)}, u32[]{:S(2)}) collective-permute-start(bf16[16,2176]{1,0:T(8,128)(2,1)S(1)} %get-tuple-element.115.own), channel_id=1, source_target_pairs={{0,4},{4,8},{8,12},{12,0},{1,5},{5,9},{9,13},{13,1},{2,6},{6,10},{... | collective-permute-start | bytes 208904 | tf_op jit(solution)/shard_map/ppermute | solution.py:805
  103.0 1.3 %collective-permute-start.29 = (bf16[16,2048]{1,0:T(8,128)(2,1)S(1)}, bf16[16,2048]{1,0:T(8,128)(2,1)S(1)}, u32[]{:S(2)}, u32[]{:S(2)}) collective-permute-start(bf16[16,2048]{1,0:T(8,128)(2,1)S(1)} %shard_map.151.mine), channel_id=1, source_target_pairs={{0,1},{1,0},{2,3},{3,2},{4,5},{5,4},{6,7},{7,6},{8,9},{9,8},{10,11... | collective-permute-start | bytes 196616 | tf_op jit(solution)/shard_map/ppermute | solution.py:799
  105.0 3.9 %collective-permute-start.30 = (bf16[16,1024]{1,0:T(8,128)(2,1)S(1)}, bf16[16,1024]{1,0:T(8,128)(2,1)S(1)}, u32[]{:S(2)}, u32[]{:S(2)}) collective-permute-start(bf16[16,1024]{1,0:T(8,128)(2,1)S(1)} %shard_map.153), channel_id=1, source_target_pairs={{0,2},{2,0},{1,3},{3,1},{4,6},{6,4},{5,7},{7,5},{8,10},{10,8},{9,1... | collective-permute-start | bytes 98312 | tf_op jit(solution)/shard_map/ppermute | solution.py:799
  (5 other events, 26.1 us)

commit v7 on v5

--- a/solution.py
+++ b/solution.py
@@ -336,7 +336,7 @@
         arrive()
         part = jnp.dot(scaled, weights[index][:, columns], preferred_element_type=F32)
         if index == 0:
-            out[:, to] = part
+            out[:, to] = part.astype(out.dtype)
             width = to.stop
         else:
             vectors += [part[:, at : at + HD] for at in range(0, part.shape[1], HD)]
@@ -345,7 +345,7 @@
         part = slice(chip * span, (chip + 1) * span)
         out[:, width + chip * HD : width + (chip + 1) * HD] = jnp.concatenate(
             [vector[part] for vector in vectors], axis=0
-        )
+        ).astype(out.dtype)
 
 
 def first_project_kernel(*refs):
@@ -399,8 +399,7 @@
     scaled = (wide * gain[...]).astype(BF16)
     scaled_ref[...] = scaled
     squares = jnp.sum(wide * wide, axis=1, keepdims=True)
-    column = lanes(wide.shape[0])
-    give[:, give.shape[1] - LANES :] = jnp.where(column == 0, squares, 0.0)
+    give[:, give.shape[1] - LANES :] = in_lanes(squares)
     project_half(scaled, weights, column_tiles(place, weights, 1 - place[0]), give)
 
 
@@ -410,7 +409,7 @@
     return pl.pallas_call(
         give_kernel,
         out_shape=[
-            jax.ShapeDtypeStruct((rows, width), F32),
+            jax.ShapeDtypeStruct((rows, width), BF16),
             jax.ShapeDtypeStruct(x.shape, BF16),
             jax.ShapeDtypeStruct(x.shape, BF16),
             jax.ShapeDtypeStruct(x.shape, F32),
@@ -427,7 +426,8 @@
     weights, keep = refs[:3], refs[3]
     scaled = scaled_ref[...]
     main = keep.shape[1] - LANES
-    keep[:, main:] = give[:, main:]
+    squares = jnp.sum(give[:, main:].astype(F32), axis=1, keepdims=True)
+    keep[:, main:] = jnp.broadcast_to(squares, (keep.shape[0], LANES))
     project_half(scaled, weights, column_tiles(place, weights, place[0]), keep)
 
 
@@ -442,18 +442,27 @@
     )(scaled, give, *[resident(weight) for weight in weights])
 
 
+def in_lanes(values):
+    column = lanes(values.shape[0])
+    block = jnp.zeros((values.shape[0], LANES), F32)
+    for n, piece in enumerate(pieces(values)):
+        block = jnp.where(column == n, piece, block)
+    return block.astype(BF16)
+
+
 def pair_sum_kernel(query_width, keep, got, total, *sent):
     place = whereabouts()
-    both = keep[...] + got[...]
+    both = keep[...] + got[...].astype(F32)
     total[...] = both
     rows = both.shape[0]
     main = both.shape[1] - LANES
+    squares = keep[:, main : main + 1] + jnp.sum(
+        got[:, main:].astype(F32), axis=1, keepdims=True
+    )
+    total[:, main:] = jnp.broadcast_to(squares, (rows, LANES))
     chips = (main - query_width) // HD
     column = lanes(rows)
-    high, middle, low = pieces(both[:, main : main + 1])
-    stats = jnp.where(
-        column == 0, high, jnp.where(column == 1, middle, jnp.where(column == 2, low, 0.0))
-    ).astype(BF16)
+    stats = in_lanes(squares)
     query = both[:, :query_width].astype(BF16)
     for hop, out in enumerate(sent, 1):
         chip = lax.rem(place[4] + hop, chips)

time: 109 us -> 109 us (level)
  no operation moved by 1% of the time
where the time goes in v7:
time: 109 us
  Pallas kernels  37.8 us (35%)
  waiting for transfers between devices  34.5 us (32%)
  starting transfers between devices  34.3 us (31%)
  other arithmetic  1.16 us (1%)
    ppermute x18, starting transfers between devices, from_others(): lax.ppermute(array, axis, [(i, (i + hop) % size) for i in range(size)])  28 us
    ppermute x18, waiting for transfers between devices, from_others(): lax.ppermute(array, axis, [(i, (i + hop) % size) for i in range(size)])  22.8 us
    pallas_call x3, Pallas kernels, attend(): pl.pallas_call(functools.partial(attend_kernel, features, step, len(got))...  14.3 us
    ppermute x13, waiting for transfers between devices, swapped(): return lax.ppermute(array, axis, [(0, 1), (1, 0)])  11.7 us
    ppermute x13, starting transfers between devices, swapped(): return lax.ppermute(array, axis, [(0, 1), (1, 0)])  6.34 us
    pallas_call x1, Pallas kernels, load_caches(): pl.pallas_call(load_caches_kernel, out_shape=half_shapes(pools) + [pltpu....  6.07 us
    pallas_call x1, Pallas kernels, first_project(): pl.pallas_call(first_project_kernel, out_shape=[jax.ShapeDtypeStruct((row...  4.83 us
    pallas_call x1, Pallas kernels, load(): pl.pallas_call(load_kernel, out_shape=[pltpu.VMEM(w.shape, w.dtype) for w...  3.93 us
  transfers between devices with their start and end apart: 31, of which 20 were waited for; matrix products, arithmetic and copies ran while one was open for 1% of the time, Pallas kernels for 17%

profile of v7, /device:TPU:0, one launch (start us, length us, event | category | flops | bytes accessed | tf_op | source)
XLA Modules:
  0.0 108.9 jit_solution(11598361381177374598)
XLA Ops:
  1.2 4.8 %shard_map.131 = (f32[16,2688]{1,0:T(8,128)S(1)}, f32[16,2688]{1,0:T(8,128)S(1)}) custom-call(bf16[1024,4096]{1,0:T(8,128)(2,1)} %refs_0_.3, bf16[1024,512]{1,0:T(8,128)(2,1)} %refs_1_.3, bf16[1024,512]{1,0:T(8,128)(2,1)} %refs_2_.3, bf16[16,1024]{1,0:T(8,128)(2,1)} %x_ref.1, f32[1,1024]{1,0:T(1,128)} %bitcast.25), custom_call_target="tpu_custom_call" | custom-call | tf_op jit(solution)/shard_map/pallas_call | solution.py:380
  6.6 1.6 %collective-permute-done.got = f32[16,2688]{1,0:T(8,128)S(1)} collective-permute-done((f32[16,2688]{1,0:T(8,128)S(1)}, f32[16,2688]{1,0:T(8,128)S(1)}, u32[]{:S(2)}, u32[]{:S(2)}) %collective-permute-start) | collective-permute-done | bytes 172064 | tf_op jit(solution)/shard_map/ppermute | solution.py:777
  9.2 2.9 %collective-permute-start.3 = (bf16[16,2304]{1,0:T(8,128)(2,1)S(1)}, bf16[16,2304]{1,0:T(8,128)(2,1)S(1)}, u32[]{:S(2)}, u32[]{:S(2)}) collective-permute-start(bf16[16,2304]{1,0:T(8,128)(2,1)S(1)} %get-tuple-element.64.after), channel_id=1, source_target_pairs={{0,4},{4,8},{8,12},{12,0},{1,5},{5,9},{9,13},{13,1},{2,6},{6,10},{... | collective-permute-start | bytes 221192 | tf_op jit(solution)/shard_map/ppermute | solution.py:783
  12.2 2.6 %collective-permute-start.4 = (bf16[16,2304]{1,0:T(8,128)(2,1)S(1)}, bf16[16,2304]{1,0:T(8,128)(2,1)S(1)}, u32[]{:S(2)}, u32[]{:S(2)}) collective-permute-start(bf16[16,2304]{1,0:T(8,128)(2,1)S(1)} %get-tuple-element.65), channel_id=1, source_target_pairs={{0,8},{4,12},{8,0},{12,4},{1,9},{5,13},{9,1},{13,5},{2,10},{6,14},... | collective-permute-start | bytes 221192 | tf_op jit(solution)/shard_map/ppermute | solution.py:783
  16.1 6.1 %shard_map.133 = (bf16[2,2,4096,128]{3,2,1,0:T(8,128)(2,1)S(1)}, bf16[2,16,2,128,128]{4,3,2,1,0:T(8,128)(2,1)S(1)}, bf16[4096,1024]{1,0:T(8,128)(2,1)S(1)}, f32[2,16,2048]{2,1,0:T(8,128)S(1)}) custom-call(s32[16]{0:T(128)S(1)} %copy-done.2, s32[16,8]{1,0:T(8,128)S(1)} %copy.14.table, bf16[1,4,4096,128]{3,2,1,0:T(8,128)(2,1)} %pk.1, ...), custom_call_target="tpu_custom_call" | custom-call | bytes 33554432 | tf_op jit(solution)/shard_map/pallas_call | solution.py:288
  22.8 5.5 %shard_map.134 = (bf16[16,2176]{1,0:T(8,128)(2,1)S(1)}, f32[16,256]{1,0:T(8,128)S(1)}, bf16[32,128]{1,0:T(8,128)(2,1)S(1)}, bf16[2,2,4096,128]{3,2,1,0:T(8,128)(2,1)S(1)}, bf16[2,16,2,128,128]{4,3,2,1,0:T(8,128)(2,1)S(1)}) custom-call(f32[16,2688]{1,0:T(8,128)S(1)} %get-tuple-element.60.refs_0_, bf16[16,2304]{1,0:T(8,128)(2,1)S(1)} %collective-permute-done.3.refs_1_, ...), custom_call_target="tpu_custom_call" | custom-call | tf_op jit(solution)/shard_map/pallas_call | solution.py:693
  28.3 4.0 %collective-permute-start.10 = (bf16[16,2176]{1,0:T(8,128)(2,1)S(1)}, bf16[16,2176]{1,0:T(8,128)(2,1)S(1)}, u32[]{:S(2)}, u32[]{:S(2)}) collective-permute-start(bf16[16,2176]{1,0:T(8,128)(2,1)S(1)} %get-tuple-element.76.own), channel_id=1, source_target_pairs={{0,12},{4,0},{8,4},{12,8},{1,13},{5,1},{9,5},{13,9},{2,14},{6,2},{... | collective-permute-start | bytes 208904 | tf_op jit(solution)/shard_map/ppermute | solution.py:783
  33.3 3.9 %shard_map.135 = (bf16[1024,4096]{1,0:T(8,128)(2,1)S(1)}, bf16[1024,512]{1,0:T(8,128)(2,1)S(1)}, bf16[1024,512]{1,0:T(8,128)(2,1)S(1)}) custom-call(bf16[1024,4096]{1,0:T(8,128)(2,1)} %refs_0_.3, bf16[1024,512]{1,0:T(8,128)(2,1)} %refs_1_.3, bf16[1024,512]{1,0:T(8,128)(2,1)} %refs_2_.3, f32[16,256]{1,0:T(8,128)S(1)} %get-tuple-element.77.refs_3_.stat), custom_call_target="tpu_custom_call" | custom-call | bytes 33554432 | tf_op jit(solution)/shard_map/pallas_call | solution.py:310
  37.3 1.6 %collective-permute-done.8.refs_0_ = bf16[16,2176]{1,0:T(8,128)(2,1)S(1)} collective-permute-done((bf16[16,2176]{1,0:T(8,128)(2,1)S(1)}, bf16[16,2176]{1,0:T(8,128)(2,1)S(1)}, u32[]{:S(2)}, u32[]{:S(2)}) %collective-permute-start.8) | collective-permute-done | bytes 69664 | tf_op jit(solution)/shard_map/ppermute | solution.py:783
  38.9 1.4 %collective-permute-done.9.refs_1_ = bf16[16,2176]{1,0:T(8,128)(2,1)S(1)} collective-permute-done((bf16[16,2176]{1,0:T(8,128)(2,1)S(1)}, bf16[16,2176]{1,0:T(8,128)(2,1)S(1)}, u32[]{:S(2)}, u32[]{:S(2)}) %collective-permute-start.9) | collective-permute-done | bytes 69664 | tf_op jit(solution)/shard_map/ppermute | solution.py:783
  42.6 1.5 %collective-permute-start.12 = (bf16[16,1024]{1,0:T(8,128)(2,1)S(1)}, bf16[16,1024]{1,0:T(8,128)(2,1)S(1)}, u32[]{:S(2)}, u32[]{:S(2)}) collective-permute-start(bf16[16,1024]{1,0:T(8,128)(2,1)S(1)} %shard_map.138.mine), channel_id=1, source_target_pairs={{0,2},{2,0},{1,3},{3,1},{4,6},{6,4},{5,7},{7,5},{8,10},{10,8},{9,1... | collective-permute-start | bytes 98312 | tf_op jit(solution)/shard_map/ppermute | solution.py:777
  44.1 2.4 %collective-permute-done.12.other = bf16[16,1024]{1,0:T(8,128)(2,1)S(1)} collective-permute-done((bf16[16,1024]{1,0:T(8,128)(2,1)S(1)}, bf16[16,1024]{1,0:T(8,128)(2,1)S(1)}, u32[]{:S(2)}, u32[]{:S(2)}) %collective-permute-start.12) | collective-permute-done | bytes 32800 | tf_op jit(solution)/shard_map/ppermute | solution.py:777
  49.2 2.0 %collective-permute-start.15 = (bf16[16,2304]{1,0:T(8,128)(2,1)S(1)}, bf16[16,2304]{1,0:T(8,128)(2,1)S(1)}, u32[]{:S(2)}, u32[]{:S(2)}) collective-permute-start(bf16[16,2304]{1,0:T(8,128)(2,1)S(1)} %get-tuple-element.94), channel_id=1, source_target_pairs={{0,8},{4,12},{8,0},{12,4},{1,9},{5,13},{9,1},{13,5},{2,10},{6,14},... | collective-permute-start | bytes 221192 | tf_op jit(solution)/shard_map/ppermute | solution.py:783
  51.2 1.5 %collective-permute-start.16 = (bf16[16,2304]{1,0:T(8,128)(2,1)S(1)}, bf16[16,2304]{1,0:T(8,128)(2,1)S(1)}, u32[]{:S(2)}, u32[]{:S(2)}) collective-permute-start(bf16[16,2304]{1,0:T(8,128)(2,1)S(1)} %get-tuple-element.95), channel_id=1, source_target_pairs={{0,12},{4,0},{8,4},{12,8},{1,13},{5,1},{9,5},{13,9},{2,14},{6,2},{... | collective-permute-start | bytes 221192 | tf_op jit(solution)/shard_map/ppermute | solution.py:783
  52.7 3.2 %collective-permute-done.14.refs_1_ = bf16[16,2304]{1,0:T(8,128)(2,1)S(1)} collective-permute-done((bf16[16,2304]{1,0:T(8,128)(2,1)S(1)}, bf16[16,2304]{1,0:T(8,128)(2,1)S(1)}, u32[]{:S(2)}, u32[]{:S(2)}) %collective-permute-start.14) | collective-permute-done | bytes 73760 | tf_op jit(solution)/shard_map/ppermute | solution.py:783
  55.9 2.2 %collective-permute-done.15.refs_2_ = bf16[16,2304]{1,0:T(8,128)(2,1)S(1)} collective-permute-done((bf16[16,2304]{1,0:T(8,128)(2,1)S(1)}, bf16[16,2304]{1,0:T(8,128)(2,1)S(1)}, u32[]{:S(2)}, u32[]{:S(2)}) %collective-permute-start.15) | collective-permute-done | bytes 73760 | tf_op jit(solution)/shard_map/ppermute | solution.py:783
  58.0 4.4 %shard_map.142 = (bf16[16,2176]{1,0:T(8,128)(2,1)S(1)}, f32[16,256]{1,0:T(8,128)S(1)}, bf16[32,128]{1,0:T(8,128)(2,1)S(1)}) custom-call(f32[16,2688]{1,0:T(8,128)S(1)} %get-tuple-element.92.refs_0_, bf16[16,2304]{1,0:T(8,128)(2,1)S(1)} %collective-permute-done.14.refs_1_, bf16[16,2304]{1,0:T(8,128)(2,1)S(1)} %collective-permute-done.15.refs_2_, ...), custom_call_target="tpu_custom_call" | custom-call | tf_op jit(solution)/shard_map/pallas_call | solution.py:693
  62.4 1.4 %collective-permute-start.17 = (bf16[16,2176]{1,0:T(8,128)(2,1)S(1)}, bf16[16,2176]{1,0:T(8,128)(2,1)S(1)}, u32[]{:S(2)}, u32[]{:S(2)}) collective-permute-start(bf16[16,2176]{1,0:T(8,128)(2,1)S(1)} %get-tuple-element.99.own), channel_id=1, source_target_pairs={{0,4},{4,8},{8,12},{12,0},{1,5},{5,9},{9,13},{13,1},{2,6},{6,10},{... | collective-permute-start | bytes 208904 | tf_op jit(solution)/shard_map/ppermute | solution.py:783
  66.3 3.0 %collective-permute-done.17.refs_0_ = bf16[16,2176]{1,0:T(8,128)(2,1)S(1)} collective-permute-done((bf16[16,2176]{1,0:T(8,128)(2,1)S(1)}, bf16[16,2176]{1,0:T(8,128)(2,1)S(1)}, u32[]{:S(2)}, u32[]{:S(2)}) %collective-permute-start.17) | collective-permute-done | bytes 69664 | tf_op jit(solution)/shard_map/ppermute | solution.py:783
  69.3 1.5 %collective-permute-done.18.refs_1_ = bf16[16,2176]{1,0:T(8,128)(2,1)S(1)} collective-permute-done((bf16[16,2176]{1,0:T(8,128)(2,1)S(1)}, bf16[16,2176]{1,0:T(8,128)(2,1)S(1)}, u32[]{:S(2)}, u32[]{:S(2)}) %collective-permute-start.18) | collective-permute-done | bytes 69664 | tf_op jit(solution)/shard_map/ppermute | solution.py:783
  73.1 1.5 %collective-permute-start.21 = (bf16[16,1024]{1,0:T(8,128)(2,1)S(1)}, bf16[16,1024]{1,0:T(8,128)(2,1)S(1)}, u32[]{:S(2)}, u32[]{:S(2)}) collective-permute-start(bf16[16,1024]{1,0:T(8,128)(2,1)S(1)} %shard_map.145.mine), channel_id=1, source_target_pairs={{0,2},{2,0},{1,3},{3,1},{4,6},{6,4},{5,7},{7,5},{8,10},{10,8},{9,1... | collective-permute-start | bytes 98312 | tf_op jit(solution)/shard_map/ppermute | solution.py:777
  74.6 2.4 %collective-permute-done.21.other = bf16[16,1024]{1,0:T(8,128)(2,1)S(1)} collective-permute-done((bf16[16,1024]{1,0:T(8,128)(2,1)S(1)}, bf16[16,1024]{1,0:T(8,128)(2,1)S(1)}, u32[]{:S(2)}, u32[]{:S(2)}) %collective-permute-start.21) | collective-permute-done | bytes 32800 | tf_op jit(solution)/shard_map/ppermute | solution.py:777
  80.6 2.1 %collective-permute-start.24 = (bf16[16,2304]{1,0:T(8,128)(2,1)S(1)}, bf16[16,2304]{1,0:T(8,128)(2,1)S(1)}, u32[]{:S(2)}, u32[]{:S(2)}) collective-permute-start(bf16[16,2304]{1,0:T(8,128)(2,1)S(1)} %get-tuple-element.106), channel_id=1, source_target_pairs={{0,8},{4,12},{8,0},{12,4},{1,9},{5,13},{9,1},{13,5},{2,10},{6,14},... | collective-permute-start | bytes 221192 | tf_op jit(solution)/shard_map/ppermute | solution.py:783
  83.2 3.2 %collective-permute-done.23.refs_1_ = bf16[16,2304]{1,0:T(8,128)(2,1)S(1)} collective-permute-done((bf16[16,2304]{1,0:T(8,128)(2,1)S(1)}, bf16[16,2304]{1,0:T(8,128)(2,1)S(1)}, u32[]{:S(2)}, u32[]{:S(2)}) %collective-permute-start.23) | collective-permute-done | bytes 73760 | tf_op jit(solution)/shard_map/ppermute | solution.py:783
  86.3 2.4 %collective-permute-done.24.refs_2_ = bf16[16,2304]{1,0:T(8,128)(2,1)S(1)} collective-permute-done((bf16[16,2304]{1,0:T(8,128)(2,1)S(1)}, bf16[16,2304]{1,0:T(8,128)(2,1)S(1)}, u32[]{:S(2)}, u32[]{:S(2)}) %collective-permute-start.24) | collective-permute-done | bytes 73760 | tf_op jit(solution)/shard_map/ppermute | solution.py:783
  88.7 4.4 %shard_map.149 = (bf16[16,2176]{1,0:T(8,128)(2,1)S(1)}, f32[16,256]{1,0:T(8,128)S(1)}) custom-call(f32[16,2688]{1,0:T(8,128)S(1)} %get-tuple-element.104.refs_0_, bf16[16,2304]{1,0:T(8,128)(2,1)S(1)} %collective-permute-done.23.refs_1_, bf16[16,2304]{1,0:T(8,128)(2,1)S(1)} %collective-permute-done.24.refs_2_, ...), custom_call_target="tpu_custom_call" | custom-call | tf_op jit(solution)/shard_map/pallas_call | solution.py:693
  93.1 2.0 %collective-permute-start.26 = (bf16[16,2176]{1,0:T(8,128)(2,1)S(1)}, bf16[16,2176]{1,0:T(8,128)(2,1)S(1)}, u32[]{:S(2)}, u32[]{:S(2)}) collective-permute-start(bf16[16,2176]{1,0:T(8,128)(2,1)S(1)} %get-tuple-element.109.own), channel_id=1, source_target_pairs={{0,4},{4,8},{8,12},{12,0},{1,5},{5,9},{9,13},{13,1},{2,6},{6,10},{... | collective-permute-start | bytes 208904 | tf_op jit(solution)/shard_map/ppermute | solution.py:783
  96.2 1.4 %collective-permute-start.28 = (bf16[16,2176]{1,0:T(8,128)(2,1)S(1)}, bf16[16,2176]{1,0:T(8,128)(2,1)S(1)}, u32[]{:S(2)}, u32[]{:S(2)}) collective-permute-start(bf16[16,2176]{1,0:T(8,128)(2,1)S(1)} %get-tuple-element.109.own), channel_id=1, source_target_pairs={{0,12},{4,0},{8,4},{12,8},{1,13},{5,1},{9,5},{13,9},{2,14},{6,2},{... | collective-permute-start | bytes 208904 | tf_op jit(solution)/shard_map/ppermute | solution.py:783
  97.6 2.2 %collective-permute-done.26.refs_0_ = bf16[16,2176]{1,0:T(8,128)(2,1)S(1)} collective-permute-done((bf16[16,2176]{1,0:T(8,128)(2,1)S(1)}, bf16[16,2176]{1,0:T(8,128)(2,1)S(1)}, u32[]{:S(2)}, u32[]{:S(2)}) %collective-permute-start.26) | collective-permute-done | bytes 69664 | tf_op jit(solution)/shard_map/ppermute | solution.py:783
  99.8 2.2 %collective-permute-done.27.refs_1_ = bf16[16,2176]{1,0:T(8,128)(2,1)S(1)} collective-permute-done((bf16[16,2176]{1,0:T(8,128)(2,1)S(1)}, bf16[16,2176]{1,0:T(8,128)(2,1)S(1)}, u32[]{:S(2)}, u32[]{:S(2)}) %collective-permute-start.27) | collective-permute-done | bytes 69664 | tf_op jit(solution)/shard_map/ppermute | solution.py:783
  104.3 1.5 %collective-permute-start.30 = (bf16[16,1024]{1,0:T(8,128)(2,1)S(1)}, bf16[16,1024]{1,0:T(8,128)(2,1)S(1)}, u32[]{:S(2)}, u32[]{:S(2)}) collective-permute-start(bf16[16,1024]{1,0:T(8,128)(2,1)S(1)} %shard_map.152), channel_id=1, source_target_pairs={{0,2},{2,0},{1,3},{3,1},{4,6},{6,4},{5,7},{7,5},{8,10},{10,8},{9,1... | collective-permute-start | bytes 98312 | tf_op jit(solution)/shard_map/ppermute | solution.py:777
  105.8 2.4 %collective-permute-done.30 = bf16[16,1024]{1,0:T(8,128)(2,1)S(1)} collective-permute-done((bf16[16,1024]{1,0:T(8,128)(2,1)S(1)}, bf16[16,1024]{1,0:T(8,128)(2,1)S(1)}, u32[]{:S(2)}, u32[]{:S(2)}) %collective-permute-start.30) | collective-permute-done | bytes 32800 | tf_op jit(solution)/shard_map/ppermute | solution.py:777
  (79 shorter events, 22.8 us)
Async XLA Ops:
  0.6 7.6 %collective-permute-start.1 = (bf16[16,4,128,128]{3,2,1,0:T(8,128)(2,1)}, bf16[16,4,128,128]{3,2,1,0:T(8,128)(2,1)S(1)}, u32[]{:S(2)}, u32[]{:S(2)}) collective-permute-start(bf16[16,4,128,128]{3,2,1,0:T(8,128)(2,1)} %sk.1), channel_id=1, source_target_pairs={{0,1},{1,0},{2,3},{3,2},{4,5},{5,4},{6,7},{7,6},{8,9},{9,8},{10,11... | collective-permute-start | bytes 6291464 | tf_op jit(solution)/shard_map/ppermute | solution.py:777
  1.1 7.1 %collective-permute-start.2 = (bf16[16,4,128,128]{3,2,1,0:T(8,128)(2,1)}, bf16[16,4,128,128]{3,2,1,0:T(8,128)(2,1)}, u32[]{:S(2)}, u32[]{:S(2)}) collective-permute-start(bf16[16,4,128,128]{3,2,1,0:T(8,128)(2,1)} %sv.1), channel_id=1, source_target_pairs={{0,1},{1,0},{2,3},{3,2},{4,5},{5,4},{6,7},{7,6},{8,9},{9,8},{10,11... | collective-permute-start | bytes 6291464 | tf_op jit(solution)/shard_map/ppermute | solution.py:777
  1.2 14.9 %copy-start.2 = (s32[16]{0:T(128)S(1)}, s32[16]{0:T(128)}, u32[]{:S(2)}) copy-start(s32[16]{0:T(128)} %lengths) | copy-start | bytes 196
  6.1 2.1 %collective-permute-start = (f32[16,2688]{1,0:T(8,128)S(1)}, f32[16,2688]{1,0:T(8,128)S(1)}, u32[]{:S(2)}, u32[]{:S(2)}) collective-permute-start(f32[16,2688]{1,0:T(8,128)S(1)} %get-tuple-element.58), channel_id=1, source_target_pairs={{0,1},{1,0},{2,3},{3,2},{4,5},{5,4},{6,7},{7,6},{8,9},{9,8},{10,11... | collective-permute-start | bytes 516104 | tf_op jit(solution)/shard_map/ppermute | solution.py:777
  8.3 14.5 %collective-permute-start.6 = (bf16[1,4,4096,128]{3,2,1,0:T(8,128)(2,1)}, bf16[1,4,4096,128]{3,2,1,0:T(8,128)(2,1)}, u32[]{:S(2)}, u32[]{:S(2)}) collective-permute-start(bf16[1,4,4096,128]{3,2,1,0:T(8,128)(2,1)} %pk.1), channel_id=1, source_target_pairs={{0,1},{1,0},{2,3},{3,2},{4,5},{5,4},{6,7},{7,6},{8,9},{9,8},{10,11... | collective-permute-start | bytes 12582920 | tf_op jit(solution)/shard_map/ppermute | solution.py:777
  8.7 14.1 %collective-permute-start.7 = (bf16[1,4,4096,128]{3,2,1,0:T(8,128)(2,1)}, bf16[1,4,4096,128]{3,2,1,0:T(8,128)(2,1)}, u32[]{:S(2)}, u32[]{:S(2)}) collective-permute-start(bf16[1,4,4096,128]{3,2,1,0:T(8,128)(2,1)} %pv.1), channel_id=1, source_target_pairs={{0,1},{1,0},{2,3},{3,2},{4,5},{5,4},{6,7},{7,6},{8,9},{9,8},{10,11... | collective-permute-start | bytes 12582920 | tf_op jit(solution)/shard_map/ppermute | solution.py:777
  9.2 13.5 %collective-permute-start.3 = (bf16[16,2304]{1,0:T(8,128)(2,1)S(1)}, bf16[16,2304]{1,0:T(8,128)(2,1)S(1)}, u32[]{:S(2)}, u32[]{:S(2)}) collective-permute-start(bf16[16,2304]{1,0:T(8,128)(2,1)S(1)} %get-tuple-element.64.after), channel_id=1, source_target_pairs={{0,4},{4,8},{8,12},{12,0},{1,5},{5,9},{9,13},{13,1},{2,6},{6,10},{... | collective-permute-start | bytes 221192 | tf_op jit(solution)/shard_map/ppermute | solution.py:783
  12.2 10.6 %collective-permute-start.4 = (bf16[16,2304]{1,0:T(8,128)(2,1)S(1)}, bf16[16,2304]{1,0:T(8,128)(2,1)S(1)}, u32[]{:S(2)}, u32[]{:S(2)}) collective-permute-start(bf16[16,2304]{1,0:T(8,128)(2,1)S(1)} %get-tuple-element.65), channel_id=1, source_target_pairs={{0,8},{4,12},{8,0},{12,4},{1,9},{5,13},{9,1},{13,5},{2,10},{6,14},... | collective-permute-start | bytes 221192 | tf_op jit(solution)/shard_map/ppermute | solution.py:783
  14.7 8.0 %collective-permute-start.5 = (bf16[16,2304]{1,0:T(8,128)(2,1)S(1)}, bf16[16,2304]{1,0:T(8,128)(2,1)S(1)}, u32[]{:S(2)}, u32[]{:S(2)}) collective-permute-start(bf16[16,2304]{1,0:T(8,128)(2,1)S(1)} %get-tuple-element.66), channel_id=1, source_target_pairs={{0,12},{4,0},{8,4},{12,8},{1,13},{5,1},{9,5},{13,9},{2,14},{6,2},{... | collective-permute-start | bytes 221192 | tf_op jit(solution)/shard_map/ppermute | solution.py:783
  28.3 9.0 %collective-permute-start.10 = (bf16[16,2176]{1,0:T(8,128)(2,1)S(1)}, bf16[16,2176]{1,0:T(8,128)(2,1)S(1)}, u32[]{:S(2)}, u32[]{:S(2)}) collective-permute-start(bf16[16,2176]{1,0:T(8,128)(2,1)S(1)} %get-tuple-element.76.own), channel_id=1, source_target_pairs={{0,12},{4,0},{8,4},{12,8},{1,13},{5,1},{9,5},{13,9},{2,14},{6,2},{... | collective-permute-start | bytes 208904 | tf_op jit(solution)/shard_map/ppermute | solution.py:783
  32.3 6.6 %collective-permute-start.8 = (bf16[16,2176]{1,0:T(8,128)(2,1)S(1)}, bf16[16,2176]{1,0:T(8,128)(2,1)S(1)}, u32[]{:S(2)}, u32[]{:S(2)}) collective-permute-start(bf16[16,2176]{1,0:T(8,128)(2,1)S(1)} %get-tuple-element.76.own), channel_id=1, source_target_pairs={{0,4},{4,8},{8,12},{12,0},{1,5},{5,9},{9,13},{13,1},{2,6},{6,10},{... | collective-permute-start | bytes 208904 | tf_op jit(solution)/shard_map/ppermute | solution.py:783
  32.3 8.0 %collective-permute-start.9 = (bf16[16,2176]{1,0:T(8,128)(2,1)S(1)}, bf16[16,2176]{1,0:T(8,128)(2,1)S(1)}, u32[]{:S(2)}, u32[]{:S(2)}) collective-permute-start(bf16[16,2176]{1,0:T(8,128)(2,1)S(1)} %get-tuple-element.76.own), channel_id=1, source_target_pairs={{0,8},{4,12},{8,0},{12,4},{1,9},{5,13},{9,1},{13,5},{2,10},{6,14},... | collective-permute-start | bytes 208904 | tf_op jit(solution)/shard_map/ppermute | solution.py:783
  40.6 1.3 %collective-permute-start.11 = (bf16[16,2048]{1,0:T(8,128)(2,1)S(1)}, bf16[16,2048]{1,0:T(8,128)(2,1)S(1)}, u32[]{:S(2)}, u32[]{:S(2)}) collective-permute-start(bf16[16,2048]{1,0:T(8,128)(2,1)S(1)} %shard_map.136.mine), channel_id=1, source_target_pairs={{0,1},{1,0},{2,3},{3,2},{4,5},{5,4},{6,7},{7,6},{8,9},{9,8},{10,11... | collective-permute-start | bytes 196616 | tf_op jit(solution)/shard_map/ppermute | solution.py:777
  42.6 3.9 %collective-permute-start.12 = (bf16[16,1024]{1,0:T(8,128)(2,1)S(1)}, bf16[16,1024]{1,0:T(8,128)(2,1)S(1)}, u32[]{:S(2)}, u32[]{:S(2)}) collective-permute-start(bf16[16,1024]{1,0:T(8,128)(2,1)S(1)} %shard_map.138.mine), channel_id=1, source_target_pairs={{0,2},{2,0},{1,3},{3,1},{4,6},{6,4},{5,7},{7,5},{8,10},{10,8},{9,1... | collective-permute-start | bytes 98312 | tf_op jit(solution)/shard_map/ppermute | solution.py:777
  47.4 1.3 %collective-permute-start.13 = (bf16[16,2688]{1,0:T(8,128)(2,1)S(1)}, bf16[16,2688]{1,0:T(8,128)(2,1)S(1)}, u32[]{:S(2)}, u32[]{:S(2)}) collective-permute-start(bf16[16,2688]{1,0:T(8,128)(2,1)S(1)} %get-tuple-element.91.give), channel_id=1, source_target_pairs={{0,1},{1,0},{2,3},{3,2},{4,5},{5,4},{6,7},{7,6},{8,9},{9,8},{10,11... | collective-permute-start | bytes 258056 | tf_op jit(solution)/shard_map/ppermute | solution.py:777
  48.8 7.0 %collective-permute-start.14 = (bf16[16,2304]{1,0:T(8,128)(2,1)S(1)}, bf16[16,2304]{1,0:T(8,128)(2,1)S(1)}, u32[]{:S(2)}, u32[]{:S(2)}) collective-permute-start(bf16[16,2304]{1,0:T(8,128)(2,1)S(1)} %get-tuple-element.93), channel_id=1, source_target_pairs={{0,4},{4,8},{8,12},{12,0},{1,5},{5,9},{9,13},{13,1},{2,6},{6,10},{... | collective-permute-start | bytes 221192 | tf_op jit(solution)/shard_map/ppermute | solution.py:783
  49.2 8.8 %collective-permute-start.15 = (bf16[16,2304]{1,0:T(8,128)(2,1)S(1)}, bf16[16,2304]{1,0:T(8,128)(2,1)S(1)}, u32[]{:S(2)}, u32[]{:S(2)}) collective-permute-start(bf16[16,2304]{1,0:T(8,128)(2,1)S(1)} %get-tuple-element.94), channel_id=1, source_target_pairs={{0,8},{4,12},{8,0},{12,4},{1,9},{5,13},{9,1},{13,5},{2,10},{6,14},... | collective-permute-start | bytes 221192 | tf_op jit(solution)/shard_map/ppermute | solution.py:783
  51.2 6.8 %collective-permute-start.16 = (bf16[16,2304]{1,0:T(8,128)(2,1)S(1)}, bf16[16,2304]{1,0:T(8,128)(2,1)S(1)}, u32[]{:S(2)}, u32[]{:S(2)}) collective-permute-start(bf16[16,2304]{1,0:T(8,128)(2,1)S(1)} %get-tuple-element.95), channel_id=1, source_target_pairs={{0,12},{4,0},{8,4},{12,8},{1,13},{5,1},{9,5},{13,9},{2,14},{6,2},{... | collective-permute-start | bytes 221192 | tf_op jit(solution)/shard_map/ppermute | solution.py:783
  62.4 6.9 %collective-permute-start.17 = (bf16[16,2176]{1,0:T(8,128)(2,1)S(1)}, bf16[16,2176]{1,0:T(8,128)(2,1)S(1)}, u32[]{:S(2)}, u32[]{:S(2)}) collective-permute-start(bf16[16,2176]{1,0:T(8,128)(2,1)S(1)} %get-tuple-element.99.own), channel_id=1, source_target_pairs={{0,4},{4,8},{8,12},{12,0},{1,5},{5,9},{9,13},{13,1},{2,6},{6,10},{... | collective-permute-start | bytes 208904 | tf_op jit(solution)/shard_map/ppermute | solution.py:783
  63.9 6.9 %collective-permute-start.18 = (bf16[16,2176]{1,0:T(8,128)(2,1)S(1)}, bf16[16,2176]{1,0:T(8,128)(2,1)S(1)}, u32[]{:S(2)}, u32[]{:S(2)}) collective-permute-start(bf16[16,2176]{1,0:T(8,128)(2,1)S(1)} %get-tuple-element.99.own), channel_id=1, source_target_pairs={{0,8},{4,12},{8,0},{12,4},{1,9},{5,13},{9,1},{13,5},{2,10},{6,14},... | collective-permute-start | bytes 208904 | tf_op jit(solution)/shard_map/ppermute | solution.py:783
  65.2 5.6 %collective-permute-start.19 = (bf16[16,2176]{1,0:T(8,128)(2,1)S(1)}, bf16[16,2176]{1,0:T(8,128)(2,1)S(1)}, u32[]{:S(2)}, u32[]{:S(2)}) collective-permute-start(bf16[16,2176]{1,0:T(8,128)(2,1)S(1)} %get-tuple-element.99.own), channel_id=1, source_target_pairs={{0,12},{4,0},{8,4},{12,8},{1,13},{5,1},{9,5},{13,9},{2,14},{6,2},{... | collective-permute-start | bytes 208904 | tf_op jit(solution)/shard_map/ppermute | solution.py:783
  71.1 1.3 %collective-permute-start.20 = (bf16[16,2048]{1,0:T(8,128)(2,1)S(1)}, bf16[16,2048]{1,0:T(8,128)(2,1)S(1)}, u32[]{:S(2)}, u32[]{:S(2)}) collective-permute-start(bf16[16,2048]{1,0:T(8,128)(2,1)S(1)} %shard_map.143.mine), channel_id=1, source_target_pairs={{0,1},{1,0},{2,3},{3,2},{4,5},{5,4},{6,7},{7,6},{8,9},{9,8},{10,11... | collective-permute-start | bytes 196616 | tf_op jit(solution)/shard_map/ppermute | solution.py:777
  73.1 3.9 %collective-permute-start.21 = (bf16[16,1024]{1,0:T(8,128)(2,1)S(1)}, bf16[16,1024]{1,0:T(8,128)(2,1)S(1)}, u32[]{:S(2)}, u32[]{:S(2)}) collective-permute-start(bf16[16,1024]{1,0:T(8,128)(2,1)S(1)} %shard_map.145.mine), channel_id=1, source_target_pairs={{0,2},{2,0},{1,3},{3,1},{4,6},{6,4},{5,7},{7,5},{8,10},{10,8},{9,1... | collective-permute-start | bytes 98312 | tf_op jit(solution)/shard_map/ppermute | solution.py:777
  77.8 1.3 %collective-permute-start.22 = (bf16[16,2688]{1,0:T(8,128)(2,1)S(1)}, bf16[16,2688]{1,0:T(8,128)(2,1)S(1)}, u32[]{:S(2)}, u32[]{:S(2)}) collective-permute-start(bf16[16,2688]{1,0:T(8,128)(2,1)S(1)} %get-tuple-element.103.give), channel_id=1, source_target_pairs={{0,1},{1,0},{2,3},{3,2},{4,5},{5,4},{6,7},{7,6},{8,9},{9,8},{10,11... | collective-permute-start | bytes 258056 | tf_op jit(solution)/shard_map/ppermute | solution.py:777
  79.3 7.0 %collective-permute-start.23 = (bf16[16,2304]{1,0:T(8,128)(2,1)S(1)}, bf16[16,2304]{1,0:T(8,128)(2,1)S(1)}, u32[]{:S(2)}, u32[]{:S(2)}) collective-permute-start(bf16[16,2304]{1,0:T(8,128)(2,1)S(1)} %get-tuple-element.105), channel_id=1, source_target_pairs={{0,4},{4,8},{8,12},{12,0},{1,5},{5,9},{9,13},{13,1},{2,6},{6,10},{... | collective-permute-start | bytes 221192 | tf_op jit(solution)/shard_map/ppermute | solution.py:783
  80.6 8.1 %collective-permute-start.24 = (bf16[16,2304]{1,0:T(8,128)(2,1)S(1)}, bf16[16,2304]{1,0:T(8,128)(2,1)S(1)}, u32[]{:S(2)}, u32[]{:S(2)}) collective-permute-start(bf16[16,2304]{1,0:T(8,128)(2,1)S(1)} %get-tuple-element.106), channel_id=1, source_target_pairs={{0,8},{4,12},{8,0},{12,4},{1,9},{5,13},{9,1},{13,5},{2,10},{6,14},... | collective-permute-start | bytes 221192 | tf_op jit(solution)/shard_map/ppermute | solution.py:783
  82.7 6.0 %collective-permute-start.25 = (bf16[16,2304]{1,0:T(8,128)(2,1)S(1)}, bf16[16,2304]{1,0:T(8,128)(2,1)S(1)}, u32[]{:S(2)}, u32[]{:S(2)}) collective-permute-start(bf16[16,2304]{1,0:T(8,128)(2,1)S(1)} %get-tuple-element.107), channel_id=1, source_target_pairs={{0,12},{4,0},{8,4},{12,8},{1,13},{5,1},{9,5},{13,9},{2,14},{6,2},{... | collective-permute-start | bytes 221192 | tf_op jit(solution)/shard_map/ppermute | solution.py:783
  93.1 6.7 %collective-permute-start.26 = (bf16[16,2176]{1,0:T(8,128)(2,1)S(1)}, bf16[16,2176]{1,0:T(8,128)(2,1)S(1)}, u32[]{:S(2)}, u32[]{:S(2)}) collective-permute-start(bf16[16,2176]{1,0:T(8,128)(2,1)S(1)} %get-tuple-element.109.own), channel_id=1, source_target_pairs={{0,4},{4,8},{8,12},{12,0},{1,5},{5,9},{9,13},{13,1},{2,6},{6,10},{... | collective-permute-start | bytes 208904 | tf_op jit(solution)/shard_map/ppermute | solution.py:783
  95.2 6.8 %collective-permute-start.27 = (bf16[16,2176]{1,0:T(8,128)(2,1)S(1)}, bf16[16,2176]{1,0:T(8,128)(2,1)S(1)}, u32[]{:S(2)}, u32[]{:S(2)}) collective-permute-start(bf16[16,2176]{1,0:T(8,128)(2,1)S(1)} %get-tuple-element.109.own), channel_id=1, source_target_pairs={{0,8},{4,12},{8,0},{12,4},{1,9},{5,13},{9,1},{13,5},{2,10},{6,14},... | collective-permute-start | bytes 208904 | tf_op jit(solution)/shard_map/ppermute | solution.py:783
  96.2 5.8 %collective-permute-start.28 = (bf16[16,2176]{1,0:T(8,128)(2,1)S(1)}, bf16[16,2176]{1,0:T(8,128)(2,1)S(1)}, u32[]{:S(2)}, u32[]{:S(2)}) collective-permute-start(bf16[16,2176]{1,0:T(8,128)(2,1)S(1)} %get-tuple-element.109.own), channel_id=1, source_target_pairs={{0,12},{4,0},{8,4},{12,8},{1,13},{5,1},{9,5},{13,9},{2,14},{6,2},{... | collective-permute-start | bytes 208904 | tf_op jit(solution)/shard_map/ppermute | solution.py:783
  102.3 1.3 %collective-permute-start.29 = (bf16[16,2048]{1,0:T(8,128)(2,1)S(1)}, bf16[16,2048]{1,0:T(8,128)(2,1)S(1)}, u32[]{:S(2)}, u32[]{:S(2)}) collective-permute-start(bf16[16,2048]{1,0:T(8,128)(2,1)S(1)} %shard_map.150.mine), channel_id=1, source_target_pairs={{0,1},{1,0},{2,3},{3,2},{4,5},{5,4},{6,7},{7,6},{8,9},{9,8},{10,11... | collective-permute-start | bytes 196616 | tf_op jit(solution)/shard_map/ppermute | solution.py:777
  104.3 3.9 %collective-permute-start.30 = (bf16[16,1024]{1,0:T(8,128)(2,1)S(1)}, bf16[16,1024]{1,0:T(8,128)(2,1)S(1)}, u32[]{:S(2)}, u32[]{:S(2)}) collective-permute-start(bf16[16,1024]{1,0:T(8,128)(2,1)S(1)} %shard_map.152), channel_id=1, source_target_pairs={{0,2},{2,0},{1,3},{3,1},{4,6},{6,4},{5,7},{7,5},{8,10},{10,8},{9,1... | collective-permute-start | bytes 98312 | tf_op jit(solution)/shard_map/ppermute | solution.py:777
  (4 other events, 32.3 us)

commit v8 on v7

--- a/solution.py
+++ b/solution.py
@@ -318,11 +318,11 @@
     )(*[in_hbm(weight) for weight in weights], after)
 
 
-def column_tiles(place, weights, who):
+def column_tiles(weights, who, most):
     tiles, at = [], 0
     for index, weight in enumerate(weights):
         half = weight.shape[1] // 2
-        tile = min(1024, half)
+        tile = min(most, half)
         for begin in range(0, half, tile):
             columns = pl.ds(pl.multiple_of(who * half + begin, tile), tile)
             tiles.append((index, columns, slice(at + begin, at + begin + tile)))
@@ -353,7 +353,7 @@
     sources, (keep, give, *buffers, sems) = refs[:5], refs[5:]
     weights, (x_ref, gain) = buffers[:3], buffers[3:]
     outs = ((give, 1 - place[0]), (keep, place[0]))
-    halves_of = [(out, column_tiles(place, weights, who)) for out, who in outs]
+    halves_of = [(out, column_tiles(weights, who, 1024)) for out, who in outs]
     pairs = list(zip(sources[3:], buffers[3:]))
     for _, tiles in halves_of:
         for index, columns, _ in tiles:
@@ -400,7 +400,7 @@
     scaled_ref[...] = scaled
     squares = jnp.sum(wide * wide, axis=1, keepdims=True)
     give[:, give.shape[1] - LANES :] = in_lanes(squares)
-    project_half(scaled, weights, column_tiles(place, weights, 1 - place[0]), give)
+    project_half(scaled, weights, column_tiles(weights, 1 - place[0], 2048), give)
 
 
 def give_project(x, gain, weights, rest):
@@ -428,7 +428,7 @@
     main = keep.shape[1] - LANES
     squares = jnp.sum(give[:, main:].astype(F32), axis=1, keepdims=True)
     keep[:, main:] = jnp.broadcast_to(squares, (keep.shape[0], LANES))
-    project_half(scaled, weights, column_tiles(place, weights, place[0]), keep)
+    project_half(scaled, weights, column_tiles(weights, place[0], 2048), keep)
 
 
 def keep_project(scaled, give, weights):

time: 109 us -> 109 us (level)
  no operation moved by 1% of the time
where the time goes in v8:
time: 109 us
  Pallas kernels  37.8 us (35%)
  waiting for transfers between devices  34.5 us (32%)
  starting transfers between devices  34.3 us (31%)
  other arithmetic  1.16 us (1%)
    ppermute x18, starting transfers between devices, from_others(): lax.ppermute(array, axis, [(i, (i + hop) % size) for i in range(size)])  28 us
    ppermute x18, waiting for transfers between devices, from_others(): lax.ppermute(array, axis, [(i, (i + hop) % size) for i in range(size)])  22.8 us
    pallas_call x3, Pallas kernels, attend(): pl.pallas_call(functools.partial(attend_kernel, features, step, len(got))...  14.3 us
    ppermute x13, waiting for transfers between devices, swapped(): return lax.ppermute(array, axis, [(0, 1), (1, 0)])  11.7 us
    ppermute x13, starting transfers between devices, swapped(): return lax.ppermute(array, axis, [(0, 1), (1, 0)])  6.34 us
    pallas_call x1, Pallas kernels, load_caches(): pl.pallas_call(load_caches_kernel, out_shape=half_shapes(pools) + [pltpu....  6.07 us
    pallas_call x1, Pallas kernels, first_project(): pl.pallas_call(first_project_kernel, out_shape=[jax.ShapeDtypeStruct((row...  4.83 us
    pallas_call x1, Pallas kernels, load(): pl.pallas_call(load_kernel, out_shape=[pltpu.VMEM(w.shape, w.dtype) for w...  3.93 us
  transfers between devices with their start and end apart: 31, of which 20 were waited for; matrix products, arithmetic and copies ran while one was open for 1% of the time, Pallas kernels for 17%

profile of v8, /device:TPU:0, one launch (start us, length us, event | category | flops | bytes accessed | tf_op | source)
XLA Modules:
  0.0 108.9 jit_solution(3872678877088693163)
XLA Ops:
  1.2 4.8 %shard_map.131 = (f32[16,2688]{1,0:T(8,128)S(1)}, f32[16,2688]{1,0:T(8,128)S(1)}) custom-call(bf16[1024,4096]{1,0:T(8,128)(2,1)} %refs_0_.3, bf16[1024,512]{1,0:T(8,128)(2,1)} %refs_1_.3, bf16[1024,512]{1,0:T(8,128)(2,1)} %refs_2_.3, bf16[16,1024]{1,0:T(8,128)(2,1)} %x_ref.1, f32[1,1024]{1,0:T(1,128)} %bitcast.25), custom_call_target="tpu_custom_call" | custom-call | tf_op jit(solution)/shard_map/pallas_call | solution.py:380
  6.6 1.6 %collective-permute-done.got = f32[16,2688]{1,0:T(8,128)S(1)} collective-permute-done((f32[16,2688]{1,0:T(8,128)S(1)}, f32[16,2688]{1,0:T(8,128)S(1)}, u32[]{:S(2)}, u32[]{:S(2)}) %collective-permute-start) | collective-permute-done | bytes 172064 | tf_op jit(solution)/shard_map/ppermute | solution.py:777
  9.2 2.9 %collective-permute-start.3 = (bf16[16,2304]{1,0:T(8,128)(2,1)S(1)}, bf16[16,2304]{1,0:T(8,128)(2,1)S(1)}, u32[]{:S(2)}, u32[]{:S(2)}) collective-permute-start(bf16[16,2304]{1,0:T(8,128)(2,1)S(1)} %get-tuple-element.64.after), channel_id=1, source_target_pairs={{0,4},{4,8},{8,12},{12,0},{1,5},{5,9},{9,13},{13,1},{2,6},{6,10},{... | collective-permute-start | bytes 221192 | tf_op jit(solution)/shard_map/ppermute | solution.py:783
  12.2 2.6 %collective-permute-start.4 = (bf16[16,2304]{1,0:T(8,128)(2,1)S(1)}, bf16[16,2304]{1,0:T(8,128)(2,1)S(1)}, u32[]{:S(2)}, u32[]{:S(2)}) collective-permute-start(bf16[16,2304]{1,0:T(8,128)(2,1)S(1)} %get-tuple-element.65), channel_id=1, source_target_pairs={{0,8},{4,12},{8,0},{12,4},{1,9},{5,13},{9,1},{13,5},{2,10},{6,14},... | collective-permute-start | bytes 221192 | tf_op jit(solution)/shard_map/ppermute | solution.py:783
  16.1 6.1 %shard_map.133 = (bf16[2,2,4096,128]{3,2,1,0:T(8,128)(2,1)S(1)}, bf16[2,16,2,128,128]{4,3,2,1,0:T(8,128)(2,1)S(1)}, bf16[4096,1024]{1,0:T(8,128)(2,1)S(1)}, f32[2,16,2048]{2,1,0:T(8,128)S(1)}) custom-call(s32[16]{0:T(128)S(1)} %copy-done.2, s32[16,8]{1,0:T(8,128)S(1)} %copy.14.table, bf16[1,4,4096,128]{3,2,1,0:T(8,128)(2,1)} %pk.1, ...), custom_call_target="tpu_custom_call" | custom-call | bytes 33554432 | tf_op jit(solution)/shard_map/pallas_call | solution.py:288
  22.8 5.5 %shard_map.134 = (bf16[16,2176]{1,0:T(8,128)(2,1)S(1)}, f32[16,256]{1,0:T(8,128)S(1)}, bf16[32,128]{1,0:T(8,128)(2,1)S(1)}, bf16[2,2,4096,128]{3,2,1,0:T(8,128)(2,1)S(1)}, bf16[2,16,2,128,128]{4,3,2,1,0:T(8,128)(2,1)S(1)}) custom-call(f32[16,2688]{1,0:T(8,128)S(1)} %get-tuple-element.60.refs_0_, bf16[16,2304]{1,0:T(8,128)(2,1)S(1)} %collective-permute-done.3.refs_1_, ...), custom_call_target="tpu_custom_call" | custom-call | tf_op jit(solution)/shard_map/pallas_call | solution.py:693
  28.3 4.0 %collective-permute-start.10 = (bf16[16,2176]{1,0:T(8,128)(2,1)S(1)}, bf16[16,2176]{1,0:T(8,128)(2,1)S(1)}, u32[]{:S(2)}, u32[]{:S(2)}) collective-permute-start(bf16[16,2176]{1,0:T(8,128)(2,1)S(1)} %get-tuple-element.76.own), channel_id=1, source_target_pairs={{0,12},{4,0},{8,4},{12,8},{1,13},{5,1},{9,5},{13,9},{2,14},{6,2},{... | collective-permute-start | bytes 208904 | tf_op jit(solution)/shard_map/ppermute | solution.py:783
  33.3 3.9 %shard_map.135 = (bf16[1024,4096]{1,0:T(8,128)(2,1)S(1)}, bf16[1024,512]{1,0:T(8,128)(2,1)S(1)}, bf16[1024,512]{1,0:T(8,128)(2,1)S(1)}) custom-call(bf16[1024,4096]{1,0:T(8,128)(2,1)} %refs_0_.3, bf16[1024,512]{1,0:T(8,128)(2,1)} %refs_1_.3, bf16[1024,512]{1,0:T(8,128)(2,1)} %refs_2_.3, f32[16,256]{1,0:T(8,128)S(1)} %get-tuple-element.77.refs_3_.stat), custom_call_target="tpu_custom_call" | custom-call | bytes 33554432 | tf_op jit(solution)/shard_map/pallas_call | solution.py:310
  37.3 1.6 %collective-permute-done.8.refs_0_ = bf16[16,2176]{1,0:T(8,128)(2,1)S(1)} collective-permute-done((bf16[16,2176]{1,0:T(8,128)(2,1)S(1)}, bf16[16,2176]{1,0:T(8,128)(2,1)S(1)}, u32[]{:S(2)}, u32[]{:S(2)}) %collective-permute-start.8) | collective-permute-done | bytes 69664 | tf_op jit(solution)/shard_map/ppermute | solution.py:783
  38.9 1.4 %collective-permute-done.9.refs_1_ = bf16[16,2176]{1,0:T(8,128)(2,1)S(1)} collective-permute-done((bf16[16,2176]{1,0:T(8,128)(2,1)S(1)}, bf16[16,2176]{1,0:T(8,128)(2,1)S(1)}, u32[]{:S(2)}, u32[]{:S(2)}) %collective-permute-start.9) | collective-permute-done | bytes 69664 | tf_op jit(solution)/shard_map/ppermute | solution.py:783
  42.6 1.5 %collective-permute-start.12 = (bf16[16,1024]{1,0:T(8,128)(2,1)S(1)}, bf16[16,1024]{1,0:T(8,128)(2,1)S(1)}, u32[]{:S(2)}, u32[]{:S(2)}) collective-permute-start(bf16[16,1024]{1,0:T(8,128)(2,1)S(1)} %shard_map.138.mine), channel_id=1, source_target_pairs={{0,2},{2,0},{1,3},{3,1},{4,6},{6,4},{5,7},{7,5},{8,10},{10,8},{9,1... | collective-permute-start | bytes 98312 | tf_op jit(solution)/shard_map/ppermute | solution.py:777
  44.1 2.4 %collective-permute-done.12.other = bf16[16,1024]{1,0:T(8,128)(2,1)S(1)} collective-permute-done((bf16[16,1024]{1,0:T(8,128)(2,1)S(1)}, bf16[16,1024]{1,0:T(8,128)(2,1)S(1)}, u32[]{:S(2)}, u32[]{:S(2)}) %collective-permute-start.12) | collective-permute-done | bytes 32800 | tf_op jit(solution)/shard_map/ppermute | solution.py:777
  49.2 2.0 %collective-permute-start.15 = (bf16[16,2304]{1,0:T(8,128)(2,1)S(1)}, bf16[16,2304]{1,0:T(8,128)(2,1)S(1)}, u32[]{:S(2)}, u32[]{:S(2)}) collective-permute-start(bf16[16,2304]{1,0:T(8,128)(2,1)S(1)} %get-tuple-element.94), channel_id=1, source_target_pairs={{0,8},{4,12},{8,0},{12,4},{1,9},{5,13},{9,1},{13,5},{2,10},{6,14},... | collective-permute-start | bytes 221192 | tf_op jit(solution)/shard_map/ppermute | solution.py:783
  51.2 1.5 %collective-permute-start.16 = (bf16[16,2304]{1,0:T(8,128)(2,1)S(1)}, bf16[16,2304]{1,0:T(8,128)(2,1)S(1)}, u32[]{:S(2)}, u32[]{:S(2)}) collective-permute-start(bf16[16,2304]{1,0:T(8,128)(2,1)S(1)} %get-tuple-element.95), channel_id=1, source_target_pairs={{0,12},{4,0},{8,4},{12,8},{1,13},{5,1},{9,5},{13,9},{2,14},{6,2},{... | collective-permute-start | bytes 221192 | tf_op jit(solution)/shard_map/ppermute | solution.py:783
  52.7 3.2 %collective-permute-done.14.refs_1_ = bf16[16,2304]{1,0:T(8,128)(2,1)S(1)} collective-permute-done((bf16[16,2304]{1,0:T(8,128)(2,1)S(1)}, bf16[16,2304]{1,0:T(8,128)(2,1)S(1)}, u32[]{:S(2)}, u32[]{:S(2)}) %collective-permute-start.14) | collective-permute-done | bytes 73760 | tf_op jit(solution)/shard_map/ppermute | solution.py:783
  55.9 2.2 %collective-permute-done.15.refs_2_ = bf16[16,2304]{1,0:T(8,128)(2,1)S(1)} collective-permute-done((bf16[16,2304]{1,0:T(8,128)(2,1)S(1)}, bf16[16,2304]{1,0:T(8,128)(2,1)S(1)}, u32[]{:S(2)}, u32[]{:S(2)}) %collective-permute-start.15) | collective-permute-done | bytes 73760 | tf_op jit(solution)/shard_map/ppermute | solution.py:783
  58.0 4.4 %shard_map.142 = (bf16[16,2176]{1,0:T(8,128)(2,1)S(1)}, f32[16,256]{1,0:T(8,128)S(1)}, bf16[32,128]{1,0:T(8,128)(2,1)S(1)}) custom-call(f32[16,2688]{1,0:T(8,128)S(1)} %get-tuple-element.92.refs_0_, bf16[16,2304]{1,0:T(8,128)(2,1)S(1)} %collective-permute-done.14.refs_1_, bf16[16,2304]{1,0:T(8,128)(2,1)S(1)} %collective-permute-done.15.refs_2_, ...), custom_call_target="tpu_custom_call" | custom-call | tf_op jit(solution)/shard_map/pallas_call | solution.py:693
  62.4 1.4 %collective-permute-start.17 = (bf16[16,2176]{1,0:T(8,128)(2,1)S(1)}, bf16[16,2176]{1,0:T(8,128)(2,1)S(1)}, u32[]{:S(2)}, u32[]{:S(2)}) collective-permute-start(bf16[16,2176]{1,0:T(8,128)(2,1)S(1)} %get-tuple-element.99.own), channel_id=1, source_target_pairs={{0,4},{4,8},{8,12},{12,0},{1,5},{5,9},{9,13},{13,1},{2,6},{6,10},{... | collective-permute-start | bytes 208904 | tf_op jit(solution)/shard_map/ppermute | solution.py:783
  66.3 3.0 %collective-permute-done.17.refs_0_ = bf16[16,2176]{1,0:T(8,128)(2,1)S(1)} collective-permute-done((bf16[16,2176]{1,0:T(8,128)(2,1)S(1)}, bf16[16,2176]{1,0:T(8,128)(2,1)S(1)}, u32[]{:S(2)}, u32[]{:S(2)}) %collective-permute-start.17) | collective-permute-done | bytes 69664 | tf_op jit(solution)/shard_map/ppermute | solution.py:783
  69.3 1.5 %collective-permute-done.18.refs_1_ = bf16[16,2176]{1,0:T(8,128)(2,1)S(1)} collective-permute-done((bf16[16,2176]{1,0:T(8,128)(2,1)S(1)}, bf16[16,2176]{1,0:T(8,128)(2,1)S(1)}, u32[]{:S(2)}, u32[]{:S(2)}) %collective-permute-start.18) | collective-permute-done | bytes 69664 | tf_op jit(solution)/shard_map/ppermute | solution.py:783
  73.1 1.5 %collective-permute-start.21 = (bf16[16,1024]{1,0:T(8,128)(2,1)S(1)}, bf16[16,1024]{1,0:T(8,128)(2,1)S(1)}, u32[]{:S(2)}, u32[]{:S(2)}) collective-permute-start(bf16[16,1024]{1,0:T(8,128)(2,1)S(1)} %shard_map.145.mine), channel_id=1, source_target_pairs={{0,2},{2,0},{1,3},{3,1},{4,6},{6,4},{5,7},{7,5},{8,10},{10,8},{9,1... | collective-permute-start | bytes 98312 | tf_op jit(solution)/shard_map/ppermute | solution.py:777
  74.6 2.4 %collective-permute-done.21.other = bf16[16,1024]{1,0:T(8,128)(2,1)S(1)} collective-permute-done((bf16[16,1024]{1,0:T(8,128)(2,1)S(1)}, bf16[16,1024]{1,0:T(8,128)(2,1)S(1)}, u32[]{:S(2)}, u32[]{:S(2)}) %collective-permute-start.21) | collective-permute-done | bytes 32800 | tf_op jit(solution)/shard_map/ppermute | solution.py:777
  80.6 2.1 %collective-permute-start.24 = (bf16[16,2304]{1,0:T(8,128)(2,1)S(1)}, bf16[16,2304]{1,0:T(8,128)(2,1)S(1)}, u32[]{:S(2)}, u32[]{:S(2)}) collective-permute-start(bf16[16,2304]{1,0:T(8,128)(2,1)S(1)} %get-tuple-element.106), channel_id=1, source_target_pairs={{0,8},{4,12},{8,0},{12,4},{1,9},{5,13},{9,1},{13,5},{2,10},{6,14},... | collective-permute-start | bytes 221192 | tf_op jit(solution)/shard_map/ppermute | solution.py:783
  83.2 3.2 %collective-permute-done.23.refs_1_ = bf16[16,2304]{1,0:T(8,128)(2,1)S(1)} collective-permute-done((bf16[16,2304]{1,0:T(8,128)(2,1)S(1)}, bf16[16,2304]{1,0:T(8,128)(2,1)S(1)}, u32[]{:S(2)}, u32[]{:S(2)}) %collective-permute-start.23) | collective-permute-done | bytes 73760 | tf_op jit(solution)/shard_map/ppermute | solution.py:783
  86.3 2.4 %collective-permute-done.24.refs_2_ = bf16[16,2304]{1,0:T(8,128)(2,1)S(1)} collective-permute-done((bf16[16,2304]{1,0:T(8,128)(2,1)S(1)}, bf16[16,2304]{1,0:T(8,128)(2,1)S(1)}, u32[]{:S(2)}, u32[]{:S(2)}) %collective-permute-start.24) | collective-permute-done | bytes 73760 | tf_op jit(solution)/shard_map/ppermute | solution.py:783
  88.7 4.4 %shard_map.149 = (bf16[16,2176]{1,0:T(8,128)(2,1)S(1)}, f32[16,256]{1,0:T(8,128)S(1)}) custom-call(f32[16,2688]{1,0:T(8,128)S(1)} %get-tuple-element.104.refs_0_, bf16[16,2304]{1,0:T(8,128)(2,1)S(1)} %collective-permute-done.23.refs_1_, bf16[16,2304]{1,0:T(8,128)(2,1)S(1)} %collective-permute-done.24.refs_2_, ...), custom_call_target="tpu_custom_call" | custom-call | tf_op jit(solution)/shard_map/pallas_call | solution.py:693
  93.1 2.0 %collective-permute-start.26 = (bf16[16,2176]{1,0:T(8,128)(2,1)S(1)}, bf16[16,2176]{1,0:T(8,128)(2,1)S(1)}, u32[]{:S(2)}, u32[]{:S(2)}) collective-permute-start(bf16[16,2176]{1,0:T(8,128)(2,1)S(1)} %get-tuple-element.109.own), channel_id=1, source_target_pairs={{0,4},{4,8},{8,12},{12,0},{1,5},{5,9},{9,13},{13,1},{2,6},{6,10},{... | collective-permute-start | bytes 208904 | tf_op jit(solution)/shard_map/ppermute | solution.py:783
  96.2 1.4 %collective-permute-start.28 = (bf16[16,2176]{1,0:T(8,128)(2,1)S(1)}, bf16[16,2176]{1,0:T(8,128)(2,1)S(1)}, u32[]{:S(2)}, u32[]{:S(2)}) collective-permute-start(bf16[16,2176]{1,0:T(8,128)(2,1)S(1)} %get-tuple-element.109.own), channel_id=1, source_target_pairs={{0,12},{4,0},{8,4},{12,8},{1,13},{5,1},{9,5},{13,9},{2,14},{6,2},{... | collective-permute-start | bytes 208904 | tf_op jit(solution)/shard_map/ppermute | solution.py:783
  97.6 2.2 %collective-permute-done.26.refs_0_ = bf16[16,2176]{1,0:T(8,128)(2,1)S(1)} collective-permute-done((bf16[16,2176]{1,0:T(8,128)(2,1)S(1)}, bf16[16,2176]{1,0:T(8,128)(2,1)S(1)}, u32[]{:S(2)}, u32[]{:S(2)}) %collective-permute-start.26) | collective-permute-done | bytes 69664 | tf_op jit(solution)/shard_map/ppermute | solution.py:783
  99.8 2.2 %collective-permute-done.27.refs_1_ = bf16[16,2176]{1,0:T(8,128)(2,1)S(1)} collective-permute-done((bf16[16,2176]{1,0:T(8,128)(2,1)S(1)}, bf16[16,2176]{1,0:T(8,128)(2,1)S(1)}, u32[]{:S(2)}, u32[]{:S(2)}) %collective-permute-start.27) | collective-permute-done | bytes 69664 | tf_op jit(solution)/shard_map/ppermute | solution.py:783
  104.3 1.5 %collective-permute-start.30 = (bf16[16,1024]{1,0:T(8,128)(2,1)S(1)}, bf16[16,1024]{1,0:T(8,128)(2,1)S(1)}, u32[]{:S(2)}, u32[]{:S(2)}) collective-permute-start(bf16[16,1024]{1,0:T(8,128)(2,1)S(1)} %shard_map.152), channel_id=1, source_target_pairs={{0,2},{2,0},{1,3},{3,1},{4,6},{6,4},{5,7},{7,5},{8,10},{10,8},{9,1... | collective-permute-start | bytes 98312 | tf_op jit(solution)/shard_map/ppermute | solution.py:777
  105.8 2.4 %collective-permute-done.30 = bf16[16,1024]{1,0:T(8,128)(2,1)S(1)} collective-permute-done((bf16[16,1024]{1,0:T(8,128)(2,1)S(1)}, bf16[16,1024]{1,0:T(8,128)(2,1)S(1)}, u32[]{:S(2)}, u32[]{:S(2)}) %collective-permute-start.30) | collective-permute-done | bytes 32800 | tf_op jit(solution)/shard_map/ppermute | solution.py:777
  (79 shorter events, 22.8 us)
Async XLA Ops:
  0.6 7.6 %collective-permute-start.1 = (bf16[16,4,128,128]{3,2,1,0:T(8,128)(2,1)}, bf16[16,4,128,128]{3,2,1,0:T(8,128)(2,1)S(1)}, u32[]{:S(2)}, u32[]{:S(2)}) collective-permute-start(bf16[16,4,128,128]{3,2,1,0:T(8,128)(2,1)} %sk.1), channel_id=1, source_target_pairs={{0,1},{1,0},{2,3},{3,2},{4,5},{5,4},{6,7},{7,6},{8,9},{9,8},{10,11... | collective-permute-start | bytes 6291464 | tf_op jit(solution)/shard_map/ppermute | solution.py:777
  1.1 7.1 %collective-permute-start.2 = (bf16[16,4,128,128]{3,2,1,0:T(8,128)(2,1)}, bf16[16,4,128,128]{3,2,1,0:T(8,128)(2,1)}, u32[]{:S(2)}, u32[]{:S(2)}) collective-permute-start(bf16[16,4,128,128]{3,2,1,0:T(8,128)(2,1)} %sv.1), channel_id=1, source_target_pairs={{0,1},{1,0},{2,3},{3,2},{4,5},{5,4},{6,7},{7,6},{8,9},{9,8},{10,11... | collective-permute-start | bytes 6291464 | tf_op jit(solution)/shard_map/ppermute | solution.py:777
  1.2 14.9 %copy-start.2 = (s32[16]{0:T(128)S(1)}, s32[16]{0:T(128)}, u32[]{:S(2)}) copy-start(s32[16]{0:T(128)} %lengths) | copy-start | bytes 196
  6.1 2.1 %collective-permute-start = (f32[16,2688]{1,0:T(8,128)S(1)}, f32[16,2688]{1,0:T(8,128)S(1)}, u32[]{:S(2)}, u32[]{:S(2)}) collective-permute-start(f32[16,2688]{1,0:T(8,128)S(1)} %get-tuple-element.58), channel_id=1, source_target_pairs={{0,1},{1,0},{2,3},{3,2},{4,5},{5,4},{6,7},{7,6},{8,9},{9,8},{10,11... | collective-permute-start | bytes 516104 | tf_op jit(solution)/shard_map/ppermute | solution.py:777
  8.3 14.5 %collective-permute-start.6 = (bf16[1,4,4096,128]{3,2,1,0:T(8,128)(2,1)}, bf16[1,4,4096,128]{3,2,1,0:T(8,128)(2,1)}, u32[]{:S(2)}, u32[]{:S(2)}) collective-permute-start(bf16[1,4,4096,128]{3,2,1,0:T(8,128)(2,1)} %pk.1), channel_id=1, source_target_pairs={{0,1},{1,0},{2,3},{3,2},{4,5},{5,4},{6,7},{7,6},{8,9},{9,8},{10,11... | collective-permute-start | bytes 12582920 | tf_op jit(solution)/shard_map/ppermute | solution.py:777
  8.7 14.1 %collective-permute-start.7 = (bf16[1,4,4096,128]{3,2,1,0:T(8,128)(2,1)}, bf16[1,4,4096,128]{3,2,1,0:T(8,128)(2,1)}, u32[]{:S(2)}, u32[]{:S(2)}) collective-permute-start(bf16[1,4,4096,128]{3,2,1,0:T(8,128)(2,1)} %pv.1), channel_id=1, source_target_pairs={{0,1},{1,0},{2,3},{3,2},{4,5},{5,4},{6,7},{7,6},{8,9},{9,8},{10,11... | collective-permute-start | bytes 12582920 | tf_op jit(solution)/shard_map/ppermute | solution.py:777
  9.2 13.5 %collective-permute-start.3 = (bf16[16,2304]{1,0:T(8,128)(2,1)S(1)}, bf16[16,2304]{1,0:T(8,128)(2,1)S(1)}, u32[]{:S(2)}, u32[]{:S(2)}) collective-permute-start(bf16[16,2304]{1,0:T(8,128)(2,1)S(1)} %get-tuple-element.64.after), channel_id=1, source_target_pairs={{0,4},{4,8},{8,12},{12,0},{1,5},{5,9},{9,13},{13,1},{2,6},{6,10},{... | collective-permute-start | bytes 221192 | tf_op jit(solution)/shard_map/ppermute | solution.py:783
  12.2 10.6 %collective-permute-start.4 = (bf16[16,2304]{1,0:T(8,128)(2,1)S(1)}, bf16[16,2304]{1,0:T(8,128)(2,1)S(1)}, u32[]{:S(2)}, u32[]{:S(2)}) collective-permute-start(bf16[16,2304]{1,0:T(8,128)(2,1)S(1)} %get-tuple-element.65), channel_id=1, source_target_pairs={{0,8},{4,12},{8,0},{12,4},{1,9},{5,13},{9,1},{13,5},{2,10},{6,14},... | collective-permute-start | bytes 221192 | tf_op jit(solution)/shard_map/ppermute | solution.py:783
  14.7 8.0 %collective-permute-start.5 = (bf16[16,2304]{1,0:T(8,128)(2,1)S(1)}, bf16[16,2304]{1,0:T(8,128)(2,1)S(1)}, u32[]{:S(2)}, u32[]{:S(2)}) collective-permute-start(bf16[16,2304]{1,0:T(8,128)(2,1)S(1)} %get-tuple-element.66), channel_id=1, source_target_pairs={{0,12},{4,0},{8,4},{12,8},{1,13},{5,1},{9,5},{13,9},{2,14},{6,2},{... | collective-permute-start | bytes 221192 | tf_op jit(solution)/shard_map/ppermute | solution.py:783
  28.3 9.0 %collective-permute-start.10 = (bf16[16,2176]{1,0:T(8,128)(2,1)S(1)}, bf16[16,2176]{1,0:T(8,128)(2,1)S(1)}, u32[]{:S(2)}, u32[]{:S(2)}) collective-permute-start(bf16[16,2176]{1,0:T(8,128)(2,1)S(1)} %get-tuple-element.76.own), channel_id=1, source_target_pairs={{0,12},{4,0},{8,4},{12,8},{1,13},{5,1},{9,5},{13,9},{2,14},{6,2},{... | collective-permute-start | bytes 208904 | tf_op jit(solution)/shard_map/ppermute | solution.py:783
  32.3 6.6 %collective-permute-start.8 = (bf16[16,2176]{1,0:T(8,128)(2,1)S(1)}, bf16[16,2176]{1,0:T(8,128)(2,1)S(1)}, u32[]{:S(2)}, u32[]{:S(2)}) collective-permute-start(bf16[16,2176]{1,0:T(8,128)(2,1)S(1)} %get-tuple-element.76.own), channel_id=1, source_target_pairs={{0,4},{4,8},{8,12},{12,0},{1,5},{5,9},{9,13},{13,1},{2,6},{6,10},{... | collective-permute-start | bytes 208904 | tf_op jit(solution)/shard_map/ppermute | solution.py:783
  32.3 8.0 %collective-permute-start.9 = (bf16[16,2176]{1,0:T(8,128)(2,1)S(1)}, bf16[16,2176]{1,0:T(8,128)(2,1)S(1)}, u32[]{:S(2)}, u32[]{:S(2)}) collective-permute-start(bf16[16,2176]{1,0:T(8,128)(2,1)S(1)} %get-tuple-element.76.own), channel_id=1, source_target_pairs={{0,8},{4,12},{8,0},{12,4},{1,9},{5,13},{9,1},{13,5},{2,10},{6,14},... | collective-permute-start | bytes 208904 | tf_op jit(solution)/shard_map/ppermute | solution.py:783
  40.6 1.3 %collective-permute-start.11 = (bf16[16,2048]{1,0:T(8,128)(2,1)S(1)}, bf16[16,2048]{1,0:T(8,128)(2,1)S(1)}, u32[]{:S(2)}, u32[]{:S(2)}) collective-permute-start(bf16[16,2048]{1,0:T(8,128)(2,1)S(1)} %shard_map.136.mine), channel_id=1, source_target_pairs={{0,1},{1,0},{2,3},{3,2},{4,5},{5,4},{6,7},{7,6},{8,9},{9,8},{10,11... | collective-permute-start | bytes 196616 | tf_op jit(solution)/shard_map/ppermute | solution.py:777
  42.6 3.9 %collective-permute-start.12 = (bf16[16,1024]{1,0:T(8,128)(2,1)S(1)}, bf16[16,1024]{1,0:T(8,128)(2,1)S(1)}, u32[]{:S(2)}, u32[]{:S(2)}) collective-permute-start(bf16[16,1024]{1,0:T(8,128)(2,1)S(1)} %shard_map.138.mine), channel_id=1, source_target_pairs={{0,2},{2,0},{1,3},{3,1},{4,6},{6,4},{5,7},{7,5},{8,10},{10,8},{9,1... | collective-permute-start | bytes 98312 | tf_op jit(solution)/shard_map/ppermute | solution.py:777
  47.4 1.3 %collective-permute-start.13 = (bf16[16,2688]{1,0:T(8,128)(2,1)S(1)}, bf16[16,2688]{1,0:T(8,128)(2,1)S(1)}, u32[]{:S(2)}, u32[]{:S(2)}) collective-permute-start(bf16[16,2688]{1,0:T(8,128)(2,1)S(1)} %get-tuple-element.91.give), channel_id=1, source_target_pairs={{0,1},{1,0},{2,3},{3,2},{4,5},{5,4},{6,7},{7,6},{8,9},{9,8},{10,11... | collective-permute-start | bytes 258056 | tf_op jit(solution)/shard_map/ppermute | solution.py:777
  48.8 7.0 %collective-permute-start.14 = (bf16[16,2304]{1,0:T(8,128)(2,1)S(1)}, bf16[16,2304]{1,0:T(8,128)(2,1)S(1)}, u32[]{:S(2)}, u32[]{:S(2)}) collective-permute-start(bf16[16,2304]{1,0:T(8,128)(2,1)S(1)} %get-tuple-element.93), channel_id=1, source_target_pairs={{0,4},{4,8},{8,12},{12,0},{1,5},{5,9},{9,13},{13,1},{2,6},{6,10},{... | collective-permute-start | bytes 221192 | tf_op jit(solution)/shard_map/ppermute | solution.py:783
  49.2 8.8 %collective-permute-start.15 = (bf16[16,2304]{1,0:T(8,128)(2,1)S(1)}, bf16[16,2304]{1,0:T(8,128)(2,1)S(1)}, u32[]{:S(2)}, u32[]{:S(2)}) collective-permute-start(bf16[16,2304]{1,0:T(8,128)(2,1)S(1)} %get-tuple-element.94), channel_id=1, source_target_pairs={{0,8},{4,12},{8,0},{12,4},{1,9},{5,13},{9,1},{13,5},{2,10},{6,14},... | collective-permute-start | bytes 221192 | tf_op jit(solution)/shard_map/ppermute | solution.py:783
  51.2 6.8 %collective-permute-start.16 = (bf16[16,2304]{1,0:T(8,128)(2,1)S(1)}, bf16[16,2304]{1,0:T(8,128)(2,1)S(1)}, u32[]{:S(2)}, u32[]{:S(2)}) collective-permute-start(bf16[16,2304]{1,0:T(8,128)(2,1)S(1)} %get-tuple-element.95), channel_id=1, source_target_pairs={{0,12},{4,0},{8,4},{12,8},{1,13},{5,1},{9,5},{13,9},{2,14},{6,2},{... | collective-permute-start | bytes 221192 | tf_op jit(solution)/shard_map/ppermute | solution.py:783
  62.4 6.9 %collective-permute-start.17 = (bf16[16,2176]{1,0:T(8,128)(2,1)S(1)}, bf16[16,2176]{1,0:T(8,128)(2,1)S(1)}, u32[]{:S(2)}, u32[]{:S(2)}) collective-permute-start(bf16[16,2176]{1,0:T(8,128)(2,1)S(1)} %get-tuple-element.99.own), channel_id=1, source_target_pairs={{0,4},{4,8},{8,12},{12,0},{1,5},{5,9},{9,13},{13,1},{2,6},{6,10},{... | collective-permute-start | bytes 208904 | tf_op jit(solution)/shard_map/ppermute | solution.py:783
  63.9 6.9 %collective-permute-start.18 = (bf16[16,2176]{1,0:T(8,128)(2,1)S(1)}, bf16[16,2176]{1,0:T(8,128)(2,1)S(1)}, u32[]{:S(2)}, u32[]{:S(2)}) collective-permute-start(bf16[16,2176]{1,0:T(8,128)(2,1)S(1)} %get-tuple-element.99.own), channel_id=1, source_target_pairs={{0,8},{4,12},{8,0},{12,4},{1,9},{5,13},{9,1},{13,5},{2,10},{6,14},... | collective-permute-start | bytes 208904 | tf_op jit(solution)/shard_map/ppermute | solution.py:783
  65.2 5.6 %collective-permute-start.19 = (bf16[16,2176]{1,0:T(8,128)(2,1)S(1)}, bf16[16,2176]{1,0:T(8,128)(2,1)S(1)}, u32[]{:S(2)}, u32[]{:S(2)}) collective-permute-start(bf16[16,2176]{1,0:T(8,128)(2,1)S(1)} %get-tuple-element.99.own), channel_id=1, source_target_pairs={{0,12},{4,0},{8,4},{12,8},{1,13},{5,1},{9,5},{13,9},{2,14},{6,2},{... | collective-permute-start | bytes 208904 | tf_op jit(solution)/shard_map/ppermute | solution.py:783
  71.1 1.3 %collective-permute-start.20 = (bf16[16,2048]{1,0:T(8,128)(2,1)S(1)}, bf16[16,2048]{1,0:T(8,128)(2,1)S(1)}, u32[]{:S(2)}, u32[]{:S(2)}) collective-permute-start(bf16[16,2048]{1,0:T(8,128)(2,1)S(1)} %shard_map.143.mine), channel_id=1, source_target_pairs={{0,1},{1,0},{2,3},{3,2},{4,5},{5,4},{6,7},{7,6},{8,9},{9,8},{10,11... | collective-permute-start | bytes 196616 | tf_op jit(solution)/shard_map/ppermute | solution.py:777
  73.1 3.9 %collective-permute-start.21 = (bf16[16,1024]{1,0:T(8,128)(2,1)S(1)}, bf16[16,1024]{1,0:T(8,128)(2,1)S(1)}, u32[]{:S(2)}, u32[]{:S(2)}) collective-permute-start(bf16[16,1024]{1,0:T(8,128)(2,1)S(1)} %shard_map.145.mine), channel_id=1, source_target_pairs={{0,2},{2,0},{1,3},{3,1},{4,6},{6,4},{5,7},{7,5},{8,10},{10,8},{9,1... | collective-permute-start | bytes 98312 | tf_op jit(solution)/shard_map/ppermute | solution.py:777
  77.8 1.3 %collective-permute-start.22 = (bf16[16,2688]{1,0:T(8,128)(2,1)S(1)}, bf16[16,2688]{1,0:T(8,128)(2,1)S(1)}, u32[]{:S(2)}, u32[]{:S(2)}) collective-permute-start(bf16[16,2688]{1,0:T(8,128)(2,1)S(1)} %get-tuple-element.103.give), channel_id=1, source_target_pairs={{0,1},{1,0},{2,3},{3,2},{4,5},{5,4},{6,7},{7,6},{8,9},{9,8},{10,11... | collective-permute-start | bytes 258056 | tf_op jit(solution)/shard_map/ppermute | solution.py:777
  79.3 7.0 %collective-permute-start.23 = (bf16[16,2304]{1,0:T(8,128)(2,1)S(1)}, bf16[16,2304]{1,0:T(8,128)(2,1)S(1)}, u32[]{:S(2)}, u32[]{:S(2)}) collective-permute-start(bf16[16,2304]{1,0:T(8,128)(2,1)S(1)} %get-tuple-element.105), channel_id=1, source_target_pairs={{0,4},{4,8},{8,12},{12,0},{1,5},{5,9},{9,13},{13,1},{2,6},{6,10},{... | collective-permute-start | bytes 221192 | tf_op jit(solution)/shard_map/ppermute | solution.py:783
  80.6 8.1 %collective-permute-start.24 = (bf16[16,2304]{1,0:T(8,128)(2,1)S(1)}, bf16[16,2304]{1,0:T(8,128)(2,1)S(1)}, u32[]{:S(2)}, u32[]{:S(2)}) collective-permute-start(bf16[16,2304]{1,0:T(8,128)(2,1)S(1)} %get-tuple-element.106), channel_id=1, source_target_pairs={{0,8},{4,12},{8,0},{12,4},{1,9},{5,13},{9,1},{13,5},{2,10},{6,14},... | collective-permute-start | bytes 221192 | tf_op jit(solution)/shard_map/ppermute | solution.py:783
  82.7 6.0 %collective-permute-start.25 = (bf16[16,2304]{1,0:T(8,128)(2,1)S(1)}, bf16[16,2304]{1,0:T(8,128)(2,1)S(1)}, u32[]{:S(2)}, u32[]{:S(2)}) collective-permute-start(bf16[16,2304]{1,0:T(8,128)(2,1)S(1)} %get-tuple-element.107), channel_id=1, source_target_pairs={{0,12},{4,0},{8,4},{12,8},{1,13},{5,1},{9,5},{13,9},{2,14},{6,2},{... | collective-permute-start | bytes 221192 | tf_op jit(solution)/shard_map/ppermute | solution.py:783
  93.1 6.7 %collective-permute-start.26 = (bf16[16,2176]{1,0:T(8,128)(2,1)S(1)}, bf16[16,2176]{1,0:T(8,128)(2,1)S(1)}, u32[]{:S(2)}, u32[]{:S(2)}) collective-permute-start(bf16[16,2176]{1,0:T(8,128)(2,1)S(1)} %get-tuple-element.109.own), channel_id=1, source_target_pairs={{0,4},{4,8},{8,12},{12,0},{1,5},{5,9},{9,13},{13,1},{2,6},{6,10},{... | collective-permute-start | bytes 208904 | tf_op jit(solution)/shard_map/ppermute | solution.py:783
  95.2 6.8 %collective-permute-start.27 = (bf16[16,2176]{1,0:T(8,128)(2,1)S(1)}, bf16[16,2176]{1,0:T(8,128)(2,1)S(1)}, u32[]{:S(2)}, u32[]{:S(2)}) collective-permute-start(bf16[16,2176]{1,0:T(8,128)(2,1)S(1)} %get-tuple-element.109.own), channel_id=1, source_target_pairs={{0,8},{4,12},{8,0},{12,4},{1,9},{5,13},{9,1},{13,5},{2,10},{6,14},... | collective-permute-start | bytes 208904 | tf_op jit(solution)/shard_map/ppermute | solution.py:783
  96.2 5.8 %collective-permute-start.28 = (bf16[16,2176]{1,0:T(8,128)(2,1)S(1)}, bf16[16,2176]{1,0:T(8,128)(2,1)S(1)}, u32[]{:S(2)}, u32[]{:S(2)}) collective-permute-start(bf16[16,2176]{1,0:T(8,128)(2,1)S(1)} %get-tuple-element.109.own), channel_id=1, source_target_pairs={{0,12},{4,0},{8,4},{12,8},{1,13},{5,1},{9,5},{13,9},{2,14},{6,2},{... | collective-permute-start | bytes 208904 | tf_op jit(solution)/shard_map/ppermute | solution.py:783
  102.3 1.3 %collective-permute-start.29 = (bf16[16,2048]{1,0:T(8,128)(2,1)S(1)}, bf16[16,2048]{1,0:T(8,128)(2,1)S(1)}, u32[]{:S(2)}, u32[]{:S(2)}) collective-permute-start(bf16[16,2048]{1,0:T(8,128)(2,1)S(1)} %shard_map.150.mine), channel_id=1, source_target_pairs={{0,1},{1,0},{2,3},{3,2},{4,5},{5,4},{6,7},{7,6},{8,9},{9,8},{10,11... | collective-permute-start | bytes 196616 | tf_op jit(solution)/shard_map/ppermute | solution.py:777
  104.3 3.9 %collective-permute-start.30 = (bf16[16,1024]{1,0:T(8,128)(2,1)S(1)}, bf16[16,1024]{1,0:T(8,128)(2,1)S(1)}, u32[]{:S(2)}, u32[]{:S(2)}) collective-permute-start(bf16[16,1024]{1,0:T(8,128)(2,1)S(1)} %shard_map.152), channel_id=1, source_target_pairs={{0,2},{2,0},{1,3},{3,1},{4,6},{6,4},{5,7},{7,5},{8,10},{10,8},{9,1... | collective-permute-start | bytes 98312 | tf_op jit(solution)/shard_map/ppermute | solution.py:777
  (4 other events, 32.3 us)
